TPU v7x, 32 devices: a whole 2x2x4 slice. The times are simulated.
32 devices in a mesh: dp: 8 (over z, x), tensor: 4 (over y, core).
Axes of the slice: x: 2, y: 2, z: 4, core: 2. Of those that a mesh axis runs over, the one named last changes fastest.
Arguments:
- layer_in: bfloat16 [16, 532, 768], P('dp', 'tensor'), may hold values from -6 to 6
- cotangent: bfloat16 [16, 532, 768], P('dp', 'tensor'), may hold values from -6 to 6
- doc_ids: int32 [16, 512], P('dp'), may hold values from 0 to 7, never falling along the last dimension, each value on 1 to 128 neighbouring positions
- reset_flags: int32 [16], P('dp'), may hold values 0 or 1
- block_slot: int32 [192], replicated, may hold values from 0 to 191, as said below
- master: float32 [4, 192, 96, 96], P('tensor', 'dp'), as said below
- first_moment: float32 [4, 192, 96, 96], P('tensor', 'dp'), as said below
- second_moment: float32 [4, 192, 96, 96], P('tensor', 'dp'), as said below
- left_stats: float32 [4, 192, 96, 96], P('tensor', 'dp'), as said below
- right_stats: float32 [4, 192, 96, 96], P('tensor', 'dp'), as said below
- left_basis: float32 [4, 192, 96, 96], P('tensor', 'dp'), as said below
- right_basis: float32 [4, 192, 96, 96], P('tensor', 'dp'), as said below
- split_params: float32 [4, 1152], P('tensor'), may hold values from -1.2 to 1.2
- split_first: float32 [4, 1152], P('tensor'), as said below
- split_second: float32 [4, 1152], P('tensor'), as said below
- shared: float32 [16, 768], replicated, as said below
- shared_first: float32 [16, 768], replicated, as said below
- shared_second: float32 [16, 768], replicated, as said below
Outputs:
- layer_out: bfloat16 [16, 532, 768], P('dp', 'tensor')
- grad_in: bfloat16 [16, 532, 768], P('dp', 'tensor')
- new_master: float32 [4, 192, 96, 96], P('tensor', 'dp')
- new_copy: bfloat16 [4, 192, 96, 96], P('tensor', 'dp')
- new_first: float32 [4, 192, 96, 96], P('tensor', 'dp')
- new_second: float32 [4, 192, 96, 96], P('tensor', 'dp')
- new_left: float32 [4, 192, 96, 96], P('tensor', 'dp')
- new_right: float32 [4, 192, 96, 96], P('tensor', 'dp')
- new_split: float32 [4, 1152], P('tensor')
- new_split_first: float32 [4, 1152], P('tensor')
- new_split_second: float32 [4, 1152], P('tensor')
- new_shared: float32 [16, 768], replicated
- new_shared_first: float32 [16, 768], replicated
- new_shared_second: float32 [16, 768], replicated
Inputs may be any that keep to these rules, and one draw needn't show every extreme that they name: `block_slot`: a permutation; slot s is owned by dp index s // 24. `master`: weights scaled by one over the square root of the fan-in of their matrix, four times that for Wo. `first_moment`: of both signs, no entry near zero. `second_moment`: positive. `left_stats`: symmetric with a dominant diagonal. `right_stats`: symmetric with a dominant diagonal. `left_basis`: orthogonal matrices. `right_basis`: orthogonal matrices. `split_first`: of both signs, no entry near zero. `split_second`: positive. `shared`: gains near one, biases small, memory rows of order one. `shared_first`: of both signs, no entry near zero. `shared_second`: positive.
All inputs are finite; a program needn't handle non-finite values. No bound on the sum of `reset_flags` on one device may be relied on, other than what follows from the above.
Results may differ from a plain program's by a relative error of at most 0.018.
Values may be sent and summed in bfloat16 or wider, within the bound.
No kernel may reach another device: no remote copies, remote signals or barrier semaphores. Data moves between devices by JAX's collectives and lax.ppermute only.
A program may use at most 128 MiB of HBM per device.

v0:
```python
import jax
import jax.numpy as jnp
from jax import lax
from jax.sharding import PartitionSpec as P

HEADS = 12
HEAD_DIM = 64
FF = 3072
SEG_TOK = 512
MEM = 10
STEP = 10


highest_precision_flag = lax.Precision.HIGHEST
beta_one = 0.9
beta_two = 0.95
adam_eps = 1e-08
norm_eps = 1e-12
rate_matrix = 0.05
rate_vector = 0.1
rate_shared = 0.75


def unpack(blocks, height, breadth):
    blk_size = blocks.shape[-1]
    leading = blocks.shape[:-3]
    grid = blocks.reshape(leading + (height // blk_size, breadth // blk_size, blk_size, blk_size))
    return jnp.swapaxes(grid, -2, -3).reshape(leading + (height, breadth))


def pack_blocks(matrix, blk_size):
    height, breadth = matrix.shape
    grid = matrix.reshape(height // blk_size, blk_size, breadth // blk_size, blk_size)
    return jnp.swapaxes(grid, -2, -3).reshape(-1, blk_size, blk_size)


def split_blocks(blocks, model_width, tensors):
    blk_size = blocks.shape[-1]
    qkv_cols = 3 * model_width // tensors
    ctx_cols = model_width // tensors
    ffn_cols = FF // tensors
    first_end = model_width * qkv_cols // (blk_size * blk_size)
    second_end = first_end + ctx_cols * model_width // (blk_size * blk_size)
    third_end = second_end + model_width * ffn_cols // (blk_size * blk_size)
    return (
        unpack(blocks[first_end * 0 : first_end], model_width, qkv_cols),
        unpack(blocks[first_end:second_end], ctx_cols, model_width),
        unpack(blocks[second_end:third_end], model_width, ffn_cols),
        unpack(blocks[third_end:], ffn_cols, model_width),
    )


def norm_parts(values, gain_vec, shift_vec):
    centred = values - jnp.mean(values, axis=-1, keepdims=True)
    inverse = lax.rsqrt(jnp.mean(centred * centred, axis=-1, keepdims=True) + norm_eps)
    normed = centred * inverse
    return (normed * gain_vec + shift_vec, normed, inverse)


def norm_back(upstream, normed, inverse, gain_vec):
    scaled = upstream * gain_vec
    result = inverse * (
        scaled
        - jnp.mean(scaled, axis=-1, keepdims=True)
        - normed * jnp.mean(scaled * normed, axis=-1, keepdims=True)
    )
    return (result, jnp.sum(upstream * normed, axis=0), jnp.sum(upstream, axis=0))


def gelu_slope(values):
    return (
        0.5 * (1.0 + jax.scipy.special.erf(values * 0.7071067811865476))
        + values * jnp.exp(-0.5 * values * values) * 0.3989422804014327
    )


def row_product(left_mat, right_mat):
    return jnp.dot(left_mat, right_mat, preferred_element_type=jnp.float32)


def row_product_back(left_mat, right_mat):
    return lax.dot_general(
        left_mat, right_mat, (((1,), (1,)), ((), ())), preferred_element_type=jnp.float32
    )


def inner_rows(left_mat, right_mat):
    return lax.dot_general(
        left_mat, right_mat, (((0,), (0,)), ((), ())), preferred_element_type=jnp.float32
    )


def soap_update(
    weight, grad_mat, first_mom, second_mom, left_stat, right_stat, left_rot, right_rot
):
    turned = jnp.einsum("...ia,...ij->...aj", left_rot, grad_mat, precision=highest_precision_flag)
    turned = jnp.einsum("...aj,...jb->...ab", turned, right_rot, precision=highest_precision_flag)
    new_first = beta_one * first_mom + (1.0 - beta_one) * turned
    new_second = beta_two * second_mom + (1.0 - beta_two) * turned * turned
    direction = (
        new_first
        / (1.0 - beta_one**STEP)
        / (jnp.sqrt(new_second / (1.0 - beta_two**STEP)) + adam_eps)
    )
    back_rot = jnp.einsum(
        "...ia,...ab->...ib", left_rot, direction, precision=highest_precision_flag
    )
    back_rot = jnp.einsum(
        "...ib,...jb->...ij", back_rot, right_rot, precision=highest_precision_flag
    )
    new_weight = weight - rate_matrix * back_rot
    new_left = beta_two * left_stat + (1.0 - beta_two) * jnp.einsum(
        "...ik,...jk->...ij", grad_mat, grad_mat, precision=highest_precision_flag
    )
    new_right = beta_two * right_stat + (1.0 - beta_two) * jnp.einsum(
        "...ki,...kj->...ij", grad_mat, grad_mat, precision=highest_precision_flag
    )
    return (new_weight, new_first, new_second, new_left, new_right)


def adam_update(values, grad_vec, first_mom, second_mom, step_rate):
    new_first = beta_one * first_mom + (1.0 - beta_one) * grad_vec
    new_second = beta_two * second_mom + (1.0 - beta_two) * grad_vec * grad_vec
    direction = (
        new_first
        / (1.0 - beta_one**STEP)
        / (jnp.sqrt(new_second / (1.0 - beta_two**STEP)) + adam_eps)
    )
    return (values - step_rate * direction, new_first, new_second)


def per_device(
    layer_in,
    cotangent,
    doc_ids,
    reset_flags,
    block_slot,
    master,
    first_moment,
    second_moment,
    left_stats,
    right_stats,
    left_basis,
    right_basis,
    split_params,
    split_first,
    split_second,
    shared,
    shared_first,
    shared_second,
):
    tensors = lax.axis_size("tensor")
    tensor_pos = lax.axis_index("tensor")
    micro_count = layer_in.shape[0]
    local_rows = layer_in.shape[1]
    model_width = layer_in.shape[2]
    all_rows = local_rows * tensors
    blk_size = master.shape[-1]
    slot_count = block_slot.shape[0]
    ctx_cols = model_width // tensors
    heads_here = HEADS // tensors
    head_scale = HEAD_DIM ** (-0.5)
    gathered = lax.all_gather(master.astype(jnp.bfloat16), "dp", axis=1, tiled=True)[0]
    blocks = jnp.take(gathered, block_slot, axis=0)
    w_qkv, w_out, up_weight, down_weight = split_blocks(blocks, model_width, tensors)
    split_vals = split_params[0]
    q_bias = split_vals[:ctx_cols]
    v_bias = split_vals[ctx_cols : 2 * ctx_cols]
    feedforward_up_bias = split_vals[2 * ctx_cols :]
    qkv_bias = jnp.concatenate([q_bias, jnp.zeros_like(q_bias), v_bias])
    attn_bias, gain_one, shift_one = (shared[0], shared[1], shared[2])
    ffn_out_bias, gain_two, shift_two = (shared[3], shared[4], shared[5])
    init_memory = shared[6:]
    row_ids = tensor_pos * local_rows + jnp.arange(local_rows)
    full_ids = jnp.arange(all_rows)
    mem_onehot = (row_ids[:, None] == jnp.arange(MEM)[None, :]).astype(jnp.float32)
    is_memory = (full_ids < MEM) | (full_ids >= MEM + SEG_TOK)
    acc_qkv = jnp.zeros(w_qkv.shape, jnp.float32)
    acc_out = jnp.zeros(w_out.shape, jnp.float32)
    acc_up = jnp.zeros(up_weight.shape, jnp.float32)
    acc_down = jnp.zeros(down_weight.shape, jnp.float32)
    acc_split = jnp.zeros(split_vals.shape, jnp.float32)
    acc_shared = jnp.zeros(shared.shape, jnp.float32)
    out_list = []
    grad_list = []
    for micro_step in range(micro_count):
        reset_now = (reset_flags[micro_step] == 1).astype(jnp.float32)
        read_local = mem_onehot * reset_now
        replaced = jnp.sum(read_local, axis=1) > 0.5
        x_zero = jnp.where(
            replaced[:, None],
            jnp.dot(read_local, init_memory, precision=highest_precision_flag),
            layer_in[micro_step].astype(jnp.float32),
        )
        whole_in = lax.all_gather(x_zero.astype(jnp.bfloat16), "tensor", axis=0, tiled=True)
        proj_b = (jnp.dot(whole_in, w_qkv, preferred_element_type=jnp.float32) + qkv_bias).astype(
            jnp.bfloat16
        )
        query_part = proj_b[:, :ctx_cols].reshape(all_rows, heads_here, HEAD_DIM)
        key_part = proj_b[:, ctx_cols : 2 * ctx_cols].reshape(all_rows, heads_here, HEAD_DIM)
        value_part = proj_b[:, 2 * ctx_cols :].reshape(all_rows, heads_here, HEAD_DIM)
        doc_full = jnp.concatenate(
            [jnp.zeros((MEM,), jnp.int32), doc_ids[micro_step], jnp.zeros((MEM,), jnp.int32)]
        )
        visible = is_memory[:, None] | is_memory[None, :] | (doc_full[:, None] == doc_full[None, :])
        raw_scores = jnp.einsum(
            "qhd,khd->hqk", query_part, key_part, preferred_element_type=jnp.float32
        )
        scores = jnp.where(visible[None], raw_scores * head_scale, -1000000000.0)
        row_max = jnp.max(scores, axis=-1, keepdims=True)
        expo_vals = jnp.exp(scores - row_max)
        attn_probs = expo_vals / jnp.sum(expo_vals, axis=-1, keepdims=True)
        probs_b = attn_probs.astype(jnp.bfloat16)
        context = jnp.einsum(
            "hqk,khd->qhd", probs_b, value_part, preferred_element_type=jnp.float32
        )
        context = context.reshape(all_rows, ctx_cols).astype(jnp.bfloat16)
        attn_own = lax.psum_scatter(
            row_product(context, w_out).astype(jnp.bfloat16),
            "tensor",
            scatter_dimension=0,
            tiled=True,
        ).astype(jnp.float32)
        h_one, normed_one, inverse_one = norm_parts(
            attn_own + attn_bias + x_zero, gain_one, shift_one
        )
        hidden_input_rows = lax.all_gather(h_one.astype(jnp.bfloat16), "tensor", axis=0, tiled=True)
        preactivation_values = (
            jnp.dot(hidden_input_rows, up_weight, preferred_element_type=jnp.float32)
            + feedforward_up_bias
        )
        act_b = jax.nn.gelu(preactivation_values, approximate=False).astype(jnp.bfloat16)
        ffn_own = lax.psum_scatter(
            row_product(act_b, down_weight).astype(jnp.bfloat16),
            "tensor",
            scatter_dimension=0,
            tiled=True,
        ).astype(jnp.float32)
        layer_rows, normed_two, inverse_two = norm_parts(
            ffn_own + ffn_out_bias + h_one, gain_two, shift_two
        )
        out_list.append(layer_rows.astype(jnp.bfloat16))
        grad_out = cotangent[micro_step].astype(jnp.float32)
        d_two, grad_gain_two, grad_shift_two = norm_back(
            grad_out, normed_two, inverse_two, gain_two
        )
        d_two_all = lax.all_gather(d_two.astype(jnp.bfloat16), "tensor", axis=0, tiled=True)
        acc_down = acc_down + inner_rows(act_b, d_two_all)
        d_act = lax.dot_general(
            d_two_all, down_weight, (((1,), (1,)), ((), ())), preferred_element_type=jnp.float32
        )
        d_pre = d_act * gelu_slope(preactivation_values)
        d_pre_b = d_pre.astype(jnp.bfloat16)
        acc_up = acc_up + inner_rows(hidden_input_rows, d_pre_b)
        d_hidden_own = lax.psum_scatter(
            row_product_back(d_pre_b, up_weight).astype(jnp.bfloat16),
            "tensor",
            scatter_dimension=0,
            tiled=True,
        ).astype(jnp.float32)
        d_one, grad_gain_one, grad_shift_one = norm_back(
            d_hidden_own + d_two, normed_one, inverse_one, gain_one
        )
        d_one_all = lax.all_gather(d_one.astype(jnp.bfloat16), "tensor", axis=0, tiled=True)
        acc_out = acc_out + inner_rows(context, d_one_all)
        d_context = lax.dot_general(
            d_one_all, w_out, (((1,), (1,)), ((), ())), preferred_element_type=jnp.float32
        )
        d_context = d_context.astype(jnp.bfloat16).reshape(all_rows, heads_here, HEAD_DIM)
        d_value = jnp.einsum("hqk,qhd->khd", probs_b, d_context, preferred_element_type=jnp.float32)
        d_probs = jnp.einsum(
            "qhd,khd->hqk", d_context, value_part, preferred_element_type=jnp.float32
        )
        row_dot = jnp.sum(d_probs * attn_probs, axis=-1, keepdims=True)
        d_scores = (attn_probs * (d_probs - row_dot) * head_scale).astype(jnp.bfloat16)
        d_query = jnp.einsum("hqk,khd->qhd", d_scores, key_part, preferred_element_type=jnp.float32)
        d_key = jnp.einsum("hqk,qhd->khd", d_scores, query_part, preferred_element_type=jnp.float32)
        d_query = d_query.reshape(all_rows, ctx_cols)
        d_key = d_key.reshape(all_rows, ctx_cols)
        d_value = d_value.reshape(all_rows, ctx_cols)
        d_proj_b = jnp.concatenate([d_query, d_key, d_value], axis=1).astype(jnp.bfloat16)
        acc_qkv = acc_qkv + inner_rows(whole_in, d_proj_b)
        d_in_own = lax.psum_scatter(
            row_product_back(d_proj_b, w_qkv).astype(jnp.bfloat16),
            "tensor",
            scatter_dimension=0,
            tiled=True,
        ).astype(jnp.float32)
        d_zero = d_in_own + d_one
        memory_grad = jnp.dot(read_local.T, d_zero, precision=highest_precision_flag)
        grad_list.append(jnp.where(replaced[:, None], 0.0, d_zero).astype(jnp.bfloat16))
        acc_split = acc_split + jnp.concatenate(
            [jnp.sum(d_query, axis=0), jnp.sum(d_value, axis=0), jnp.sum(d_pre, axis=0)]
        )
        norm_rows = jnp.stack(
            [
                jnp.sum(d_one, axis=0),
                grad_gain_one,
                grad_shift_one,
                jnp.sum(d_two, axis=0),
                grad_gain_two,
                grad_shift_two,
            ]
        )
        acc_shared = acc_shared + jnp.concatenate([norm_rows, memory_grad], axis=0)
    packed = jnp.concatenate(
        [
            pack_blocks(acc_qkv, blk_size),
            pack_blocks(acc_out, blk_size),
            pack_blocks(acc_up, blk_size),
            pack_blocks(acc_down, blk_size),
        ],
        axis=0,
    )
    inverse_slot = (
        jnp.zeros((slot_count,), jnp.int32)
        .at[block_slot]
        .set(jnp.arange(slot_count, dtype=jnp.int32))
    )
    owned_grads = lax.psum_scatter(
        jnp.take(packed, inverse_slot, axis=0), "dp", scatter_dimension=0, tiled=True
    )
    picker = (jnp.arange(tensors) == tensor_pos).astype(jnp.float32)[:, None]
    total_split, total_shared = lax.psum(
        (picker * acc_split[None, :], acc_shared), ("dp", "tensor")
    )
    grad_split = lax.dynamic_slice_in_dim(total_split, tensor_pos, 1, 0)
    new_master, new_first, new_second, new_left, new_right = soap_update(
        master[0],
        owned_grads,
        first_moment[0],
        second_moment[0],
        left_stats[0],
        right_stats[0],
        left_basis[0],
        right_basis[0],
    )
    new_split, new_split_first, new_split_second = adam_update(
        split_params, grad_split, split_first, split_second, rate_vector
    )
    new_shared, new_shared_first, new_shared_second = adam_update(
        shared, total_shared, shared_first, shared_second, rate_shared
    )
    return (
        jnp.stack(out_list),
        jnp.stack(grad_list),
        new_master[None],
        new_master[None].astype(jnp.bfloat16),
        new_first[None],
        new_second[None],
        new_left[None],
        new_right[None],
        new_split,
        new_split_first,
        new_split_second,
        new_shared,
        new_shared_first,
        new_shared_second,
    )


def solution(mesh):
    placed = (
        P("dp", "tensor", None),
        P("dp", "tensor", None),
        P("dp", None),
        P("dp"),
        P(),
        P("tensor", "dp", None, None),
        P("tensor", "dp", None, None),
        P("tensor", "dp", None, None),
        P("tensor", "dp", None, None),
        P("tensor", "dp", None, None),
        P("tensor", "dp", None, None),
        P("tensor", "dp", None, None),
        P("tensor", None),
        P("tensor", None),
        P("tensor", None),
        P(),
        P(),
        P(),
    )
    return jax.shard_map(
        per_device,
        mesh=mesh,
        in_specs=placed,
        out_specs=(
            P("dp", "tensor", None),
            P("dp", "tensor", None),
            P("tensor", "dp", None, None),
            P("tensor", "dp", None, None),
            P("tensor", "dp", None, None),
            P("tensor", "dp", None, None),
            P("tensor", "dp", None, None),
            P("tensor", "dp", None, None),
            P("tensor", None),
            P("tensor", None),
            P("tensor", None),
            P(),
            P(),
            P(),
        ),
        check_vma=False,
    )
```

profile of v0, /device:TPU:8, one launch (start us, length us, event | category | flops | bytes accessed | tf_op | source)
XLA Modules:
  0.0 792.4 jit_solution(11524912805326661941)
XLA Ops:
  7.3 2.3 bitcast_convert_fusion
  13.6 8.9 %all-gather = bf16[4,133,768]{2,1,0:T(8,128)(2,1)S(1)} all-gather(bf16[1,133,768]{2,1,0:T(8,128)(2,1)S(1)} %convert_bitcast_fusion.8), channel_id=1, replica_groups=mesh['dp'=8,'tensor'=4] {'tensor'}, dimensions={0}, use_global_device_ids=true | all-gather | bytes 1021440 | tf_op jit(solution)/shard_map/all_gather | solution.py:195
  24.9 9.0 %all-gather.2 = bf16[4,133,768]{2,1,0:T(8,128)(2,1)S(1)} all-gather(bf16[1,133,768]{2,1,0:T(8,128)(2,1)S(1)} %convert_bitcast_fusion.7), channel_id=1, replica_groups=mesh['dp'=8,'tensor'=4] {'tensor'}, dimensions={0}, use_global_device_ids=true | all-gather | bytes 1021440 | tf_op jit(solution)/shard_map/all_gather | solution.py:195
  43.4 47.6 %all-gather.10.cloned.1.call-done = bf16[1,192,96,96]{3,2,0,1:T(8,128)(2,1)} async-done(((bf16[1,24,96,96]{3,2,0,1:T(8,128)(2,1)}), bf16[1,192,96,96]{3,2,0,1:T(8,128)(2,1)}) %all-gather.10.cloned.1.call-update) | async-done | bytes 3538960 | tf_op jit(solution)/shard_map/all_gather | solution.py:163
  90.9 5.9 gather_fusion
  96.8 2.8 broadcast_select_fusion.1
  105.8 2.9 reshape.444
  116.6 3.6 fusion.235
  120.2 2.8 convolution_convert_fusion.9
  123.5 4.6 fusion.234
  128.1 2.7 convolution_convert_fusion.8
  131.3 19.1 %fusion.209 = (bf16[136,768]{1,0:T(8,128)(2,1)}, bf16[136,768]{1,0:T(8,128)(2,1)}) fusion(bf16[532,768]{1,0:T(8,128)(2,1)S(1)} %convolution_convert_fusion.5, bf16[532,768]{1,0:T(8,128)(2,1)S(1)} %convolution_convert_fusion.7), kind=kCustom, calls=%all-reduce-scatter.11 | all-reduce-scatter fusion | flops 835585 | bytes 2052608
  153.2 3.3 collective-permute-start.2
  160.5 4.2 reshape.453
  166.5 3.9 reshape.451
  176.7 8.7 %all-gather.1 = bf16[4,133,768]{2,1,0:T(8,128)(2,1)S(1)} all-gather(bf16[1,133,768]{2,1,0:T(8,128)(2,1)S(1)} %get-tuple-element.167), channel_id=1, replica_groups=mesh['dp'=8,'tensor'=4] {'tensor'}, dimensions={0}, use_global_device_ids=true | all-gather | bytes 1021440 | tf_op jit(solution)/shard_map/all_gather | solution.py:227
  186.5 9.0 %all-gather.3 = bf16[4,133,768]{2,1,0:T(8,128)(2,1)S(1)} all-gather(bf16[1,133,768]{2,1,0:T(8,128)(2,1)S(1)} %get-tuple-element.168), channel_id=1, replica_groups=mesh['dp'=8,'tensor'=4] {'tensor'}, dimensions={0}, use_global_device_ids=true | all-gather | bytes 1021440 | tf_op jit(solution)/shard_map/all_gather | solution.py:227
  196.6 2.5 fusion.242
  199.1 8.1 %fusion.44 = (bf16[532,768]{1,0:T(8,128)(2,1)S(1)}, bf16[532,768]{1,0:T(8,128)(2,1)S(1)}, f32[532,768]{1,0:T(8,128)}) fusion(f32[768]{0:T(1024)S(1)} %copy-done.109, f32[532,768]{1,0:T(8,128)S(1)} %fusion.242, bf16[532,768]{1,0:T(8,128)(2,1)S(1)} %copy-done.49, bf16[768,768]{1,0:T(8,128)(2,1)S(1)} %copy-done.28), kind=kOutput, calls=%fused_computation.49 | convolution fusion | flops 681504768 | bytes 6902784 | tf_op jit(solution)/shard_map/dot_general | solution.py:229
  210.2 18.8 %fusion.208 = (bf16[136,768]{1,0:T(8,128)(2,1)S(1)}, bf16[136,768]{1,0:T(8,128)(2,1)S(1)}) fusion(bf16[532,768]{1,0:T(8,128)(2,1)} %convolution_convert_fusion.4, bf16[532,768]{1,0:T(8,128)(2,1)S(1)} %convolution_convert_fusion.6), kind=kCustom, calls=%all-reduce-scatter.10 | all-reduce-scatter fusion | flops 835585 | bytes 2052608
  230.4 3.4 collective-permute-start.3
  243.0 9.3 %all-gather.4 = bf16[4,133,768]{2,1,0:T(8,128)(2,1)} all-gather(bf16[1,133,768]{2,1,0:T(8,128)(2,1)S(1)} %convert_bitcast_fusion.6), channel_id=1, replica_groups=mesh['dp'=8,'tensor'=4] {'tensor'}, dimensions={0}, use_global_device_ids=true | all-gather | bytes 1021440 | tf_op jit(solution)/shard_map/all_gather | solution.py:247
  252.3 2.3 reshape.513
  254.6 4.1 fusion.246
  262.3 2.5 fusion.135
  267.2 9.4 %all-gather.6 = bf16[4,133,768]{2,1,0:T(8,128)(2,1)} all-gather(bf16[1,133,768]{2,1,0:T(8,128)(2,1)S(1)} %convert_bitcast_fusion.4), channel_id=1, replica_groups=mesh['dp'=8,'tensor'=4] {'tensor'}, dimensions={0}, use_global_device_ids=true | all-gather | bytes 1021440 | tf_op jit(solution)/shard_map/all_gather | solution.py:247
  278.9 4.8 fusion.241
  283.8 2.5 convolution_add_fusion
  286.3 4.4 reshape.471
  290.7 4.3 copy.150
  296.8 19.7 %fusion.207 = (bf16[136,768]{1,0:T(8,128)(2,1)S(1)}, bf16[136,768]{1,0:T(8,128)(2,1)}) fusion(bf16[532,768]{1,0:T(8,128)(2,1)} %convolution_convert_fusion.2, bf16[532,768]{1,0:T(8,128)(2,1)} %convolution_convert_fusion.3), kind=kCustom, calls=%all-reduce-scatter.9 | all-reduce-scatter fusion | flops 835585 | bytes 2052608
  318.5 3.4 collective-permute-start.6
  321.9 4.7 convolution_add_fusion.1
  326.6 4.4 reshape.469
  331.0 4.1 copy.149
  335.1 2.3 concatenate.66
  337.4 2.5 multiply_reduce_fusion.3
  340.2 2.8 fusion.217
  343.8 8.7 %all-gather.5 = bf16[4,133,768]{2,1,0:T(8,128)(2,1)S(1)} all-gather(bf16[1,133,768]{2,1,0:T(8,128)(2,1)S(1)} %convert_bitcast_fusion.5), channel_id=1, replica_groups=mesh['dp'=8,'tensor'=4] {'tensor'}, dimensions={0}, use_global_device_ids=true | all-gather | bytes 1021440 | tf_op jit(solution)/shard_map/all_gather | solution.py:264
  357.7 9.4 %all-gather.7 = bf16[4,133,768]{2,1,0:T(8,128)(2,1)S(1)} all-gather(bf16[1,133,768]{2,1,0:T(8,128)(2,1)S(1)} %convert_bitcast_fusion.3), channel_id=1, replica_groups=mesh['dp'=8,'tensor'=4] {'tensor'}, dimensions={0}, use_global_device_ids=true | all-gather | bytes 1021440 | tf_op jit(solution)/shard_map/all_gather | solution.py:264
  367.8 3.7 fusion.225
  371.5 2.8 fusion.244
  374.4 8.1 %fusion.85 = bf16[3,64,532]{2,1,0:T(8,128)(2,1)} fusion(bf16[532,3,64]{0,2,1:T(8,128)(2,1)S(1)} %bitcast.318, f32[3,532,532]{1,2,0:T(8,128)} %fusion.244, f32[3,532,532]{1,2,0:T(8,128)} %get-tuple-element.192, f32[3,532]{1,0:T(4,128)S(1)} %copy-done.124), kind=kOutput, calls=%fused_computation.123 | convolution fusion | flops 114728992 | bytes 7207536 | tf_op jit(solution)/shard_map/hqk,qhd->khd/dot_general | solution.py:277
  382.5 8.1 %fusion.226 = (f32[3,64]{1,0:T(4,128)S(1)}, bf16[532,3,64]{0,2,1:T(8,128)(2,1)}) fusion(bf16[532,3,64]{0,2,1:T(8,128)(2,1)S(1)} %bitcast.314, f32[3,532,532]{1,2,0:T(8,128)} %fusion.244, f32[3,532,532]{1,2,0:T(8,128)} %get-tuple-element.192, f32[3,532]{1,0:T(4,128)S(1)} %copy-done.124), kind=kOutput, calls=%fused_computation.354 | convolution fusion | flops 114830944 | bytes 7208304 | tf_op jit(solution)/shard_map/hqk,khd->qhd/dot_general | solution.py:276
  390.6 3.1 fusion.227
  393.7 2.9 fusion.243
  396.6 7.4 fusion.88
  404.0 7.4 fusion.228
  412.1 3.0 convolution_convert_fusion.1
  415.1 3.1 fusion.143
  421.5 2.4 convolution_convert_fusion
  424.0 18.8 %fusion.206 = (bf16[136,768]{1,0:T(8,128)(2,1)S(1)}, bf16[136,768]{1,0:T(8,128)(2,1)S(1)}) fusion(bf16[532,768]{1,0:T(8,128)(2,1)S(1)} %convolution_convert_fusion, bf16[532,768]{1,0:T(8,128)(2,1)S(1)} %copy-done.55), kind=kCustom, calls=%all-reduce-scatter.8 | all-reduce-scatter fusion | flops 835585 | bytes 2052608
  446.0 3.5 collective-permute-start.7
  449.4 2.7 convolution_add_fusion.2
  452.2 2.4 reshape.465
  459.6 7.7 pad_maximum_fusion
  467.4 8.8 %gather_fusion.1 = f32[192,96,96]{2,1,0:T(8,128)} fusion(f32[192,96,96]{2,1,0:T(8,128)} %pad_maximum_fusion, s32[1024]{0:T(1024)} %pad_clamp_fusion), kind=kCustom, calls=%fused_computation.1 | custom fusion | bytes 14156544 | tf_op jit(solution)/shard_map/jit(_take)/gather | solution.py:321
  480.3 8.1 %broadcast_select_fusion = f32[192,96,96]{2,1,0:T(8,128)} fusion(f32[192,96,96]{2,1,0:T(8,128)} %gather_fusion.1, pred[192]{0:T(512)(128)(4,1)S(1)} %copy-done.115), kind=kLoop, calls=%fused_computation.8 | loop fusion | flops 1769472 | bytes 14155968 | tf_op jit(solution)/shard_map/jit(_take)/select_n | solution.py:321
  491.9 108.3 %all-reduce.23.cloned.1.call-done = (f32[4,1152]{1,0:T(4,128)}, f32[16,768]{1,0:T(8,128)}) async-done(((f32[4,1152]{1,0:T(4,128)}, f32[16,768]{1,0:T(8,128)}), (f32[4,1152]{1,0:T(4,128)}, f32[16,768]{1,0:T(8,128)})) %all-reduce.23.cloned.1.call-update) | async-done | bytes 67600 | tf_op jit(solution)/shard_map/psum | solution.py:324
  603.0 162.6 %reduce-scatter.18.cloned.1.call-done = f32[24,96,96]{2,1,0:T(8,128)} async-done(((f32[192,96,96]{2,1,0:T(8,128)}), f32[24,96,96]{2,1,0:T(8,128)}) %reduce-scatter.18.cloned.1.call-update) | async-done | bytes 884752 | tf_op jit(solution)/shard_map/reduce_scatter | solution.py:320
  765.6 3.3 fusion.97
  774.5 2.5 fusion.74
  778.9 3.2 fusion.76
  782.1 3.6 fusion.75
  (420 shorter events, 108.0 us)
Async XLA Ops:
  7.2 758.4 %copy-start = (f32[1,24,96,96]{3,2,1,0:T(8,128)S(1)}, f32[1,24,96,96]{3,2,1,0:T(8,128)}, u32[]{:S(2)}) copy-start(f32[1,24,96,96]{3,2,1,0:T(8,128)} %param.28) | copy-start | bytes 2654212
  7.2 5.0 copy-start.56
  7.2 83.7 %all-gather.10.cloned.1.call-start = ((), (), s32[]{:S(2)}) async-start(), calls=%async_computation.1 | async-start | bytes 5308416 | tf_op jit(solution)/shard_map/all_gather | solution.py:163
  9.6 590.6 %all-reduce.23.cloned.1.call-start = ((), (), s32[]{:S(2)}) async-start(), calls=%async_computation.3 | async-start | bytes 135168 | tf_op jit(solution)/shard_map/psum | solution.py:324
  11.5 12.0 %copy-start.83 = (s32[133]{0:T(256)}, s32[133]{0:T(256)S(1)}, u32[]{:S(2)}) copy-start(s32[133]{0:T(256)S(1)} %iota_add_fusion) | copy-start | bytes 1600
  11.6 12.0 %copy-start.105 = (pred[133]{0:T(512)(128)(4,1)}, pred[133]{0:T(512)(128)(4,1)S(1)}, u32[]{:S(2)}) copy-start(pred[133]{0:T(512)(128)(4,1)S(1)} %get-tuple-element.204) | copy-start | bytes 403
  24.1 9.9 %copy-start.116 = (u32[32]{0:T(128)S(1)}, u32[32]{0:T(128)}, u32[]{:S(2)}) copy-start(u32[32]{0:T(128)} %constant.196) | copy-start | bytes 388
  24.1 11.3 %copy-start.114 = (s32[192]{0:T(256)S(1)}, s32[192]{0:T(256)}, u32[]{:S(2)}) copy-start(s32[192]{0:T(256)} %param.22) | copy-start | bytes 2308
  24.2 13.1 %copy-start.85 = (f32[1,1152]{1,0:T(1,128)S(1)}, f32[1,1152]{1,0:T(1,128)}, u32[]{:S(2)}) copy-start(f32[1,1152]{1,0:T(1,128)} %param.30) | copy-start | bytes 13828
  24.2 13.9 %copy-start.112 = (s32[2,512]{1,0:T(2,128)S(1)}, s32[2,512]{1,0:T(2,128)}, u32[]{:S(2)}) copy-start(s32[2,512]{1,0:T(2,128)} %param.20) | copy-start | bytes 12292
  24.2 15.8 %copy-start.23 = (bf16[2,133,768]{2,0,1:T(2,128)(2,1)S(1)}, bf16[2,133,768]{2,0,1:T(2,128)(2,1)}, u32[]{:S(2)}) copy-start(bf16[2,133,768]{2,0,1:T(2,128)(2,1)} %param.19) | copy-start | bytes 1225732
  34.1 74.6 %copy-start.7 = (bf16[532,768]{1,0:T(8,128)(2,1)}, bf16[532,768]{1,0:T(8,128)(2,1)S(1)}, u32[]{:S(2)}) copy-start(bf16[532,768]{1,0:T(8,128)(2,1)S(1)} %reshape.509) | copy-start | bytes 2451460
  104.1 4.6 copy-start.111
  123.1 5.1 copy-start.33
  130.9 19.6 %copy-start.34 = (bf16[3,64,532]{2,1,0:T(8,128)(2,1)}, bf16[3,64,532]{2,1,0:T(8,128)(2,1)S(1)}, u32[]{:S(2)}) copy-start(bf16[3,64,532]{2,1,0:T(8,128)(2,1)S(1)} %convolution_convert_fusion.8) | copy-start | bytes 612868
  151.9 18.5 %collective-permute-start = (bf16[9,768]{1,0:T(8,128)(2,1)S(1)}, bf16[9,768]{1,0:T(8,128)(2,1)S(1)}, u32[]{:S(2)}, u32[]{:S(2)}) collective-permute-start(bf16[9,768]{1,0:T(8,128)(2,1)S(1)} %slice.135), channel_id=1, source_target_pairs={{0,1},{1,2},{2,3},{4,5},{5,6},{6,7},{8,9},{9,10},{10,11},{12,13},{... | collective-permute-start | bytes 41480
  153.2 19.3 %collective-permute-start.2 = (bf16[9,768]{1,0:T(8,128)(2,1)S(1)}, bf16[9,768]{1,0:T(8,128)(2,1)S(1)}, u32[]{:S(2)}, u32[]{:S(2)}) collective-permute-start(bf16[9,768]{1,0:T(8,128)(2,1)S(1)} %slice.137), channel_id=1, source_target_pairs={{0,1},{1,2},{2,3},{4,5},{5,6},{6,7},{8,9},{9,10},{10,11},{12,13},{... | collective-permute-start | bytes 41480
  166.5 6.0 copy-start.44
  166.5 8.1 %copy-start.12 = (f32[133,768]{1,0:T(8,128)S(1)}, f32[133,768]{1,0:T(8,128)}, u32[]{:S(2)}) copy-start(f32[133,768]{1,0:T(8,128)} %copy-done.11) | copy-start | bytes 1225732
  166.5 8.1 %copy-start.14 = (f32[133,768]{1,0:T(8,128)S(1)}, f32[133,768]{1,0:T(8,128)}, u32[]{:S(2)}) copy-start(f32[133,768]{1,0:T(8,128)} %copy-done.13) | copy-start | bytes 1225732
  166.5 8.1 %copy-start.94 = (f32[768]{0:T(1024)S(1)}, f32[768]{0:T(1024)}, u32[]{:S(2)}) copy-start(f32[768]{0:T(1024)} %get-tuple-element.88) | copy-start | bytes 9220
  176.0 10.5 %copy-start.74 = (f32[133]{0:T(256)}, f32[133]{0:T(256)S(1)}, u32[]{:S(2)}) copy-start(f32[133]{0:T(256)S(1)} %broadcast_multiply_fusion.12) | copy-start | bytes 1600
  176.0 10.5 %copy-start.71 = (f32[133]{0:T(256)}, f32[133]{0:T(256)S(1)}, u32[]{:S(2)}) copy-start(f32[133]{0:T(256)S(1)} %broadcast_multiply_fusion.10) | copy-start | bytes 1600
  176.2 10.3 %copy-start.78 = (f32[133]{0:T(256)}, f32[133]{0:T(256)S(1)}, u32[]{:S(2)}) copy-start(f32[133]{0:T(256)S(1)} %add_rsqrt_fusion.1) | copy-start | bytes 1600
  176.5 10.0 %copy-start.81 = (f32[133]{0:T(256)}, f32[133]{0:T(256)S(1)}, u32[]{:S(2)}) copy-start(f32[133]{0:T(256)S(1)} %add_rsqrt_fusion.3) | copy-start | bytes 1600
  199.1 8.1 %copy-start.118 = (f32[532,768]{1,0:T(8,128)}, f32[532,768]{1,0:T(8,128)S(1)}, u32[]{:S(2)}) copy-start(f32[532,768]{1,0:T(8,128)S(1)} %fusion.242) | copy-start | bytes 4902916
  199.1 8.1 %copy-start.31 = (bf16[768,768]{1,0:T(8,128)(2,1)S(1)}, bf16[768,768]{1,0:T(8,128)(2,1)}, u32[]{:S(2)}) copy-start(bf16[768,768]{1,0:T(8,128)(2,1)} %reshape.453) | copy-start | bytes 3538948
  229.1 7.8 collective-permute-start.1
  230.4 6.9 collective-permute-start.3
  278.9 4.9 copy-start.15
  278.9 4.9 copy-start.16
  278.9 4.9 copy-start.53
  317.2 17.9 %collective-permute-start.4 = (bf16[9,768]{1,0:T(8,128)(2,1)S(1)}, bf16[9,768]{1,0:T(8,128)(2,1)S(1)}, u32[]{:S(2)}, u32[]{:S(2)}) collective-permute-start(bf16[9,768]{1,0:T(8,128)(2,1)S(1)} %slice.139), channel_id=1, source_target_pairs={{0,1},{1,2},{2,3},{4,5},{5,6},{6,7},{8,9},{9,10},{10,11},{12,13},{... | collective-permute-start | bytes 41480
  318.5 21.4 %collective-permute-start.6 = (bf16[9,768]{1,0:T(8,128)(2,1)S(1)}, bf16[9,768]{1,0:T(8,128)(2,1)S(1)}, u32[]{:S(2)}, u32[]{:S(2)}) collective-permute-start(bf16[9,768]{1,0:T(8,128)(2,1)S(1)} %slice.141), channel_id=1, source_target_pairs={{0,1},{1,2},{2,3},{4,5},{5,6},{6,7},{8,9},{9,10},{10,11},{12,13},{... | collective-permute-start | bytes 41480
  331.0 6.4 copy-start.75
  331.0 6.4 copy-start.82
  335.1 5.1 copy-start.72
  335.1 5.1 copy-start.79
  374.4 8.1 %copy-start.63 = (bf16[532,192]{0,1:T(8,128)(2,1)S(1)}, bf16[532,192]{0,1:T(8,128)(2,1)}, u32[]{:S(2)}) copy-start(bf16[532,192]{0,1:T(8,128)(2,1)} %copy.137) | copy-start | bytes 612868
  382.5 8.1 %copy-start.68 = (bf16[532,192]{0,1:T(8,128)(2,1)S(1)}, bf16[532,192]{0,1:T(8,128)(2,1)}, u32[]{:S(2)}) copy-start(bf16[532,192]{0,1:T(8,128)(2,1)} %convolution_convert_fusion.11) | copy-start | bytes 612868
  382.5 8.1 %copy-start.122 = (f32[3,532]{1,0:T(4,128)S(1)}, f32[3,532]{1,0:T(4,128)}, u32[]{:S(2)}) copy-start(f32[3,532]{1,0:T(4,128)} %copy-done.121) | copy-start | bytes 19156
  396.6 7.4 copy-start.61
  424.0 25.5 %copy-start.67 = (bf16[532,3,64]{0,2,1:T(8,128)(2,1)S(1)}, bf16[532,3,64]{0,2,1:T(8,128)(2,1)}, u32[]{:S(2)}) copy-start(bf16[532,3,64]{0,2,1:T(8,128)(2,1)} %get-tuple-element.149) | copy-start | bytes 612868
  444.1 33.6 %collective-permute-start.5 = (bf16[9,768]{1,0:T(8,128)(2,1)}, bf16[9,768]{1,0:T(8,128)(2,1)}, u32[]{:S(2)}, u32[]{:S(2)}) collective-permute-start(bf16[9,768]{1,0:T(8,128)(2,1)} %slice.140), channel_id=1, source_target_pairs={{0,1},{1,2},{2,3},{4,5},{5,6},{6,7},{8,9},{9,10},{10,11},{12,13},{... | collective-permute-start | bytes 41480
  446.0 30.2 %collective-permute-start.7 = (bf16[9,768]{1,0:T(8,128)(2,1)}, bf16[9,768]{1,0:T(8,128)(2,1)}, u32[]{:S(2)}, u32[]{:S(2)}) collective-permute-start(bf16[9,768]{1,0:T(8,128)(2,1)} %slice.142), channel_id=1, source_target_pairs={{0,1},{1,2},{2,3},{4,5},{5,6},{6,7},{8,9},{9,10},{10,11},{12,13},{... | collective-permute-start | bytes 41480
  459.5 7.7 copy-start.88
  459.6 7.7 copy-start.87
  459.6 7.7 copy-start.91
  459.6 7.7 copy-start.92
  459.6 7.8 copy-start.90
  459.6 7.8 copy-start.89
  467.4 8.9 %copy-start.43 = (bf16[136,768]{1,0:T(8,128)(2,1)S(1)}, bf16[136,768]{1,0:T(8,128)(2,1)}, u32[]{:S(2)}) copy-start(bf16[136,768]{1,0:T(8,128)(2,1)} %copy-done.42) | copy-start | bytes 626692
  467.4 9.9 %copy-start.6 = (f32[133,768]{1,0:T(8,128)S(1)}, f32[133,768]{1,0:T(8,128)}, u32[]{:S(2)}) copy-start(f32[133,768]{1,0:T(8,128)} %copy-done.5) | copy-start | bytes 1225732
  467.4 9.9 %copy-start.84 = (s32[133]{0:T(256)S(1)}, s32[133]{0:T(256)}, u32[]{:S(2)}) copy-start(s32[133]{0:T(256)} %copy-done.83) | copy-start | bytes 1600
  467.4 10.3 %copy-start.41 = (bf16[136,768]{1,0:T(8,128)(2,1)S(1)}, bf16[136,768]{1,0:T(8,128)(2,1)}, u32[]{:S(2)}) copy-start(bf16[136,768]{1,0:T(8,128)(2,1)} %copy-done.40) | copy-start | bytes 626692
  480.2 285.4 %reduce-scatter.18.cloned.1.call-start = ((), (), s32[]{:S(2)}) async-start(), calls=%async_computation.2 | async-start | bytes 10616832 | tf_op jit(solution)/shard_map/reduce_scatter | solution.py:320
  490.5 109.7 %copy-start.57 = (f32[16,768]{1,0:T(8,128)S(1)}, f32[16,768]{1,0:T(8,128)}, u32[]{:S(2)}) copy-start(f32[16,768]{1,0:T(8,128)} %param.33) | copy-start | bytes 147460
  490.5 109.7 %copy-start.69 = (f32[16,768]{1,0:T(8,128)S(1)}, f32[16,768]{1,0:T(8,128)}, u32[]{:S(2)}) copy-start(f32[16,768]{1,0:T(8,128)} %param.34) | copy-start | bytes 147460
  490.5 109.7 %copy-start.70 = (f32[16,768]{1,0:T(8,128)S(1)}, f32[16,768]{1,0:T(8,128)}, u32[]{:S(2)}) copy-start(f32[16,768]{1,0:T(8,128)} %param.35) | copy-start | bytes 147460
  490.5 111.1 %copy-start.86 = (f32[1,1152]{1,0:T(1,128)S(1)}, f32[1,1152]{1,0:T(1,128)}, u32[]{:S(2)}) copy-start(f32[1,1152]{1,0:T(1,128)} %param.30) | copy-start | bytes 13828
  490.5 111.1 %copy-start.101 = (f32[1,1152]{1,0:T(1,128)S(1)}, f32[1,1152]{1,0:T(1,128)}, u32[]{:S(2)}) copy-start(f32[1,1152]{1,0:T(1,128)} %param.31) | copy-start | bytes 13828
  490.5 111.1 %copy-start.102 = (f32[1,1152]{1,0:T(1,128)S(1)}, f32[1,1152]{1,0:T(1,128)}, u32[]{:S(2)}) copy-start(f32[1,1152]{1,0:T(1,128)} %param.32) | copy-start | bytes 13828
  603.0 165.9 %copy-start.8 = (f32[1,24,96,96]{3,2,1,0:T(8,128)S(1)}, f32[1,24,96,96]{3,2,1,0:T(8,128)}, u32[]{:S(2)}) copy-start(f32[1,24,96,96]{3,2,1,0:T(8,128)} %param.29) | copy-start | bytes 2654212
  777.0 5.1 copy-start.10
  (72 other events, 201.1 us)
Sparse Core Ops, SparseCore 0:
  10.8 80.0 all-gather.9
  480.3 119.8 all-reduce.22
  603.8 161.7 reduce-scatter.17
where the time goes:
time: 803 us; the launch traced here: 792 us
  waiting for transfers between devices  319 us (40%)
  blocking collectives  149 us (19%)
  matrix products  133 us (17%)
  local copies, waits for them, and re-layouts  110 us (14%)
  other arithmetic  45.7 us (6%)
  starting transfers between devices  19.4 us (2%)
  between operations  17.6 us (2%)
    reduce_scatter x1, waiting for transfers between devices, per_device(): lax.psum_scatter(jnp.take(packed, inverse_slot, axis=0), 'dp', scatter_di...  163 us
    psum x1, waiting for transfers between devices, per_device(): lax.psum((picker * acc_split[None, :], acc_shared), ('dp', 'tensor'))  108 us
    unnamed x4, blocking collectives  76.4 us
    all_gather x1, waiting for transfers between devices, per_device(): lax.all_gather(master.astype(jnp.bfloat16), 'dp', axis=1, tiled=True)[0]  47.6 us
    unnamed x277, local copies, waits for them, and re-layouts  35.3 us
    reshape x8, local copies, waits for them, and re-layouts, pack_blocks(): matrix.reshape(height // blk_size, blk_size, breadth // blk_size, blk_size)  23.1 us
    dot_general x8, matrix products, inner_rows(): lax.dot_general(left_mat, right_mat, (((0,), (0,)), ((), ())), preferred_...  22.2 us
    unnamed x8, starting transfers between devices  19.3 us
  transfers between devices with their start and end apart: 11, of which 3 were waited for; matrix products, arithmetic and copies ran while one was open for 11% of the time, Pallas kernels for 0%

commit v1 on v0

v1 whole, which is shorter than its diff:
```python
import functools

import jax
import jax.numpy as jnp
from jax import lax
from jax.experimental import pallas as pl
from jax.experimental.pallas import tpu as pltpu
from jax.sharding import PartitionSpec as P

HEADS = 12
HEAD_DIM = 64
FF = 3072
SEG_TOK = 512
MEM = 10
STEP = 10

highest = lax.Precision.HIGHEST
beta_one = 0.9
beta_two = 0.95
adam_eps = 1e-08
norm_eps = 1e-12
rate_matrix = 0.05
rate_vector = 0.1
rate_shared = 0.75

BF = jnp.bfloat16
F32 = jnp.float32
VMEM_LIMIT = 56 * 1024 * 1024
VMEM_SPEC = pl.BlockSpec(memory_space=pltpu.VMEM)
SMEM_SPEC = pl.BlockSpec(memory_space=pltpu.SMEM)
ANY_SPEC = pl.BlockSpec(memory_space=pl.ANY)
GROUP = 4
TILES = 3
RP = 144
AG_ORDER = (0, 1, 3, 2)
RS_ORDER = (2, 3, 1, 0)


def sds(shape, dtype):
    return jax.ShapeDtypeStruct(shape, dtype)


def params(**kw):
    return pltpu.CompilerParams(vmem_limit_bytes=VMEM_LIMIT, **kw)


def xor_pairs(size, step):
    return [(i, i ^ step) for i in range(size)]


def pack_plain(blocks):
    lead = blocks.shape[:-3]
    grp = blocks.reshape(lead + (-1, GROUP, 96, 96))
    last = jnp.swapaxes(grp[..., 3, :, :].reshape(lead + (-1, 96, 3, 32)), -3, -2)
    return jnp.concatenate([grp[..., :3, :, :], last], axis=-1)


def unpack_plain(groups):
    last = jnp.swapaxes(groups[..., 96:], -3, -2)
    last = last.reshape(groups.shape[:-3] + (1, 96, 96))
    grp = jnp.concatenate([groups[..., :96], last], axis=-3)
    return grp.reshape(groups.shape[:-4] + (-1, 96, 96))


def pack_body(m_ref, out_ref):
    for g in range(out_ref.shape[0]):
        last = m_ref[GROUP * g + 3].astype(BF)
        for k in range(TILES):
            out_ref[g, k] = jnp.concatenate(
                [m_ref[GROUP * g + k].astype(BF), last[:, 32 * k : 32 * k + 32]], axis=-1
            )


def pack_owned(blocks):
    n = blocks.shape[0] // GROUP
    return pl.pallas_call(
        pack_body,
        out_shape=sds((n, TILES, 96, 128), BF),
        in_specs=[VMEM_SPEC],
        out_specs=VMEM_SPEC,
        compiler_params=params(),
        name="pack_owned",
    )(blocks)


def weights_body(n_pieces, places, pos_ref, me_ref, *refs):
    pieces = refs[:n_pieces]
    wqkv_ref, wo_ref, w1_ref, w2_ref, al, sem = refs[n_pieces:]
    dp, t = me_ref[0], me_ref[1]
    copies = []
    for ref, (jt, jd, first) in zip(pieces, places):
        n = ref.shape[-4]
        if jd is None:
            copy = pltpu.make_async_copy(ref, al.at[:, :, pl.ds(0, TILES)], sem)
        else:
            base = (dp ^ jd) * (al.shape[1] // 8) + first
            copy = pltpu.make_async_copy(
                ref, al.at[t ^ jt, pl.ds(base, n), pl.ds(0, TILES)], sem
            )
        copy.start()
        copies.append(copy)
    for copy in copies:
        copy.wait()
    groups = al.shape[1]

    for s in range(4):

        def fix(g, carry, s=s):
            al[s, g, 3, :, 0:96] = jnp.concatenate(
                [al[s, g, k, :, 96:128] for k in range(TILES)], axis=-1
            )
            return carry

        lax.fori_loop(0, groups, fix, 0, unroll=8)

    def block(s, b):
        p = pos_ref[b]
        return al[s, p // GROUP, p % GROUP][:, :96]

    def strip(i, carry):
        rows = pl.ds(pl.multiple_of(i * 96, 96), 96)
        for part in range(3):
            for half in range(2):
                col = part * 768 + half * 384
                wqkv_ref[rows, col : col + 384] = jnp.concatenate(
                    [block(2 * half + j // 2, i * 6 + part * 2 + j % 2) for j in range(4)],
                    axis=-1,
                )
        for s in range(4):
            for half in range(2):
                w1_ref[rows, s * 768 + half * 384 : s * 768 + half * 384 + 384] = jnp.concatenate(
                    [block(s, 64 + i * 8 + half * 4 + j) for j in range(4)], axis=-1
                )
                lower = pl.ds(pl.multiple_of(s * 768 + i * 96, 96), 96)
                w2_ref[lower, half * 384 : half * 384 + 384] = jnp.concatenate(
                    [block(s, 128 + i * 8 + half * 4 + j) for j in range(4)], axis=-1
                )
        for half in range(2):
            wo_ref[rows, half * 384 : half * 384 + 384] = jnp.concatenate(
                [block(i // 2, 48 + (i % 2) * 8 + half * 4 + j) for j in range(4)], axis=-1
            )
        return carry

    lax.fori_loop(0, 8, strip, 0)


def build_weights(pos, me, pieces, places, slots):
    return pl.pallas_call(
        functools.partial(weights_body, len(pieces), places),
        out_shape=(
            sds((768, 2304), BF),
            sds((768, 768), BF),
            sds((768, 3072), BF),
            sds((3072, 768), BF),
        ),
        in_specs=[SMEM_SPEC, SMEM_SPEC] + [ANY_SPEC] * len(pieces),
        out_specs=(VMEM_SPEC,) * 4,
        scratch_shapes=[
            pltpu.VMEM((4, slots // GROUP, GROUP, 96, 128), BF),
            pltpu.SemaphoreType.DMA,
        ],
        compiler_params=params(),
        name="build_weights",
    )(pos, me, *pieces)


def grads_body(places, pos_ref, me_ref, gq_ref, go_ref, g1_ref, g2_ref, *refs):
    outs = refs[: len(places)]
    al, sem = refs[len(places) :]
    groups = al.shape[1]

    def put(s, b, blk):
        p = pos_ref[b]
        al[s, p // GROUP, p % GROUP, :, 0:96] = blk

    def strip(i, carry):
        rows = pl.ds(pl.multiple_of(i * 96, 96), 96)
        for s in range(2):
            strip_q = gq_ref[s, rows, :]
            for j in range(6):
                put(s, i * 6 + j, strip_q[:, 96 * j : 96 * j + 96])
            for ref, first in ((g1_ref, 64), (g2_ref, 128)):
                for half in range(2):
                    vals = ref[s, rows, half * 384 : half * 384 + 384]
                    for j in range(4):
                        put(s, first + i * 8 + half * 4 + j, vals[:, 96 * j : 96 * j + 96])
        return carry

    lax.fori_loop(0, 8, strip, 0)
    for i in range(2):
        for s in range(2):
            for half in range(2):
                vals = go_ref[s, i * 96 : i * 96 + 96, half * 384 : half * 384 + 384]
                for j in range(4):
                    put(s, 48 + i * 8 + half * 4 + j, vals[:, 96 * j : 96 * j + 96])
    for s in range(2):

        def fix(g, carry, s=s):
            last = al[s, g, 3]
            for k in range(TILES):
                al[s, g, k, :, 96:128] = last[:, 32 * k : 32 * k + 32]
            return carry

        lax.fori_loop(0, groups, fix, 0, unroll=8)

    dp, y = me_ref[0], me_ref[1] // 2
    copies = []
    for ref, (jy, jd, first) in zip(outs, places):
        if jd is None:
            copy = pltpu.make_async_copy(al.at[:, :, pl.ds(0, TILES)], ref, sem)
        else:
            base = (dp ^ jd) * (groups // 8) + first
            copy = pltpu.make_async_copy(
                al.at[y ^ jy, pl.ds(base, ref.shape[0]), pl.ds(0, TILES)], ref, sem
            )
        copy.start()
        copies.append(copy)
    for copy in copies:
        copy.wait()


def pack_grads(pos, me, gq, go, g1, g2, places, out_shapes, slots):
    return pl.pallas_call(
        functools.partial(grads_body, places),
        out_shape=tuple(sds(s, BF) for s in out_shapes),
        in_specs=[SMEM_SPEC, SMEM_SPEC] + [VMEM_SPEC] * 4,
        out_specs=(ANY_SPEC,) * len(places),
        scratch_shapes=[
            pltpu.VMEM((2, slots // GROUP, GROUP, 96, 128), BF),
            pltpu.SemaphoreType.DMA,
        ],
        compiler_params=params(),
        name="pack_grads",
    )(pos, me, gq, go, g1, g2)


def attend_body(cq_ref, ck_ref, q_ref, ka_ref, va_ref, kb_ref, vb_ref, ctx_ref, p_ref, vis):
    @pl.when(pl.program_id(0) == 0)
    def _():
        cq, ck = cq_ref[...], ck_ref[...]
        seen = ((cq == -1) | (ck == -1) | (cq == ck)) & (ck != -2)
        vis[...] = jnp.where(seen, 1.0, 0.0)

    q = q_ref[...]
    k = jnp.concatenate([ka_ref[...], kb_ref[...]], axis=0)
    v = jnp.concatenate([va_ref[...], vb_ref[...]], axis=0)
    lane = lax.broadcasted_iota(jnp.int32, q.shape, 1)
    outs = []
    for h in range(2):
        mine = (lane < HEAD_DIM) if h == 0 else (lane >= HEAD_DIM)
        qh = jnp.where(mine, q, jnp.zeros_like(q))
        raw = lax.dot_general(qh, k, (((1,), (1,)), ((), ())), preferred_element_type=F32)
        scores = jnp.where(vis[...] > 0.5, raw * HEAD_DIM ** (-0.5), -1000000000.0)
        e = jnp.exp(scores - jnp.max(scores, axis=-1, keepdims=True))
        p = (e / jnp.sum(e, axis=-1, keepdims=True)).astype(BF)
        p_ref[h] = p
        outs.append(jnp.dot(p, v, preferred_element_type=F32))
    ctx_ref[...] = jnp.where(lane < HEAD_DIM, outs[0], outs[1]).astype(BF)


def attend(code_q, code_k, proj, kv_other):
    rows = proj.shape[0]
    pairs = HEADS // 2

    def col(off):
        return pl.BlockSpec((rows, 128), lambda h: (0, h + off))

    return pl.pallas_call(
        attend_body,
        grid=(pairs,),
        out_shape=(sds((rows, 768), BF), sds((HEADS, rows, 2 * rows), BF)),
        in_specs=[
            pl.BlockSpec((rows, 1), lambda h: (0, 0)),
            pl.BlockSpec((1, 2 * rows), lambda h: (0, 0)),
            col(0),
            col(pairs),
            col(2 * pairs),
            col(0),
            col(pairs),
        ],
        out_specs=(col(0), pl.BlockSpec((2, rows, 2 * rows), lambda h: (h, 0, 0))),
        scratch_shapes=[pltpu.VMEM((rows, 2 * rows), F32)],
        compiler_params=params(),
        name="attend",
    )(code_q, code_k, proj, proj, proj, kv_other, kv_other)


def attend_back_body(
    dc_ref, p_ref, q_ref, ka_ref, va_ref, kb_ref, vb_ref, dq_ref, dka_ref, dva_ref, dkb_ref, dvb_ref
):
    q, dc = q_ref[...], dc_ref[...]
    rows = q.shape[0]
    k = jnp.concatenate([ka_ref[...], kb_ref[...]], axis=0)
    v = jnp.concatenate([va_ref[...], vb_ref[...]], axis=0)
    lane = lax.broadcasted_iota(jnp.int32, q.shape, 1)
    lane_all = lax.broadcasted_iota(jnp.int32, k.shape, 1)
    dqs, dks, dvs = [], [], []
    for h in range(2):
        mine = (lane < HEAD_DIM) if h == 0 else (lane >= HEAD_DIM)
        dch = jnp.where(mine, dc, jnp.zeros_like(dc))
        p = p_ref[h]
        dvs.append(lax.dot_general(p, dc, (((0,), (0,)), ((), ())), preferred_element_type=F32))
        dp = lax.dot_general(dch, v, (((1,), (1,)), ((), ())), preferred_element_type=F32)
        pf = p.astype(F32)
        row = jnp.sum(dp * pf, axis=-1, keepdims=True)
        ds = (pf * (dp - row) * HEAD_DIM ** (-0.5)).astype(BF)
        dqs.append(jnp.dot(ds, k, preferred_element_type=F32))
        dks.append(lax.dot_general(ds, q, (((0,), (0,)), ((), ())), preferred_element_type=F32))
    dq_ref[...] = jnp.where(lane < HEAD_DIM, dqs[0], dqs[1])
    dk = jnp.where(lane_all < HEAD_DIM, dks[0], dks[1])
    dv = jnp.where(lane_all < HEAD_DIM, dvs[0], dvs[1])
    dka_ref[...] = dk[:rows]
    dkb_ref[...] = dk[rows:]
    dva_ref[...] = dv[:rows]
    dvb_ref[...] = dv[rows:]


def attend_back(dctx, probs, proj, kv_other):
    rows = proj.shape[0]
    pairs = HEADS // 2

    def col(off):
        return pl.BlockSpec((rows, 128), lambda h: (0, h + off))

    return pl.pallas_call(
        attend_back_body,
        grid=(pairs,),
        out_shape=(sds((rows, 768), F32),) * 5,
        in_specs=[
            col(0),
            pl.BlockSpec((2, rows, 2 * rows), lambda h: (h, 0, 0)),
            col(0),
            col(pairs),
            col(2 * pairs),
            col(0),
            col(pairs),
        ],
        out_specs=(col(0),) * 5,
        compiler_params=params(),
        name="attend_back",
    )(dctx, probs, proj, proj, proj, kv_other, kv_other)


def norm_parts(values, gain_vec, shift_vec):
    centred = values - jnp.mean(values, axis=-1, keepdims=True)
    inverse = lax.rsqrt(jnp.mean(centred * centred, axis=-1, keepdims=True) + norm_eps)
    normed = centred * inverse
    return (normed * gain_vec + shift_vec, normed, inverse)


def norm_back(upstream, normed, inverse, gain_vec):
    scaled = upstream * gain_vec
    result = inverse * (
        scaled
        - jnp.mean(scaled, axis=-1, keepdims=True)
        - normed * jnp.mean(scaled * normed, axis=-1, keepdims=True)
    )
    return (result, jnp.sum(upstream * normed, axis=0), jnp.sum(upstream, axis=0))


def dot(left, right):
    return jnp.dot(left, right, preferred_element_type=F32)


def dot_back(left, right):
    return lax.dot_general(left, right, (((1,), (1,)), ((), ())), preferred_element_type=F32)


def inner_rows(left, right):
    return lax.dot_general(left, right, (((0,), (0,)), ((), ())), preferred_element_type=F32)


def soap_update(weight, grad, first_mom, second_mom, left_stat, right_stat, left_rot, right_rot):
    turned = jnp.einsum("...ia,...ij->...aj", left_rot, grad, precision=highest)
    turned = jnp.einsum("...aj,...jb->...ab", turned, right_rot, precision=highest)
    new_first = beta_one * first_mom + (1.0 - beta_one) * turned
    new_second = beta_two * second_mom + (1.0 - beta_two) * turned * turned
    direction = (
        new_first
        / (1.0 - beta_one**STEP)
        / (jnp.sqrt(new_second / (1.0 - beta_two**STEP)) + adam_eps)
    )
    back = jnp.einsum("...ia,...ab->...ib", left_rot, direction, precision=highest)
    back = jnp.einsum("...ib,...jb->...ij", back, right_rot, precision=highest)
    new_weight = weight - rate_matrix * back
    new_left = beta_two * left_stat + (1.0 - beta_two) * jnp.einsum(
        "...ik,...jk->...ij", grad, grad, precision=highest
    )
    new_right = beta_two * right_stat + (1.0 - beta_two) * jnp.einsum(
        "...ki,...kj->...ij", grad, grad, precision=highest
    )
    return (new_weight, new_first, new_second, new_left, new_right)


def adam_update(values, grad_vec, first_mom, second_mom, step_rate):
    new_first = beta_one * first_mom + (1.0 - beta_one) * grad_vec
    new_second = beta_two * second_mom + (1.0 - beta_two) * grad_vec * grad_vec
    direction = (
        new_first
        / (1.0 - beta_one**STEP)
        / (jnp.sqrt(new_second / (1.0 - beta_two**STEP)) + adam_eps)
    )
    return (values - step_rate * direction, new_first, new_second)


def per_device(
    n_dp,
    n_tensor,
    layer_in,
    cotangent,
    doc_ids,
    reset_flags,
    block_slot,
    master,
    first_moment,
    second_moment,
    left_stats,
    right_stats,
    left_basis,
    right_basis,
    split_params,
    split_first,
    split_second,
    shared,
    shared_first,
    shared_second,
):
    meshed = n_dp == 8 and master.shape[1] % GROUP == 0
    dp = lax.axis_index("dp")
    t = lax.axis_index("tensor")
    y, c = t // 2, t % 2
    me = jnp.stack([dp, t])
    slots = block_slot.shape[0]
    quarter = layer_in.shape[1]

    def swap(axis, step):
        size = n_dp if axis == "dp" else n_tensor
        return lambda v: lax.ppermute(v, axis, xor_pairs(size, step))

    core, yswap, xswap = swap("tensor", 1), swap("tensor", 2), swap("dp", 1)

    def two_quarters(arr):
        other = yswap(lax.dynamic_index_in_dim(arr, 1 - y, 0, keepdims=False))
        mine = lax.dynamic_index_in_dim(arr, y, 0, keepdims=False)
        return mine, other

    def pad_rows(arr):
        return jnp.pad(arr, ((0, RP - quarter), (0, 0)))

    in_mine, in_other = two_quarters(layer_in)

    if meshed:
        own = pack_owned(master[0])
        half = own.shape[0] // 2
        pieces, places = [], []
        for jz in AG_ORDER:
            unit = own if jz == 0 else swap("dp", 2 * jz)(own)
            x_unit, y_unit = xswap(unit), yswap(unit)
            diag_a, diag_b = yswap(x_unit[:half]), xswap(y_unit[half:])
            for val, jy, jx, first in (
                (unit, 0, 0, 0),
                (x_unit, 0, 1, 0),
                (y_unit, 1, 0, 0),
                (diag_a, 1, 1, 0),
                (diag_b, 1, 1, half),
            ):
                for jc in range(2):
                    pieces.append(val if jc == 0 else core(val))
                    places.append((2 * jy + jc, 2 * jz + jx, first))
    else:
        every = lax.all_gather(master.astype(BF), "dp", axis=1, tiled=True)
        every = lax.all_gather(every, "tensor", axis=0, tiled=True)
        pieces, places = [pack_plain(every)], [(0, None, 0)]
    w_qkv, w_out, w_up, w_down = build_weights(block_slot, me, pieces, tuple(places), slots)

    pair = jnp.concatenate([split_params, core(split_params)], axis=0)
    quad = jnp.concatenate([pair, yswap(pair)], axis=0)
    quad = jnp.take(quad, jnp.arange(4) ^ t, axis=0)
    qb, vb, up_bias = (quad[:, :192].reshape(-1), quad[:, 192:384].reshape(-1), quad[:, 384:].reshape(-1))
    qkv_bias = jnp.concatenate([qb, jnp.zeros_like(qb), vb])
    attn_bias, gain_one, shift_one = (shared[0], shared[1], shared[2])
    ffn_bias, gain_two, shift_two = (shared[3], shared[4], shared[5])

    docs = lax.dynamic_index_in_dim(doc_ids, y, 0, keepdims=False)
    edge = jnp.full((MEM,), -1, jnp.int32)
    codes = jnp.concatenate([edge, docs, edge]).reshape(4, quarter)
    codes = jnp.pad(codes, ((0, 0), (0, RP - quarter)), constant_values=-2)
    codes = jnp.take(codes, t ^ jnp.array([0, 2, 1, 3]), axis=0).reshape(-1)
    code_q, code_k = codes[: 2 * RP, None], codes[None, :]

    reset_now = lax.dynamic_index_in_dim(reset_flags, y, 0, keepdims=False) == 1
    has_read = (c == 0) & reset_now
    row = jnp.arange(2 * RP)
    replaced = ((row - y * RP >= 0) & (row - y * RP < MEM) & has_read)[:, None]
    memory_rows = jnp.pad(shared[6:], ((0, RP - MEM), (0, 0)))
    memory_rows = jnp.concatenate([memory_rows, memory_rows], axis=0)
    x_zero = jnp.where(
        replaced,
        memory_rows,
        jnp.concatenate([pad_rows(in_mine), pad_rows(in_other)], axis=0).astype(F32),
    )
    x_in = x_zero.astype(BF)

    proj = (dot(x_in, w_qkv) + qkv_bias).astype(BF)
    kv_other = core(proj[:, 768:])
    context, probs = attend(code_q, code_k, proj, kv_other)
    h_one, normed_one, inverse_one = norm_parts(
        dot(context, w_out) + attn_bias + x_zero, gain_one, shift_one
    )
    h_in = h_one.astype(BF)
    pre = dot(h_in, w_up) + up_bias
    cdf = 0.5 * (1.0 + lax.erf(pre * 0.7071067811865476))
    act = (pre * cdf).astype(BF)
    slope = cdf + pre * jnp.exp(-0.5 * pre * pre) * 0.3989422804014327
    rows_out, normed_two, inverse_two = norm_parts(
        dot(act, w_down) + ffn_bias + h_one, gain_two, shift_two
    )

    def to_owner(arr):
        mine, other = arr[:quarter], yswap(arr[RP : RP + quarter])
        both = jnp.stack([mine, other])
        return jnp.where(y == 0, both, both[::-1])

    layer_out = to_owner(rows_out.astype(BF))

    cot_mine, cot_other = two_quarters(cotangent)
    grad_out = jnp.concatenate([pad_rows(cot_mine), pad_rows(cot_other)], axis=0).astype(F32)
    d_two, gain_two_g, shift_two_g = norm_back(grad_out, normed_two, inverse_two, gain_two)
    d_two_b = d_two.astype(BF)
    d_pre = dot_back(d_two_b, w_down) * slope
    d_pre_b = d_pre.astype(BF)
    d_hidden = dot_back(d_pre_b, w_up) + d_two
    d_one, gain_one_g, shift_one_g = norm_back(d_hidden, normed_one, inverse_one, gain_one)
    d_one_b = d_one.astype(BF)
    d_context = dot_back(d_one_b, w_out).astype(BF)
    d_q, dk_a, dv_a, dk_b, dv_b = attend_back(d_context, probs, proj, kv_other)
    back = core(jnp.concatenate([dk_b, dv_b], axis=1).astype(BF)).astype(F32)
    d_proj = jnp.concatenate([d_q, dk_a + back[:, :768], dv_a + back[:, 768:]], axis=1).astype(BF)
    d_zero = dot_back(d_proj, w_qkv) + d_one
    grad_in = to_owner(jnp.where(replaced, 0.0, d_zero).astype(BF))
    memory_grad = lax.dynamic_slice_in_dim(d_zero, y * RP, MEM, 0)
    memory_grad = jnp.where(has_read, memory_grad, 0.0)

    def both_rows(arr):
        return jnp.concatenate([arr, core(arr)], axis=0)

    def own_slices(arr, width):
        parts = arr.reshape(arr.shape[0], -1, 2, 2, width)
        mine = lax.dynamic_index_in_dim(parts, c, 3, keepdims=False)
        other = core(lax.dynamic_index_in_dim(parts, 1 - c, 3, keepdims=False))
        parts = jnp.concatenate([mine, other], axis=0)
        return [parts[:, :, k].reshape(parts.shape[0], -1) for k in range(2)]

    x_rows, h_rows, d2_rows, d1_rows = (both_rows(v) for v in (x_in, h_in, d_two_b, d_one_b))
    act_s, dpre_s = own_slices(act, 768), own_slices(d_pre_b, 768)
    ctx_s, dproj_s = own_slices(context, 192), own_slices(d_proj, 192)
    g_down = jnp.stack([inner_rows(act_s[k], d2_rows).astype(BF) for k in range(2)])
    g_up = jnp.stack([inner_rows(h_rows, dpre_s[k]).astype(BF) for k in range(2)])
    g_out = jnp.stack([inner_rows(ctx_s[k], d1_rows).astype(BF) for k in range(2)])
    g_qkv = jnp.stack([inner_rows(x_rows, dproj_s[k]).astype(BF) for k in range(2)])

    if meshed:
        per = master.shape[1] // GROUP
        half = per // 2
        places, shapes = [], []
        for jz in RS_ORDER:
            for jy, jx, first, n in ((0, 0, 0, per), (0, 1, 0, per), (1, 0, 0, per), (1, 1, 0, half), (1, 1, half, per - half)):
                places.append((jy, 2 * jz + jx, first))
                shapes.append((n, TILES, 96, 128))
        packed = pack_grads(block_slot, me, g_qkv, g_out, g_up, g_down, tuple(places), shapes, slots)

        def plus(a, b):
            return (a.astype(F32) + b.astype(F32)).astype(BF)

        total = None
        for n, jz in enumerate(RS_ORDER):
            own, x_unit, y_unit, diag_a, diag_b = packed[5 * n : 5 * n + 5]
            from_y, from_x = yswap(diag_a), xswap(diag_b)
            x_unit = jnp.concatenate([plus(x_unit[:half], from_y), x_unit[half:]], axis=0)
            y_unit = jnp.concatenate([y_unit[:half], plus(y_unit[half:], from_x)], axis=0)
            part = own.astype(F32) + xswap(x_unit).astype(F32) + yswap(y_unit).astype(F32)
            if jz:
                part = swap("dp", 2 * jz)(part.astype(BF)).astype(F32)
            total = part if total is None else total + part
        owned = unpack_plain(total)
    else:
        packed = pack_grads(
            block_slot,
            me,
            g_qkv,
            g_out,
            g_up,
            g_down,
            ((0, None, 0),),
            [(2, slots // GROUP, TILES, 96, 128)],
            slots,
        )[0]
        blocks = unpack_plain(packed)
        blocks = lax.psum_scatter(blocks, "dp", scatter_dimension=1, tiled=True)
        mine = lax.dynamic_index_in_dim(blocks, y, 0, keepdims=False)
        other = yswap(lax.dynamic_index_in_dim(blocks, 1 - y, 0, keepdims=False))
        owned = mine.astype(F32) + other.astype(F32)

    vec = jnp.concatenate(
        [
            jnp.stack(
                [
                    jnp.sum(d_one, axis=0),
                    gain_one_g,
                    shift_one_g,
                    jnp.sum(d_two, axis=0),
                    gain_two_g,
                    shift_two_g,
                ]
            ),
            memory_grad,
            jnp.sum(d_q, axis=0)[None],
            (jnp.sum(dv_a, axis=0) + jnp.sum(dv_b, axis=0))[None],
            jnp.sum(d_pre, axis=0).reshape(4, 768),
        ],
        axis=0,
    )
    for axis, size in (("tensor", n_tensor), ("dp", n_dp)):
        step = 1
        while step < size:
            vec = vec + swap(axis, step)(vec)
            step *= 2
    total_shared = vec[:16]
    grad_split = jnp.concatenate(
        [
            lax.dynamic_slice_in_dim(vec[16], t * 192, 192, 0),
            lax.dynamic_slice_in_dim(vec[17], t * 192, 192, 0),
            lax.dynamic_index_in_dim(vec[18:], t, 0, keepdims=False),
        ]
    )[None]

    new_master, new_first, new_second, new_left, new_right = soap_update(
        master[0],
        owned,
        first_moment[0],
        second_moment[0],
        left_stats[0],
        right_stats[0],
        left_basis[0],
        right_basis[0],
    )
    new_split, new_split_first, new_split_second = adam_update(
        split_params, grad_split, split_first, split_second, rate_vector
    )
    new_shared, new_shared_first, new_shared_second = adam_update(
        shared, total_shared, shared_first, shared_second, rate_shared
    )
    return (
        layer_out,
        grad_in,
        new_master[None],
        new_master[None].astype(BF),
        new_first[None],
        new_second[None],
        new_left[None],
        new_right[None],
        new_split,
        new_split_first,
        new_split_second,
        new_shared,
        new_shared_first,
        new_shared_second,
    )


def solution(mesh):
    rows = P("dp", "tensor", None)
    state = P("tensor", "dp", None, None)
    split = P("tensor", None)
    return jax.shard_map(
        functools.partial(per_device, mesh.shape["dp"], mesh.shape["tensor"]),
        mesh=mesh,
        in_specs=(rows, rows, P("dp", None), P("dp"), P()) + (state,) * 7 + (split,) * 3 + (P(),) * 3,
        out_specs=(rows, rows) + (state,) * 6 + (split,) * 3 + (P(),) * 3,
        check_vma=False,
    )
```

time: 803 us -> 446 us (0.56)
  the two profiles are of different devices: /device:TPU:8 before, /device:TPU:0 now
where the time goes in v1:
time: 446 us; the launch traced here: 439 us
  waiting for transfers between devices  158 us (35%)
  local copies, waits for them, and re-layouts  74.7 us (17%)
  Pallas kernels  63.1 us (14%)
  starting transfers between devices  55.6 us (12%)
  matrix products  55.2 us (12%)
  other arithmetic  29.8 us (7%)
    ppermute x79, waiting for transfers between devices, swap(): return lambda v: lax.ppermute(v, axis, xor_pairs(size, step))  158 us
    ppermute x79, starting transfers between devices, swap(): return lambda v: lax.ppermute(v, axis, xor_pairs(size, step))  55.6 us
    pallas_call x1, Pallas kernels, build_weights(): pl.pallas_call(functools.partial(weights_body, len(pieces), places), out_...  21.9 us
    unnamed x214, local copies, waits for them, and re-layouts  20 us
    dot_general x8, matrix products, inner_rows(): lax.dot_general(left, right, (((0,), (0,)), ((), ())), preferred_element_...  16.9 us
    pallas_call x1, Pallas kernels, pack_grads(): pl.pallas_call(functools.partial(grads_body, places), out_shape=tuple((sd...  16.3 us
    dot_general x4, matrix products, dot_back(): lax.dot_general(left, right, (((1,), (1,)), ((), ())), preferred_element_...  12.8 us
    pallas_call x1, Pallas kernels, attend_back(): pl.pallas_call(attend_back_body, grid=(pairs,), out_shape=(sds((rows, 768...  11.9 us
  transfers between devices with their start and end apart: 79, of which 33 were waited for; matrix products, arithmetic and copies ran while one was open for 29% of the time, Pallas kernels for 10%

profile of v1, /device:TPU:0, one launch (start us, length us, event | category | flops | bytes accessed | tf_op | source)
XLA Modules:
  0.0 439.5 jit_solution(18166171494888208925)
XLA Ops:
  0.7 2.3 pack_owned.1.refs_0_
  3.5 2.5 collective-permute-start.2
  10.6 12.6 %collective-permute-done.41 = f32[2,1152]{1,0:T(2,128)S(1)} collective-permute-done((f32[2,1152]{1,0:T(2,128)S(1)}, f32[2,1152]{1,0:T(2,128)S(1)}, u32[]{:S(2)}, u32[]{:S(2)}) %collective-permute-start.41) | collective-permute-done | bytes 9248 | tf_op jit(solution)/shard_map/ppermute | solution.py:438
  24.7 2.5 collective-permute-start.20
  30.1 5.3 %collective-permute-done.10.refs_10_ = bf16[6,3,96,128]{3,2,1,0:T(8,128)(2,1)} collective-permute-done((bf16[6,3,96,128]{3,2,1,0:T(8,128)(2,1)S(1)}, bf16[6,3,96,128]{3,2,1,0:T(8,128)(2,1)}, u32[]{:S(2)}, u32[]{:S(2)}) %collective-permute-start.10) | collective-permute-done | bytes 442400 | tf_op jit(solution)/shard_map/ppermute | solution.py:438
  35.4 12.6 %collective-permute-done.20.refs_20_ = bf16[6,3,96,128]{3,2,1,0:T(8,128)(2,1)} collective-permute-done((bf16[6,3,96,128]{3,2,1,0:T(8,128)(2,1)S(1)}, bf16[6,3,96,128]{3,2,1,0:T(8,128)(2,1)}, u32[]{:S(2)}, u32[]{:S(2)}) %collective-permute-start.20) | collective-permute-done | bytes 442400 | tf_op jit(solution)/shard_map/ppermute | solution.py:438
  48.5 16.8 %collective-permute-done.30.refs_30_ = bf16[6,3,96,128]{3,2,1,0:T(8,128)(2,1)} collective-permute-done((bf16[6,3,96,128]{3,2,1,0:T(8,128)(2,1)S(1)}, bf16[6,3,96,128]{3,2,1,0:T(8,128)(2,1)}, u32[]{:S(2)}, u32[]{:S(2)}) %collective-permute-start.30) | collective-permute-done | bytes 442400 | tf_op jit(solution)/shard_map/ppermute | solution.py:438
  73.9 4.8 %collective-permute-done.12.refs_12_ = bf16[6,3,96,128]{3,2,1,0:T(8,128)(2,1)} collective-permute-done((bf16[6,3,96,128]{3,2,1,0:T(8,128)(2,1)}, bf16[6,3,96,128]{3,2,1,0:T(8,128)(2,1)}, u32[]{:S(2)}, u32[]{:S(2)}) %collective-permute-start.12) | collective-permute-done | bytes 442400 | tf_op jit(solution)/shard_map/ppermute | solution.py:438
  83.3 4.8 %collective-permute-done.22.refs_22_ = bf16[6,3,96,128]{3,2,1,0:T(8,128)(2,1)} collective-permute-done((bf16[6,3,96,128]{3,2,1,0:T(8,128)(2,1)}, bf16[6,3,96,128]{3,2,1,0:T(8,128)(2,1)}, u32[]{:S(2)}, u32[]{:S(2)}) %collective-permute-start.22) | collective-permute-done | bytes 442400 | tf_op jit(solution)/shard_map/ppermute | solution.py:438
  91.9 5.3 %collective-permute-done.32.refs_32_ = bf16[6,3,96,128]{3,2,1,0:T(8,128)(2,1)} collective-permute-done((bf16[6,3,96,128]{3,2,1,0:T(8,128)(2,1)}, bf16[6,3,96,128]{3,2,1,0:T(8,128)(2,1)}, u32[]{:S(2)}, u32[]{:S(2)}) %collective-permute-start.32) | collective-permute-done | bytes 442400 | tf_op jit(solution)/shard_map/ppermute | solution.py:438
  97.7 2.2 collective-permute-done.34.refs_34_
  100.6 1.6 slice.234
  102.2 1.6 slice.235
  103.8 1.6 slice.236
  112.0 3.0 collective-permute-done.26.refs_26_
  116.6 2.8 collective-permute-done.36.refs_36_
  128.8 21.9 %build_weights.1 = (bf16[768,2304]{1,0:T(8,128)(2,1)}, bf16[768,768]{1,0:T(8,128)(2,1)}, bf16[768,3072]{1,0:T(8,128)(2,1)}, bf16[3072,768]{1,0:T(8,128)(2,1)}) custom-call(s32[192]{0:T(256)} %pos_ref.3, s32[2]{0:T(128)} %pad_add_fusion.1.me_ref, bf16[6,3,96,128]{3,2,1,0:T(8,128)(2,1)} %pack_owned.1.refs_0_, ...), custom_call_target="tpu_custom_call" | custom-call | tf_op jit(solution)/shard_map/build_weights/pallas_call | solution.py:148
  150.7 3.2 fusion.q_ref.ka_ref.va_ref
  157.4 1.7 copy.96
  161.6 10.7 %attend.1 = (bf16[288,768]{1,0:T(8,128)(2,1)}, bf16[12,288,576]{2,1,0:T(8,128)(2,1)}) custom-call(s32[288,1]{1,0:T(8,128)} %broadcast_in_dim.97.cq_ref, s32[1,576]{1,0:T(1,128)} %broadcast_in_dim_reshape.4.ck_ref, bf16[288,2304]{1,0:T(8,128)(2,1)} %copy-done.1, bf16[288,2304]{1,0:T(8,128)(2,1)} %copy-done.1, bf16[288,2304]{1,0:T(8,128)(2,1)} %copy-done.1, ...), custom_call_target="tpu_custom_call" | custom-call | tf_op jit(solution)/shard_map/attend/pallas_call | solution.py:268
  172.4 1.7 fusion.117
  174.6 3.9 multiply_convert_fusion
  178.5 1.7 fusion.118
  181.9 1.9 fusion.109
  184.7 4.8 %fusion.112 = (f32[3072]{0:T(1024)}, bf16[288,3072]{1,0:T(8,128)(2,1)S(1)}) fusion(f32[288,3072]{1,0:T(8,128)S(1)} %get-tuple-element.167, bf16[288,768]{1,0:T(8,128)(2,1)} %convert_element_type.212, bf16[3072,768]{1,0:T(8,128)(2,1)S(1)} %bitcast.181), kind=kOutput, calls=%fused_computation.260 | convolution fusion | flops 1368683520 | bytes 10481664 | tf_op jit(solution)/shard_map/dot_general | solution.py:366
  189.6 2.4 multiply_reduce_fusion
  193.1 2.4 convolution_convert_fusion.6.dc_ref
  195.6 4.4 %reshape.275 = bf16[288,1,2,2,768]{4,3,2,0,1:T(2,128)(2,1)S(1)} reshape(bf16[288,3072]{1,0:T(8,128)(2,1)} %copy-done.17) | data formatting | bytes 3538944 | tf_op jit(solution)/shard_map/reshape | solution.py:548
  200.6 5.3 %reshape.276 = bf16[288,1,2,2,768]{4,3,2,0,1:T(2,128)(2,1)} reshape(bf16[288,3072]{1,0:T(8,128)(2,1)} %copy-done.16) | data formatting | bytes 3538944 | tf_op jit(solution)/shard_map/reshape | solution.py:548
  207.7 11.9 %attend_back.1 = (f32[288,768]{1,0:T(8,128)}, f32[288,768]{1,0:T(8,128)}, f32[288,768]{1,0:T(8,128)}, f32[288,768]{1,0:T(8,128)}, f32[288,768]{1,0:T(8,128)}) custom-call(bf16[288,768]{1,0:T(8,128)(2,1)} %convolution_convert_fusion.6.dc_ref, bf16[12,288,576]{2,1,0:T(8,128)(2,1)} %get-tuple-element.50.p_ref, bf16[288,2304]{1,0:T(8,128)(2,1)} %copy-done.1, ...), custom_call_target="tpu_custom_call" | custom-call | tf_op jit(solution)/shard_map/attend_back/pallas_call | solution.py:325
  219.6 1.6 fusion.113
  225.5 5.4 %constant_dynamic-slice_fusion.6 = (bf16[288,1,2,1,768]{4,3,2,0,1:T(2,128)(2,1)}, bf16[288,1,2,1,768]{4,3,2,0,1:T(2,128)(2,1)}) fusion(bf16[288,1,2,2,768]{4,3,2,0,1:T(2,128)(2,1)S(1)} %reshape.275, s32[]{:T(128)S(6)} %select_n.120, s32[]{:T(128)S(6)} %select_n.121), kind=kLoop, calls=%fused_computation.204 | loop fusion | bytes 3538952 | tf_op jit(solution)/shard_map/jit(dynamic_index_in_dim)/dynamic_slice | solution.py:549
  231.0 4.9 %constant_dynamic-slice_fusion.4 = (bf16[288,1,2,1,768]{4,3,2,0,1:T(2,128)(2,1)S(1)}, bf16[288,1,2,1,768]{4,3,2,0,1:T(2,128)(2,1)}) fusion(bf16[288,1,2,2,768]{4,3,2,0,1:T(2,128)(2,1)S(1)} %copy-done.2, s32[]{:T(128)S(6)} %select_n.120, s32[]{:T(128)S(6)} %select_n.121), kind=kLoop, calls=%fused_computation.202 | loop fusion | bytes 3538952 | tf_op jit(solution)/shard_map/jit(dynamic_index_in_dim)/dynamic_slice | solution.py:549
  260.0 3.2 select_convert_fusion
  263.5 2.6 dynamic-slice_bitcast_fusion.1
  267.2 2.3 fusion.6
  269.5 2.3 fusion.5
  273.9 2.4 fusion.7
  277.4 2.4 fusion.8
  282.3 1.6 pad_maximum_fusion.1.g2_ref
  285.3 4.3 collective-permute-done.77
  289.6 1.7 collective-permute-start.78
  292.5 3.0 collective-permute-done.78
  296.7 1.7 fusion.55
  300.5 2.3 fusion.15
  302.9 2.1 fusion.14
  305.0 1.7 pad_maximum_fusion.2.gq_ref
  306.6 16.3 %pack_grads.1 = (bf16[6,3,96,128]{3,2,1,0:T(8,128)(2,1)}, bf16[6,3,96,128]{3,2,1,0:T(8,128)(2,1)}, bf16[6,3,96,128]{3,2,1,0:T(8,128)(2,1)}, bf16[3,3,96,128]{3,2...) custom-call(s32[192]{0:T(256)} %pos_ref.3, ...), custom_call_target="tpu_custom_call" | custom-call | tf_op jit(solution)/shard_map/pack_grads/pallas_call | solution.py:223
  338.0 2.6 collective-permute-done.65
  343.0 2.4 collective-permute-done.60
  347.5 2.6 collective-permute-done.55
  350.8 18.2 %collective-permute-done.68 = bf16[6,3,96,128]{3,2,1,0:T(8,128)(2,1)S(1)} collective-permute-done((bf16[6,3,96,128]{3,2,1,0:T(8,128)(2,1)S(1)}, bf16[6,3,96,128]{3,2,1,0:T(8,128)(2,1)S(1)}, u32[]{:S(2)}, u32[]{:S(2)}) %collective-permute-start.68) | collective-permute-done | bytes 442400 | tf_op jit(solution)/shard_map/ppermute | solution.py:438
  370.9 7.4 %collective-permute-done.63 = bf16[6,3,96,128]{3,2,1,0:T(8,128)(2,1)S(1)} collective-permute-done((bf16[6,3,96,128]{3,2,1,0:T(8,128)(2,1)S(1)}, bf16[6,3,96,128]{3,2,1,0:T(8,128)(2,1)S(1)}, u32[]{:S(2)}, u32[]{:S(2)}) %collective-permute-start.63) | collective-permute-done | bytes 442400 | tf_op jit(solution)/shard_map/ppermute | solution.py:438
  379.3 3.7 collective-permute-done.58
  383.1 2.4 collective-permute-start.64
  386.6 5.5 %collective-permute-done.69 = bf16[6,3,96,128]{3,2,1,0:T(8,128)(2,1)S(1)} collective-permute-done((bf16[6,3,96,128]{3,2,1,0:T(8,128)(2,1)S(1)}, bf16[6,3,96,128]{3,2,1,0:T(8,128)(2,1)S(1)}, u32[]{:S(2)}, u32[]{:S(2)}) %collective-permute-start.69) | collective-permute-done | bytes 442400 | tf_op jit(solution)/shard_map/ppermute | solution.py:438
  392.1 9.4 %collective-permute-done.64 = bf16[6,3,96,128]{3,2,1,0:T(8,128)(2,1)S(1)} collective-permute-done((bf16[6,3,96,128]{3,2,1,0:T(8,128)(2,1)S(1)}, bf16[6,3,96,128]{3,2,1,0:T(8,128)(2,1)S(1)}, u32[]{:S(2)}, u32[]{:S(2)}) %collective-permute-start.64) | collective-permute-done | bytes 442400 | tf_op jit(solution)/shard_map/ppermute | solution.py:438
  401.5 17.3 %collective-permute-done.59 = bf16[6,3,96,128]{3,2,1,0:T(8,128)(2,1)S(1)} collective-permute-done((bf16[6,3,96,128]{3,2,1,0:T(8,128)(2,1)S(1)}, bf16[6,3,96,128]{3,2,1,0:T(8,128)(2,1)S(1)}, u32[]{:S(2)}, u32[]{:S(2)}) %collective-permute-start.59) | collective-permute-done | bytes 442400 | tf_op jit(solution)/shard_map/ppermute | solution.py:438
  420.0 2.0 fusion.36
  423.7 2.1 fusion.34
  425.8 1.8 fusion.76
  427.6 2.7 fusion.11
  432.3 3.6 fusion.12
  435.9 3.1 fusion.13
  (484 shorter events, 126.6 us)
Async XLA Ops:
  3.0 24.2 %collective-permute-start.1 = (bf16[6,3,96,128]{3,2,1,0:T(8,128)(2,1)}, bf16[6,3,96,128]{3,2,1,0:T(8,128)(2,1)}, u32[]{:S(2)}, u32[]{:S(2)}) collective-permute-start(bf16[6,3,96,128]{3,2,1,0:T(8,128)(2,1)} %pack_owned.1.refs_0_), channel_id=1, source_target_pairs={{0,1},{1,0},{2,3},{3,2},{4,5},{5,4},{6,7},{7,6},{8,9},{9,8},{10,11... | collective-permute-start | bytes 1327112 | tf_op jit(solution)/shard_map/ppermute | solution.py:438
  3.5 23.9 %collective-permute-start.2 = (bf16[6,3,96,128]{3,2,1,0:T(8,128)(2,1)}, bf16[6,3,96,128]{3,2,1,0:T(8,128)(2,1)S(1)}, u32[]{:S(2)}, u32[]{:S(2)}) collective-permute-start(bf16[6,3,96,128]{3,2,1,0:T(8,128)(2,1)} %pack_owned.1.refs_0_), channel_id=1, source_target_pairs={{0,4},{4,0},{8,12},{12,8},{16,20},{20,16},{24,28},{28,24},{1,5},{5... | collective-permute-start | bytes 1327112 | tf_op jit(solution)/shard_map/ppermute | solution.py:438
  6.0 21.6 %collective-permute-start.4 = (bf16[6,3,96,128]{3,2,1,0:T(8,128)(2,1)}, bf16[6,3,96,128]{3,2,1,0:T(8,128)(2,1)}, u32[]{:S(2)}, u32[]{:S(2)}) collective-permute-start(bf16[6,3,96,128]{3,2,1,0:T(8,128)(2,1)} %pack_owned.1.refs_0_), channel_id=1, source_target_pairs={{0,2},{1,3},{2,0},{3,1},{4,6},{5,7},{6,4},{7,5},{8,10},{9,11},{10,... | collective-permute-start | bytes 1327112 | tf_op jit(solution)/shard_map/ppermute | solution.py:438
  8.4 16.3 %collective-permute-start = (bf16[133,768]{1,0:T(8,128)(2,1)S(1)}, bf16[133,768]{1,0:T(8,128)(2,1)S(1)}, u32[]{:S(2)}, u32[]{:S(2)}) collective-permute-start(bf16[133,768]{1,0:T(8,128)(2,1)S(1)} %bitcast.176), channel_id=1, source_target_pairs={{0,2},{1,3},{2,0},{3,1},{4,6},{5,7},{6,4},{7,5},{8,10},{9,11},{10,... | collective-permute-start | bytes 612872 | tf_op jit(solution)/shard_map/ppermute | solution.py:438
  9.0 14.2 %collective-permute-start.41 = (f32[2,1152]{1,0:T(2,128)S(1)}, f32[2,1152]{1,0:T(2,128)S(1)}, u32[]{:S(2)}, u32[]{:S(2)}) collective-permute-start(f32[2,1152]{1,0:T(2,128)S(1)} %pad_maximum_fusion.34), channel_id=1, source_target_pairs={{0,2},{1,3},{2,0},{3,1},{4,6},{5,7},{6,4},{7,5},{8,10},{9,11},{10,... | collective-permute-start | bytes 27656 | tf_op jit(solution)/shard_map/ppermute | solution.py:438
  23.1 12.2 %collective-permute-start.10 = (bf16[6,3,96,128]{3,2,1,0:T(8,128)(2,1)S(1)}, bf16[6,3,96,128]{3,2,1,0:T(8,128)(2,1)}, u32[]{:S(2)}, u32[]{:S(2)}) collective-permute-start(bf16[6,3,96,128]{3,2,1,0:T(8,128)(2,1)S(1)} %copy-done.21), channel_id=1, source_target_pairs={{0,8},{4,12},{8,0},{12,4},{16,24},{20,28},{24,16},{28,20},{1,9},{5... | collective-permute-start | bytes 1327112 | tf_op jit(solution)/shard_map/ppermute | solution.py:438
  24.7 23.2 %collective-permute-start.20 = (bf16[6,3,96,128]{3,2,1,0:T(8,128)(2,1)S(1)}, bf16[6,3,96,128]{3,2,1,0:T(8,128)(2,1)}, u32[]{:S(2)}, u32[]{:S(2)}) collective-permute-start(bf16[6,3,96,128]{3,2,1,0:T(8,128)(2,1)S(1)} %copy-done.21), channel_id=1, source_target_pairs={{0,24},{4,28},{8,16},{12,20},{16,8},{20,12},{24,0},{28,4},{1,25},{... | collective-permute-start | bytes 1327112 | tf_op jit(solution)/shard_map/ppermute | solution.py:438
  27.2 38.1 %collective-permute-start.30 = (bf16[6,3,96,128]{3,2,1,0:T(8,128)(2,1)S(1)}, bf16[6,3,96,128]{3,2,1,0:T(8,128)(2,1)}, u32[]{:S(2)}, u32[]{:S(2)}) collective-permute-start(bf16[6,3,96,128]{3,2,1,0:T(8,128)(2,1)S(1)} %copy-done.21), channel_id=1, source_target_pairs={{0,16},{4,20},{8,24},{12,28},{16,0},{20,4},{24,8},{28,12},{1,17},{... | collective-permute-start | bytes 1327112 | tf_op jit(solution)/shard_map/ppermute | solution.py:438
  27.4 38.7 %collective-permute-start.3 = (bf16[6,3,96,128]{3,2,1,0:T(8,128)(2,1)S(1)}, bf16[6,3,96,128]{3,2,1,0:T(8,128)(2,1)S(1)}, u32[]{:S(2)}, u32[]{:S(2)}) collective-permute-start(bf16[6,3,96,128]{3,2,1,0:T(8,128)(2,1)S(1)} %collective-permute-done.2.refs_2_), channel_id=1, source_target_pairs={{0,1},{1,0},{2,3},{3,2},{4,5},{5,4},{6,7},{7,6},{8,9},{9,8},{10,11... | collective-permute-start | bytes 1327112 | tf_op jit(solution)/shard_map/ppermute | solution.py:438
  27.5 37.8 %collective-permute-start.6 = (bf16[3,3,96,128]{3,2,1,0:T(8,128)(2,1)S(1)}, bf16[3,3,96,128]{3,2,1,0:T(8,128)(2,1)S(1)}, u32[]{:S(2)}, u32[]{:S(2)}) collective-permute-start(bf16[3,3,96,128]{3,2,1,0:T(8,128)(2,1)S(1)} %slice.230), channel_id=1, source_target_pairs={{0,2},{1,3},{2,0},{3,1},{4,6},{5,7},{6,4},{7,5},{8,10},{9,11},{10,... | collective-permute-start | bytes 663560 | tf_op jit(solution)/shard_map/ppermute | solution.py:438
  35.3 31.5 %collective-permute-start.5 = (bf16[6,3,96,128]{3,2,1,0:T(8,128)(2,1)}, bf16[6,3,96,128]{3,2,1,0:T(8,128)(2,1)S(1)}, u32[]{:S(2)}, u32[]{:S(2)}) collective-permute-start(bf16[6,3,96,128]{3,2,1,0:T(8,128)(2,1)} %collective-permute-done.4.refs_4_), channel_id=1, source_target_pairs={{0,1},{1,0},{2,3},{3,2},{4,5},{5,4},{6,7},{7,6},{8,9},{9,8},{10,11... | collective-permute-start | bytes 1327112 | tf_op jit(solution)/shard_map/ppermute | solution.py:438
  48.0 18.0 %collective-permute-start.8 = (bf16[3,3,96,128]{3,2,1,0:T(8,128)(2,1)S(1)}, bf16[3,3,96,128]{3,2,1,0:T(8,128)(2,1)}, u32[]{:S(2)}, u32[]{:S(2)}) collective-permute-start(bf16[3,3,96,128]{3,2,1,0:T(8,128)(2,1)S(1)} %slice.231), channel_id=1, source_target_pairs={{0,4},{4,0},{8,12},{12,8},{16,20},{20,16},{24,28},{28,24},{1,5},{5... | collective-permute-start | bytes 663560 | tf_op jit(solution)/shard_map/ppermute | solution.py:438
  65.3 8.0 %collective-permute-start.11 = (bf16[6,3,96,128]{3,2,1,0:T(8,128)(2,1)}, bf16[6,3,96,128]{3,2,1,0:T(8,128)(2,1)S(1)}, u32[]{:S(2)}, u32[]{:S(2)}) collective-permute-start(bf16[6,3,96,128]{3,2,1,0:T(8,128)(2,1)} %collective-permute-done.10.refs_10_), channel_id=1, source_target_pairs={{0,1},{1,0},{2,3},{3,2},{4,5},{5,4},{6,7},{7,6},{8,9},{9,8},{10,11... | collective-permute-start | bytes 1327112 | tf_op jit(solution)/shard_map/ppermute | solution.py:438
  65.3 13.4 %collective-permute-start.12 = (bf16[6,3,96,128]{3,2,1,0:T(8,128)(2,1)}, bf16[6,3,96,128]{3,2,1,0:T(8,128)(2,1)}, u32[]{:S(2)}, u32[]{:S(2)}) collective-permute-start(bf16[6,3,96,128]{3,2,1,0:T(8,128)(2,1)} %collective-permute-done.10.refs_10_), channel_id=1, source_target_pairs={{0,4},{4,0},{8,12},{12,8},{16,20},{20,16},{24,28},{28,24},{1,5},{5... | collective-permute-start | bytes 1327112 | tf_op jit(solution)/shard_map/ppermute | solution.py:438
  66.1 6.7 %collective-permute-start.9 = (bf16[3,3,96,128]{3,2,1,0:T(8,128)(2,1)}, bf16[3,3,96,128]{3,2,1,0:T(8,128)(2,1)}, u32[]{:S(2)}, u32[]{:S(2)}) collective-permute-start(bf16[3,3,96,128]{3,2,1,0:T(8,128)(2,1)} %collective-permute-done.8.refs_8_), channel_id=1, source_target_pairs={{0,1},{1,0},{2,3},{3,2},{4,5},{5,4},{6,7},{7,6},{8,9},{9,8},{10,11... | collective-permute-start | bytes 663560 | tf_op jit(solution)/shard_map/ppermute | solution.py:438
  67.6 15.6 %collective-permute-start.14 = (bf16[6,3,96,128]{3,2,1,0:T(8,128)(2,1)}, bf16[6,3,96,128]{3,2,1,0:T(8,128)(2,1)S(1)}, u32[]{:S(2)}, u32[]{:S(2)}) collective-permute-start(bf16[6,3,96,128]{3,2,1,0:T(8,128)(2,1)} %collective-permute-done.10.refs_10_), channel_id=1, source_target_pairs={{0,2},{1,3},{2,0},{3,1},{4,6},{5,7},{6,4},{7,5},{8,10},{9,11},{10,... | collective-permute-start | bytes 1327112 | tf_op jit(solution)/shard_map/ppermute | solution.py:438
  69.9 18.3 %collective-permute-start.22 = (bf16[6,3,96,128]{3,2,1,0:T(8,128)(2,1)}, bf16[6,3,96,128]{3,2,1,0:T(8,128)(2,1)}, u32[]{:S(2)}, u32[]{:S(2)}) collective-permute-start(bf16[6,3,96,128]{3,2,1,0:T(8,128)(2,1)} %collective-permute-done.20.refs_20_), channel_id=1, source_target_pairs={{0,4},{4,0},{8,12},{12,8},{16,20},{20,16},{24,28},{28,24},{1,5},{5... | collective-permute-start | bytes 1327112 | tf_op jit(solution)/shard_map/ppermute | solution.py:438
  72.8 17.6 %collective-permute-start.24 = (bf16[6,3,96,128]{3,2,1,0:T(8,128)(2,1)}, bf16[6,3,96,128]{3,2,1,0:T(8,128)(2,1)}, u32[]{:S(2)}, u32[]{:S(2)}) collective-permute-start(bf16[6,3,96,128]{3,2,1,0:T(8,128)(2,1)} %collective-permute-done.20.refs_20_), channel_id=1, source_target_pairs={{0,2},{1,3},{2,0},{3,1},{4,6},{5,7},{6,4},{7,5},{8,10},{9,11},{10,... | collective-permute-start | bytes 1327112 | tf_op jit(solution)/shard_map/ppermute | solution.py:438
  73.3 23.8 %collective-permute-start.32 = (bf16[6,3,96,128]{3,2,1,0:T(8,128)(2,1)}, bf16[6,3,96,128]{3,2,1,0:T(8,128)(2,1)}, u32[]{:S(2)}, u32[]{:S(2)}) collective-permute-start(bf16[6,3,96,128]{3,2,1,0:T(8,128)(2,1)} %collective-permute-done.30.refs_30_), channel_id=1, source_target_pairs={{0,4},{4,0},{8,12},{12,8},{16,20},{20,16},{24,28},{28,24},{1,5},{5... | collective-permute-start | bytes 1327112 | tf_op jit(solution)/shard_map/ppermute | solution.py:438
  78.7 21.2 %collective-permute-start.34 = (bf16[6,3,96,128]{3,2,1,0:T(8,128)(2,1)}, bf16[6,3,96,128]{3,2,1,0:T(8,128)(2,1)}, u32[]{:S(2)}, u32[]{:S(2)}) collective-permute-start(bf16[6,3,96,128]{3,2,1,0:T(8,128)(2,1)} %collective-permute-done.30.refs_30_), channel_id=1, source_target_pairs={{0,2},{1,3},{2,0},{3,1},{4,6},{5,7},{6,4},{7,5},{8,10},{9,11},{10,... | collective-permute-start | bytes 1327112 | tf_op jit(solution)/shard_map/ppermute | solution.py:438
  83.3 23.2 %collective-permute-start.21 = (bf16[6,3,96,128]{3,2,1,0:T(8,128)(2,1)}, bf16[6,3,96,128]{3,2,1,0:T(8,128)(2,1)S(1)}, u32[]{:S(2)}, u32[]{:S(2)}) collective-permute-start(bf16[6,3,96,128]{3,2,1,0:T(8,128)(2,1)} %collective-permute-done.20.refs_20_), channel_id=1, source_target_pairs={{0,1},{1,0},{2,3},{3,2},{4,5},{5,4},{6,7},{7,6},{8,9},{9,8},{10,11... | collective-permute-start | bytes 1327112 | tf_op jit(solution)/shard_map/ppermute | solution.py:438
  88.2 19.9 %collective-permute-start.31 = (bf16[6,3,96,128]{3,2,1,0:T(8,128)(2,1)}, bf16[6,3,96,128]{3,2,1,0:T(8,128)(2,1)S(1)}, u32[]{:S(2)}, u32[]{:S(2)}) collective-permute-start(bf16[6,3,96,128]{3,2,1,0:T(8,128)(2,1)} %collective-permute-done.30.refs_30_), channel_id=1, source_target_pairs={{0,1},{1,0},{2,3},{3,2},{4,5},{5,4},{6,7},{7,6},{8,9},{9,8},{10,11... | collective-permute-start | bytes 1327112 | tf_op jit(solution)/shard_map/ppermute | solution.py:438
  90.4 19.1 %collective-permute-start.16 = (bf16[3,3,96,128]{3,2,1,0:T(8,128)(2,1)S(1)}, bf16[3,3,96,128]{3,2,1,0:T(8,128)(2,1)S(1)}, u32[]{:S(2)}, u32[]{:S(2)}) collective-permute-start(bf16[3,3,96,128]{3,2,1,0:T(8,128)(2,1)S(1)} %slice.232), channel_id=1, source_target_pairs={{0,2},{1,3},{2,0},{3,1},{4,6},{5,7},{6,4},{7,5},{8,10},{9,11},{10,... | collective-permute-start | bytes 663560 | tf_op jit(solution)/shard_map/ppermute | solution.py:438
  97.2 12.9 %collective-permute-start.18 = (bf16[3,3,96,128]{3,2,1,0:T(8,128)(2,1)S(1)}, bf16[3,3,96,128]{3,2,1,0:T(8,128)(2,1)S(1)}, u32[]{:S(2)}, u32[]{:S(2)}) collective-permute-start(bf16[3,3,96,128]{3,2,1,0:T(8,128)(2,1)S(1)} %slice.233), channel_id=1, source_target_pairs={{0,4},{4,0},{8,12},{12,8},{16,20},{20,16},{24,28},{28,24},{1,5},{5... | collective-permute-start | bytes 663560 | tf_op jit(solution)/shard_map/ppermute | solution.py:438
  99.9 20.8 %collective-permute-start.13 = (bf16[6,3,96,128]{3,2,1,0:T(8,128)(2,1)}, bf16[6,3,96,128]{3,2,1,0:T(8,128)(2,1)}, u32[]{:S(2)}, u32[]{:S(2)}) collective-permute-start(bf16[6,3,96,128]{3,2,1,0:T(8,128)(2,1)} %collective-permute-done.12.refs_12_), channel_id=1, source_target_pairs={{0,1},{1,0},{2,3},{3,2},{4,5},{5,4},{6,7},{7,6},{8,9},{9,8},{10,11... | collective-permute-start | bytes 1327112 | tf_op jit(solution)/shard_map/ppermute | solution.py:438
  106.5 8.6 %collective-permute-start.26 = (bf16[3,3,96,128]{3,2,1,0:T(8,128)(2,1)}, bf16[3,3,96,128]{3,2,1,0:T(8,128)(2,1)}, u32[]{:S(2)}, u32[]{:S(2)}) collective-permute-start(bf16[3,3,96,128]{3,2,1,0:T(8,128)(2,1)} %slice.234), channel_id=1, source_target_pairs={{0,2},{1,3},{2,0},{3,1},{4,6},{5,7},{6,4},{7,5},{8,10},{9,11},{10,... | collective-permute-start | bytes 663560 | tf_op jit(solution)/shard_map/ppermute | solution.py:438
  108.0 8.6 %collective-permute-start.28 = (bf16[3,3,96,128]{3,2,1,0:T(8,128)(2,1)}, bf16[3,3,96,128]{3,2,1,0:T(8,128)(2,1)}, u32[]{:S(2)}, u32[]{:S(2)}) collective-permute-start(bf16[3,3,96,128]{3,2,1,0:T(8,128)(2,1)} %slice.235), channel_id=1, source_target_pairs={{0,4},{4,0},{8,12},{12,8},{16,20},{20,16},{24,28},{28,24},{1,5},{5... | collective-permute-start | bytes 663560 | tf_op jit(solution)/shard_map/ppermute | solution.py:438
  109.5 9.9 %collective-permute-start.36 = (bf16[3,3,96,128]{3,2,1,0:T(8,128)(2,1)}, bf16[3,3,96,128]{3,2,1,0:T(8,128)(2,1)}, u32[]{:S(2)}, u32[]{:S(2)}) collective-permute-start(bf16[3,3,96,128]{3,2,1,0:T(8,128)(2,1)} %slice.236), channel_id=1, source_target_pairs={{0,2},{1,3},{2,0},{3,1},{4,6},{5,7},{6,4},{7,5},{8,10},{9,11},{10,... | collective-permute-start | bytes 663560 | tf_op jit(solution)/shard_map/ppermute | solution.py:438
  110.1 10.6 %collective-permute-start.38 = (bf16[3,3,96,128]{3,2,1,0:T(8,128)(2,1)S(1)}, bf16[3,3,96,128]{3,2,1,0:T(8,128)(2,1)}, u32[]{:S(2)}, u32[]{:S(2)}) collective-permute-start(bf16[3,3,96,128]{3,2,1,0:T(8,128)(2,1)S(1)} %slice.237), channel_id=1, source_target_pairs={{0,4},{4,0},{8,12},{12,8},{16,20},{20,16},{24,28},{28,24},{1,5},{5... | collective-permute-start | bytes 663560 | tf_op jit(solution)/shard_map/ppermute | solution.py:438
  115.1 6.2 %collective-permute-start.15 = (bf16[6,3,96,128]{3,2,1,0:T(8,128)(2,1)}, bf16[6,3,96,128]{3,2,1,0:T(8,128)(2,1)S(1)}, u32[]{:S(2)}, u32[]{:S(2)}) collective-permute-start(bf16[6,3,96,128]{3,2,1,0:T(8,128)(2,1)} %copy-done.29), channel_id=1, source_target_pairs={{0,1},{1,0},{2,3},{3,2},{4,5},{5,4},{6,7},{7,6},{8,9},{9,8},{10,11... | collective-permute-start | bytes 1327112 | tf_op jit(solution)/shard_map/ppermute | solution.py:438
  116.6 6.7 %collective-permute-start.23 = (bf16[6,3,96,128]{3,2,1,0:T(8,128)(2,1)}, bf16[6,3,96,128]{3,2,1,0:T(8,128)(2,1)}, u32[]{:S(2)}, u32[]{:S(2)}) collective-permute-start(bf16[6,3,96,128]{3,2,1,0:T(8,128)(2,1)} %collective-permute-done.22.refs_22_), channel_id=1, source_target_pairs={{0,1},{1,0},{2,3},{3,2},{4,5},{5,4},{6,7},{7,6},{8,9},{9,8},{10,11... | collective-permute-start | bytes 1327112 | tf_op jit(solution)/shard_map/ppermute | solution.py:438
  121.3 6.1 %collective-permute-start.33 = (bf16[6,3,96,128]{3,2,1,0:T(8,128)(2,1)}, bf16[6,3,96,128]{3,2,1,0:T(8,128)(2,1)}, u32[]{:S(2)}, u32[]{:S(2)}) collective-permute-start(bf16[6,3,96,128]{3,2,1,0:T(8,128)(2,1)} %collective-permute-done.32.refs_32_), channel_id=1, source_target_pairs={{0,1},{1,0},{2,3},{3,2},{4,5},{5,4},{6,7},{7,6},{8,9},{9,8},{10,11... | collective-permute-start | bytes 1327112 | tf_op jit(solution)/shard_map/ppermute | solution.py:438
  126.3 54.2 %collective-permute-start.44 = (bf16[133,768]{1,0:T(8,128)(2,1)}, bf16[133,768]{1,0:T(8,128)(2,1)}, u32[]{:S(2)}, u32[]{:S(2)}) collective-permute-start(bf16[133,768]{1,0:T(8,128)(2,1)} %bitcast.174), channel_id=1, source_target_pairs={{0,2},{1,3},{2,0},{3,1},{4,6},{5,7},{6,4},{7,5},{8,10},{9,11},{10,... | collective-permute-start | bytes 612872 | tf_op jit(solution)/shard_map/ppermute | solution.py:438
  154.9 5.8 %collective-permute-start.42 = (bf16[288,1536]{1,0:T(8,128)(2,1)}, bf16[288,1536]{1,0:T(8,128)(2,1)S(1)}, u32[]{:S(2)}, u32[]{:S(2)}) collective-permute-start(bf16[288,1536]{1,0:T(8,128)(2,1)} %slice.240), channel_id=1, source_target_pairs={{0,1},{1,0},{2,3},{3,2},{4,5},{5,4},{6,7},{7,6},{8,9},{9,8},{10,11... | collective-permute-start | bytes 2654216 | tf_op jit(solution)/shard_map/ppermute | solution.py:438
  160.2 140.3 %collective-permute-start.47 = (bf16[288,768]{1,0:T(8,128)(2,1)}, bf16[288,768]{1,0:T(8,128)(2,1)}, u32[]{:S(2)}, u32[]{:S(2)}) collective-permute-start(bf16[288,768]{1,0:T(8,128)(2,1)} %copy-done.43), channel_id=1, source_target_pairs={{0,1},{1,0},{2,3},{3,2},{4,5},{5,4},{6,7},{7,6},{8,9},{9,8},{10,11... | collective-permute-start | bytes 1327112 | tf_op jit(solution)/shard_map/ppermute | solution.py:438
  195.5 52.6 %collective-permute-start.50 = (bf16[288,768]{1,0:T(8,128)(2,1)}, bf16[288,768]{1,0:T(8,128)(2,1)}, u32[]{:S(2)}, u32[]{:S(2)}) collective-permute-start(bf16[288,768]{1,0:T(8,128)(2,1)} %convert_element_type.214), channel_id=1, source_target_pairs={{0,1},{1,0},{2,3},{3,2},{4,5},{5,4},{6,7},{7,6},{8,9},{9,8},{10,11... | collective-permute-start | bytes 1327112 | tf_op jit(solution)/shard_map/ppermute | solution.py:438
  200.1 66.0 %collective-permute-start.51 = (bf16[288,768]{1,0:T(8,128)(2,1)}, bf16[288,768]{1,0:T(8,128)(2,1)}, u32[]{:S(2)}, u32[]{:S(2)}) collective-permute-start(bf16[288,768]{1,0:T(8,128)(2,1)} %copy-done.54), channel_id=1, source_target_pairs={{0,1},{1,0},{2,3},{3,2},{4,5},{5,4},{6,7},{7,6},{8,9},{9,8},{10,11... | collective-permute-start | bytes 1327112 | tf_op jit(solution)/shard_map/ppermute | solution.py:438
  206.7 38.8 %collective-permute-start.43 = (bf16[133,768]{1,0:T(8,128)(2,1)}, bf16[133,768]{1,0:T(8,128)(2,1)}, u32[]{:S(2)}, u32[]{:S(2)}) collective-permute-start(bf16[133,768]{1,0:T(8,128)(2,1)} %get-tuple-element.155), channel_id=1, source_target_pairs={{0,2},{1,3},{2,0},{3,1},{4,6},{5,7},{6,4},{7,5},{8,10},{9,11},{10,... | collective-permute-start | bytes 612872 | tf_op jit(solution)/shard_map/ppermute | solution.py:438
  222.3 30.3 %collective-permute-start.45 = (bf16[288,1536]{1,0:T(8,128)(2,1)}, bf16[288,1536]{1,0:T(8,128)(2,1)}, u32[]{:S(2)}, u32[]{:S(2)}) collective-permute-start(bf16[288,1536]{1,0:T(8,128)(2,1)} %pad_maximum_fusion.7), channel_id=1, source_target_pairs={{0,1},{1,0},{2,3},{3,2},{4,5},{5,4},{6,7},{7,6},{8,9},{9,8},{10,11... | collective-permute-start | bytes 2654216 | tf_op jit(solution)/shard_map/ppermute | solution.py:438
  247.9 25.5 %collective-permute-start.54 = (bf16[288,768]{1,0:T(8,128)(2,1)}, bf16[288,768]{1,0:T(8,128)(2,1)}, u32[]{:S(2)}, u32[]{:S(2)}) collective-permute-start(bf16[288,768]{1,0:T(8,128)(2,1)} %convert_element_type.212), channel_id=1, source_target_pairs={{0,1},{1,0},{2,3},{3,2},{4,5},{5,4},{6,7},{7,6},{8,9},{9,8},{10,11... | collective-permute-start | bytes 1327112 | tf_op jit(solution)/shard_map/ppermute | solution.py:438
  248.2 19.0 %collective-permute-start.52 = (bf16[288,1,2,768]{3,0,2,1:T(8,128)(2,1)}, bf16[288,1,2,768]{3,0,2,1:T(8,128)(2,1)}, u32[]{:S(2)}, u32[]{:S(2)}) collective-permute-start(bf16[288,1,2,768]{3,0,2,1:T(8,128)(2,1)} %bitcast.145), channel_id=1, source_target_pairs={{0,1},{1,0},{2,3},{3,2},{4,5},{5,4},{6,7},{7,6},{8,9},{9,8},{10,11... | collective-permute-start | bytes 2654216 | tf_op jit(solution)/shard_map/ppermute | solution.py:438
  252.6 21.2 %collective-permute-start.53 = (bf16[288,1,2,768]{3,0,2,1:T(8,128)(2,1)}, bf16[288,1,2,768]{3,0,2,1:T(8,128)(2,1)}, u32[]{:S(2)}, u32[]{:S(2)}) collective-permute-start(bf16[288,1,2,768]{3,0,2,1:T(8,128)(2,1)} %bitcast.143), channel_id=1, source_target_pairs={{0,1},{1,0},{2,3},{3,2},{4,5},{5,4},{6,7},{7,6},{8,9},{9,8},{10,11... | collective-permute-start | bytes 2654216 | tf_op jit(solution)/shard_map/ppermute | solution.py:438
  266.1 19.1 %collective-permute-start.46 = (bf16[133,768]{1,0:T(8,128)(2,1)S(1)}, bf16[133,768]{1,0:T(8,128)(2,1)S(1)}, u32[]{:S(2)}, u32[]{:S(2)}) collective-permute-start(bf16[133,768]{1,0:T(8,128)(2,1)S(1)} %get-tuple-element.153), channel_id=1, source_target_pairs={{0,2},{1,3},{2,0},{3,1},{4,6},{5,7},{6,4},{7,5},{8,10},{9,11},{10,... | collective-permute-start | bytes 612872 | tf_op jit(solution)/shard_map/ppermute | solution.py:438
  267.2 28.6 %collective-permute-start.48 = (bf16[288,3,2,192]{3,0,2,1:T(8,128)(2,1)S(1)}, bf16[288,3,2,192]{3,0,2,1:T(8,128)(2,1)S(1)}, u32[]{:S(2)}, u32[]{:S(2)}) collective-permute-start(bf16[288,3,2,192]{3,0,2,1:T(8,128)(2,1)S(1)} %get-tuple-element.139), channel_id=1, source_target_pairs={{0,1},{1,0},{2,3},{3,2},{4,5},{5,4},{6,7},{7,6},{8,9},{9,8},{10,11... | collective-permute-start | bytes 1990664 | tf_op jit(solution)/shard_map/ppermute | solution.py:438
  289.6 5.8 %collective-permute-start.78 = (f32[22,768]{1,0:T(8,128)S(1)}, f32[22,768]{1,0:T(8,128)S(1)}, u32[]{:S(2)}, u32[]{:S(2)}) collective-permute-start(f32[22,768]{1,0:T(8,128)S(1)} %add.372), channel_id=1, source_target_pairs={{0,16},{4,20},{8,24},{12,28},{16,0},{20,4},{24,8},{28,12},{1,17},{... | collective-permute-start | bytes 202760 | tf_op jit(solution)/shard_map/ppermute | solution.py:438
  323.0 10.5 %collective-permute-start.72 = (bf16[3,3,96,128]{3,2,1,0:T(8,128)(2,1)}, bf16[3,3,96,128]{3,2,1,0:T(8,128)(2,1)S(1)}, u32[]{:S(2)}, u32[]{:S(2)}) collective-permute-start(bf16[3,3,96,128]{3,2,1,0:T(8,128)(2,1)} %get-tuple-element.75), channel_id=1, source_target_pairs={{0,4},{4,0},{8,12},{12,8},{16,20},{20,16},{24,28},{28,24},{1,5},{5... | collective-permute-start | bytes 663560 | tf_op jit(solution)/shard_map/ppermute | solution.py:438
  327.3 8.6 %collective-permute-start.70 = (bf16[3,3,96,128]{3,2,1,0:T(8,128)(2,1)}, bf16[3,3,96,128]{3,2,1,0:T(8,128)(2,1)S(1)}, u32[]{:S(2)}, u32[]{:S(2)}) collective-permute-start(bf16[3,3,96,128]{3,2,1,0:T(8,128)(2,1)} %get-tuple-element.73), channel_id=1, source_target_pairs={{0,2},{1,3},{2,0},{3,1},{4,6},{5,7},{6,4},{7,5},{8,10},{9,11},{10,... | collective-permute-start | bytes 663560 | tf_op jit(solution)/shard_map/ppermute | solution.py:438
  328.4 8.6 %collective-permute-start.67 = (bf16[3,3,96,128]{3,2,1,0:T(8,128)(2,1)}, bf16[3,3,96,128]{3,2,1,0:T(8,128)(2,1)S(1)}, u32[]{:S(2)}, u32[]{:S(2)}) collective-permute-start(bf16[3,3,96,128]{3,2,1,0:T(8,128)(2,1)} %get-tuple-element.70), channel_id=1, source_target_pairs={{0,4},{4,0},{8,12},{12,8},{16,20},{20,16},{24,28},{28,24},{1,5},{5... | collective-permute-start | bytes 663560 | tf_op jit(solution)/shard_map/ppermute | solution.py:438
  330.8 9.8 %collective-permute-start.65 = (bf16[3,3,96,128]{3,2,1,0:T(8,128)(2,1)}, bf16[3,3,96,128]{3,2,1,0:T(8,128)(2,1)S(1)}, u32[]{:S(2)}, u32[]{:S(2)}) collective-permute-start(bf16[3,3,96,128]{3,2,1,0:T(8,128)(2,1)} %get-tuple-element.68), channel_id=1, source_target_pairs={{0,2},{1,3},{2,0},{3,1},{4,6},{5,7},{6,4},{7,5},{8,10},{9,11},{10,... | collective-permute-start | bytes 663560 | tf_op jit(solution)/shard_map/ppermute | solution.py:438
  331.9 10.0 %collective-permute-start.62 = (bf16[3,3,96,128]{3,2,1,0:T(8,128)(2,1)S(1)}, bf16[3,3,96,128]{3,2,1,0:T(8,128)(2,1)S(1)}, u32[]{:S(2)}, u32[]{:S(2)}) collective-permute-start(bf16[3,3,96,128]{3,2,1,0:T(8,128)(2,1)S(1)} %copy-done.94), channel_id=1, source_target_pairs={{0,4},{4,0},{8,12},{12,8},{16,20},{20,16},{24,28},{28,24},{1,5},{5... | collective-permute-start | bytes 663560 | tf_op jit(solution)/shard_map/ppermute | solution.py:438
  333.5 11.9 %collective-permute-start.60 = (bf16[3,3,96,128]{3,2,1,0:T(8,128)(2,1)S(1)}, bf16[3,3,96,128]{3,2,1,0:T(8,128)(2,1)S(1)}, u32[]{:S(2)}, u32[]{:S(2)}) collective-permute-start(bf16[3,3,96,128]{3,2,1,0:T(8,128)(2,1)S(1)} %copy-done.93), channel_id=1, source_target_pairs={{0,2},{1,3},{2,0},{3,1},{4,6},{5,7},{6,4},{7,5},{8,10},{9,11},{10,... | collective-permute-start | bytes 663560 | tf_op jit(solution)/shard_map/ppermute | solution.py:438
  335.9 10.5 %collective-permute-start.57 = (bf16[3,3,96,128]{3,2,1,0:T(8,128)(2,1)S(1)}, bf16[3,3,96,128]{3,2,1,0:T(8,128)(2,1)S(1)}, u32[]{:S(2)}, u32[]{:S(2)}) collective-permute-start(bf16[3,3,96,128]{3,2,1,0:T(8,128)(2,1)S(1)} %copy-done.92), channel_id=1, source_target_pairs={{0,4},{4,0},{8,12},{12,8},{16,20},{20,16},{24,28},{28,24},{1,5},{5... | collective-permute-start | bytes 663560 | tf_op jit(solution)/shard_map/ppermute | solution.py:438
  337.0 13.2 %collective-permute-start.55 = (bf16[3,3,96,128]{3,2,1,0:T(8,128)(2,1)S(1)}, bf16[3,3,96,128]{3,2,1,0:T(8,128)(2,1)S(1)}, u32[]{:S(2)}, u32[]{:S(2)}) collective-permute-start(bf16[3,3,96,128]{3,2,1,0:T(8,128)(2,1)S(1)} %copy-done.91), channel_id=1, source_target_pairs={{0,2},{1,3},{2,0},{3,1},{4,6},{5,7},{6,4},{7,5},{8,10},{9,11},{10,... | collective-permute-start | bytes 663560 | tf_op jit(solution)/shard_map/ppermute | solution.py:438
  340.6 45.7 %collective-permute-start.73 = (bf16[6,3,96,128]{3,2,1,0:T(8,128)(2,1)S(1)}, bf16[6,3,96,128]{3,2,1,0:T(8,128)(2,1)S(1)}, u32[]{:S(2)}, u32[]{:S(2)}) collective-permute-start(bf16[6,3,96,128]{3,2,1,0:T(8,128)(2,1)S(1)} %pad_maximum_fusion.28), channel_id=1, source_target_pairs={{0,2},{1,3},{2,0},{3,1},{4,6},{5,7},{6,4},{7,5},{8,10},{9,11},{10,... | collective-permute-start | bytes 1327112 | tf_op jit(solution)/shard_map/ppermute | solution.py:438
  341.9 27.2 %collective-permute-start.68 = (bf16[6,3,96,128]{3,2,1,0:T(8,128)(2,1)S(1)}, bf16[6,3,96,128]{3,2,1,0:T(8,128)(2,1)S(1)}, u32[]{:S(2)}, u32[]{:S(2)}) collective-permute-start(bf16[6,3,96,128]{3,2,1,0:T(8,128)(2,1)S(1)} %pad_maximum_fusion.26), channel_id=1, source_target_pairs={{0,2},{1,3},{2,0},{3,1},{4,6},{5,7},{6,4},{7,5},{8,10},{9,11},{10,... | collective-permute-start | bytes 1327112 | tf_op jit(solution)/shard_map/ppermute | solution.py:438
  345.4 24.7 %collective-permute-start.66 = (bf16[6,3,96,128]{3,2,1,0:T(8,128)(2,1)S(1)}, bf16[6,3,96,128]{3,2,1,0:T(8,128)(2,1)S(1)}, u32[]{:S(2)}, u32[]{:S(2)}) collective-permute-start(bf16[6,3,96,128]{3,2,1,0:T(8,128)(2,1)S(1)} %pad_maximum_fusion.25), channel_id=1, source_target_pairs={{0,4},{4,0},{8,12},{12,8},{16,20},{20,16},{24,28},{28,24},{1,5},{5... | collective-permute-start | bytes 1327112 | tf_op jit(solution)/shard_map/ppermute | solution.py:438
  346.4 31.9 %collective-permute-start.63 = (bf16[6,3,96,128]{3,2,1,0:T(8,128)(2,1)S(1)}, bf16[6,3,96,128]{3,2,1,0:T(8,128)(2,1)S(1)}, u32[]{:S(2)}, u32[]{:S(2)}) collective-permute-start(bf16[6,3,96,128]{3,2,1,0:T(8,128)(2,1)S(1)} %pad_maximum_fusion.24), channel_id=1, source_target_pairs={{0,2},{1,3},{2,0},{3,1},{4,6},{5,7},{6,4},{7,5},{8,10},{9,11},{10,... | collective-permute-start | bytes 1327112 | tf_op jit(solution)/shard_map/ppermute | solution.py:438
  350.1 29.0 %collective-permute-start.61 = (bf16[6,3,96,128]{3,2,1,0:T(8,128)(2,1)S(1)}, bf16[6,3,96,128]{3,2,1,0:T(8,128)(2,1)S(1)}, u32[]{:S(2)}, u32[]{:S(2)}) collective-permute-start(bf16[6,3,96,128]{3,2,1,0:T(8,128)(2,1)S(1)} %pad_maximum_fusion.23), channel_id=1, source_target_pairs={{0,4},{4,0},{8,12},{12,8},{16,20},{20,16},{24,28},{28,24},{1,5},{5... | collective-permute-start | bytes 1327112 | tf_op jit(solution)/shard_map/ppermute | solution.py:438
  369.1 14.0 %collective-permute-start.58 = (bf16[6,3,96,128]{3,2,1,0:T(8,128)(2,1)S(1)}, bf16[6,3,96,128]{3,2,1,0:T(8,128)(2,1)S(1)}, u32[]{:S(2)}, u32[]{:S(2)}) collective-permute-start(bf16[6,3,96,128]{3,2,1,0:T(8,128)(2,1)S(1)} %pad_maximum_fusion.22), channel_id=1, source_target_pairs={{0,2},{1,3},{2,0},{3,1},{4,6},{5,7},{6,4},{7,5},{8,10},{9,11},{10,... | collective-permute-start | bytes 1327112 | tf_op jit(solution)/shard_map/ppermute | solution.py:438
  370.1 15.3 %collective-permute-start.56 = (bf16[6,3,96,128]{3,2,1,0:T(8,128)(2,1)S(1)}, bf16[6,3,96,128]{3,2,1,0:T(8,128)(2,1)S(1)}, u32[]{:S(2)}, u32[]{:S(2)}) collective-permute-start(bf16[6,3,96,128]{3,2,1,0:T(8,128)(2,1)S(1)} %pad_maximum_fusion.21), channel_id=1, source_target_pairs={{0,4},{4,0},{8,12},{12,8},{16,20},{20,16},{24,28},{28,24},{1,5},{5... | collective-permute-start | bytes 1327112 | tf_op jit(solution)/shard_map/ppermute | solution.py:438
  378.3 8.3 %collective-permute-start.71 = (bf16[6,3,96,128]{3,2,1,0:T(8,128)(2,1)S(1)}, bf16[6,3,96,128]{3,2,1,0:T(8,128)(2,1)S(1)}, u32[]{:S(2)}, u32[]{:S(2)}) collective-permute-start(bf16[6,3,96,128]{3,2,1,0:T(8,128)(2,1)S(1)} %pad_maximum_fusion.27), channel_id=1, source_target_pairs={{0,4},{4,0},{8,12},{12,8},{16,20},{20,16},{24,28},{28,24},{1,5},{5... | collective-permute-start | bytes 1327112 | tf_op jit(solution)/shard_map/ppermute | solution.py:438
  379.1 13.0 %collective-permute-start.69 = (bf16[6,3,96,128]{3,2,1,0:T(8,128)(2,1)S(1)}, bf16[6,3,96,128]{3,2,1,0:T(8,128)(2,1)S(1)}, u32[]{:S(2)}, u32[]{:S(2)}) collective-permute-start(bf16[6,3,96,128]{3,2,1,0:T(8,128)(2,1)S(1)} %add_convert_fusion), channel_id=1, source_target_pairs={{0,8},{4,12},{8,0},{12,4},{16,24},{20,28},{24,16},{28,20},{1,9},{5... | collective-permute-start | bytes 1327112 | tf_op jit(solution)/shard_map/ppermute | solution.py:438
  383.1 18.5 %collective-permute-start.64 = (bf16[6,3,96,128]{3,2,1,0:T(8,128)(2,1)S(1)}, bf16[6,3,96,128]{3,2,1,0:T(8,128)(2,1)S(1)}, u32[]{:S(2)}, u32[]{:S(2)}) collective-permute-start(bf16[6,3,96,128]{3,2,1,0:T(8,128)(2,1)S(1)} %add_convert_fusion.1), channel_id=1, source_target_pairs={{0,24},{4,28},{8,16},{12,20},{16,8},{20,12},{24,0},{28,4},{1,25},{... | collective-permute-start | bytes 1327112 | tf_op jit(solution)/shard_map/ppermute | solution.py:438
  385.6 33.2 %collective-permute-start.59 = (bf16[6,3,96,128]{3,2,1,0:T(8,128)(2,1)S(1)}, bf16[6,3,96,128]{3,2,1,0:T(8,128)(2,1)S(1)}, u32[]{:S(2)}, u32[]{:S(2)}) collective-permute-start(bf16[6,3,96,128]{3,2,1,0:T(8,128)(2,1)S(1)} %add_convert_fusion.2), channel_id=1, source_target_pairs={{0,16},{4,20},{8,24},{12,28},{16,0},{20,4},{24,8},{28,12},{1,17},{... | collective-permute-start | bytes 1327112 | tf_op jit(solution)/shard_map/ppermute | solution.py:438
  (115 other events, 1456.3 us)

commit v2 on v1

v2 whole, which is shorter than its diff:
```python
import functools

import jax
import jax.numpy as jnp
from jax import lax
from jax.experimental import pallas as pl
from jax.experimental.pallas import tpu as pltpu
from jax.sharding import PartitionSpec as P

HEADS = 12
HEAD_DIM = 64
FF = 3072
SEG_TOK = 512
MEM = 10
STEP = 10

beta_one = 0.9
beta_two = 0.95
adam_eps = 1e-08
norm_eps = 1e-12
rate_matrix = 0.05
rate_vector = 0.1
rate_shared = 0.75

BF = jnp.bfloat16
F32 = jnp.float32
VMEM_LIMIT = 56 * 1024 * 1024
VMEM_SPEC = pl.BlockSpec(memory_space=pltpu.VMEM)
SMEM_SPEC = pl.BlockSpec(memory_space=pltpu.SMEM)
ANY_SPEC = pl.BlockSpec(memory_space=pl.ANY)
GROUP = 4
TILES = 3
RP = 144
RS_ORDER = (3, 2, 1, 0)


def sds(shape, dtype):
    return jax.ShapeDtypeStruct(shape, dtype)


def params(**kw):
    return pltpu.CompilerParams(vmem_limit_bytes=VMEM_LIMIT, **kw)


def after(vals, deps):
    return lax.optimization_barrier((vals, deps))[0]


def cost(gflop, mbytes):
    return pl.CostEstimate(
        flops=int(gflop * 1e9), bytes_accessed=int(mbytes * 1e6), transcendentals=0
    )


def xor_pairs(size, step):
    return [(i, i ^ step) for i in range(size)]


def z_pairs(pairs):
    return [(2 * a + x, 2 * b + x) for a, b in pairs for x in range(2)]


def pack_plain(blocks):
    lead = blocks.shape[:-3]
    grp = blocks.reshape(lead + (-1, GROUP, 96, 96))
    last = jnp.swapaxes(grp[..., 3, :, :].reshape(lead + (-1, 96, 3, 32)), -3, -2)
    return jnp.concatenate([grp[..., :3, :, :], last], axis=-1)


def unpack_plain(groups):
    last = jnp.swapaxes(groups[..., 96:], -3, -2)
    last = last.reshape(groups.shape[:-3] + (1, 96, 96))
    grp = jnp.concatenate([groups[..., :96], last], axis=-3)
    return grp.reshape(groups.shape[:-4] + (-1, 96, 96))


def pack_body(m_ref, out_ref):
    for g in range(out_ref.shape[0]):
        last = m_ref[GROUP * g + 3].astype(BF)
        for k in range(TILES):
            out_ref[g, k] = jnp.concatenate(
                [m_ref[GROUP * g + k].astype(BF), last[:, 32 * k : 32 * k + 32]], axis=-1
            )


def pack_owned(blocks):
    n = blocks.shape[0] // GROUP
    return pl.pallas_call(
        pack_body,
        out_shape=sds((n, TILES, 96, 128), BF),
        in_specs=[VMEM_SPEC],
        out_specs=VMEM_SPEC,
        compiler_params=params(),
        cost_estimate=cost(0.1, 2),
        name="pack_owned",
    )(blocks)


def weights_body(n_pieces, places, pos_ref, me_ref, *refs):
    pieces = refs[:n_pieces]
    wqkv_ref, wo_ref, w1_ref, w2_ref, al, sem = refs[n_pieces:]
    dp, y = me_ref[0], me_ref[1] // 2
    copies = []
    for ref, (jy, jd) in zip(pieces, places):
        n = ref.shape[-4]
        if jd is None:
            copy = pltpu.make_async_copy(ref, al.at[:, :, pl.ds(0, TILES)], sem)
        else:
            copy = pltpu.make_async_copy(
                ref, al.at[y ^ jy, pl.ds((dp ^ jd) * n, n), pl.ds(0, TILES)], sem
            )
        copy.start()
        copies.append(copy)
    for copy in copies:
        copy.wait()
    groups = al.shape[1]

    for s in range(2):

        def fix(g, carry, s=s):
            al[s, g, 3, :, 0:96] = jnp.concatenate(
                [al[s, g, k, :, 96:128] for k in range(TILES)], axis=-1
            )
            return carry

        lax.fori_loop(0, groups, fix, 0, unroll=8)

    def block(s, b):
        p = pos_ref[b]
        return al[s, p // GROUP, p % GROUP][:, :96]

    def strip(i, carry):
        rows = pl.ds(pl.multiple_of(i * 96, 96), 96)
        for part in range(3):
            wqkv_ref[rows, part * 384 : part * 384 + 384] = jnp.concatenate(
                [block(j // 2, i * 6 + part * 2 + j % 2) for j in range(4)], axis=-1
            )
        for s in range(2):
            for half in range(2):
                cols = slice(half * 384, half * 384 + 384)
                w1_ref[s, rows, cols] = jnp.concatenate(
                    [block(s, 64 + i * 8 + half * 4 + j) for j in range(4)], axis=-1
                )
                w2_ref[s, rows, cols] = jnp.concatenate(
                    [block(s, 128 + i * 8 + half * 4 + j) for j in range(4)], axis=-1
                )
        return carry

    lax.fori_loop(0, 8, strip, 0, unroll=2)
    for i in range(4):
        for half in range(2):
            wo_ref[i * 96 : i * 96 + 96, half * 384 : half * 384 + 384] = jnp.concatenate(
                [block(i // 2, 48 + (i % 2) * 8 + half * 4 + j) for j in range(4)], axis=-1
            )


def build_weights(pos, me, pieces, places, slots):
    return pl.pallas_call(
        functools.partial(weights_body, len(pieces), places),
        out_shape=(
            sds((768, 1152), BF),
            sds((384, 768), BF),
            sds((2, 768, 768), BF),
            sds((2, 768, 768), BF),
        ),
        in_specs=[SMEM_SPEC, SMEM_SPEC] + [ANY_SPEC] * len(pieces),
        out_specs=(VMEM_SPEC,) * 4,
        scratch_shapes=[
            pltpu.VMEM((2, slots // GROUP, GROUP, 96, 128), BF),
            pltpu.SemaphoreType.DMA,
        ],
        compiler_params=params(),
        cost_estimate=cost(0.1, 30),
        name="build_weights",
    )(pos, me, *pieces)


def product(left, right, out, width=256):
    def step(i, carry):
        col = pl.multiple_of(i * width, width)
        out[pl.ds(col, width), :] = inner_rows(left[:, pl.ds(col, width)], right[...]).astype(BF)
        return carry

    lax.fori_loop(0, out.shape[0] // width, step, 0)


def feed_grads_body(act_ref, d2_ref, h_ref, dpre_ref, g1_ref, g2_ref):
    for s in range(2):
        product(act_ref.at[s], d2_ref, g2_ref.at[s])
        product(h_ref, dpre_ref.at[s], g1_ref.at[s])


def feed_grads(act, d_two, h_in, d_pre):
    rows = h_in.shape[0]
    return pl.pallas_call(
        feed_grads_body,
        out_shape=(sds((2, 768, 768), BF),) * 2,
        in_specs=[VMEM_SPEC] * 4,
        out_specs=(VMEM_SPEC,) * 2,
        compiler_params=params(),
        cost_estimate=pl.CostEstimate(
            flops=2 * rows * 768 * 768 * 4, bytes_accessed=10 * 1024 * 1024, transcendentals=0
        ),
        name="feed_grads",
    )(act, d_two, h_in, d_pre)


def grads_body(places, pos_ref, me_ref, *refs):
    x, dproj, ctx, d1, g1, g2 = refs[:6]
    outs = refs[6 : 6 + len(places)]
    gq, go, al, sem = refs[6 + len(places) :]
    groups = al.shape[1]
    product(ctx, d1, go, 128)
    product(x, dproj, gq)

    def put(s, b, blk):
        p = pos_ref[b]
        al[s, p // GROUP, p % GROUP, :, 0:96] = blk

    def strip(i, carry):
        rows = pl.ds(pl.multiple_of(i * 96, 96), 96)
        for part in range(3):
            vals = gq[rows, part * 384 : part * 384 + 384]
            for j in range(4):
                put(j // 2, i * 6 + part * 2 + j % 2, vals[:, 96 * j : 96 * j + 96])
        for s in range(2):
            for ref, first in ((g1, 64), (g2, 128)):
                for half in range(2):
                    vals = ref[s, rows, half * 384 : half * 384 + 384]
                    for j in range(4):
                        put(s, first + i * 8 + half * 4 + j, vals[:, 96 * j : 96 * j + 96])
        return carry

    lax.fori_loop(0, 8, strip, 0, unroll=2)
    for i in range(4):
        for half in range(2):
            vals = go[i * 96 : i * 96 + 96, half * 384 : half * 384 + 384]
            for j in range(4):
                put(i // 2, 48 + (i % 2) * 8 + half * 4 + j, vals[:, 96 * j : 96 * j + 96])
    for s in range(2):

        def fix(g, carry, s=s):
            last = al[s, g, 3]
            for k in range(TILES):
                al[s, g, k, :, 96:128] = last[:, 32 * k : 32 * k + 32]
            return carry

        lax.fori_loop(0, groups, fix, 0, unroll=8)

    dp, y = me_ref[0], me_ref[1] // 2
    copies = []
    for ref, (jy, jd, first) in zip(outs, places):
        if jd is None:
            copy = pltpu.make_async_copy(al.at[:, :, pl.ds(0, TILES)], ref, sem)
        else:
            base = (dp ^ jd) * (groups // 8) + first
            copy = pltpu.make_async_copy(
                al.at[y ^ jy, pl.ds(base, ref.shape[0]), pl.ds(0, TILES)], ref, sem
            )
        copy.start()
        copies.append(copy)
    for copy in copies:
        copy.wait()


def weight_grads(pos, me, srcs, places, out_shapes, slots):
    return pl.pallas_call(
        functools.partial(grads_body, places),
        out_shape=tuple(sds(s, BF) for s in out_shapes),
        in_specs=[SMEM_SPEC, SMEM_SPEC] + [VMEM_SPEC] * 6,
        out_specs=(ANY_SPEC,) * len(places),
        scratch_shapes=[
            pltpu.VMEM((768, 1152), BF),
            pltpu.VMEM((384, 768), BF),
            pltpu.VMEM((2, slots // GROUP, GROUP, 96, 128), BF),
            pltpu.SemaphoreType.DMA,
        ],
        compiler_params=params(),
        cost_estimate=cost(2.0, 30),
        name="weight_grads",
    )(pos, me, *srcs)


def project_body(flags_ref, xa, xb, xc, xd, sh_ref, w_ref, b_ref, proj_ref, x0_ref, xin_ref, bias):
    @pl.when(pl.program_id(0) == 0)
    def _():
        n = xa.shape[0]
        gap = jnp.zeros((RP - n, x0_ref.shape[1]), F32)
        for k, ref in enumerate((xa, xb, xc, xd)):
            x0_ref[k * RP : k * RP + n, :] = ref[...].astype(F32)
            x0_ref[k * RP + n : k * RP + RP, :] = gap

            @pl.when((flags_ref[0] == k) & (flags_ref[1] == 1))
            def _(k=k):
                x0_ref[k * RP : k * RP + MEM, :] = sh_ref[6 : 6 + MEM, :]

        xin_ref[...] = x0_ref[...].astype(BF)
        for part, col in ((0, 0), (2, 192)):
            bias[part] = jnp.concatenate([b_ref[s : s + 1, col : col + 192] for s in range(2)], axis=1)
        bias[1] = jnp.zeros((1, 384), F32)

    proj_ref[...] = (dot(xin_ref[...], w_ref[...]) + bias[pl.program_id(0)]).astype(BF)


def project(flags, quarters, shared, w_qkv, biases):
    rows = 4 * RP

    def whole(shape):
        return pl.BlockSpec(shape, lambda i: (0, 0))

    return pl.pallas_call(
        project_body,
        grid=(3,),
        out_shape=(sds((rows, 1152), BF), sds((rows, 768), F32), sds((rows, 768), BF)),
        in_specs=[
            SMEM_SPEC,
            *[whole(q.shape) for q in quarters],
            whole(shared.shape),
            pl.BlockSpec((768, 384), lambda i: (0, i)),
            whole(biases.shape),
        ],
        out_specs=(
            pl.BlockSpec((rows, 384), lambda i: (0, i)),
            whole((rows, 768)),
            whole((rows, 768)),
        ),
        scratch_shapes=[pltpu.VMEM((3, 1, 384), F32)],
        compiler_params=params(),
        cost_estimate=cost(1.0, 5),
        name="project",
    )(flags, *quarters, shared, w_qkv, biases)


def head_masks(shape):
    lane = lax.broadcasted_iota(jnp.int32, shape, 1)
    return lane < HEAD_DIM, lane >= HEAD_DIM


def attend_body(cq_ref, ck_ref, q_ref, k_ref, v_ref, wo_ref, ctx_ref, p_ref, part_ref, vis):
    h = pl.program_id(0)

    @pl.when(h == 0)
    def _():
        cq, ck = cq_ref[...], ck_ref[...]
        seen = ((cq == -1) | (ck == -1) | (cq == ck)) & (ck != -2)
        vis[...] = jnp.where(seen, 1.0, 0.0)

    q, k, v = q_ref[...], k_ref[...], v_ref[...]
    masks = head_masks(q.shape)
    outs = []
    for n in range(2):
        qh = jnp.where(masks[n], q, jnp.zeros_like(q))
        scores = jnp.where(vis[...] > 0.5, dot_back(qh, k) * HEAD_DIM ** (-0.5), -1000000000.0)
        e = jnp.exp(scores - jnp.max(scores, axis=-1, keepdims=True))
        p = (e * (1.0 / jnp.sum(e, axis=-1, keepdims=True))).astype(BF)
        p_ref[n] = p
        outs.append(dot(p, v))
    ctx_ref[:, pl.ds(pl.multiple_of(h * 128, 128), 128)] = jnp.where(masks[0], outs[0], outs[1]).astype(BF)

    @pl.when(h == pl.num_programs(0) - 1)
    def _():
        part_ref[...] = dot(ctx_ref[...], wo_ref[...]).astype(BF)


def head_col(rows, off):
    return pl.BlockSpec((rows, 128), lambda h: (0, h + off))


def all_steps(shape):
    return pl.BlockSpec(shape, lambda h: (0,) * len(shape))


def attend(code_q, code_k, proj, w_out):
    rows = proj.shape[0]
    pairs = HEADS // 4
    return pl.pallas_call(
        attend_body,
        grid=(pairs,),
        out_shape=(sds((rows, 384), BF), sds((2 * pairs, rows, rows), BF), sds((rows, 768), BF)),
        in_specs=[
            all_steps((rows, 1)),
            all_steps((1, rows)),
            head_col(rows, 0),
            head_col(rows, pairs),
            head_col(rows, 2 * pairs),
            all_steps((384, 768)),
        ],
        out_specs=(
            all_steps((rows, 384)),
            pl.BlockSpec((2, rows, rows), lambda h: (h, 0, 0)),
            all_steps((rows, 768)),
        ),
        scratch_shapes=[pltpu.VMEM((rows, rows), F32)],
        compiler_params=params(),
        cost_estimate=cost(2.5, 8),
        name="attend",
    )(code_q, code_k, proj, proj, proj, w_out)


def both_cores(mine_ref, other_ref):
    half = mine_ref.shape[0] // 2
    other = jnp.concatenate([other_ref[half:, :], other_ref[:half, :]], axis=0)
    return mine_ref[...].astype(F32) + other.astype(F32)


def col_sum(v):
    return jnp.sum(v, axis=0, keepdims=True)


def feed_body(mine_ref, other_ref, x0_ref, sh_ref, b_ref, w1_hbm, w2_hbm, h_ref, n_ref, r_ref, act_ref, slope_ref, part_ref, w1, w2, acc, sems):
    copies = []
    for s in range(2):
        copies.append(pltpu.make_async_copy(w1_hbm.at[s], w1.at[s], sems.at[s]))
        copies.append(pltpu.make_async_copy(w2_hbm.at[s], w2.at[s], sems.at[2 + s]))
    for copy in copies:
        copy.start()
    total = both_cores(mine_ref, other_ref) + sh_ref[0:1, :] + x0_ref[...]
    h_one, normed, inverse = norm_parts(total, sh_ref[1:2, :], sh_ref[2:3, :])
    h_ref[...] = h_one.astype(BF)
    n_ref[...] = normed
    r_ref[...] = inverse
    for s in range(2):
        copies[2 * s].wait()
        pre = dot(h_ref[...], w1[s]) + b_ref[s : s + 1, 384:]
        cdf = 0.5 * (1.0 + lax.erf(pre * 0.7071067811865476))
        act_ref[s] = (pre * cdf).astype(BF)
        slope_ref[s] = (cdf + pre * jnp.exp(-0.5 * pre * pre) * 0.3989422804014327).astype(BF)
        copies[2 * s + 1].wait()
        part = dot(act_ref[s], w2[s])
        acc[...] = part if s == 0 else acc[...] + part
    part_ref[...] = acc[...].astype(BF)


def feed(mine, other, x_zero, shared, biases, w1, w2):
    rows = x_zero.shape[0]
    one, two = sds((rows, 768), BF), sds((2, rows, 768), BF)
    return pl.pallas_call(
        feed_body,
        out_shape=(one, sds((rows, 768), F32), sds((rows, 1), F32), two, two, one),
        in_specs=[VMEM_SPEC] * 5 + [ANY_SPEC] * 2,
        out_specs=(VMEM_SPEC,) * 6,
        scratch_shapes=[
            pltpu.VMEM((2, 768, 768), BF),
            pltpu.VMEM((2, 768, 768), BF),
            pltpu.VMEM((rows, 768), F32),
            pltpu.SemaphoreType.DMA((4,)),
        ],
        compiler_params=params(),
        cost_estimate=cost(2.8, 16),
        name="feed",
    )(mine, other, x_zero, shared, biases, w1, w2)


def feed_back_body(mine_ref, other_ref, n_ref, slope_ref, ca, cb, cc, cd, sh_ref, w1_hbm, w2_hbm, out_ref, d2_ref, d2b_ref, dpre_ref, part_ref, sums_ref, bsum_ref, w1, w2, g, acc, sems):
    copies = []
    for s in range(2):
        copies.append(pltpu.make_async_copy(w2_hbm.at[s], w2.at[s], sems.at[2 + s]))
        copies.append(pltpu.make_async_copy(w1_hbm.at[s], w1.at[s], sems.at[s]))
    for copy in copies:
        copy.start()
    n = ca.shape[0]
    for k, ref in enumerate((ca, cb, cc, cd)):
        g[k * RP : k * RP + n, :] = ref[...].astype(F32)
        g[k * RP + n : k * RP + RP, :] = jnp.zeros((RP - n, 768), F32)
    own = g.shape[0] // 2

    def row(i):
        return sh_ref[i : i + 1, :]

    h_one = n_ref[...] * row(1) + row(2)
    total = both_cores(mine_ref, other_ref) + row(3) + h_one
    rows_out, normed, inverse = norm_parts(total, row(4), row(5))
    out_ref[...] = rows_out[:own].astype(BF)
    grad = g[...]
    d_two = norm_back(grad, normed, inverse, row(4))
    d2_ref[...] = d_two
    d2b_ref[...] = d_two.astype(BF)
    sums_ref[0:3, :] = jnp.concatenate(
        [col_sum(d_two[:own]), col_sum(grad[:own] * normed[:own]), col_sum(grad[:own])], axis=0
    )
    sums_ref[3:8, :] = jnp.zeros((5, 768), F32)
    for s in range(2):
        copies[2 * s].wait()
        d_pre = dot_back(d2b_ref[...], w2[s]) * slope_ref[s].astype(F32)
        bsum_ref[s : s + 1, :] = col_sum(d_pre)
        dpre_ref[s] = d_pre.astype(BF)
        copies[2 * s + 1].wait()
        part = dot_back(dpre_ref[s], w1[s])
        acc[...] = part if s == 0 else acc[...] + part
    part_ref[...] = acc[...].astype(BF)


def feed_back(mine, other, normed, slope, cots, shared, w1, w2):
    rows = normed.shape[0]
    one = sds((rows, 768), BF)
    return pl.pallas_call(
        feed_back_body,
        out_shape=(
            sds((rows // 2, 768), BF),
            sds((rows, 768), F32),
            one,
            sds((2, rows, 768), BF),
            one,
            sds((8, 768), F32),
            sds((2, 768), F32),
        ),
        in_specs=[VMEM_SPEC] * 9 + [ANY_SPEC] * 2,
        out_specs=(VMEM_SPEC,) * 7,
        scratch_shapes=[
            pltpu.VMEM((2, 768, 768), BF),
            pltpu.VMEM((2, 768, 768), BF),
            pltpu.VMEM((rows, 768), F32),
            pltpu.VMEM((rows, 768), F32),
            pltpu.SemaphoreType.DMA((4,)),
        ],
        compiler_params=params(),
        cost_estimate=cost(2.8, 16),
        name="feed_back",
    )(mine, other, normed, slope, *cots, shared, w1, w2)


def attend_back_body(mine_ref, other_ref, d2_ref, n_ref, r_ref, sh_ref, wo_ref, wqkv_ref, p_ref, q_ref, k_ref, v_ref, d1_ref, d1b_ref, dproj_ref, part_ref, sums_ref, bsum_ref, dctx):
    h = pl.program_id(0)
    pairs = pl.num_programs(0)
    own = d1_ref.shape[0]

    @pl.when(h == 0)
    def _():
        dh = both_cores(mine_ref, other_ref) + d2_ref[...]
        normed = n_ref[...]
        d_one = norm_back(dh, normed, r_ref[...], sh_ref[1:2, :])
        d1_ref[...] = d_one[:own]
        d1b_ref[...] = d_one.astype(BF)
        sums_ref[0:3, :] = jnp.concatenate(
            [col_sum(d_one[:own]), col_sum(dh[:own] * normed[:own]), col_sum(dh[:own])], axis=0
        )
        sums_ref[3:8, :] = jnp.zeros((5, 768), F32)
        back = dot_back(d1b_ref[...], wo_ref[...]).astype(BF)
        for m in range(3):
            dctx[m] = back[:, m * 128 : m * 128 + 128]

    q, k, v, dc = q_ref[...], k_ref[...], v_ref[...], dctx[h]
    masks = head_masks(q.shape)
    dqs, dks, dvs = [], [], []
    for m in range(2):
        dch = jnp.where(masks[m], dc, jnp.zeros_like(dc))
        p = p_ref[m]
        dvs.append(inner_rows(p, dc))
        dp = dot_back(dch, v)
        pf = p.astype(F32)
        row = jnp.sum(dp * pf, axis=-1, keepdims=True)
        ds = (pf * (dp - row) * HEAD_DIM ** (-0.5)).astype(BF)
        dqs.append(dot(ds, k))
        dks.append(inner_rows(ds, q))
    dq, dk, dv = (jnp.where(masks[0], d[0], d[1]) for d in (dqs, dks, dvs))
    for part, d in enumerate((dq, dk, dv)):
        dproj_ref[:, pl.ds(pl.multiple_of(part * 384 + h * 128, 128), 128)] = d.astype(BF)
    bsum_ref[...] = jnp.concatenate([col_sum(dq), col_sum(dv), jnp.zeros((6, 128), F32)], axis=0)

    @pl.when(h == pairs - 1)
    def _():
        part_ref[...] = dot_back(dproj_ref[...], wqkv_ref[...]).astype(BF)


def attend_back(mine, other, d_two, normed, inverse, shared, w_out, w_qkv, probs, proj):
    rows = proj.shape[0]
    pairs = HEADS // 4
    return pl.pallas_call(
        attend_back_body,
        grid=(pairs,),
        out_shape=(
            sds((rows // 2, 768), F32),
            sds((rows, 768), BF),
            sds((rows, 1152), BF),
            sds((rows, 768), BF),
            sds((8, 768), F32),
            sds((8, 384), F32),
        ),
        in_specs=[
            all_steps((rows, 768)),
            all_steps((rows, 768)),
            all_steps((rows, 768)),
            all_steps((rows, 768)),
            all_steps((rows, 1)),
            all_steps(shared.shape),
            all_steps((384, 768)),
            all_steps((768, 1152)),
            pl.BlockSpec((2, rows, rows), lambda h: (h, 0, 0)),
            head_col(rows, 0),
            head_col(rows, pairs),
            head_col(rows, 2 * pairs),
        ],
        out_specs=(
            all_steps((rows // 2, 768)),
            all_steps((rows, 768)),
            all_steps((rows, 1152)),
            all_steps((rows, 768)),
            all_steps((8, 768)),
            pl.BlockSpec((8, 128), lambda h: (0, h)),
        ),
        scratch_shapes=[pltpu.VMEM((3, rows, 128), BF)],
        compiler_params=params(),
        cost_estimate=pl.CostEstimate(
            flops=2 * rows * rows * 64 * 4 * HEADS, bytes_accessed=10 * 1024 * 1024, transcendentals=0
        ),
        name="attend_back",
    )(mine, other, d_two, normed, inverse, shared, w_out, w_qkv, probs, proj, proj, proj)


def finish_body(flags_ref, part_ref, other_ref, d1_ref, gin_ref, mem_ref):
    own = d1_ref.shape[0]
    d_zero = part_ref[:own, :].astype(F32) + other_ref[...].astype(F32) + d1_ref[...]
    gin_ref[...] = d_zero.astype(BF)
    mem_ref[...] = jnp.zeros_like(mem_ref)
    for k in range(2):

        @pl.when((flags_ref[0] == k) & (flags_ref[1] == 1))
        def _(k=k):
            row = lax.broadcasted_iota(jnp.int32, (16, d_zero.shape[1]), 0)
            top = d_zero[k * RP : k * RP + 16, :]
            mem_ref[...] = jnp.where(row < MEM, top, 0.0)
            gin_ref[k * RP : k * RP + 16, :] = jnp.where(row < MEM, 0.0, top).astype(BF)


def finish(flags, part, other, d_one):
    return pl.pallas_call(
        finish_body,
        out_shape=(sds(d_one.shape, BF), sds((16, 768), F32)),
        in_specs=[SMEM_SPEC] + [VMEM_SPEC] * 3,
        out_specs=(VMEM_SPEC,) * 2,
        compiler_params=params(),
        cost_estimate=cost(0.1, 4),
        name="finish",
    )(flags, part, other, d_one)


def soap_body(n_terms, *refs):
    terms = refs[:n_terms]
    w_ref, m_ref, v_ref, sl_ref, sr_ref, l_ref, r_ref = refs[n_terms : n_terms + 7]
    nw_ref, nc_ref, nm_ref, nv_ref, nl_ref, nr_ref = refs[n_terms + 7 :]
    blocks = w_ref.shape[0]
    if n_terms == 1:
        grads = [terms[0][b] for b in range(blocks)]
    else:
        tiles = [sum(ref[0, k].astype(F32) for ref in terms) for k in range(TILES)]
        grads = [tile[:, :96] for tile in tiles]
        grads.append(jnp.concatenate([tile[:, 96:] for tile in tiles], axis=-1))
    for b in range(blocks):
        gb = grads[b].astype(BF)
        lb, rb = l_ref[b].astype(BF), r_ref[b].astype(BF)
        turned = dot(inner_rows(lb, gb).astype(BF), rb)
        new_first = beta_one * m_ref[b] + (1.0 - beta_one) * turned
        new_second = beta_two * v_ref[b] + (1.0 - beta_two) * turned * turned
        direction = (
            new_first
            / (1.0 - beta_one**STEP)
            / (jnp.sqrt(new_second / (1.0 - beta_two**STEP)) + adam_eps)
        )
        back = dot_back(dot(lb, direction.astype(BF)).astype(BF), rb)
        new_weight = w_ref[b] - rate_matrix * back
        nw_ref[b] = new_weight
        nc_ref[b] = new_weight.astype(BF)
        nm_ref[b] = new_first
        nv_ref[b] = new_second
        nl_ref[b] = beta_two * sl_ref[b] + (1.0 - beta_two) * dot_back(gb, gb)
        nr_ref[b] = beta_two * sr_ref[b] + (1.0 - beta_two) * inner_rows(gb, gb)


def soap(terms, master, first, second, left, right, left_rot, right_rot):
    count = master.shape[0]
    step = GROUP if len(terms) > 1 else 1
    spec = pl.BlockSpec((step, 96, 96), lambda i: (i, 0, 0))
    packed = pl.BlockSpec((1, TILES, 96, 128), lambda i: (i, 0, 0, 0))
    full = sds(master.shape, F32)
    return pl.pallas_call(
        functools.partial(soap_body, len(terms)),
        grid=(count // step,),
        out_shape=(full, sds(master.shape, BF), full, full, full, full),
        in_specs=[packed if len(terms) > 1 else spec] * len(terms) + [spec] * 7,
        out_specs=(spec,) * 6,
        compiler_params=params(),
        cost_estimate=cost(0.3, 24),
        name="soap",
    )(*terms, master, first, second, left, right, left_rot, right_rot)


def norm_parts(values, gain_vec, shift_vec):
    centred = values - jnp.mean(values, axis=-1, keepdims=True)
    inverse = lax.rsqrt(jnp.mean(centred * centred, axis=-1, keepdims=True) + norm_eps)
    normed = centred * inverse
    return (normed * gain_vec + shift_vec, normed, inverse)


def norm_back(upstream, normed, inverse, gain_vec):
    scaled = upstream * gain_vec
    result = inverse * (
        scaled
        - jnp.mean(scaled, axis=-1, keepdims=True)
        - normed * jnp.mean(scaled * normed, axis=-1, keepdims=True)
    )
    return result


def dot(left, right):
    return jnp.dot(left, right, preferred_element_type=F32)


def dot_back(left, right):
    return lax.dot_general(left, right, (((1,), (1,)), ((), ())), preferred_element_type=F32)


def inner_rows(left, right):
    return lax.dot_general(left, right, (((0,), (0,)), ((), ())), preferred_element_type=F32)


def adam_update(values, grad_vec, first_mom, second_mom, step_rate):
    new_first = beta_one * first_mom + (1.0 - beta_one) * grad_vec
    new_second = beta_two * second_mom + (1.0 - beta_two) * grad_vec * grad_vec
    direction = (
        new_first
        / (1.0 - beta_one**STEP)
        / (jnp.sqrt(new_second / (1.0 - beta_two**STEP)) + adam_eps)
    )
    return (values - step_rate * direction, new_first, new_second)


def per_device(
    n_dp,
    n_tensor,
    layer_in,
    cotangent,
    doc_ids,
    reset_flags,
    block_slot,
    master,
    first_moment,
    second_moment,
    left_stats,
    right_stats,
    left_basis,
    right_basis,
    split_params,
    split_first,
    split_second,
    shared,
    shared_first,
    shared_second,
):
    meshed = n_dp == 8 and master.shape[1] % GROUP == 0
    dp = lax.axis_index("dp")
    t = lax.axis_index("tensor")
    y, c = t // 2, t % 2
    me = jnp.stack([dp, t])
    barrier = lax.optimization_barrier
    slots = block_slot.shape[0]
    quarter = layer_in.shape[1]

    def swap(axis, step):
        size = n_dp if axis == "dp" else n_tensor
        return lambda v: lax.ppermute(v, axis, xor_pairs(size, step))

    core, yswap, xswap = swap("tensor", 1), swap("tensor", 2), swap("dp", 1)

    def along_z(*pairs):
        return lambda v: lax.ppermute(v, "dp", z_pairs(pairs))

    outer, middle = along_z((0, 1), (1, 0), (2, 3), (3, 2)), along_z((1, 2), (2, 1))
    inward, outward = along_z((0, 1), (3, 2)), along_z((1, 0), (2, 3))

    docs = lax.dynamic_index_in_dim(doc_ids, y, 0, keepdims=False)
    edge = jnp.full((MEM,), -1, jnp.int32)
    codes = jnp.concatenate([edge, docs, edge]).reshape(4, quarter)
    codes = jnp.pad(codes, ((0, 0), (0, RP - quarter)), constant_values=-2)
    codes = jnp.concatenate(
        [lax.dynamic_index_in_dim(codes, t ^ j, 0, keepdims=False) for j in (0, 2, 1, 3)]
    )
    code_q, code_k = codes[:, None], codes[None, :]
    reset_now = lax.dynamic_index_in_dim(reset_flags, y, 0, keepdims=False) == 1
    flags = jnp.stack([y + 2 * c, reset_now.astype(jnp.int32)])

    split_other = yswap(split_params)
    biases = jnp.concatenate(
        [jnp.where(y == 0, split_params, split_other), jnp.where(y == 0, split_other, split_params)], axis=0
    )
    def inputs_of(arr):
        mine = lax.dynamic_index_in_dim(arr, y, 0, keepdims=False)
        other = lax.dynamic_index_in_dim(arr, 1 - y, 0, keepdims=False)
        return mine, other

    (in_mine, in_send), (cot_mine, cot_send) = inputs_of(layer_in), inputs_of(cotangent)

    if meshed:
        own = pack_owned(master[0])
        near = outer(own)
        mid = middle(own)
        x0, y0 = xswap(own), yswap(own)
        near, mid, x0, y0 = barrier((near, mid, x0, y0))
        far_mid, far_end = middle(near), outward(mid)
        x1, diag0 = xswap(near), yswap(x0)
        small = (code_q, code_k, flags, biases, me, in_mine, in_send, cot_mine, cot_send)
        x1, diag0, far_mid, far_end, y0, small = barrier((x1, diag0, far_mid, far_end, y0, small))
        code_q, code_k, flags, biases, me, in_mine, in_send, cot_mine, cot_send = small
        far = far_mid + far_end
        last_end = outward(far_mid)
        x2, y2 = xswap(far), yswap(far)
        x2, y2, last_end, y0, diag0, in_send = barrier((x2, y2, last_end, y0, diag0, in_send))
        last = mid + last_end
        x3, y3, y1 = xswap(last), yswap(last), outer(y0)
        x3, y3, y1, x2, diag0 = barrier((x3, y3, y1, x2, diag0))
        diag3, diag2, diag1 = xswap(y3), yswap(x2), outer(diag0)
        in_other = yswap(in_send)
        diag3, diag2, diag1, cot_send = barrier((diag3, diag2, diag1, cot_send))
        pieces, places = [], []
        for jz, vals in enumerate(
            ((own, x0, y0, diag0), (near, x1, y1, diag1), (far, x2, y2, diag2), (last, x3, y3, diag3))
        ):
            pieces.extend(vals)
            places.extend([(0, 2 * jz), (0, 2 * jz + 1), (1, 2 * jz), (1, 2 * jz + 1)])
    else:
        every = lax.all_gather(master.astype(BF), "dp", axis=1, tiled=True)
        every_other = yswap(every)
        every = jnp.concatenate(
            [jnp.where(y == 0, every, every_other), jnp.where(y == 0, every_other, every)], axis=0
        )
        pieces, places = [pack_plain(every)], [(0, None)]
        in_other = yswap(in_send)
    w_qkv, w_out, w_up, w_down = build_weights(block_slot, me, pieces, tuple(places), slots)

    cot_other = yswap(cot_send)
    quarters = (in_mine, in_other, core(in_mine), core(in_other))
    cots = (cot_mine, cot_other, core(cot_mine), core(cot_other))
    proj, x_zero, x_in = project(flags, quarters, shared, w_qkv, biases)
    proj, cots = barrier((proj, cots))
    context, probs, attn = attend(code_q, code_k, proj, w_out)
    h_in, normed, inverse, act, slope, ffn = feed(attn, core(attn), x_zero, shared, biases, w_up, w_down)
    rows_out, d_two, d_two_b, d_pre, d_hidden, sums_two, up_sums = feed_back(
        ffn, core(ffn), normed, slope, cots, shared, w_up, w_down
    )
    d_hidden_other = core(d_hidden)
    g_up, g_down = feed_grads(act, d_two_b, h_in, d_pre)
    d_one, d_one_b, d_proj, d_in, sums_one, head_sums = attend_back(
        d_hidden, d_hidden_other, d_two, normed, inverse, shared, w_out, w_qkv, probs, proj
    )
    d_in_send = d_in[2 * RP :]

    def to_owner(arr):
        mine, other = arr[:quarter], yswap(arr[RP : RP + quarter])
        both = jnp.stack([mine, other])
        return jnp.where(y == 0, both, both[::-1])

    layer_out = to_owner(rows_out)
    d_proj, layer_out = barrier((d_proj, layer_out))
    d_in_other = core(d_in_send)
    srcs = (x_in, d_proj, context, d_one_b, g_up, g_down)
    grad_rows, memory_grad = finish(flags, d_in, d_in_other, d_one)
    vec = jnp.concatenate([sums_one[:3], sums_two[:3], memory_grad[:MEM]], axis=0)
    halves = head_sums[:2].reshape(2, 2, 192).swapaxes(0, 1).reshape(2, 384)
    splits = jnp.concatenate([halves, up_sums], axis=1).reshape(3, 768)

    def add_core(vec):
        return jnp.concatenate([vec + core(vec), splits], axis=0)

    if meshed:
        per = master.shape[1] // GROUP
        half = per // 2
        places, shapes = [], []
        for jz in RS_ORDER:
            for jy in range(2):
                for jx in range(2):
                    places.append((jy, 2 * jz + jx, 0))
                    shapes.append((per, TILES, 96, 128))
        packed = weight_grads(block_slot, me, srcs, tuple(places), shapes, slots)
        own, x_unit, y_unit, diag = {}, {}, {}, {}
        for n, jz in enumerate(RS_ORDER):
            own[jz], x_unit[jz], y_unit[jz], diag[jz] = packed[4 * n : 4 * n + 4]

        def plus(*vals):
            return sum(v.astype(F32) for v in vals).astype(BF)

        d3, d2, n1 = xswap(diag[3]), yswap(diag[2]), outer(diag[1])
        vec = add_core(after(vec, packed[0]))
        d3, d2, n1, vec, x_unit[3], y_unit[1] = barrier((d3, d2, n1, vec, x_unit[3], y_unit[1]))
        x3, y3, m1 = xswap(x_unit[3]), yswap(plus(y_unit[3], d3)), outer(y_unit[1])
        vec = vec + yswap(vec)
        x3, y3, m1, vec, y_unit[2] = barrier((x3, y3, m1, vec, y_unit[2]))
        x2, y2 = xswap(plus(x_unit[2], d2)), yswap(y_unit[2])
        part3 = plus(own[3], x3, y3)
        e3 = inward(part3)
        vec = vec + swap("dp", 1)(vec)
        x2, y2, e3, x_unit[1], vec = barrier((x2, y2, e3, x_unit[1], vec))
        x1, d0 = xswap(x_unit[1]), yswap(plus(diag[0], n1))
        part2 = plus(own[2], x2, y2, e3)
        fm, fe = middle(part2), inward(part2)
        vec = vec + swap("dp", 2)(vec)
        x1, d0, fm, fe, vec, m1 = barrier((x1, d0, fm, fe, vec, m1))
        x0, y0 = xswap(plus(x_unit[0], d0)), yswap(plus(y_unit[0], m1))
        near, mid = outer(plus(own[1], x1, fm)), middle(plus(part3, fe))
        vec = vec + swap("dp", 4)(vec)
        x0, y0, near, mid, vec, grad_rows = barrier((x0, y0, near, mid, vec, grad_rows))
        terms = (own[0], x0, y0, near, mid)
    else:
        packed = weight_grads(
            block_slot, me, srcs, ((0, None, 0),), [(2, slots // GROUP, TILES, 96, 128)], slots
        )[0]
        blocks = unpack_plain(packed)
        blocks = lax.psum_scatter(blocks, "dp", scatter_dimension=1, tiled=True)
        mine = lax.dynamic_index_in_dim(blocks, y, 0, keepdims=False)
        other = yswap(lax.dynamic_index_in_dim(blocks, 1 - y, 0, keepdims=False))
        terms = (mine.astype(F32) + other.astype(F32),)

        vec = add_core(vec)
        vec = vec + yswap(vec)
        step = 1
        while step < n_dp:
            vec = vec + swap("dp", step)(vec)
            step *= 2

    grad_in = to_owner(grad_rows)
    total_shared = vec[:16]
    grad_split = lax.dynamic_index_in_dim(vec[16:].reshape(2, -1), y, 0, keepdims=True)

    new_master, new_copy, new_first, new_second, new_left, new_right = soap(
        terms,
        master[0],
        first_moment[0],
        second_moment[0],
        left_stats[0],
        right_stats[0],
        left_basis[0],
        right_basis[0],
    )
    new_split, new_split_first, new_split_second = adam_update(
        split_params, grad_split, split_first, split_second, rate_vector
    )
    new_shared, new_shared_first, new_shared_second = adam_update(
        shared, total_shared, shared_first, shared_second, rate_shared
    )
    return (
        layer_out,
        grad_in,
        new_master[None],
        new_copy[None],
        new_first[None],
        new_second[None],
        new_left[None],
        new_right[None],
        new_split,
        new_split_first,
        new_split_second,
        new_shared,
        new_shared_first,
        new_shared_second,
    )


def solution(mesh):
    rows = P("dp", "tensor", None)
    state = P("tensor", "dp", None, None)
    split = P("tensor", None)
    return jax.shard_map(
        functools.partial(per_device, mesh.shape["dp"], mesh.shape["tensor"]),
        mesh=mesh,
        in_specs=(rows, rows, P("dp", None), P("dp"), P()) + (state,) * 7 + (split,) * 3 + (P(),) * 3,
        out_specs=(rows, rows) + (state,) * 6 + (split,) * 3 + (P(),) * 3,
        check_vma=False,
    )
```

time: 446 us -> 280 us (0.63)
  the two profiles are of different devices: /device:TPU:0 before, /device:TPU:8 now
where the time goes in v2:
time: 280 us; the launch traced here: 276 us
  Pallas kernels  111 us (40%)
  waiting for transfers between devices  86.3 us (31%)
  starting transfers between devices  56.9 us (20%)
  local copies, waits for them, and re-layouts  13.6 us (5%)
  other arithmetic  5.57 us (2%)
    ppermute x38, waiting for transfers between devices, swap(): return lambda v: lax.ppermute(v, axis, xor_pairs(size, step))  70.1 us
    ppermute x38, starting transfers between devices, swap(): return lambda v: lax.ppermute(v, axis, xor_pairs(size, step))  29.6 us
    ppermute x14, starting transfers between devices, along_z(): return lambda v: lax.ppermute(v, 'dp', z_pairs(pairs))  27.3 us
    pallas_call x1, Pallas kernels, weight_grads(): pl.pallas_call(functools.partial(grads_body, places), out_shape=tuple((sd...  19.3 us
    ppermute x14, waiting for transfers between devices, along_z(): return lambda v: lax.ppermute(v, 'dp', z_pairs(pairs))  16.1 us
    pallas_call x1, Pallas kernels, attend_back(): pl.pallas_call(attend_back_body, grid=(pairs,), out_shape=(sds((rows // 2...  16 us
    pallas_call x1, Pallas kernels, soap(): pl.pallas_call(functools.partial(soap_body, len(terms)), grid=(count // s...  12.1 us
    pallas_call x1, Pallas kernels, build_weights(): pl.pallas_call(functools.partial(weights_body, len(pieces), places), out_...  12 us
  transfers between devices with their start and end apart: 52, of which 30 were waited for; matrix products, arithmetic and copies ran while one was open for 5% of the time, Pallas kernels for 28%

profile of v2, /device:TPU:8, one launch (start us, length us, event | category | flops | bytes accessed | tf_op | source)
XLA Modules:
  0.0 275.6 jit_solution(17661360127775079408)
XLA Ops:
  0.7 2.3 pack_owned.1.refs_0_
  3.0 1.5 collective-permute-start.3
  4.5 1.5 collective-permute-start.2
  6.0 3.5 %collective-permute-start.1 = (bf16[6,3,96,128]{3,2,1,0:T(8,128)(2,1)}, bf16[6,3,96,128]{3,2,1,0:T(8,128)(2,1)S(1)}, u32[]{:S(2)}, u32[]{:S(2)}) collective-permute-start(bf16[6,3,96,128]{3,2,1,0:T(8,128)(2,1)} %pack_owned.1.refs_0_), channel_id=1, source_target_pairs={{8,16},{12,20},{16,8},{20,12},{9,17},{13,21},{17,9},{21,13},{10,18... | collective-permute-start | bytes 1327112 | tf_op jit(solution)/shard_map/ppermute | solution.py:765
  11.7 1.7 constant_dynamic-slice_fusion.1
  15.2 1.3 collective-permute-done.2.refs_1_
  16.5 3.0 %collective-permute-done.1 = bf16[6,3,96,128]{3,2,1,0:T(8,128)(2,1)S(1)} collective-permute-done((bf16[6,3,96,128]{3,2,1,0:T(8,128)(2,1)}, bf16[6,3,96,128]{3,2,1,0:T(8,128)(2,1)S(1)}, u32[]{:S(2)}, u32[]{:S(2)}) %collective-permute-start.1) | collective-permute-done | bytes 442400 | tf_op jit(solution)/shard_map/ppermute | solution.py:765
  19.4 1.5 collective-permute-done.refs_4_
  20.9 2.3 collective-permute-start.6
  24.4 1.3 collective-permute-start.7
  26.4 7.8 %collective-permute-done.5.refs_3_ = bf16[6,3,96,128]{3,2,1,0:T(8,128)(2,1)S(1)} collective-permute-done((bf16[6,3,96,128]{3,2,1,0:T(8,128)(2,1)}, bf16[6,3,96,128]{3,2,1,0:T(8,128)(2,1)S(1)}, u32[]{:S(2)}, u32[]{:S(2)}) %collective-permute-start.5) | collective-permute-done | bytes 442400 | tf_op jit(solution)/shard_map/ppermute | solution.py:760
  34.9 1.5 collective-permute-start.9
  36.4 4.1 %collective-permute-start.11 = (bf16[6,3,96,128]{3,2,1,0:T(8,128)(2,1)S(1)}, bf16[6,3,96,128]{3,2,1,0:T(8,128)(2,1)S(1)}, u32[]{:S(2)}, u32[]{:S(2)}) collective-permute-start(bf16[6,3,96,128]{3,2,1,0:T(8,128)(2,1)S(1)} %collective-permute-done.6), channel_id=1, source_target_pairs={{8,0},{12,4},{16,24},{20,28},{9,1},{13,5},{17,25},{21,29},{10,2},{... | collective-permute-start | bytes 1327112 | tf_op jit(solution)/shard_map/ppermute | solution.py:765
  40.4 2.8 %collective-permute-done.10.refs_10_ = bf16[6,3,96,128]{3,2,1,0:T(8,128)(2,1)S(1)} collective-permute-done((bf16[6,3,96,128]{3,2,1,0:T(8,128)(2,1)S(1)}, bf16[6,3,96,128]{3,2,1,0:T(8,128)(2,1)S(1)}, u32[]{:S(2)}, u32[]{:S(2)}) %collective-permute-start.10) | collective-permute-done | bytes 442400 | tf_op jit(solution)/shard_map/ppermute | solution.py:760
  43.9 3.7 %collective-permute-done.11 = bf16[6,3,96,128]{3,2,1,0:T(8,128)(2,1)S(1)} collective-permute-done((bf16[6,3,96,128]{3,2,1,0:T(8,128)(2,1)S(1)}, bf16[6,3,96,128]{3,2,1,0:T(8,128)(2,1)S(1)}, u32[]{:S(2)}, u32[]{:S(2)}) %collective-permute-start.11) | collective-permute-done | bytes 442400 | tf_op jit(solution)/shard_map/ppermute | solution.py:765
  48.0 2.5 collective-permute-start.17
  50.5 5.7 %collective-permute-done.16.refs_14_ = bf16[6,3,96,128]{3,2,1,0:T(8,128)(2,1)S(1)} collective-permute-done((bf16[6,3,96,128]{3,2,1,0:T(8,128)(2,1)S(1)}, bf16[6,3,96,128]{3,2,1,0:T(8,128)(2,1)S(1)}, u32[]{:S(2)}, u32[]{:S(2)}) %collective-permute-start.16) | collective-permute-done | bytes 442400 | tf_op jit(solution)/shard_map/ppermute | solution.py:760
  56.8 2.6 collective-permute-done.17.refs_6_
  59.4 2.3 collective-permute-start.20
  61.7 3.2 %collective-permute-start.18 = (bf16[6,3,96,128]{3,2,1,0:T(8,128)(2,1)S(1)}, bf16[6,3,96,128]{3,2,1,0:T(8,128)(2,1)S(1)}, u32[]{:S(2)}, u32[]{:S(2)}) collective-permute-start(bf16[6,3,96,128]{3,2,1,0:T(8,128)(2,1)S(1)} %collective-permute-done.16.refs_14_), channel_id=1, source_target_pairs={{0,4},{4,0},{8,12},{12,8},{16,20},{20,16},{24,28},{28,24},{1,5},{5... | collective-permute-start | bytes 1327112 | tf_op jit(solution)/shard_map/ppermute | solution.py:760
  64.9 2.3 collective-permute-start.19
  68.0 3.2 %collective-permute-done.18.refs_15_ = bf16[6,3,96,128]{3,2,1,0:T(8,128)(2,1)S(1)} collective-permute-done((bf16[6,3,96,128]{3,2,1,0:T(8,128)(2,1)S(1)}, bf16[6,3,96,128]{3,2,1,0:T(8,128)(2,1)S(1)}, u32[]{:S(2)}, u32[]{:S(2)}) %collective-permute-start.18) | collective-permute-done | bytes 442400 | tf_op jit(solution)/shard_map/ppermute | solution.py:760
  71.2 2.3 collective-permute-done.19.refs_11_
  73.4 2.0 collective-permute-start.21
  76.2 3.0 %collective-permute-done.21.cb = bf16[133,768]{1,0:T(8,128)(2,1)S(1)} collective-permute-done((bf16[133,768]{1,0:T(8,128)(2,1)S(1)}, bf16[133,768]{1,0:T(8,128)(2,1)S(1)}, u32[]{:S(2)}, u32[]{:S(2)}) %collective-permute-start.21) | collective-permute-done | bytes 204320 | tf_op jit(solution)/shard_map/ppermute | solution.py:760
  80.2 12.0 %build_weights.1 = (bf16[768,1152]{1,0:T(8,128)(2,1)}, bf16[384,768]{1,0:T(8,128)(2,1)}, bf16[2,768,768]{2,1,0:T(8,128)(2,1)}, bf16[2,768,768]{2,1,0:T(8,128)(2,1)}) custom-call(s32[192]{0:T(256)} %pos_ref.3, s32[2]{0:T(128)} %get-tuple-element.152.me_ref, bf16[6,3,96,128]{3,2,1,0:T(8,128)(2,1)} %pack_owned.1.refs_0_, ...), custom_call_target="tpu_custom_call" | custom-call | flops 100000000 | bytes 30000000 | tf_op jit(solution)/shard_map/build_weights/pallas_call | solution.py:158
  92.3 5.1 %project.1 = (bf16[576,1152]{1,0:T(8,128)(2,1)}, f32[576,768]{1,0:T(8,128)}, bf16[576,768]{1,0:T(8,128)(2,1)}) custom-call(s32[2]{0:T(128)} %get-tuple-element.144.flags_ref, bf16[133,768]{1,0:T(8,128)(2,1)} %bitcast.52, bf16[133,768]{1,0:T(8,128)(2,1)} %copy-done.49, bf16[133,768]{1,0:T(8,128)(2,1)} %collective-permute-done.13.xc, ...), custom_call_target="tpu_custom_call" | custom-call | flops 1000000000 | bytes 5000000 | tf_op jit(solution)/shard_map/project/pallas_call | solution.py:311
  97.4 10.7 %attend.1 = (bf16[576,384]{1,0:T(8,128)(2,1)}, bf16[6,576,576]{2,1,0:T(8,128)(2,1)}, bf16[576,768]{1,0:T(8,128)(2,1)}) custom-call(s32[576,1]{1,0:T(8,128)} %copy.39.cq_ref, s32[1,576]{1,0:T(1,128)} %broadcast_in_dim.25.ck_ref, bf16[576,1152]{1,0:T(8,128)(2,1)} %get-tuple-element.173.q_ref.k_ref.v_ref, ...), custom_call_target="tpu_custom_call" | custom-call | flops 2500000000 | bytes 8000000 | tf_op jit(solution)/shard_map/attend/pallas_call | solution.py:376
  108.6 2.3 collective-permute-done.24.other_ref
  110.9 0.9 copy-done.45
  111.8 10.1 %feed.1 = (bf16[576,768]{1,0:T(8,128)(2,1)}, f32[576,768]{1,0:T(8,128)}, f32[576,1]{1,0:T(8,128)}, bf16[2,576,768]{2,1,0:T(8,128)(2,1)}, bf16[2,576,768]{2,1,0:T(8,128)(2,1)}, /*index=5*/bf16[576,768]{1,0:T(8,128)(2,1)}) custom-call(bf16[576,768]{1,0:T(8,128)(2,1)} %get-tuple-element.175.mine_ref, bf16[576,768]{1,0:T(8,128)(2,1)} %copy-done.45, ...), custom_call_target="tpu_custom_call" | custom-call | flops 2800000000 | bytes 16000000 | tf_op jit(solution)/shard_map/feed/pallas_call | solution.py:437
  122.3 2.3 collective-permute-done.25.other_ref
  124.6 0.9 copy-done.7
  125.5 10.2 %feed_back.1 = (bf16[288,768]{1,0:T(8,128)(2,1)}, f32[576,768]{1,0:T(8,128)}, bf16[576,768]{1,0:T(8,128)(2,1)}, bf16[2,576,768]{2,1,0:T(8,128)(2,1)}, bf16[576,7...) custom-call(bf16[576,768]{1,0:T(8,128)(2,1)} %get-tuple-element.179.mine_ref, bf16[576,768]{1,0:T(8,128)(2,1)} %copy-done.7, ...), custom_call_target="tpu_custom_call" | custom-call | flops 2800000000 | bytes 16000000 | tf_op jit(solution)/shard_map/feed_back/pallas_call | solution.py:496
  136.2 1.1 slice_bitcast_fusion.1
  137.3 2.1 collective-permute-start.27
  139.4 10.5 %feed_grads.1 = (bf16[2,768,768]{2,1,0:T(8,128)(2,1)}, bf16[2,768,768]{2,1,0:T(8,128)(2,1)}) custom-call(bf16[2,576,768]{2,1,0:T(8,128)(2,1)} %get-tuple-element.197.act_ref, bf16[576,768]{1,0:T(8,128)(2,1)} %get-tuple-element.198.d2_ref, bf16[576,768]{1,0:T(8,128)(2,1)} %get-tuple-element.199.h_ref, bf16[2,576,768]{2,1,0:T(8,128)(2,1)} %get-tuple-element.200.dpre_ref), custom_call_target="tpu_custom_call" | custom-call | flops 2717908992 | bytes 10485760 | tf_op jit(solution)/shard_map/feed_grads/pallas_call | solution.py:195
  149.9 0.9 copy-done.6
  150.8 16.0 %attend_back.1 = (f32[288,768]{1,0:T(8,128)}, bf16[576,768]{1,0:T(8,128)(2,1)}, bf16[576,1152]{1,0:T(8,128)(2,1)}, bf16[576,768]{1,0:T(8,128)(2,1)}, f32[8,768]{1,0:T(8,128)}, /*index=5*/f32[8,384]{1,0:T(8,128)}) custom-call(bf16[576,768]{1,0:T(8,128)(2,1)} %get-tuple-element.186.mine_ref, bf16[576,768]{1,0:T(8,128)(2,1)} %copy-done.6, ...), custom_call_target="tpu_custom_call" | custom-call | flops 2038431744 | bytes 10485760 | tf_op jit(solution)/shard_map/attend_back/pallas_call | solution.py:568
  166.9 1.0 slice.37
  169.0 19.3 %weight_grads.1 = (bf16[6,3,96,128]{3,2,1,0:T(8,128)(2,1)}, bf16[6,3,96,128]{3,2,1,0:T(8,128)(2,1)}, bf16[6,3,96,128]{3,2,1,0:T(8,128)(2,1)}, bf16[6,3,96,128]{3...) custom-call(s32[192]{0:T(256)} %pos_ref.3, ...), custom_call_target="tpu_custom_call" | custom-call | flops 2000000000 | bytes 30000000 | tf_op jit(solution)/shard_map/weight_grads/pallas_call | solution.py:267
  188.7 1.3 collective-permute-start.30
  190.7 2.5 finish.1
  194.3 1.2 collective-permute-done.32
  195.5 5.7 %collective-permute-done.28 = bf16[6,3,96,128]{3,2,1,0:T(8,128)(2,1)S(1)} collective-permute-done((bf16[6,3,96,128]{3,2,1,0:T(8,128)(2,1)}, bf16[6,3,96,128]{3,2,1,0:T(8,128)(2,1)S(1)}, u32[]{:S(2)}, u32[]{:S(2)}) %collective-permute-start.28) | collective-permute-done | bytes 442400 | tf_op jit(solution)/shard_map/ppermute | solution.py:760
  201.4 1.6 collective-permute-start.34
  203.1 1.8 collective-permute-start.35
  205.6 1.0 collective-permute-start.33
  206.6 9.3 %collective-permute-done.37 = f32[19,768]{1,0:T(8,128)S(1)} collective-permute-done((f32[19,768]{1,0:T(8,128)S(1)}, f32[19,768]{1,0:T(8,128)S(1)}, u32[]{:S(2)}, u32[]{:S(2)}) %collective-permute-start.37) | collective-permute-done | bytes 58400 | tf_op jit(solution)/shard_map/ppermute | solution.py:760
  216.2 1.3 collective-permute-start.39
  217.5 1.5 collective-permute-start.38
  220.5 3.8 %collective-permute-done.40 = f32[19,768]{1,0:T(8,128)S(1)} collective-permute-done((f32[19,768]{1,0:T(8,128)S(1)}, f32[19,768]{1,0:T(8,128)S(1)}, u32[]{:S(2)}, u32[]{:S(2)}) %collective-permute-start.40) | collective-permute-done | bytes 58400 | tf_op jit(solution)/shard_map/ppermute | solution.py:760
  224.4 3.9 %collective-permute-done.39 = bf16[6,3,96,128]{3,2,1,0:T(8,128)(2,1)S(1)} collective-permute-done((bf16[6,3,96,128]{3,2,1,0:T(8,128)(2,1)S(1)}, bf16[6,3,96,128]{3,2,1,0:T(8,128)(2,1)S(1)}, u32[]{:S(2)}, u32[]{:S(2)}) %collective-permute-start.39) | collective-permute-done | bytes 442400 | tf_op jit(solution)/shard_map/ppermute | solution.py:765
  228.3 2.3 collective-permute-done.38
  230.9 1.4 collective-permute-start.44
  232.3 3.4 %collective-permute-start.43 = (bf16[6,3,96,128]{3,2,1,0:T(8,128)(2,1)S(1)}, bf16[6,3,96,128]{3,2,1,0:T(8,128)(2,1)S(1)}, u32[]{:S(2)}, u32[]{:S(2)}) collective-permute-start(bf16[6,3,96,128]{3,2,1,0:T(8,128)(2,1)S(1)} %add_convert_fusion.4), channel_id=1, source_target_pairs={{8,16},{12,20},{16,8},{20,12},{9,17},{13,21},{17,9},{21,13},{10,18... | collective-permute-start | bytes 1327112 | tf_op jit(solution)/shard_map/ppermute | solution.py:765
  236.6 5.5 %collective-permute-done.45 = f32[19,768]{1,0:T(8,128)S(1)} collective-permute-done((f32[19,768]{1,0:T(8,128)S(1)}, f32[19,768]{1,0:T(8,128)S(1)}, u32[]{:S(2)}, u32[]{:S(2)}) %collective-permute-start.45) | collective-permute-done | bytes 58400 | tf_op jit(solution)/shard_map/ppermute | solution.py:760
  242.5 4.1 %collective-permute-done.41 = bf16[6,3,96,128]{3,2,1,0:T(8,128)(2,1)S(1)} collective-permute-done((bf16[6,3,96,128]{3,2,1,0:T(8,128)(2,1)S(1)}, bf16[6,3,96,128]{3,2,1,0:T(8,128)(2,1)S(1)}, u32[]{:S(2)}, u32[]{:S(2)}) %collective-permute-start.41) | collective-permute-done | bytes 442400 | tf_op jit(solution)/shard_map/ppermute | solution.py:760
  246.9 1.7 collective-permute-start.47
  249.2 3.4 %collective-permute-start.49 = (bf16[6,3,96,128]{3,2,1,0:T(8,128)(2,1)S(1)}, bf16[6,3,96,128]{3,2,1,0:T(8,128)(2,1)S(1)}, u32[]{:S(2)}, u32[]{:S(2)}) collective-permute-start(bf16[6,3,96,128]{3,2,1,0:T(8,128)(2,1)S(1)} %add_convert_fusion), channel_id=1, source_target_pairs={{8,16},{12,20},{16,8},{20,12},{9,17},{13,21},{17,9},{21,13},{10,18... | collective-permute-start | bytes 1327112 | tf_op jit(solution)/shard_map/ppermute | solution.py:765
  252.7 1.1 copy.41
  253.8 6.2 %collective-permute-done.50 = f32[19,768]{1,0:T(8,128)S(1)} collective-permute-done((f32[19,768]{1,0:T(8,128)S(1)}, f32[19,768]{1,0:T(8,128)S(1)}, u32[]{:S(2)}, u32[]{:S(2)}) %collective-permute-start.50) | collective-permute-done | bytes 58400 | tf_op jit(solution)/shard_map/ppermute | solution.py:760
  261.6 12.1 %soap.1 = (f32[24,96,96]{2,1,0:T(8,128)}, bf16[24,96,96]{2,1,0:T(8,128)(2,1)}, f32[24,96,96]{2,1,0:T(8,128)}, f32[24,96,96]{2,1,0:T(8,128)}, f32[24,96,96]{2,1,0:T(8,128)}, /*index=5*/f32[24,96,96]{2,1,0:T(8,128)}) custom-call(bf16[6,3,96,128]{3,2,1,0:T(8,128)(2,1)} %get-tuple-element.250.refs_0_, bf16[6,3,96,128]{3,2,1,0:T(8,128)(2,1)} %copy-done.28, ...), custom_call_target="tpu_custom_call" | custom-call | flops 300000000 | bytes 24000000 | tf_op jit(solution)/shard_map/soap/pallas_call | solution.py:675
  274.5 1.1 copy.42
  (210 shorter events, 21.9 us)
Async XLA Ops:
  3.0 12.2 %collective-permute-start.3 = (bf16[6,3,96,128]{3,2,1,0:T(8,128)(2,1)}, bf16[6,3,96,128]{3,2,1,0:T(8,128)(2,1)S(1)}, u32[]{:S(2)}, u32[]{:S(2)}) collective-permute-start(bf16[6,3,96,128]{3,2,1,0:T(8,128)(2,1)} %pack_owned.1.refs_0_), channel_id=1, source_target_pairs={{0,2},{1,3},{2,0},{3,1},{4,6},{5,7},{6,4},{7,5},{8,10},{9,11},{10,... | collective-permute-start | bytes 1327112 | tf_op jit(solution)/shard_map/ppermute | solution.py:760
  4.5 11.9 %collective-permute-start.2 = (bf16[6,3,96,128]{3,2,1,0:T(8,128)(2,1)}, bf16[6,3,96,128]{3,2,1,0:T(8,128)(2,1)}, u32[]{:S(2)}, u32[]{:S(2)}) collective-permute-start(bf16[6,3,96,128]{3,2,1,0:T(8,128)(2,1)} %pack_owned.1.refs_0_), channel_id=1, source_target_pairs={{0,4},{4,0},{8,12},{12,8},{16,20},{20,16},{24,28},{28,24},{1,5},{5... | collective-permute-start | bytes 1327112 | tf_op jit(solution)/shard_map/ppermute | solution.py:760
  6.0 13.4 %collective-permute-start.1 = (bf16[6,3,96,128]{3,2,1,0:T(8,128)(2,1)}, bf16[6,3,96,128]{3,2,1,0:T(8,128)(2,1)S(1)}, u32[]{:S(2)}, u32[]{:S(2)}) collective-permute-start(bf16[6,3,96,128]{3,2,1,0:T(8,128)(2,1)} %pack_owned.1.refs_0_), channel_id=1, source_target_pairs={{8,16},{12,20},{16,8},{20,12},{9,17},{13,21},{17,9},{21,13},{10,18... | collective-permute-start | bytes 1327112 | tf_op jit(solution)/shard_map/ppermute | solution.py:765
  9.5 11.4 %collective-permute-start = (bf16[6,3,96,128]{3,2,1,0:T(8,128)(2,1)}, bf16[6,3,96,128]{3,2,1,0:T(8,128)(2,1)}, u32[]{:S(2)}, u32[]{:S(2)}) collective-permute-start(bf16[6,3,96,128]{3,2,1,0:T(8,128)(2,1)} %pack_owned.1.refs_0_), channel_id=1, source_target_pairs={{0,8},{4,12},{8,0},{12,4},{16,24},{20,28},{24,16},{28,20},{1,9},{5... | collective-permute-start | bytes 1327112 | tf_op jit(solution)/shard_map/ppermute | solution.py:765
  9.6 16.1 %collective-permute-start.8 = (f32[1,1152]{1,0:T(1,128)S(1)}, f32[1,1152]{1,0:T(1,128)S(1)}, u32[]{:S(2)}, u32[]{:S(2)}) collective-permute-start(f32[1,1152]{1,0:T(1,128)S(1)} %copy-done.39), channel_id=1, source_target_pairs={{0,2},{1,3},{2,0},{3,1},{4,6},{5,7},{6,4},{7,5},{8,10},{9,11},{10,... | collective-permute-start | bytes 13832 | tf_op jit(solution)/shard_map/ppermute | solution.py:760
  14.7 61.3 %copy-start.8 = (bf16[1,133,768]{2,1,0:T(8,128)(2,1)}, bf16[1,133,768]{2,1,0:T(8,128)(2,1)S(1)}, u32[]{:S(2)}) copy-start(bf16[1,133,768]{2,1,0:T(8,128)(2,1)S(1)} %copy.52) | copy-start | bytes 612868
  14.7 60.7 %copy-start.35 = (bf16[1,133,768]{2,1,0:T(8,128)(2,1)}, bf16[1,133,768]{2,1,0:T(8,128)(2,1)S(1)}, u32[]{:S(2)}) copy-start(bf16[1,133,768]{2,1,0:T(8,128)(2,1)S(1)} %copy.54) | copy-start | bytes 612868
  15.2 32.8 %copy-start.17 = (bf16[6,3,96,128]{3,2,1,0:T(8,128)(2,1)}, bf16[6,3,96,128]{3,2,1,0:T(8,128)(2,1)S(1)}, u32[]{:S(2)}) copy-start(bf16[6,3,96,128]{3,2,1,0:T(8,128)(2,1)S(1)} %collective-permute-done.3.refs_2_) | copy-start | bytes 1327108
  20.9 13.3 %collective-permute-start.6 = (bf16[6,3,96,128]{3,2,1,0:T(8,128)(2,1)}, bf16[6,3,96,128]{3,2,1,0:T(8,128)(2,1)S(1)}, u32[]{:S(2)}, u32[]{:S(2)}) collective-permute-start(bf16[6,3,96,128]{3,2,1,0:T(8,128)(2,1)} %collective-permute-done.refs_4_), channel_id=1, source_target_pairs={{8,16},{12,20},{16,8},{20,12},{9,17},{13,21},{17,9},{21,13},{10,18... | collective-permute-start | bytes 1327112 | tf_op jit(solution)/shard_map/ppermute | solution.py:765
  23.3 10.9 %collective-permute-start.4 = (bf16[6,3,96,128]{3,2,1,0:T(8,128)(2,1)}, bf16[6,3,96,128]{3,2,1,0:T(8,128)(2,1)S(1)}, u32[]{:S(2)}, u32[]{:S(2)}) collective-permute-start(bf16[6,3,96,128]{3,2,1,0:T(8,128)(2,1)} %collective-permute-done.refs_4_), channel_id=1, source_target_pairs={{0,4},{4,0},{8,12},{12,8},{16,20},{20,16},{24,28},{28,24},{1,5},{5... | collective-permute-start | bytes 1327112 | tf_op jit(solution)/shard_map/ppermute | solution.py:760
  23.9 10.3 %collective-permute-start.5 = (bf16[6,3,96,128]{3,2,1,0:T(8,128)(2,1)}, bf16[6,3,96,128]{3,2,1,0:T(8,128)(2,1)S(1)}, u32[]{:S(2)}, u32[]{:S(2)}) collective-permute-start(bf16[6,3,96,128]{3,2,1,0:T(8,128)(2,1)} %collective-permute-done.2.refs_1_), channel_id=1, source_target_pairs={{0,2},{1,3},{2,0},{3,1},{4,6},{5,7},{6,4},{7,5},{8,10},{9,11},{10,... | collective-permute-start | bytes 1327112 | tf_op jit(solution)/shard_map/ppermute | solution.py:760
  24.4 9.8 %collective-permute-start.7 = (bf16[6,3,96,128]{3,2,1,0:T(8,128)(2,1)S(1)}, bf16[6,3,96,128]{3,2,1,0:T(8,128)(2,1)S(1)}, u32[]{:S(2)}, u32[]{:S(2)}) collective-permute-start(bf16[6,3,96,128]{3,2,1,0:T(8,128)(2,1)S(1)} %collective-permute-done.1), channel_id=1, source_target_pairs={{8,0},{12,4},{16,24},{20,28},{9,1},{13,5},{17,25},{21,29},{10,2},{... | collective-permute-start | bytes 1327112 | tf_op jit(solution)/shard_map/ppermute | solution.py:765
  34.2 25.2 %copy-start.20 = (bf16[6,3,96,128]{3,2,1,0:T(8,128)(2,1)}, bf16[6,3,96,128]{3,2,1,0:T(8,128)(2,1)S(1)}, u32[]{:S(2)}) copy-start(bf16[6,3,96,128]{3,2,1,0:T(8,128)(2,1)S(1)} %collective-permute-done.5.refs_3_) | copy-start | bytes 1327108
  34.4 45.8 %copy-start.2 = (bf16[6,3,96,128]{3,2,1,0:T(8,128)(2,1)}, bf16[6,3,96,128]{3,2,1,0:T(8,128)(2,1)S(1)}, u32[]{:S(2)}) copy-start(bf16[6,3,96,128]{3,2,1,0:T(8,128)(2,1)S(1)} %add.131.refs_8_) | copy-start | bytes 1327108
  34.4 8.8 %collective-permute-start.10 = (bf16[6,3,96,128]{3,2,1,0:T(8,128)(2,1)S(1)}, bf16[6,3,96,128]{3,2,1,0:T(8,128)(2,1)S(1)}, u32[]{:S(2)}, u32[]{:S(2)}) collective-permute-start(bf16[6,3,96,128]{3,2,1,0:T(8,128)(2,1)S(1)} %add.131.refs_8_), channel_id=1, source_target_pairs={{0,2},{1,3},{2,0},{3,1},{4,6},{5,7},{6,4},{7,5},{8,10},{9,11},{10,... | collective-permute-start | bytes 1327112 | tf_op jit(solution)/shard_map/ppermute | solution.py:760
  34.9 8.3 %collective-permute-start.9 = (bf16[6,3,96,128]{3,2,1,0:T(8,128)(2,1)S(1)}, bf16[6,3,96,128]{3,2,1,0:T(8,128)(2,1)S(1)}, u32[]{:S(2)}, u32[]{:S(2)}) collective-permute-start(bf16[6,3,96,128]{3,2,1,0:T(8,128)(2,1)S(1)} %add.131.refs_8_), channel_id=1, source_target_pairs={{0,4},{4,0},{8,12},{12,8},{16,20},{20,16},{24,28},{28,24},{1,5},{5... | collective-permute-start | bytes 1327112 | tf_op jit(solution)/shard_map/ppermute | solution.py:760
  36.4 11.3 %collective-permute-start.11 = (bf16[6,3,96,128]{3,2,1,0:T(8,128)(2,1)S(1)}, bf16[6,3,96,128]{3,2,1,0:T(8,128)(2,1)S(1)}, u32[]{:S(2)}, u32[]{:S(2)}) collective-permute-start(bf16[6,3,96,128]{3,2,1,0:T(8,128)(2,1)S(1)} %collective-permute-done.6), channel_id=1, source_target_pairs={{8,0},{12,4},{16,24},{20,28},{9,1},{13,5},{17,25},{21,29},{10,2},{... | collective-permute-start | bytes 1327112 | tf_op jit(solution)/shard_map/ppermute | solution.py:765
  43.9 32.2 %copy-start.22 = (bf16[6,3,96,128]{3,2,1,0:T(8,128)(2,1)}, bf16[6,3,96,128]{3,2,1,0:T(8,128)(2,1)S(1)}, u32[]{:S(2)}) copy-start(bf16[6,3,96,128]{3,2,1,0:T(8,128)(2,1)S(1)} %collective-permute-done.9.refs_9_) | copy-start | bytes 1327108
  47.8 32.4 %copy-start.3 = (bf16[6,3,96,128]{3,2,1,0:T(8,128)(2,1)}, bf16[6,3,96,128]{3,2,1,0:T(8,128)(2,1)S(1)}, u32[]{:S(2)}) copy-start(bf16[6,3,96,128]{3,2,1,0:T(8,128)(2,1)S(1)} %add.132.refs_12_) | copy-start | bytes 1327108
  47.8 8.4 %collective-permute-start.16 = (bf16[6,3,96,128]{3,2,1,0:T(8,128)(2,1)S(1)}, bf16[6,3,96,128]{3,2,1,0:T(8,128)(2,1)S(1)}, u32[]{:S(2)}, u32[]{:S(2)}) collective-permute-start(bf16[6,3,96,128]{3,2,1,0:T(8,128)(2,1)S(1)} %add.132.refs_12_), channel_id=1, source_target_pairs={{0,2},{1,3},{2,0},{3,1},{4,6},{5,7},{6,4},{7,5},{8,10},{9,11},{10,... | collective-permute-start | bytes 1327112 | tf_op jit(solution)/shard_map/ppermute | solution.py:760
  47.9 9.0 %collective-permute-start.15 = (bf16[6,3,96,128]{3,2,1,0:T(8,128)(2,1)S(1)}, bf16[6,3,96,128]{3,2,1,0:T(8,128)(2,1)S(1)}, u32[]{:S(2)}, u32[]{:S(2)}) collective-permute-start(bf16[6,3,96,128]{3,2,1,0:T(8,128)(2,1)S(1)} %add.132.refs_12_), channel_id=1, source_target_pairs={{0,4},{4,0},{8,12},{12,8},{16,20},{20,16},{24,28},{28,24},{1,5},{5... | collective-permute-start | bytes 1327112 | tf_op jit(solution)/shard_map/ppermute | solution.py:760
  48.0 11.4 %collective-permute-start.17 = (bf16[6,3,96,128]{3,2,1,0:T(8,128)(2,1)S(1)}, bf16[6,3,96,128]{3,2,1,0:T(8,128)(2,1)S(1)}, u32[]{:S(2)}, u32[]{:S(2)}) collective-permute-start(bf16[6,3,96,128]{3,2,1,0:T(8,128)(2,1)S(1)} %collective-permute-done.3.refs_2_), channel_id=1, source_target_pairs={{0,8},{4,12},{8,0},{12,4},{16,24},{20,28},{24,16},{28,20},{1,9},{5... | collective-permute-start | bytes 1327112 | tf_op jit(solution)/shard_map/ppermute | solution.py:765
  56.2 24.0 %copy-start.23 = (bf16[6,3,96,128]{3,2,1,0:T(8,128)(2,1)}, bf16[6,3,96,128]{3,2,1,0:T(8,128)(2,1)S(1)}, u32[]{:S(2)}) copy-start(bf16[6,3,96,128]{3,2,1,0:T(8,128)(2,1)S(1)} %collective-permute-done.16.refs_14_) | copy-start | bytes 1327108
  56.8 23.4 %copy-start.24 = (bf16[6,3,96,128]{3,2,1,0:T(8,128)(2,1)}, bf16[6,3,96,128]{3,2,1,0:T(8,128)(2,1)S(1)}, u32[]{:S(2)}) copy-start(bf16[6,3,96,128]{3,2,1,0:T(8,128)(2,1)S(1)} %collective-permute-done.15.refs_13_) | copy-start | bytes 1327108
  59.4 20.8 %copy-start.25 = (bf16[6,3,96,128]{3,2,1,0:T(8,128)(2,1)}, bf16[6,3,96,128]{3,2,1,0:T(8,128)(2,1)S(1)}, u32[]{:S(2)}) copy-start(bf16[6,3,96,128]{3,2,1,0:T(8,128)(2,1)S(1)} %collective-permute-done.17.refs_6_) | copy-start | bytes 1327108
  59.4 8.6 %collective-permute-start.20 = (bf16[6,3,96,128]{3,2,1,0:T(8,128)(2,1)S(1)}, bf16[6,3,96,128]{3,2,1,0:T(8,128)(2,1)S(1)}, u32[]{:S(2)}, u32[]{:S(2)}) collective-permute-start(bf16[6,3,96,128]{3,2,1,0:T(8,128)(2,1)S(1)} %collective-permute-done.5.refs_3_), channel_id=1, source_target_pairs={{0,8},{4,12},{8,0},{12,4},{16,24},{20,28},{24,16},{28,20},{1,9},{5... | collective-permute-start | bytes 1327112 | tf_op jit(solution)/shard_map/ppermute | solution.py:765
  61.7 9.4 %collective-permute-start.18 = (bf16[6,3,96,128]{3,2,1,0:T(8,128)(2,1)S(1)}, bf16[6,3,96,128]{3,2,1,0:T(8,128)(2,1)S(1)}, u32[]{:S(2)}, u32[]{:S(2)}) collective-permute-start(bf16[6,3,96,128]{3,2,1,0:T(8,128)(2,1)S(1)} %collective-permute-done.16.refs_14_), channel_id=1, source_target_pairs={{0,4},{4,0},{8,12},{12,8},{16,20},{20,16},{24,28},{28,24},{1,5},{5... | collective-permute-start | bytes 1327112 | tf_op jit(solution)/shard_map/ppermute | solution.py:760
  64.9 8.6 %collective-permute-start.19 = (bf16[6,3,96,128]{3,2,1,0:T(8,128)(2,1)S(1)}, bf16[6,3,96,128]{3,2,1,0:T(8,128)(2,1)S(1)}, u32[]{:S(2)}, u32[]{:S(2)}) collective-permute-start(bf16[6,3,96,128]{3,2,1,0:T(8,128)(2,1)S(1)} %collective-permute-done.9.refs_9_), channel_id=1, source_target_pairs={{0,2},{1,3},{2,0},{3,1},{4,6},{5,7},{6,4},{7,5},{8,10},{9,11},{10,... | collective-permute-start | bytes 1327112 | tf_op jit(solution)/shard_map/ppermute | solution.py:760
  67.2 8.5 %collective-permute-start.12 = (bf16[133,768]{1,0:T(8,128)(2,1)S(1)}, bf16[133,768]{1,0:T(8,128)(2,1)S(1)}, u32[]{:S(2)}, u32[]{:S(2)}) collective-permute-start(bf16[133,768]{1,0:T(8,128)(2,1)S(1)} %bitcast.54), channel_id=1, source_target_pairs={{0,2},{1,3},{2,0},{3,1},{4,6},{5,7},{6,4},{7,5},{8,10},{9,11},{10,... | collective-permute-start | bytes 612872 | tf_op jit(solution)/shard_map/ppermute | solution.py:760
  73.4 5.8 %collective-permute-start.21 = (bf16[133,768]{1,0:T(8,128)(2,1)S(1)}, bf16[133,768]{1,0:T(8,128)(2,1)S(1)}, u32[]{:S(2)}, u32[]{:S(2)}) collective-permute-start(bf16[133,768]{1,0:T(8,128)(2,1)S(1)} %bitcast.53), channel_id=1, source_target_pairs={{0,2},{1,3},{2,0},{3,1},{4,6},{5,7},{6,4},{7,5},{8,10},{9,11},{10,... | collective-permute-start | bytes 612872 | tf_op jit(solution)/shard_map/ppermute | solution.py:760
  75.5 16.8 %collective-permute-start.13 = (bf16[133,768]{1,0:T(8,128)(2,1)S(1)}, bf16[133,768]{1,0:T(8,128)(2,1)}, u32[]{:S(2)}, u32[]{:S(2)}) collective-permute-start(bf16[133,768]{1,0:T(8,128)(2,1)S(1)} %bitcast.51), channel_id=1, source_target_pairs={{0,1},{1,0},{2,3},{3,2},{4,5},{5,4},{6,7},{7,6},{8,9},{9,8},{10,11... | collective-permute-start | bytes 612872 | tf_op jit(solution)/shard_map/ppermute | solution.py:760
  75.7 16.6 %copy-start.49 = (bf16[133,768]{1,0:T(8,128)(2,1)}, bf16[133,768]{1,0:T(8,128)(2,1)S(1)}, u32[]{:S(2)}) copy-start(bf16[133,768]{1,0:T(8,128)(2,1)S(1)} %collective-permute-done.12.xb) | copy-start | bytes 612868
  75.7 16.6 %collective-permute-start.14 = (bf16[133,768]{1,0:T(8,128)(2,1)S(1)}, bf16[133,768]{1,0:T(8,128)(2,1)}, u32[]{:S(2)}, u32[]{:S(2)}) collective-permute-start(bf16[133,768]{1,0:T(8,128)(2,1)S(1)} %collective-permute-done.12.xb), channel_id=1, source_target_pairs={{0,1},{1,0},{2,3},{3,2},{4,5},{5,4},{6,7},{7,6},{8,9},{9,8},{10,11... | collective-permute-start | bytes 612872 | tf_op jit(solution)/shard_map/ppermute | solution.py:760
  76.0 21.4 %collective-permute-start.22 = (bf16[133,768]{1,0:T(8,128)(2,1)S(1)}, bf16[133,768]{1,0:T(8,128)(2,1)}, u32[]{:S(2)}, u32[]{:S(2)}) collective-permute-start(bf16[133,768]{1,0:T(8,128)(2,1)S(1)} %bitcast.49), channel_id=1, source_target_pairs={{0,1},{1,0},{2,3},{3,2},{4,5},{5,4},{6,7},{7,6},{8,9},{9,8},{10,11... | collective-permute-start | bytes 612872 | tf_op jit(solution)/shard_map/ppermute | solution.py:760
  79.2 18.2 %collective-permute-start.23 = (bf16[133,768]{1,0:T(8,128)(2,1)S(1)}, bf16[133,768]{1,0:T(8,128)(2,1)}, u32[]{:S(2)}, u32[]{:S(2)}) collective-permute-start(bf16[133,768]{1,0:T(8,128)(2,1)S(1)} %collective-permute-done.21.cb), channel_id=1, source_target_pairs={{0,1},{1,0},{2,3},{3,2},{4,5},{5,4},{6,7},{7,6},{8,9},{9,8},{10,11... | collective-permute-start | bytes 612872 | tf_op jit(solution)/shard_map/ppermute | solution.py:760
  108.1 2.8 %collective-permute-start.24 = (bf16[576,768]{1,0:T(8,128)(2,1)}, bf16[576,768]{1,0:T(8,128)(2,1)S(1)}, u32[]{:S(2)}, u32[]{:S(2)}) collective-permute-start(bf16[576,768]{1,0:T(8,128)(2,1)} %get-tuple-element.175.mine_ref), channel_id=1, source_target_pairs={{0,1},{1,0},{2,3},{3,2},{4,5},{5,4},{6,7},{7,6},{8,9},{9,8},{10,11... | collective-permute-start | bytes 2654216 | tf_op jit(solution)/shard_map/ppermute | solution.py:760
  121.9 2.7 collective-permute-start.25
  135.8 14.1 %collective-permute-start.26 = (bf16[576,768]{1,0:T(8,128)(2,1)}, bf16[576,768]{1,0:T(8,128)(2,1)S(1)}, u32[]{:S(2)}, u32[]{:S(2)}) collective-permute-start(bf16[576,768]{1,0:T(8,128)(2,1)} %get-tuple-element.186.mine_ref), channel_id=1, source_target_pairs={{0,1},{1,0},{2,3},{3,2},{4,5},{5,4},{6,7},{7,6},{8,9},{9,8},{10,11... | collective-permute-start | bytes 2654216 | tf_op jit(solution)/shard_map/ppermute | solution.py:760
  137.3 30.7 %collective-permute-start.27 = (bf16[133,768]{1,0:T(8,128)(2,1)S(1)}, bf16[133,768]{1,0:T(8,128)(2,1)S(1)}, u32[]{:S(2)}, u32[]{:S(2)}) collective-permute-start(bf16[133,768]{1,0:T(8,128)(2,1)S(1)} %get-tuple-element.299), channel_id=1, source_target_pairs={{0,2},{1,3},{2,0},{3,1},{4,6},{5,7},{6,4},{7,5},{8,10},{9,11},{10,... | collective-permute-start | bytes 612872 | tf_op jit(solution)/shard_map/ppermute | solution.py:760
  167.9 22.0 %collective-permute-start.31 = (bf16[288,768]{1,0:T(8,128)(2,1)S(1)}, bf16[288,768]{1,0:T(8,128)(2,1)S(1)}, u32[]{:S(2)}, u32[]{:S(2)}) collective-permute-start(bf16[288,768]{1,0:T(8,128)(2,1)S(1)} %slice.37), channel_id=1, source_target_pairs={{0,1},{1,0},{2,3},{3,2},{4,5},{5,4},{6,7},{7,6},{8,9},{9,8},{10,11... | collective-permute-start | bytes 1327112 | tf_op jit(solution)/shard_map/ppermute | solution.py:760
  188.3 12.8 %collective-permute-start.28 = (bf16[6,3,96,128]{3,2,1,0:T(8,128)(2,1)}, bf16[6,3,96,128]{3,2,1,0:T(8,128)(2,1)S(1)}, u32[]{:S(2)}, u32[]{:S(2)}) collective-permute-start(bf16[6,3,96,128]{3,2,1,0:T(8,128)(2,1)} %get-tuple-element.205), channel_id=1, source_target_pairs={{0,4},{4,0},{8,12},{12,8},{16,20},{20,16},{24,28},{28,24},{1,5},{5... | collective-permute-start | bytes 1327112 | tf_op jit(solution)/shard_map/ppermute | solution.py:760
  188.5 12.8 %collective-permute-start.29 = (bf16[6,3,96,128]{3,2,1,0:T(8,128)(2,1)}, bf16[6,3,96,128]{3,2,1,0:T(8,128)(2,1)S(1)}, u32[]{:S(2)}, u32[]{:S(2)}) collective-permute-start(bf16[6,3,96,128]{3,2,1,0:T(8,128)(2,1)} %get-tuple-element.206), channel_id=1, source_target_pairs={{0,2},{1,3},{2,0},{3,1},{4,6},{5,7},{6,4},{7,5},{8,10},{9,11},{10,... | collective-permute-start | bytes 1327112 | tf_op jit(solution)/shard_map/ppermute | solution.py:760
  188.7 12.7 %collective-permute-start.30 = (bf16[6,3,96,128]{3,2,1,0:T(8,128)(2,1)}, bf16[6,3,96,128]{3,2,1,0:T(8,128)(2,1)S(1)}, u32[]{:S(2)}, u32[]{:S(2)}) collective-permute-start(bf16[6,3,96,128]{3,2,1,0:T(8,128)(2,1)} %get-tuple-element.207), channel_id=1, source_target_pairs={{0,8},{4,12},{8,0},{12,4},{16,24},{20,28},{24,16},{28,20},{1,9},{5... | collective-permute-start | bytes 1327112 | tf_op jit(solution)/shard_map/ppermute | solution.py:765
  194.2 1.3 collective-permute-start.32
  201.4 14.5 %collective-permute-start.34 = (bf16[6,3,96,128]{3,2,1,0:T(8,128)(2,1)}, bf16[6,3,96,128]{3,2,1,0:T(8,128)(2,1)S(1)}, u32[]{:S(2)}, u32[]{:S(2)}) collective-permute-start(bf16[6,3,96,128]{3,2,1,0:T(8,128)(2,1)} %get-tuple-element.220), channel_id=1, source_target_pairs={{0,4},{4,0},{8,12},{12,8},{16,20},{20,16},{24,28},{28,24},{1,5},{5... | collective-permute-start | bytes 1327112 | tf_op jit(solution)/shard_map/ppermute | solution.py:760
  203.1 12.8 %collective-permute-start.35 = (bf16[6,3,96,128]{3,2,1,0:T(8,128)(2,1)S(1)}, bf16[6,3,96,128]{3,2,1,0:T(8,128)(2,1)S(1)}, u32[]{:S(2)}, u32[]{:S(2)}) collective-permute-start(bf16[6,3,96,128]{3,2,1,0:T(8,128)(2,1)S(1)} %add_convert_fusion.7), channel_id=1, source_target_pairs={{0,2},{1,3},{2,0},{3,1},{4,6},{5,7},{6,4},{7,5},{8,10},{9,11},{10,... | collective-permute-start | bytes 1327112 | tf_op jit(solution)/shard_map/ppermute | solution.py:760
  204.9 11.0 %collective-permute-start.36 = (bf16[6,3,96,128]{3,2,1,0:T(8,128)(2,1)S(1)}, bf16[6,3,96,128]{3,2,1,0:T(8,128)(2,1)S(1)}, u32[]{:S(2)}, u32[]{:S(2)}) collective-permute-start(bf16[6,3,96,128]{3,2,1,0:T(8,128)(2,1)S(1)} %copy-done.48), channel_id=1, source_target_pairs={{0,8},{4,12},{8,0},{12,4},{16,24},{20,28},{24,16},{28,20},{1,9},{5... | collective-permute-start | bytes 1327112 | tf_op jit(solution)/shard_map/ppermute | solution.py:765
  205.2 10.7 %collective-permute-start.37 = (f32[19,768]{1,0:T(8,128)S(1)}, f32[19,768]{1,0:T(8,128)S(1)}, u32[]{:S(2)}, u32[]{:S(2)}) collective-permute-start(f32[19,768]{1,0:T(8,128)S(1)} %pad_maximum_fusion.2), channel_id=1, source_target_pairs={{0,2},{1,3},{2,0},{3,1},{4,6},{5,7},{6,4},{7,5},{8,10},{9,11},{10,... | collective-permute-start | bytes 175112 | tf_op jit(solution)/shard_map/ppermute | solution.py:760
  205.6 18.8 %collective-permute-start.33 = (bf16[6,3,96,128]{3,2,1,0:T(8,128)(2,1)S(1)}, bf16[6,3,96,128]{3,2,1,0:T(8,128)(2,1)S(1)}, u32[]{:S(2)}, u32[]{:S(2)}) collective-permute-start(bf16[6,3,96,128]{3,2,1,0:T(8,128)(2,1)S(1)} %add_convert_fusion.8), channel_id=1, source_target_pairs={{0,4},{4,0},{8,12},{12,8},{16,20},{20,16},{24,28},{28,24},{1,5},{5... | collective-permute-start | bytes 1327112 | tf_op jit(solution)/shard_map/ppermute | solution.py:760
  216.2 12.1 %collective-permute-start.39 = (bf16[6,3,96,128]{3,2,1,0:T(8,128)(2,1)S(1)}, bf16[6,3,96,128]{3,2,1,0:T(8,128)(2,1)S(1)}, u32[]{:S(2)}, u32[]{:S(2)}) collective-permute-start(bf16[6,3,96,128]{3,2,1,0:T(8,128)(2,1)S(1)} %add_convert_fusion.6), channel_id=1, source_target_pairs={{0,8},{4,12},{24,16},{28,20},{1,9},{5,13},{25,17},{29,21},{2,10},{... | collective-permute-start | bytes 1327112 | tf_op jit(solution)/shard_map/ppermute | solution.py:765
  217.5 13.2 %collective-permute-start.38 = (bf16[6,3,96,128]{3,2,1,0:T(8,128)(2,1)S(1)}, bf16[6,3,96,128]{3,2,1,0:T(8,128)(2,1)S(1)}, u32[]{:S(2)}, u32[]{:S(2)}) collective-permute-start(bf16[6,3,96,128]{3,2,1,0:T(8,128)(2,1)S(1)} %copy-done.47), channel_id=1, source_target_pairs={{0,2},{1,3},{2,0},{3,1},{4,6},{5,7},{6,4},{7,5},{8,10},{9,11},{10,... | collective-permute-start | bytes 1327112 | tf_op jit(solution)/shard_map/ppermute | solution.py:760
  219.0 5.4 %collective-permute-start.40 = (f32[19,768]{1,0:T(8,128)S(1)}, f32[19,768]{1,0:T(8,128)S(1)}, u32[]{:S(2)}, u32[]{:S(2)}) collective-permute-start(f32[19,768]{1,0:T(8,128)S(1)} %add.136), channel_id=1, source_target_pairs={{0,4},{4,0},{8,12},{12,8},{16,20},{20,16},{24,28},{28,24},{1,5},{5... | collective-permute-start | bytes 175112 | tf_op jit(solution)/shard_map/ppermute | solution.py:760
  219.8 16.0 %copy-start.46 = (bf16[6,3,96,128]{3,2,1,0:T(8,128)(2,1)S(1)}, bf16[6,3,96,128]{3,2,1,0:T(8,128)(2,1)}, u32[]{:S(2)}) copy-start(bf16[6,3,96,128]{3,2,1,0:T(8,128)(2,1)} %get-tuple-element.231) | copy-start | bytes 1327108
  219.8 22.3 %collective-permute-start.42 = (bf16[6,3,96,128]{3,2,1,0:T(8,128)(2,1)S(1)}, bf16[6,3,96,128]{3,2,1,0:T(8,128)(2,1)S(1)}, u32[]{:S(2)}, u32[]{:S(2)}) collective-permute-start(bf16[6,3,96,128]{3,2,1,0:T(8,128)(2,1)S(1)} %add_convert_fusion.5), channel_id=1, source_target_pairs={{0,2},{1,3},{2,0},{3,1},{4,6},{5,7},{6,4},{7,5},{8,10},{9,11},{10,... | collective-permute-start | bytes 1327112 | tf_op jit(solution)/shard_map/ppermute | solution.py:760
  230.9 11.2 %collective-permute-start.44 = (bf16[6,3,96,128]{3,2,1,0:T(8,128)(2,1)S(1)}, bf16[6,3,96,128]{3,2,1,0:T(8,128)(2,1)S(1)}, u32[]{:S(2)}, u32[]{:S(2)}) collective-permute-start(bf16[6,3,96,128]{3,2,1,0:T(8,128)(2,1)S(1)} %add_convert_fusion.4), channel_id=1, source_target_pairs={{0,8},{4,12},{24,16},{28,20},{1,9},{5,13},{25,17},{29,21},{2,10},{... | collective-permute-start | bytes 1327112 | tf_op jit(solution)/shard_map/ppermute | solution.py:765
  232.3 10.2 %collective-permute-start.43 = (bf16[6,3,96,128]{3,2,1,0:T(8,128)(2,1)S(1)}, bf16[6,3,96,128]{3,2,1,0:T(8,128)(2,1)S(1)}, u32[]{:S(2)}, u32[]{:S(2)}) collective-permute-start(bf16[6,3,96,128]{3,2,1,0:T(8,128)(2,1)S(1)} %add_convert_fusion.4), channel_id=1, source_target_pairs={{8,16},{12,20},{16,8},{20,12},{9,17},{13,21},{17,9},{21,13},{10,18... | collective-permute-start | bytes 1327112 | tf_op jit(solution)/shard_map/ppermute | solution.py:765
  235.8 10.9 %collective-permute-start.41 = (bf16[6,3,96,128]{3,2,1,0:T(8,128)(2,1)S(1)}, bf16[6,3,96,128]{3,2,1,0:T(8,128)(2,1)S(1)}, u32[]{:S(2)}, u32[]{:S(2)}) collective-permute-start(bf16[6,3,96,128]{3,2,1,0:T(8,128)(2,1)S(1)} %copy-done.46), channel_id=1, source_target_pairs={{0,4},{4,0},{8,12},{12,8},{16,20},{20,16},{24,28},{28,24},{1,5},{5... | collective-permute-start | bytes 1327112 | tf_op jit(solution)/shard_map/ppermute | solution.py:760
  236.5 5.5 %collective-permute-start.45 = (f32[19,768]{1,0:T(8,128)S(1)}, f32[19,768]{1,0:T(8,128)S(1)}, u32[]{:S(2)}, u32[]{:S(2)}) collective-permute-start(f32[19,768]{1,0:T(8,128)S(1)} %add.139), channel_id=1, source_target_pairs={{0,8},{4,12},{8,0},{12,4},{16,24},{20,28},{24,16},{28,20},{1,9},{5... | collective-permute-start | bytes 175112 | tf_op jit(solution)/shard_map/ppermute | solution.py:760
  246.9 13.1 %collective-permute-start.47 = (bf16[6,3,96,128]{3,2,1,0:T(8,128)(2,1)S(1)}, bf16[6,3,96,128]{3,2,1,0:T(8,128)(2,1)S(1)}, u32[]{:S(2)}, u32[]{:S(2)}) collective-permute-start(bf16[6,3,96,128]{3,2,1,0:T(8,128)(2,1)S(1)} %add_convert_fusion.2), channel_id=1, source_target_pairs={{0,2},{1,3},{2,0},{3,1},{4,6},{5,7},{6,4},{7,5},{8,10},{9,11},{10,... | collective-permute-start | bytes 1327112 | tf_op jit(solution)/shard_map/ppermute | solution.py:760
  248.7 11.3 %collective-permute-start.46 = (bf16[6,3,96,128]{3,2,1,0:T(8,128)(2,1)S(1)}, bf16[6,3,96,128]{3,2,1,0:T(8,128)(2,1)S(1)}, u32[]{:S(2)}, u32[]{:S(2)}) collective-permute-start(bf16[6,3,96,128]{3,2,1,0:T(8,128)(2,1)S(1)} %add_convert_fusion.3), channel_id=1, source_target_pairs={{0,4},{4,0},{8,12},{12,8},{16,20},{20,16},{24,28},{28,24},{1,5},{5... | collective-permute-start | bytes 1327112 | tf_op jit(solution)/shard_map/ppermute | solution.py:760
  249.2 10.9 %collective-permute-start.48 = (bf16[6,3,96,128]{3,2,1,0:T(8,128)(2,1)S(1)}, bf16[6,3,96,128]{3,2,1,0:T(8,128)(2,1)S(1)}, u32[]{:S(2)}, u32[]{:S(2)}) collective-permute-start(bf16[6,3,96,128]{3,2,1,0:T(8,128)(2,1)S(1)} %add_convert_fusion.1), channel_id=1, source_target_pairs={{0,8},{4,12},{8,0},{12,4},{16,24},{20,28},{24,16},{28,20},{1,9},{5... | collective-permute-start | bytes 1327112 | tf_op jit(solution)/shard_map/ppermute | solution.py:765
  249.2 11.0 %collective-permute-start.49 = (bf16[6,3,96,128]{3,2,1,0:T(8,128)(2,1)S(1)}, bf16[6,3,96,128]{3,2,1,0:T(8,128)(2,1)S(1)}, u32[]{:S(2)}, u32[]{:S(2)}) collective-permute-start(bf16[6,3,96,128]{3,2,1,0:T(8,128)(2,1)S(1)} %add_convert_fusion), channel_id=1, source_target_pairs={{8,16},{12,20},{16,8},{20,12},{9,17},{13,21},{17,9},{21,13},{10,18... | collective-permute-start | bytes 1327112 | tf_op jit(solution)/shard_map/ppermute | solution.py:765
  252.6 7.4 %collective-permute-start.50 = (f32[19,768]{1,0:T(8,128)S(1)}, f32[19,768]{1,0:T(8,128)S(1)}, u32[]{:S(2)}, u32[]{:S(2)}) collective-permute-start(f32[19,768]{1,0:T(8,128)S(1)} %add.144), channel_id=1, source_target_pairs={{0,16},{4,20},{8,24},{12,28},{16,0},{20,4},{24,8},{28,12},{1,17},{... | collective-permute-start | bytes 175112 | tf_op jit(solution)/shard_map/ppermute | solution.py:760
  260.3 14.1 %collective-permute-start.51 = (bf16[133,768]{1,0:T(8,128)(2,1)S(1)}, bf16[133,768]{1,0:T(8,128)(2,1)S(1)}, u32[]{:S(2)}, u32[]{:S(2)}) collective-permute-start(bf16[133,768]{1,0:T(8,128)(2,1)S(1)} %get-tuple-element.297), channel_id=1, source_target_pairs={{0,2},{1,3},{2,0},{3,1},{4,6},{5,7},{6,4},{7,5},{8,10},{9,11},{10,... | collective-permute-start | bytes 612872 | tf_op jit(solution)/shard_map/ppermute | solution.py:760
  (39 other events, 319.7 us)

commit v3 on v2

--- a/solution.py
+++ b/solution.py
@@ -24,12 +24,15 @@
 
 BF = jnp.bfloat16
 F32 = jnp.float32
-VMEM_LIMIT = 56 * 1024 * 1024
+VMEM_LIMIT = 24 * 1024 * 1024
+BIG_LIMIT = 61 * 1024 * 1024
 VMEM_SPEC = pl.BlockSpec(memory_space=pltpu.VMEM)
 SMEM_SPEC = pl.BlockSpec(memory_space=pltpu.SMEM)
 ANY_SPEC = pl.BlockSpec(memory_space=pl.ANY)
+HBM_SPEC = pl.BlockSpec(memory_space=pltpu.HBM)
 GROUP = 4
 TILES = 3
+UNROLL = 4
 RP = 144
 RS_ORDER = (3, 2, 1, 0)
 
@@ -38,8 +41,8 @@
     return jax.ShapeDtypeStruct(shape, dtype)
 
 
-def params(**kw):
-    return pltpu.CompilerParams(vmem_limit_bytes=VMEM_LIMIT, **kw)
+def params(limit=VMEM_LIMIT):
+    return pltpu.CompilerParams(vmem_limit_bytes=limit)
 
 
 def after(vals, deps):
@@ -50,6 +53,21 @@
     return pl.CostEstimate(
         flops=int(gflop * 1e9), bytes_accessed=int(mbytes * 1e6), transcendentals=0
     )
+
+
+def copy_body(v_ref, out_ref):
+    out_ref[...] = v_ref[...]
+
+
+def fence(token):
+    return pl.pallas_call(
+        copy_body,
+        out_shape=sds(token.shape, token.dtype),
+        in_specs=[VMEM_SPEC],
+        out_specs=VMEM_SPEC,
+        compiler_params=params(BIG_LIMIT),
+        name="fence",
+    )(token)
 
 
 def xor_pairs(size, step):
@@ -74,7 +92,7 @@
     return grp.reshape(groups.shape[:-4] + (-1, 96, 96))
 
 
-def pack_body(m_ref, out_ref):
+def pack_owned_body(m_ref, out_ref):
     for g in range(out_ref.shape[0]):
         last = m_ref[GROUP * g + 3].astype(BF)
         for k in range(TILES):
@@ -86,7 +104,7 @@
 def pack_owned(blocks):
     n = blocks.shape[0] // GROUP
     return pl.pallas_call(
-        pack_body,
+        pack_owned_body,
         out_shape=sds((n, TILES, 96, 128), BF),
         in_specs=[VMEM_SPEC],
         out_specs=VMEM_SPEC,
@@ -98,24 +116,25 @@
 
 def weights_body(n_pieces, places, pos_ref, me_ref, *refs):
     pieces = refs[:n_pieces]
-    wqkv_ref, wo_ref, w1_ref, w2_ref, al, sem = refs[n_pieces:]
+    outs = refs[n_pieces : n_pieces + 4]
+    wqkv_ref, wo_ref, w1_ref, w2_ref, al, sems, out_sem = refs[n_pieces + 4 :]
     dp, y = me_ref[0], me_ref[1] // 2
+    groups = al.shape[1]
     copies = []
     for ref, (jy, jd) in zip(pieces, places):
         n = ref.shape[-4]
         if jd is None:
-            copy = pltpu.make_async_copy(ref, al.at[:, :, pl.ds(0, TILES)], sem)
+            for s in range(2):
+                dst = al.at[s, :, pl.ds(0, TILES)]
+                copies.append(((s,), pltpu.make_async_copy(ref.at[s], dst, sems.at[s])))
         else:
-            copy = pltpu.make_async_copy(
-                ref, al.at[y ^ jy, pl.ds((dp ^ jd) * n, n), pl.ds(0, TILES)], sem
-            )
+            dst = al.at[y ^ jy, pl.ds((dp ^ jd) * n, n), pl.ds(0, TILES)]
+            copies.append(((0, 1), pltpu.make_async_copy(ref, dst, sems.at[y ^ jy])))
+    for _, copy in copies:
         copy.start()
-        copies.append(copy)
-    for copy in copies:
-        copy.wait()
-    groups = al.shape[1]
-
     for s in range(2):
+        whole = al.at[s, :, pl.ds(0, TILES)]
+        pltpu.make_async_copy(whole, whole, sems.at[s]).wait()
 
         def fix(g, carry, s=s):
             al[s, g, 3, :, 0:96] = jnp.concatenate(
@@ -123,35 +142,48 @@
             )
             return carry
 
-        lax.fori_loop(0, groups, fix, 0, unroll=8)
+        lax.fori_loop(0, groups, fix, 0, unroll=16)
 
     def block(s, b):
         p = pos_ref[b]
         return al[s, p // GROUP, p % GROUP][:, :96]
 
-    def strip(i, carry):
+    def strip_qkv(i, carry):
         rows = pl.ds(pl.multiple_of(i * 96, 96), 96)
         for part in range(3):
             wqkv_ref[rows, part * 384 : part * 384 + 384] = jnp.concatenate(
                 [block(j // 2, i * 6 + part * 2 + j % 2) for j in range(4)], axis=-1
             )
+        return carry
+
+    def strip(i, carry, ref, first):
+        rows = pl.ds(pl.multiple_of(i * 96, 96), 96)
         for s in range(2):
             for half in range(2):
-                cols = slice(half * 384, half * 384 + 384)
-                w1_ref[s, rows, cols] = jnp.concatenate(
-                    [block(s, 64 + i * 8 + half * 4 + j) for j in range(4)], axis=-1
-                )
-                w2_ref[s, rows, cols] = jnp.concatenate(
-                    [block(s, 128 + i * 8 + half * 4 + j) for j in range(4)], axis=-1
+                ref[s, rows, half * 384 : half * 384 + 384] = jnp.concatenate(
+                    [block(s, first + i * 8 + half * 4 + j) for j in range(4)], axis=-1
                 )
         return carry
 
-    lax.fori_loop(0, 8, strip, 0, unroll=2)
+    def send(k):
+        copy = pltpu.make_async_copy((wqkv_ref, wo_ref, w1_ref, w2_ref)[k], outs[k], out_sem.at[k])
+        copy.start()
+        return copy
+
+    lax.fori_loop(0, 8, functools.partial(strip, ref=w1_ref, first=64), 0, unroll=UNROLL)
+    sent = [send(2)]
+    lax.fori_loop(0, 8, functools.partial(strip, ref=w2_ref, first=128), 0, unroll=UNROLL)
+    sent.append(send(3))
+    lax.fori_loop(0, 8, strip_qkv, 0, unroll=UNROLL)
+    sent.append(send(0))
     for i in range(4):
         for half in range(2):
             wo_ref[i * 96 : i * 96 + 96, half * 384 : half * 384 + 384] = jnp.concatenate(
                 [block(i // 2, 48 + (i % 2) * 8 + half * 4 + j) for j in range(4)], axis=-1
             )
+    sent.append(send(1))
+    for copy in sent:
+        copy.wait()
 
 
 def build_weights(pos, me, pieces, places, slots):
@@ -163,13 +195,18 @@
             sds((2, 768, 768), BF),
             sds((2, 768, 768), BF),
         ),
-        in_specs=[SMEM_SPEC, SMEM_SPEC] + [ANY_SPEC] * len(pieces),
-        out_specs=(VMEM_SPEC,) * 4,
+        in_specs=[SMEM_SPEC, SMEM_SPEC] + [HBM_SPEC] * len(pieces),
+        out_specs=(HBM_SPEC,) * 4,
         scratch_shapes=[
+            pltpu.VMEM((768, 1152), BF),
+            pltpu.VMEM((384, 768), BF),
+            pltpu.VMEM((2, 768, 768), BF),
+            pltpu.VMEM((2, 768, 768), BF),
             pltpu.VMEM((2, slots // GROUP, GROUP, 96, 128), BF),
-            pltpu.SemaphoreType.DMA,
+            pltpu.SemaphoreType.DMA((2,)),
+            pltpu.SemaphoreType.DMA((4,)),
         ],
-        compiler_params=params(),
+        compiler_params=params(BIG_LIMIT),
         cost_estimate=cost(0.1, 30),
         name="build_weights",
     )(pos, me, *pieces)
@@ -184,59 +221,86 @@
     lax.fori_loop(0, out.shape[0] // width, step, 0)
 
 
-def feed_grads_body(act_ref, d2_ref, h_ref, dpre_ref, g1_ref, g2_ref):
+def down_grads_body(act_ref, d2_ref, out_ref):
     for s in range(2):
-        product(act_ref.at[s], d2_ref, g2_ref.at[s])
-        product(h_ref, dpre_ref.at[s], g1_ref.at[s])
-
-
-def feed_grads(act, d_two, h_in, d_pre):
-    rows = h_in.shape[0]
-    return pl.pallas_call(
-        feed_grads_body,
-        out_shape=(sds((2, 768, 768), BF),) * 2,
-        in_specs=[VMEM_SPEC] * 4,
-        out_specs=(VMEM_SPEC,) * 2,
+        product(act_ref.at[s], d2_ref, out_ref.at[s])
+
+
+def up_grads_body(h_ref, dpre_ref, later_ref, out_ref):
+    for s in range(2):
+        product(h_ref, dpre_ref.at[s], out_ref.at[s])
+
+
+def down_grads(act, d_two):
+    return pl.pallas_call(
+        down_grads_body,
+        out_shape=sds((2, 768, 768), BF),
+        in_specs=[VMEM_SPEC] * 2,
+        out_specs=VMEM_SPEC,
         compiler_params=params(),
-        cost_estimate=pl.CostEstimate(
-            flops=2 * rows * 768 * 768 * 4, bytes_accessed=10 * 1024 * 1024, transcendentals=0
-        ),
-        name="feed_grads",
-    )(act, d_two, h_in, d_pre)
-
-
-def grads_body(places, pos_ref, me_ref, *refs):
-    x, dproj, ctx, d1, g1, g2 = refs[:6]
+        cost_estimate=cost(1.4, 8),
+        name="down_grads",
+    )(act, d_two)
+
+
+def up_grads(h_in, d_pre, later):
+    return pl.pallas_call(
+        up_grads_body,
+        out_shape=sds((2, 768, 768), BF),
+        in_specs=[VMEM_SPEC] * 2 + [ANY_SPEC],
+        out_specs=VMEM_SPEC,
+        compiler_params=params(),
+        cost_estimate=cost(1.4, 8),
+        name="up_grads",
+    )(h_in, d_pre, later)
+
+
+def pack_body(places, pos_ref, me_ref, *refs):
+    token_ref = refs[5]
     outs = refs[6 : 6 + len(places)]
-    gq, go, al, sem = refs[6 + len(places) :]
+    g2, g1, go, gq, al, sem, sems = refs[6 + len(places) :]
+    loads = [pltpu.make_async_copy(src, dst, sems.at[k]) for k, (src, dst) in enumerate(zip(refs, (g2, g1, go, gq)))]
+    for load in loads:
+        load.start()
     groups = al.shape[1]
-    product(ctx, d1, go, 128)
-    product(x, dproj, gq)
+    token_ref[...] = jnp.zeros_like(token_ref)
 
     def put(s, b, blk):
         p = pos_ref[b]
         al[s, p // GROUP, p % GROUP, :, 0:96] = blk
 
-    def strip(i, carry):
+    def strip(i, carry, ref, first):
+        rows = pl.ds(pl.multiple_of(i * 96, 96), 96)
+        for s in range(2):
+            for half in range(2):
+                vals = ref[s, rows, half * 384 : half * 384 + 384]
+                for j in range(4):
+                    put(s, first + i * 8 + half * 4 + j, vals[:, 96 * j : 96 * j + 96])
+        return carry
+
+    def strip_qkv(i, carry):
         rows = pl.ds(pl.multiple_of(i * 96, 96), 96)
         for part in range(3):
             vals = gq[rows, part * 384 : part * 384 + 384]
             for j in range(4):
                 put(j // 2, i * 6 + part * 2 + j % 2, vals[:, 96 * j : 96 * j + 96])
-        for s in range(2):
-            for ref, first in ((g1, 64), (g2, 128)):
-                for half in range(2):
-                    vals = ref[s, rows, half * 384 : half * 384 + 384]
-                    for j in range(4):
-                        put(s, first + i * 8 + half * 4 + j, vals[:, 96 * j : 96 * j + 96])
         return carry
 
-    lax.fori_loop(0, 8, strip, 0, unroll=2)
+    loads[0].wait()
+    lax.fori_loop(0, 8, functools.partial(strip, ref=g2, first=128), 0, unroll=UNROLL)
+    loads[1].wait()
+    lax.fori_loop(0, 8, functools.partial(strip, ref=g1, first=64), 0, unroll=UNROLL)
+    loads[2].wait()
     for i in range(4):
         for half in range(2):
             vals = go[i * 96 : i * 96 + 96, half * 384 : half * 384 + 384]
             for j in range(4):
                 put(i // 2, 48 + (i % 2) * 8 + half * 4 + j, vals[:, 96 * j : 96 * j + 96])
+    loads[3].wait()
+    lax.fori_loop(0, 8, strip_qkv, 0, unroll=UNROLL)
+
+    dp, y = me_ref[0], me_ref[1] // 2
+    copies = []
     for s in range(2):
 
         def fix(g, carry, s=s):
@@ -245,43 +309,48 @@
                 al[s, g, k, :, 96:128] = last[:, 32 * k : 32 * k + 32]
             return carry
 
-        lax.fori_loop(0, groups, fix, 0, unroll=8)
-
-    dp, y = me_ref[0], me_ref[1] // 2
-    copies = []
-    for ref, (jy, jd, first) in zip(outs, places):
-        if jd is None:
-            copy = pltpu.make_async_copy(al.at[:, :, pl.ds(0, TILES)], ref, sem)
+        lax.fori_loop(0, groups, fix, 0, unroll=16)
+        for ref, (jy, jd) in zip(outs, places):
+            if jd is None:
+                copies.append((None, pltpu.make_async_copy(al.at[s, :, pl.ds(0, TILES)], ref.at[s], sem)))
+            else:
+                n = ref.shape[0]
+                src = al.at[s, pl.ds((dp ^ jd) * n, n), pl.ds(0, TILES)]
+                copies.append(((y ^ jy) == s, pltpu.make_async_copy(src, ref, sem)))
+        for mine, copy in copies[s * len(outs) :]:
+            if mine is None:
+                copy.start()
+            else:
+                pl.when(mine)(copy.start)
+    for mine, copy in copies:
+        if mine is None:
+            copy.wait()
         else:
-            base = (dp ^ jd) * (groups // 8) + first
-            copy = pltpu.make_async_copy(
-                al.at[y ^ jy, pl.ds(base, ref.shape[0]), pl.ds(0, TILES)], ref, sem
-            )
-        copy.start()
-        copies.append(copy)
-    for copy in copies:
-        copy.wait()
-
-
-def weight_grads(pos, me, srcs, places, out_shapes, slots):
-    return pl.pallas_call(
-        functools.partial(grads_body, places),
-        out_shape=tuple(sds(s, BF) for s in out_shapes),
-        in_specs=[SMEM_SPEC, SMEM_SPEC] + [VMEM_SPEC] * 6,
-        out_specs=(ANY_SPEC,) * len(places),
+            pl.when(mine)(copy.wait)
+
+
+def pack_grads(pos, me, grads, places, out_shapes, slots):
+    return pl.pallas_call(
+        functools.partial(pack_body, places),
+        out_shape=(sds((8, 128), F32), *(sds(s, BF) for s in out_shapes)),
+        in_specs=[SMEM_SPEC, SMEM_SPEC] + [HBM_SPEC] * 4 + [ANY_SPEC],
+        out_specs=(VMEM_SPEC,) + (HBM_SPEC,) * len(places),
         scratch_shapes=[
+            pltpu.VMEM((2, 768, 768), BF),
+            pltpu.VMEM((2, 768, 768), BF),
+            pltpu.VMEM((384, 768), BF),
             pltpu.VMEM((768, 1152), BF),
-            pltpu.VMEM((384, 768), BF),
             pltpu.VMEM((2, slots // GROUP, GROUP, 96, 128), BF),
             pltpu.SemaphoreType.DMA,
+            pltpu.SemaphoreType.DMA((4,)),
         ],
-        compiler_params=params(),
-        cost_estimate=cost(2.0, 30),
-        name="weight_grads",
-    )(pos, me, *srcs)
-
-
-def project_body(flags_ref, xa, xb, xc, xd, sh_ref, w_ref, b_ref, proj_ref, x0_ref, xin_ref, bias):
+        compiler_params=params(BIG_LIMIT),
+        cost_estimate=cost(0.1, 30),
+        name="pack_grads",
+    )(pos, me, *grads)
+
+
+def project_body(flags_ref, xa, xb, xc, xd, sh_ref, w_ref, b_ref, later_ref, proj_ref, x0_ref, xin_ref, bias):
     @pl.when(pl.program_id(0) == 0)
     def _():
         n = xa.shape[0]
@@ -302,7 +371,7 @@
     proj_ref[...] = (dot(xin_ref[...], w_ref[...]) + bias[pl.program_id(0)]).astype(BF)
 
 
-def project(flags, quarters, shared, w_qkv, biases):
+def project(flags, quarters, shared, w_qkv, biases, later):
     rows = 4 * RP
 
     def whole(shape):
@@ -318,6 +387,7 @@
             whole(shared.shape),
             pl.BlockSpec((768, 384), lambda i: (0, i)),
             whole(biases.shape),
+            ANY_SPEC,
         ],
         out_specs=(
             pl.BlockSpec((rows, 384), lambda i: (0, i)),
@@ -328,7 +398,7 @@
         compiler_params=params(),
         cost_estimate=cost(1.0, 5),
         name="project",
-    )(flags, *quarters, shared, w_qkv, biases)
+    )(flags, *quarters, shared, w_qkv, biases, later)
 
 
 def head_masks(shape):
@@ -519,7 +589,7 @@
     )(mine, other, normed, slope, *cots, shared, w1, w2)
 
 
-def attend_back_body(mine_ref, other_ref, d2_ref, n_ref, r_ref, sh_ref, wo_ref, wqkv_ref, p_ref, q_ref, k_ref, v_ref, d1_ref, d1b_ref, dproj_ref, part_ref, sums_ref, bsum_ref, dctx):
+def attend_back_body(mine_ref, other_ref, d2_ref, n_ref, r_ref, sh_ref, wo_ref, wqkv_ref, x_ref, ctx_ref, later_ref, p_ref, q_ref, k_ref, v_ref, d1_ref, gq_ref, go_ref, part_ref, sums_ref, bsum_ref, d1b_ref, dproj_ref, dctx):
     h = pl.program_id(0)
     pairs = pl.num_programs(0)
     own = d1_ref.shape[0]
@@ -560,9 +630,11 @@
     @pl.when(h == pairs - 1)
     def _():
         part_ref[...] = dot_back(dproj_ref[...], wqkv_ref[...]).astype(BF)
-
-
-def attend_back(mine, other, d_two, normed, inverse, shared, w_out, w_qkv, probs, proj):
+        product(ctx_ref, d1b_ref, go_ref, 128)
+        product(x_ref, dproj_ref, gq_ref)
+
+
+def attend_back(mine, other, d_two, normed, inverse, shared, w_out, w_qkv, x_in, context, later, probs, proj):
     rows = proj.shape[0]
     pairs = HEADS // 4
     return pl.pallas_call(
@@ -570,8 +642,8 @@
         grid=(pairs,),
         out_shape=(
             sds((rows // 2, 768), F32),
-            sds((rows, 768), BF),
-            sds((rows, 1152), BF),
+            sds((768, 1152), BF),
+            sds((384, 768), BF),
             sds((rows, 768), BF),
             sds((8, 768), F32),
             sds((8, 384), F32),
@@ -585,6 +657,9 @@
             all_steps(shared.shape),
             all_steps((384, 768)),
             all_steps((768, 1152)),
+            all_steps((rows, 768)),
+            all_steps((rows, 384)),
+            ANY_SPEC,
             pl.BlockSpec((2, rows, rows), lambda h: (h, 0, 0)),
             head_col(rows, 0),
             head_col(rows, pairs),
@@ -592,19 +667,23 @@
         ],
         out_specs=(
             all_steps((rows // 2, 768)),
-            all_steps((rows, 768)),
-            all_steps((rows, 1152)),
+            all_steps((768, 1152)),
+            all_steps((384, 768)),
             all_steps((rows, 768)),
             all_steps((8, 768)),
             pl.BlockSpec((8, 128), lambda h: (0, h)),
         ),
-        scratch_shapes=[pltpu.VMEM((3, rows, 128), BF)],
+        scratch_shapes=[
+            pltpu.VMEM((rows, 768), BF),
+            pltpu.VMEM((rows, 1152), BF),
+            pltpu.VMEM((3, rows, 128), BF),
+        ],
         compiler_params=params(),
         cost_estimate=pl.CostEstimate(
             flops=2 * rows * rows * 64 * 4 * HEADS, bytes_accessed=10 * 1024 * 1024, transcendentals=0
         ),
         name="attend_back",
-    )(mine, other, d_two, normed, inverse, shared, w_out, w_qkv, probs, proj, proj, proj)
+    )(mine, other, d_two, normed, inverse, shared, w_out, w_qkv, x_in, context, later, probs, proj, proj, proj)
 
 
 def finish_body(flags_ref, part_ref, other_ref, d1_ref, gin_ref, mem_ref):
@@ -645,25 +724,32 @@
         tiles = [sum(ref[0, k].astype(F32) for ref in terms) for k in range(TILES)]
         grads = [tile[:, :96] for tile in tiles]
         grads.append(jnp.concatenate([tile[:, 96:] for tile in tiles], axis=-1))
-    for b in range(blocks):
-        gb = grads[b].astype(BF)
-        lb, rb = l_ref[b].astype(BF), r_ref[b].astype(BF)
-        turned = dot(inner_rows(lb, gb).astype(BF), rb)
-        new_first = beta_one * m_ref[b] + (1.0 - beta_one) * turned
-        new_second = beta_two * v_ref[b] + (1.0 - beta_two) * turned * turned
+    every = range(blocks)
+    gb = [g.astype(BF) for g in grads]
+    lb, rb = [l_ref[b].astype(BF) for b in every], [r_ref[b].astype(BF) for b in every]
+    half = [inner_rows(lb[b], gb[b]).astype(BF) for b in every]
+    for b in every:
+        nl_ref[b] = beta_two * sl_ref[b] + (1.0 - beta_two) * dot_back(gb[b], gb[b])
+    turned = [dot(half[b], rb[b]) for b in every]
+    for b in every:
+        nr_ref[b] = beta_two * sr_ref[b] + (1.0 - beta_two) * inner_rows(gb[b], gb[b])
+    steps = []
+    for b in every:
+        new_first = beta_one * m_ref[b] + (1.0 - beta_one) * turned[b]
+        new_second = beta_two * v_ref[b] + (1.0 - beta_two) * turned[b] * turned[b]
+        nm_ref[b] = new_first
+        nv_ref[b] = new_second
         direction = (
             new_first
             / (1.0 - beta_one**STEP)
             / (jnp.sqrt(new_second / (1.0 - beta_two**STEP)) + adam_eps)
         )
-        back = dot_back(dot(lb, direction.astype(BF)).astype(BF), rb)
-        new_weight = w_ref[b] - rate_matrix * back
+        steps.append(direction.astype(BF))
+    half = [dot(lb[b], steps[b]).astype(BF) for b in every]
+    for b in every:
+        new_weight = w_ref[b] - rate_matrix * dot_back(half[b], rb[b])
         nw_ref[b] = new_weight
         nc_ref[b] = new_weight.astype(BF)
-        nm_ref[b] = new_first
-        nv_ref[b] = new_second
-        nl_ref[b] = beta_two * sl_ref[b] + (1.0 - beta_two) * dot_back(gb, gb)
-        nr_ref[b] = beta_two * sr_ref[b] + (1.0 - beta_two) * inner_rows(gb, gb)
 
 
 def soap(terms, master, first, second, left, right, left_rot, right_rot):
@@ -678,7 +764,7 @@
         out_shape=(full, sds(master.shape, BF), full, full, full, full),
         in_specs=[packed if len(terms) > 1 else spec] * len(terms) + [spec] * 7,
         out_specs=(spec,) * 6,
-        compiler_params=params(),
+        compiler_params=params(BIG_LIMIT),
         cost_estimate=cost(0.3, 24),
         name="soap",
     )(*terms, master, first, second, left, right, left_rot, right_rot)
@@ -791,25 +877,26 @@
 
     if meshed:
         own = pack_owned(master[0])
-        near = outer(own)
-        mid = middle(own)
+        near, mid = outer(own), middle(own)
         x0, y0 = xswap(own), yswap(own)
-        near, mid, x0, y0 = barrier((near, mid, x0, y0))
+        tok = biases[:, :128]
+        near, mid, x0, y0, tok = barrier((near, mid, x0, y0, tok))
         far_mid, far_end = middle(near), outward(mid)
         x1, diag0 = xswap(near), yswap(x0)
-        small = (code_q, code_k, flags, biases, me, in_mine, in_send, cot_mine, cot_send)
-        x1, diag0, far_mid, far_end, y0, small = barrier((x1, diag0, far_mid, far_end, y0, small))
-        code_q, code_k, flags, biases, me, in_mine, in_send, cot_mine, cot_send = small
+        small = (code_q, code_k, flags, biases, me, in_send, cot_send, fence(tok))
+        x1, diag0, far_mid, far_end, small = barrier((x1, diag0, far_mid, far_end, small))
+        code_q, code_k, flags, biases, me, in_send, cot_send, tok = small
         far = far_mid + far_end
         last_end = outward(far_mid)
         x2, y2 = xswap(far), yswap(far)
-        x2, y2, last_end, y0, diag0, in_send = barrier((x2, y2, last_end, y0, diag0, in_send))
+        x2, y2, last_end, tok = barrier((x2, y2, last_end, fence(tok)))
         last = mid + last_end
         x3, y3, y1 = xswap(last), yswap(last), outer(y0)
-        x3, y3, y1, x2, diag0 = barrier((x3, y3, y1, x2, diag0))
+        x3, y3, y1, in_send, tok = barrier((x3, y3, y1, in_send, fence(tok)))
         diag3, diag2, diag1 = xswap(y3), yswap(x2), outer(diag0)
         in_other = yswap(in_send)
-        diag3, diag2, diag1, cot_send = barrier((diag3, diag2, diag1, cot_send))
+        diag3, diag2, diag1, cot_send, tok = barrier((diag3, diag2, diag1, cot_send, fence(tok)))
+        me = after(me, fence(tok))
         pieces, places = [], []
         for jz, vals in enumerate(
             ((own, x0, y0, diag0), (near, x1, y1, diag1), (far, x2, y2, diag2), (last, x3, y3, diag3))
@@ -828,18 +915,17 @@
 
     cot_other = yswap(cot_send)
     quarters = (in_mine, in_other, core(in_mine), core(in_other))
+    proj, x_zero, x_in = project(flags, quarters, shared, w_qkv, biases, cot_other)
     cots = (cot_mine, cot_other, core(cot_mine), core(cot_other))
-    proj, x_zero, x_in = project(flags, quarters, shared, w_qkv, biases)
-    proj, cots = barrier((proj, cots))
     context, probs, attn = attend(code_q, code_k, proj, w_out)
     h_in, normed, inverse, act, slope, ffn = feed(attn, core(attn), x_zero, shared, biases, w_up, w_down)
     rows_out, d_two, d_two_b, d_pre, d_hidden, sums_two, up_sums = feed_back(
         ffn, core(ffn), normed, slope, cots, shared, w_up, w_down
     )
     d_hidden_other = core(d_hidden)
-    g_up, g_down = feed_grads(act, d_two_b, h_in, d_pre)
-    d_one, d_one_b, d_proj, d_in, sums_one, head_sums = attend_back(
-        d_hidden, d_hidden_other, d_two, normed, inverse, shared, w_out, w_qkv, probs, proj
+    g_down = down_grads(act, d_two_b)
+    d_one, g_qkv, g_out, d_in, sums_one, head_sums = attend_back(
+        d_hidden, d_hidden_other, d_two, normed, inverse, shared, w_out, w_qkv, x_in, context, g_down, probs, proj
     )
     d_in_send = d_in[2 * RP :]
 
@@ -849,10 +935,11 @@
         return jnp.where(y == 0, both, both[::-1])
 
     layer_out = to_owner(rows_out)
-    d_proj, layer_out = barrier((d_proj, layer_out))
+    me = after(me, layer_out)
     d_in_other = core(d_in_send)
-    srcs = (x_in, d_proj, context, d_one_b, g_up, g_down)
+    g_up = up_grads(h_in, d_pre, d_in)
     grad_rows, memory_grad = finish(flags, d_in, d_in_other, d_one)
+    grads = (g_down, g_up, g_out, g_qkv, memory_grad)
     vec = jnp.concatenate([sums_one[:3], sums_two[:3], memory_grad[:MEM]], axis=0)
     halves = head_sums[:2].reshape(2, 2, 192).swapaxes(0, 1).reshape(2, 384)
     splits = jnp.concatenate([halves, up_sums], axis=1).reshape(3, 768)
@@ -867,9 +954,9 @@
         for jz in RS_ORDER:
             for jy in range(2):
                 for jx in range(2):
-                    places.append((jy, 2 * jz + jx, 0))
+                    places.append((jy, 2 * jz + jx))
                     shapes.append((per, TILES, 96, 128))
-        packed = weight_grads(block_slot, me, srcs, tuple(places), shapes, slots)
+        token, *packed = pack_grads(block_slot, me, grads, tuple(places), shapes, slots)
         own, x_unit, y_unit, diag = {}, {}, {}, {}
         for n, jz in enumerate(RS_ORDER):
             own[jz], x_unit[jz], y_unit[jz], diag[jz] = packed[4 * n : 4 * n + 4]
@@ -877,31 +964,31 @@
         def plus(*vals):
             return sum(v.astype(F32) for v in vals).astype(BF)
 
+        vec = after(add_core(vec), token)
         d3, d2, n1 = xswap(diag[3]), yswap(diag[2]), outer(diag[1])
-        vec = add_core(after(vec, packed[0]))
-        d3, d2, n1, vec, x_unit[3], y_unit[1] = barrier((d3, d2, n1, vec, x_unit[3], y_unit[1]))
+        vec = vec + yswap(vec)
+        d3, d2, n1, vec, tok = barrier((d3, d2, n1, vec, fence(token)))
         x3, y3, m1 = xswap(x_unit[3]), yswap(plus(y_unit[3], d3)), outer(y_unit[1])
-        vec = vec + yswap(vec)
-        x3, y3, m1, vec, y_unit[2] = barrier((x3, y3, m1, vec, y_unit[2]))
+        vec = vec + swap("dp", 1)(vec)
+        x3, y3, m1, vec, tok = barrier((x3, y3, m1, vec, fence(tok)))
         x2, y2 = xswap(plus(x_unit[2], d2)), yswap(y_unit[2])
         part3 = plus(own[3], x3, y3)
         e3 = inward(part3)
-        vec = vec + swap("dp", 1)(vec)
-        x2, y2, e3, x_unit[1], vec = barrier((x2, y2, e3, x_unit[1], vec))
+        vec = vec + swap("dp", 2)(vec)
+        x2, y2, e3, vec, tok = barrier((x2, y2, e3, vec, fence(tok)))
         x1, d0 = xswap(x_unit[1]), yswap(plus(diag[0], n1))
         part2 = plus(own[2], x2, y2, e3)
         fm, fe = middle(part2), inward(part2)
-        vec = vec + swap("dp", 2)(vec)
-        x1, d0, fm, fe, vec, m1 = barrier((x1, d0, fm, fe, vec, m1))
+        vec = vec + swap("dp", 4)(vec)
+        x1, d0, fm, fe, vec, tok = barrier((x1, d0, fm, fe, vec, fence(tok)))
         x0, y0 = xswap(plus(x_unit[0], d0)), yswap(plus(y_unit[0], m1))
         near, mid = outer(plus(own[1], x1, fm)), middle(plus(part3, fe))
-        vec = vec + swap("dp", 4)(vec)
-        x0, y0, near, mid, vec, grad_rows = barrier((x0, y0, near, mid, vec, grad_rows))
+        x0, y0, near, mid, grad_rows, tok = barrier((x0, y0, near, mid, grad_rows, fence(tok)))
         terms = (own[0], x0, y0, near, mid)
     else:
-        packed = weight_grads(
-            block_slot, me, srcs, ((0, None, 0),), [(2, slots // GROUP, TILES, 96, 128)], slots
-        )[0]
+        packed = pack_grads(
+            block_slot, me, grads, ((0, None),), [(2, slots // GROUP, TILES, 96, 128)], slots
+        )[1]
         blocks = unpack_plain(packed)
         blocks = lax.psum_scatter(blocks, "dp", scatter_dimension=1, tiled=True)
         mine = lax.dynamic_index_in_dim(blocks, y, 0, keepdims=False)

time: 280 us -> 253 us (0.904)
  Pallas kernels: 111 us -> 79.8 us
  waiting for transfers between devices: 86.3 us -> 73.7 us
  starting transfers between devices: 56.9 us -> 64.8 us
  local copies, waits for them, and re-layouts: 13.6 us -> 19.2 us
  other arithmetic: 5.57 us -> 8.47 us
    ppermute x38, waiting for transfers between devices: 70.1 us -> 53.9 us  [swap(): return lambda v: lax.ppermute(v, axis, xor_pairs(size, step))]
    pallas_call x3 -> x4, Pallas kernels: 32.1 us -> 21.1 us  [the longest x1 14.6 us: pack_grads(): pl.pallas_call(functools.partial(pack_body, places), out_shape=(sds((8, 1...]
    unnamed x108 -> x120, local copies, waits for them, and re-layouts: 6.7 us -> 14.9 us
    ppermute x14, starting transfers between devices: 27.3 us -> 31.4 us  [along_z(): return lambda v: lax.ppermute(v, 'dp', z_pairs(pairs))]
    ppermute x38, starting transfers between devices: 29.6 us -> 33.4 us  [swap(): return lambda v: lax.ppermute(v, axis, xor_pairs(size, step))]
    ppermute x14, waiting for transfers between devices: 16.1 us -> 19.8 us  [along_z(): return lambda v: lax.ppermute(v, 'dp', z_pairs(pairs))]
    pallas_call x1, Pallas kernels: 10.1 us -> 6.7 us  [feed(): pl.pallas_call(feed_body, out_shape=(one, sds((rows, 768), F32), sds((row...]
    pallas_call x1, Pallas kernels: 10.2 us -> 7.33 us  [feed_back(): pl.pallas_call(feed_back_body, out_shape=(sds((rows // 2, 768), BF), sds(...]
  transfers between devices with their start and end apart: 52 -> 52, of which waited for: 30 -> 25; matrix products, arithmetic and copies ran while one was open for 5% -> 5% of each run, Pallas kernels for 28% -> 22%
where the time goes in v3:
time: 253 us; the launch traced here: 249 us
  Pallas kernels  79.8 us (32%)
  waiting for transfers between devices  73.7 us (29%)
  starting transfers between devices  64.8 us (26%)
  local copies, waits for them, and re-layouts  19.2 us (8%)
  other arithmetic  8.47 us (3%)
  between operations  2.77 us (1%)
    ppermute x38, waiting for transfers between devices, swap(): return lambda v: lax.ppermute(v, axis, xor_pairs(size, step))  53.9 us
    ppermute x38, starting transfers between devices, swap(): return lambda v: lax.ppermute(v, axis, xor_pairs(size, step))  33.4 us
    ppermute x14, starting transfers between devices, along_z(): return lambda v: lax.ppermute(v, 'dp', z_pairs(pairs))  31.4 us
    ppermute x14, waiting for transfers between devices, along_z(): return lambda v: lax.ppermute(v, 'dp', z_pairs(pairs))  19.8 us
    unnamed x120, local copies, waits for them, and re-layouts  14.9 us
    pallas_call x1, Pallas kernels, pack_grads(): pl.pallas_call(functools.partial(pack_body, places), out_shape=(sds((8, 1...  14.6 us
    pallas_call x1, Pallas kernels, attend_back(): pl.pallas_call(attend_back_body, grid=(pairs,), out_shape=(sds((rows // 2...  13.5 us
    pallas_call x1, Pallas kernels, build_weights(): pl.pallas_call(functools.partial(weights_body, len(pieces), places), out_...  10 us
  transfers between devices with their start and end apart: 52, of which 25 were waited for; matrix products, arithmetic and copies ran while one was open for 5% of the time, Pallas kernels for 22%

profile of v3, /device:TPU:8, one launch (start us, length us, event | category | flops | bytes accessed | tf_op | source)
XLA Modules:
  0.0 248.7 jit_solution(16561353806591576560)
XLA Ops:
  0.7 1.3 copy-done.6
  2.1 1.6 collective-permute-start.3
  3.7 1.5 collective-permute-start.2
  5.2 3.5 %collective-permute-start.1 = (bf16[6,3,96,128]{3,2,1,0:T(8,128)(2,1)S(1)}, bf16[6,3,96,128]{3,2,1,0:T(8,128)(2,1)}, u32[]{:S(2)}, u32[]{:S(2)}) collective-permute-start(bf16[6,3,96,128]{3,2,1,0:T(8,128)(2,1)S(1)} %pack_owned.1.refs_0_), channel_id=1, source_target_pairs={{8,16},{12,20},{16,8},{20,12},{9,17},{13,21},{17,9},{21,13},{10,18... | collective-permute-start | bytes 1327112 | tf_op jit(solution)/shard_map/ppermute | solution.py:851
  9.4 1.2 dynamic_slice.43
  11.6 1.7 constant_dynamic-slice_fusion.1
  14.3 1.2 collective-permute-done.2.refs_1_
  15.5 3.1 %collective-permute-done.1 = bf16[6,3,96,128]{3,2,1,0:T(8,128)(2,1)} collective-permute-done((bf16[6,3,96,128]{3,2,1,0:T(8,128)(2,1)S(1)}, bf16[6,3,96,128]{3,2,1,0:T(8,128)(2,1)}, u32[]{:S(2)}, u32[]{:S(2)}) %collective-permute-start.1) | collective-permute-done | bytes 442400 | tf_op jit(solution)/shard_map/ppermute | solution.py:851
  18.6 1.4 collective-permute-done.refs_4_
  19.9 2.3 collective-permute-start.6
  23.4 1.3 collective-permute-start.7
  24.8 7.9 %collective-permute-done.5.refs_3_ = bf16[6,3,96,128]{3,2,1,0:T(8,128)(2,1)S(1)} collective-permute-done((bf16[6,3,96,128]{3,2,1,0:T(8,128)(2,1)}, bf16[6,3,96,128]{3,2,1,0:T(8,128)(2,1)S(1)}, u32[]{:S(2)}, u32[]{:S(2)}) %collective-permute-start.5) | collective-permute-done | bytes 442400 | tf_op jit(solution)/shard_map/ppermute | solution.py:846
  34.6 1.5 collective-permute-start.9
  36.1 4.3 %collective-permute-start.11 = (bf16[6,3,96,128]{3,2,1,0:T(8,128)(2,1)S(1)}, bf16[6,3,96,128]{3,2,1,0:T(8,128)(2,1)S(1)}, u32[]{:S(2)}, u32[]{:S(2)}) collective-permute-start(bf16[6,3,96,128]{3,2,1,0:T(8,128)(2,1)S(1)} %collective-permute-done.6), channel_id=1, source_target_pairs={{8,0},{12,4},{16,24},{20,28},{9,1},{13,5},{17,25},{21,29},{10,2},{... | collective-permute-start | bytes 1327112 | tf_op jit(solution)/shard_map/ppermute | solution.py:851
  40.5 2.0 collective-permute-done.10.refs_10_
  43.2 7.8 %collective-permute-done.11 = bf16[6,3,96,128]{3,2,1,0:T(8,128)(2,1)S(1)} collective-permute-done((bf16[6,3,96,128]{3,2,1,0:T(8,128)(2,1)S(1)}, bf16[6,3,96,128]{3,2,1,0:T(8,128)(2,1)S(1)}, u32[]{:S(2)}, u32[]{:S(2)}) %collective-permute-start.11) | collective-permute-done | bytes 442400 | tf_op jit(solution)/shard_map/ppermute | solution.py:851
  53.2 2.5 collective-permute-start.20
  55.7 1.5 collective-permute-start.19
  57.2 3.1 %collective-permute-done.14.refs_6_ = bf16[6,3,96,128]{3,2,1,0:T(8,128)(2,1)S(1)} collective-permute-done((bf16[6,3,96,128]{3,2,1,0:T(8,128)(2,1)}, bf16[6,3,96,128]{3,2,1,0:T(8,128)(2,1)S(1)}, u32[]{:S(2)}, u32[]{:S(2)}) %collective-permute-start.14) | collective-permute-done | bytes 442400 | tf_op jit(solution)/shard_map/ppermute | solution.py:851
  60.3 1.3 collective-permute-done.13.refs_14_
  61.6 1.2 collective-permute-done.12.refs_13_
  64.2 5.0 %collective-permute-done.15.xb = bf16[133,768]{1,0:T(8,128)(2,1)S(1)} collective-permute-done((bf16[133,768]{1,0:T(8,128)(2,1)S(1)}, bf16[133,768]{1,0:T(8,128)(2,1)S(1)}, u32[]{:S(2)}, u32[]{:S(2)}) %collective-permute-start.15) | collective-permute-done | bytes 204320 | tf_op jit(solution)/shard_map/ppermute | solution.py:846
  69.3 1.9 collective-permute-done.18.refs_15_
  72.9 10.0 %build_weights.1 = (bf16[768,1152]{1,0:T(8,128)(2,1)}, bf16[384,768]{1,0:T(8,128)(2,1)}, bf16[2,768,768]{2,1,0:T(8,128)(2,1)}, bf16[2,768,768]{2,1,0:T(8,128)(2,1)}) custom-call(s32[192]{0:T(256)} %pos_ref.3, s32[2]{0:T(128)} %get-tuple-element.153.me_ref, bf16[6,3,96,128]{3,2,1,0:T(8,128)(2,1)} %copy-done.14, ...), custom_call_target="tpu_custom_call" | custom-call | flops 100000000 | bytes 30000000 | tf_op jit(solution)/shard_map/build_weights/pallas_call | solution.py:190
  83.0 1.5 copy-done.9
  84.4 2.9 %project.1 = (bf16[576,1152]{1,0:T(8,128)(2,1)S(1)}, f32[576,768]{1,0:T(8,128)S(1)}, bf16[576,768]{1,0:T(8,128)(2,1)S(1)}) custom-call(s32[2]{0:T(128)S(1)} %get-tuple-element.121.flags_ref, bf16[133,768]{1,0:T(8,128)(2,1)S(1)} %bitcast.48, bf16[133,768]{1,0:T(8,128)(2,1)S(1)} %collective-permute-done.15.xb, ...), custom_call_target="tpu_custom_call" | custom-call | flops 1000000000 | bytes 5000000 | tf_op jit(solution)/shard_map/project/pallas_call | solution.py:380
  87.4 7.9 %attend.1 = (bf16[576,384]{1,0:T(8,128)(2,1)S(1)}, bf16[6,576,576]{2,1,0:T(8,128)(2,1)S(1)}, bf16[576,768]{1,0:T(8,128)(2,1)S(1)}) custom-call(s32[576,1]{1,0:T(8,128)S(1)} %copy.38.cq_ref, s32[1,576]{1,0:T(1,128)S(1)} %broadcast_in_dim.25.ck_ref, bf16[576,1152]{1,0:T(8,128)(2,1)S(1)} %get-tuple-element.143.q_ref.k_ref.v_ref, ...), custom_call_target="tpu_custom_call" | custom-call | flops 2500000000 | bytes 8000000 | tf_op jit(solution)/shard_map/attend/pallas_call | solution.py:446
  95.4 2.4 collective-permute-done.22.other_ref
  97.8 6.7 %feed.1 = (bf16[576,768]{1,0:T(8,128)(2,1)S(1)}, f32[576,768]{1,0:T(8,128)S(1)}, f32[576,1]{1,0:T(8,128)S(1)}, bf16[2,576,768]{2,1,0:T(8,128)(2,1)S(1)}, bf16[2,...) custom-call(bf16[576,768]{1,0:T(8,128)(2,1)S(1)} %get-tuple-element.145.mine_ref, ...), custom_call_target="tpu_custom_call" | custom-call | flops 2800000000 | bytes 16000000 | tf_op jit(solution)/shard_map/feed/pallas_call | solution.py:507
  106.2 2.0 collective-permute-done.24.cc
  108.5 7.3 %feed_back.1 = (bf16[288,768]{1,0:T(8,128)(2,1)S(1)}, f32[576,768]{1,0:T(8,128)S(1)}, bf16[576,768]{1,0:T(8,128)(2,1)S(1)}, bf16[2,576,768]{2,1,0:T(8,128)(2,1)S...) custom-call(bf16[576,768]{1,0:T(8,128)(2,1)S(1)} %get-tuple-element.149.mine_ref, ...), custom_call_target="tpu_custom_call" | custom-call | flops 2800000000 | bytes 16000000 | tf_op jit(solution)/shard_map/feed_back/pallas_call | solution.py:566
  116.0 1.7 collective-permute-start.26
  117.7 3.2 %down_grads.1.later_ref.refs_0_ = bf16[2,768,768]{2,1,0:T(8,128)(2,1)S(1)} custom-call(bf16[2,576,768]{2,1,0:T(8,128)(2,1)S(1)} %get-tuple-element.154.act_ref, bf16[576,768]{1,0:T(8,128)(2,1)S(1)} %get-tuple-element.155.d2_ref), custom_call_target="tpu_custom_call" | custom-call | flops 1400000000 | bytes 8000000 | tf_op jit(solution)/shard_map/down_grads/pallas_call | solution.py:235
  120.9 13.5 %attend_back.1 = (f32[288,768]{1,0:T(8,128)S(1)}, bf16[768,1152]{1,0:T(8,128)(2,1)S(1)}, bf16[384,768]{1,0:T(8,128)(2,1)S(1)}, bf16[576,768]{1,0:T(8,128)(2,1)S(...) custom-call(bf16[576,768]{1,0:T(8,128)(2,1)S(1)} %get-tuple-element.158.mine_ref, ...), custom_call_target="tpu_custom_call" | custom-call | flops 2038431744 | bytes 10485760 | tf_op jit(solution)/shard_map/attend_back/pallas_call | solution.py:640
  134.4 1.2 copy-done.13
  139.7 1.5 copy-done.12
  141.2 3.1 %up_grads.1.refs_1_ = bf16[2,768,768]{2,1,0:T(8,128)(2,1)S(1)} custom-call(bf16[576,768]{1,0:T(8,128)(2,1)S(1)} %copy-done.18, bf16[2,576,768]{2,1,0:T(8,128)(2,1)S(1)} %copy-done.12, bf16[576,768]{1,0:T(8,128)(2,1)S(1)} %copy-done.5), custom_call_target="tpu_custom_call" | custom-call | flops 1400000000 | bytes 8000000 | tf_op jit(solution)/shard_map/up_grads/pallas_call | solution.py:247
  144.3 1.4 copy-done.3
  147.1 14.6 %pack_grads.1 = (f32[8,128]{1,0:T(8,128)}, bf16[6,3,96,128]{3,2,1,0:T(8,128)(2,1)}, bf16[6,3,96,128]{3,2,1,0:T(8,128)(2,1)}, bf16[6,3,96,128]{3,2,1,0:T(8,128)(2...) custom-call(s32[192]{0:T(256)} %pos_ref.3, ...), custom_call_target="tpu_custom_call" | custom-call | flops 100000000 | bytes 30000000 | tf_op jit(solution)/shard_map/pack_grads/pallas_call | solution.py:333
  162.7 2.8 %collective-permute-start.32 = (bf16[6,3,96,128]{3,2,1,0:T(8,128)(2,1)}, bf16[6,3,96,128]{3,2,1,0:T(8,128)(2,1)S(1)}, u32[]{:S(2)}, u32[]{:S(2)}) collective-permute-start(bf16[6,3,96,128]{3,2,1,0:T(8,128)(2,1)} %get-tuple-element.174), channel_id=1, source_target_pairs={{0,8},{4,12},{8,0},{12,4},{16,24},{20,28},{24,16},{28,20},{1,9},{5... | collective-permute-start | bytes 1327112 | tf_op jit(solution)/shard_map/ppermute | solution.py:851
  166.4 1.3 collective-permute-start.34
  167.7 1.5 collective-permute-start.38
  169.2 7.1 %collective-permute-done.34 = f32[19,768]{1,0:T(8,128)S(1)} collective-permute-done((f32[19,768]{1,0:T(8,128)S(1)}, f32[19,768]{1,0:T(8,128)S(1)}, u32[]{:S(2)}, u32[]{:S(2)}) %collective-permute-start.34) | collective-permute-done | bytes 58400 | tf_op jit(solution)/shard_map/ppermute | solution.py:846
  176.3 2.4 collective-permute-start.40
  178.8 1.3 add_convert_fusion.6
  180.9 1.2 collective-permute-start.37
  182.1 1.5 collective-permute-start.41
  183.8 2.7 %collective-permute-done.41 = f32[19,768]{1,0:T(8,128)S(1)} collective-permute-done((f32[19,768]{1,0:T(8,128)S(1)}, f32[19,768]{1,0:T(8,128)S(1)}, u32[]{:S(2)}, u32[]{:S(2)}) %collective-permute-start.41) | collective-permute-done | bytes 58400 | tf_op jit(solution)/shard_map/ppermute | solution.py:846
  186.5 1.5 collective-permute-start.36
  188.6 4.6 %collective-permute-done.39 = bf16[6,3,96,128]{3,2,1,0:T(8,128)(2,1)S(1)} collective-permute-done((bf16[6,3,96,128]{3,2,1,0:T(8,128)(2,1)S(1)}, bf16[6,3,96,128]{3,2,1,0:T(8,128)(2,1)S(1)}, u32[]{:S(2)}, u32[]{:S(2)}) %collective-permute-start.39) | collective-permute-done | bytes 442400 | tf_op jit(solution)/shard_map/ppermute | solution.py:846
  193.4 1.3 collective-permute-start.42
  194.7 1.5 collective-permute-start.29
  196.3 2.7 %collective-permute-start.43 = (f32[19,768]{1,0:T(8,128)S(1)}, f32[19,768]{1,0:T(8,128)S(1)}, u32[]{:S(2)}, u32[]{:S(2)}) collective-permute-start(f32[19,768]{1,0:T(8,128)S(1)} %add.138), channel_id=1, source_target_pairs={{0,8},{4,12},{8,0},{12,4},{16,24},{20,28},{24,16},{28,20},{1,9},{5... | collective-permute-start | bytes 175112 | tf_op jit(solution)/shard_map/ppermute | solution.py:846
  199.1 6.1 %collective-permute-done.43 = f32[19,768]{1,0:T(8,128)S(1)} collective-permute-done((f32[19,768]{1,0:T(8,128)S(1)}, f32[19,768]{1,0:T(8,128)S(1)}, u32[]{:S(2)}, u32[]{:S(2)}) %collective-permute-start.43) | collective-permute-done | bytes 58400 | tf_op jit(solution)/shard_map/ppermute | solution.py:846
  206.3 1.4 collective-permute-start.45
  207.7 3.4 %collective-permute-start.44 = (bf16[6,3,96,128]{3,2,1,0:T(8,128)(2,1)S(1)}, bf16[6,3,96,128]{3,2,1,0:T(8,128)(2,1)S(1)}, u32[]{:S(2)}, u32[]{:S(2)}) collective-permute-start(bf16[6,3,96,128]{3,2,1,0:T(8,128)(2,1)S(1)} %add_convert_fusion.4), channel_id=1, source_target_pairs={{8,16},{12,20},{16,8},{20,12},{9,17},{13,21},{17,9},{21,13},{10,18... | collective-permute-start | bytes 1327112 | tf_op jit(solution)/shard_map/ppermute | solution.py:851
  214.0 4.9 %collective-permute-done.46 = f32[19,768]{1,0:T(8,128)S(1)} collective-permute-done((f32[19,768]{1,0:T(8,128)S(1)}, f32[19,768]{1,0:T(8,128)S(1)}, u32[]{:S(2)}, u32[]{:S(2)}) %collective-permute-start.46) | collective-permute-done | bytes 58400 | tf_op jit(solution)/shard_map/ppermute | solution.py:846
  218.8 1.2 collective-permute-start.48
  221.3 2.6 %collective-permute-start.49 = (bf16[6,3,96,128]{3,2,1,0:T(8,128)(2,1)S(1)}, bf16[6,3,96,128]{3,2,1,0:T(8,128)(2,1)S(1)}, u32[]{:S(2)}, u32[]{:S(2)}) collective-permute-start(bf16[6,3,96,128]{3,2,1,0:T(8,128)(2,1)S(1)} %add_convert_fusion.1), channel_id=1, source_target_pairs={{0,8},{4,12},{8,0},{12,4},{16,24},{20,28},{24,16},{28,20},{1,9},{5... | collective-permute-start | bytes 1327112 | tf_op jit(solution)/shard_map/ppermute | solution.py:851
  224.0 1.5 collective-permute-start.47
  225.5 3.5 %collective-permute-start.50 = (bf16[6,3,96,128]{3,2,1,0:T(8,128)(2,1)S(1)}, bf16[6,3,96,128]{3,2,1,0:T(8,128)(2,1)S(1)}, u32[]{:S(2)}, u32[]{:S(2)}) collective-permute-start(bf16[6,3,96,128]{3,2,1,0:T(8,128)(2,1)S(1)} %copy-done.35), channel_id=1, source_target_pairs={{8,16},{12,20},{16,8},{20,12},{9,17},{13,21},{17,9},{21,13},{10,18... | collective-permute-start | bytes 1327112 | tf_op jit(solution)/shard_map/ppermute | solution.py:851
  230.2 2.2 collective-permute-done.47.refs_1_
  232.4 3.3 %collective-permute-done.50.refs_4_ = bf16[6,3,96,128]{3,2,1,0:T(8,128)(2,1)S(1)} collective-permute-done((bf16[6,3,96,128]{3,2,1,0:T(8,128)(2,1)S(1)}, bf16[6,3,96,128]{3,2,1,0:T(8,128)(2,1)S(1)}, u32[]{:S(2)}, u32[]{:S(2)}) %collective-permute-start.50) | collective-permute-done | bytes 442400 | tf_op jit(solution)/shard_map/ppermute | solution.py:851
  237.4 9.7 %soap.1 = (f32[24,96,96]{2,1,0:T(8,128)}, bf16[24,96,96]{2,1,0:T(8,128)(2,1)}, f32[24,96,96]{2,1,0:T(8,128)}, f32[24,96,96]{2,1,0:T(8,128)}, f32[24,96,96]{2,1,0:T(8,128)}, /*index=5*/f32[24,96,96]{2,1,0:T(8,128)}) custom-call(bf16[6,3,96,128]{3,2,1,0:T(8,128)(2,1)} %get-tuple-element.206.refs_0_, bf16[6,3,96,128]{3,2,1,0:T(8,128)(2,1)} %copy-done.48, ...), custom_call_target="tpu_custom_call" | custom-call | flops 300000000 | bytes 24000000 | tf_op jit(solution)/shard_map/soap/pallas_call | solution.py:761
  (223 shorter events, 31.8 us)
Async XLA Ops:
  2.1 12.1 %collective-permute-start.3 = (bf16[6,3,96,128]{3,2,1,0:T(8,128)(2,1)S(1)}, bf16[6,3,96,128]{3,2,1,0:T(8,128)(2,1)}, u32[]{:S(2)}, u32[]{:S(2)}) collective-permute-start(bf16[6,3,96,128]{3,2,1,0:T(8,128)(2,1)S(1)} %pack_owned.1.refs_0_), channel_id=1, source_target_pairs={{0,2},{1,3},{2,0},{3,1},{4,6},{5,7},{6,4},{7,5},{8,10},{9,11},{10,... | collective-permute-start | bytes 1327112 | tf_op jit(solution)/shard_map/ppermute | solution.py:846
  3.7 11.7 %collective-permute-start.2 = (bf16[6,3,96,128]{3,2,1,0:T(8,128)(2,1)S(1)}, bf16[6,3,96,128]{3,2,1,0:T(8,128)(2,1)}, u32[]{:S(2)}, u32[]{:S(2)}) collective-permute-start(bf16[6,3,96,128]{3,2,1,0:T(8,128)(2,1)S(1)} %pack_owned.1.refs_0_), channel_id=1, source_target_pairs={{0,4},{4,0},{8,12},{12,8},{16,20},{20,16},{24,28},{28,24},{1,5},{5... | collective-permute-start | bytes 1327112 | tf_op jit(solution)/shard_map/ppermute | solution.py:846
  5.2 13.3 %collective-permute-start.1 = (bf16[6,3,96,128]{3,2,1,0:T(8,128)(2,1)S(1)}, bf16[6,3,96,128]{3,2,1,0:T(8,128)(2,1)}, u32[]{:S(2)}, u32[]{:S(2)}) collective-permute-start(bf16[6,3,96,128]{3,2,1,0:T(8,128)(2,1)S(1)} %pack_owned.1.refs_0_), channel_id=1, source_target_pairs={{8,16},{12,20},{16,8},{20,12},{9,17},{13,21},{17,9},{21,13},{10,18... | collective-permute-start | bytes 1327112 | tf_op jit(solution)/shard_map/ppermute | solution.py:851
  8.7 11.2 %collective-permute-start = (bf16[6,3,96,128]{3,2,1,0:T(8,128)(2,1)S(1)}, bf16[6,3,96,128]{3,2,1,0:T(8,128)(2,1)}, u32[]{:S(2)}, u32[]{:S(2)}) collective-permute-start(bf16[6,3,96,128]{3,2,1,0:T(8,128)(2,1)S(1)} %pack_owned.1.refs_0_), channel_id=1, source_target_pairs={{0,8},{4,12},{8,0},{12,4},{16,24},{20,28},{24,16},{28,20},{1,9},{5... | collective-permute-start | bytes 1327112 | tf_op jit(solution)/shard_map/ppermute | solution.py:851
  8.8 15.9 %collective-permute-start.8 = (f32[1,1152]{1,0:T(1,128)}, f32[1,1152]{1,0:T(1,128)S(1)}, u32[]{:S(2)}, u32[]{:S(2)}) collective-permute-start(f32[1,1152]{1,0:T(1,128)} %param.30), channel_id=1, source_target_pairs={{0,2},{1,3},{2,0},{3,1},{4,6},{5,7},{6,4},{7,5},{8,10},{9,11},{10,... | collective-permute-start | bytes 13832 | tf_op jit(solution)/shard_map/ppermute | solution.py:846
  19.9 12.8 %collective-permute-start.6 = (bf16[6,3,96,128]{3,2,1,0:T(8,128)(2,1)}, bf16[6,3,96,128]{3,2,1,0:T(8,128)(2,1)S(1)}, u32[]{:S(2)}, u32[]{:S(2)}) collective-permute-start(bf16[6,3,96,128]{3,2,1,0:T(8,128)(2,1)} %collective-permute-done.refs_4_), channel_id=1, source_target_pairs={{8,16},{12,20},{16,8},{20,12},{9,17},{13,21},{17,9},{21,13},{10,18... | collective-permute-start | bytes 1327112 | tf_op jit(solution)/shard_map/ppermute | solution.py:851
  22.3 10.4 %collective-permute-start.4 = (bf16[6,3,96,128]{3,2,1,0:T(8,128)(2,1)}, bf16[6,3,96,128]{3,2,1,0:T(8,128)(2,1)S(1)}, u32[]{:S(2)}, u32[]{:S(2)}) collective-permute-start(bf16[6,3,96,128]{3,2,1,0:T(8,128)(2,1)} %collective-permute-done.refs_4_), channel_id=1, source_target_pairs={{0,4},{4,0},{8,12},{12,8},{16,20},{20,16},{24,28},{28,24},{1,5},{5... | collective-permute-start | bytes 1327112 | tf_op jit(solution)/shard_map/ppermute | solution.py:846
  22.9 9.8 %collective-permute-start.5 = (bf16[6,3,96,128]{3,2,1,0:T(8,128)(2,1)}, bf16[6,3,96,128]{3,2,1,0:T(8,128)(2,1)S(1)}, u32[]{:S(2)}, u32[]{:S(2)}) collective-permute-start(bf16[6,3,96,128]{3,2,1,0:T(8,128)(2,1)} %collective-permute-done.2.refs_1_), channel_id=1, source_target_pairs={{0,2},{1,3},{2,0},{3,1},{4,6},{5,7},{6,4},{7,5},{8,10},{9,11},{10,... | collective-permute-start | bytes 1327112 | tf_op jit(solution)/shard_map/ppermute | solution.py:846
  23.4 9.3 %collective-permute-start.7 = (bf16[6,3,96,128]{3,2,1,0:T(8,128)(2,1)}, bf16[6,3,96,128]{3,2,1,0:T(8,128)(2,1)S(1)}, u32[]{:S(2)}, u32[]{:S(2)}) collective-permute-start(bf16[6,3,96,128]{3,2,1,0:T(8,128)(2,1)} %collective-permute-done.1), channel_id=1, source_target_pairs={{8,0},{12,4},{16,24},{20,28},{9,1},{13,5},{17,25},{21,29},{10,2},{... | collective-permute-start | bytes 1327112 | tf_op jit(solution)/shard_map/ppermute | solution.py:851
  32.7 38.5 %copy-start.38 = (bf16[6,3,96,128]{3,2,1,0:T(8,128)(2,1)}, bf16[6,3,96,128]{3,2,1,0:T(8,128)(2,1)S(1)}, u32[]{:S(2)}) copy-start(bf16[6,3,96,128]{3,2,1,0:T(8,128)(2,1)S(1)} %collective-permute-done.5.refs_3_) | copy-start | bytes 1327108
  33.7 39.2 %copy-start.23 = (bf16[6,3,96,128]{3,2,1,0:T(8,128)(2,1)}, bf16[6,3,96,128]{3,2,1,0:T(8,128)(2,1)S(1)}, u32[]{:S(2)}) copy-start(bf16[6,3,96,128]{3,2,1,0:T(8,128)(2,1)S(1)} %add.131.refs_8_) | copy-start | bytes 1327108
  33.7 8.8 %collective-permute-start.10 = (bf16[6,3,96,128]{3,2,1,0:T(8,128)(2,1)S(1)}, bf16[6,3,96,128]{3,2,1,0:T(8,128)(2,1)S(1)}, u32[]{:S(2)}, u32[]{:S(2)}) collective-permute-start(bf16[6,3,96,128]{3,2,1,0:T(8,128)(2,1)S(1)} %add.131.refs_8_), channel_id=1, source_target_pairs={{0,2},{1,3},{2,0},{3,1},{4,6},{5,7},{6,4},{7,5},{8,10},{9,11},{10,... | collective-permute-start | bytes 1327112 | tf_op jit(solution)/shard_map/ppermute | solution.py:846
  34.6 8.4 %collective-permute-start.9 = (bf16[6,3,96,128]{3,2,1,0:T(8,128)(2,1)S(1)}, bf16[6,3,96,128]{3,2,1,0:T(8,128)(2,1)S(1)}, u32[]{:S(2)}, u32[]{:S(2)}) collective-permute-start(bf16[6,3,96,128]{3,2,1,0:T(8,128)(2,1)S(1)} %add.131.refs_8_), channel_id=1, source_target_pairs={{0,4},{4,0},{8,12},{12,8},{16,20},{20,16},{24,28},{28,24},{1,5},{5... | collective-permute-start | bytes 1327112 | tf_op jit(solution)/shard_map/ppermute | solution.py:846
  36.1 14.9 %collective-permute-start.11 = (bf16[6,3,96,128]{3,2,1,0:T(8,128)(2,1)S(1)}, bf16[6,3,96,128]{3,2,1,0:T(8,128)(2,1)S(1)}, u32[]{:S(2)}, u32[]{:S(2)}) collective-permute-start(bf16[6,3,96,128]{3,2,1,0:T(8,128)(2,1)S(1)} %collective-permute-done.6), channel_id=1, source_target_pairs={{8,0},{12,4},{16,24},{20,28},{9,1},{13,5},{17,25},{21,29},{10,2},{... | collective-permute-start | bytes 1327112 | tf_op jit(solution)/shard_map/ppermute | solution.py:851
  40.4 19.9 %collective-permute-start.14 = (bf16[6,3,96,128]{3,2,1,0:T(8,128)(2,1)}, bf16[6,3,96,128]{3,2,1,0:T(8,128)(2,1)S(1)}, u32[]{:S(2)}, u32[]{:S(2)}) collective-permute-start(bf16[6,3,96,128]{3,2,1,0:T(8,128)(2,1)} %collective-permute-done.3.refs_2_), channel_id=1, source_target_pairs={{0,8},{4,12},{8,0},{12,4},{16,24},{20,28},{24,16},{28,20},{1,9},{5... | collective-permute-start | bytes 1327112 | tf_op jit(solution)/shard_map/ppermute | solution.py:851
  43.2 28.0 %copy-start.40 = (bf16[6,3,96,128]{3,2,1,0:T(8,128)(2,1)}, bf16[6,3,96,128]{3,2,1,0:T(8,128)(2,1)S(1)}, u32[]{:S(2)}) copy-start(bf16[6,3,96,128]{3,2,1,0:T(8,128)(2,1)S(1)} %collective-permute-done.9.refs_9_) | copy-start | bytes 1327108
  52.1 20.8 %copy-start.24 = (bf16[6,3,96,128]{3,2,1,0:T(8,128)(2,1)}, bf16[6,3,96,128]{3,2,1,0:T(8,128)(2,1)S(1)}, u32[]{:S(2)}) copy-start(bf16[6,3,96,128]{3,2,1,0:T(8,128)(2,1)S(1)} %add.132.refs_12_) | copy-start | bytes 1327108
  52.1 9.5 %collective-permute-start.13 = (bf16[6,3,96,128]{3,2,1,0:T(8,128)(2,1)S(1)}, bf16[6,3,96,128]{3,2,1,0:T(8,128)(2,1)S(1)}, u32[]{:S(2)}, u32[]{:S(2)}) collective-permute-start(bf16[6,3,96,128]{3,2,1,0:T(8,128)(2,1)S(1)} %add.132.refs_12_), channel_id=1, source_target_pairs={{0,2},{1,3},{2,0},{3,1},{4,6},{5,7},{6,4},{7,5},{8,10},{9,11},{10,... | collective-permute-start | bytes 1327112 | tf_op jit(solution)/shard_map/ppermute | solution.py:846
  52.7 10.2 %collective-permute-start.12 = (bf16[6,3,96,128]{3,2,1,0:T(8,128)(2,1)S(1)}, bf16[6,3,96,128]{3,2,1,0:T(8,128)(2,1)S(1)}, u32[]{:S(2)}, u32[]{:S(2)}) collective-permute-start(bf16[6,3,96,128]{3,2,1,0:T(8,128)(2,1)S(1)} %add.132.refs_12_), channel_id=1, source_target_pairs={{0,4},{4,0},{8,12},{12,8},{16,20},{20,16},{24,28},{28,24},{1,5},{5... | collective-permute-start | bytes 1327112 | tf_op jit(solution)/shard_map/ppermute | solution.py:846
  53.2 16.0 %collective-permute-start.20 = (bf16[6,3,96,128]{3,2,1,0:T(8,128)(2,1)S(1)}, bf16[6,3,96,128]{3,2,1,0:T(8,128)(2,1)S(1)}, u32[]{:S(2)}, u32[]{:S(2)}) collective-permute-start(bf16[6,3,96,128]{3,2,1,0:T(8,128)(2,1)S(1)} %collective-permute-done.5.refs_3_), channel_id=1, source_target_pairs={{0,8},{4,12},{8,0},{12,4},{16,24},{20,28},{24,16},{28,20},{1,9},{5... | collective-permute-start | bytes 1327112 | tf_op jit(solution)/shard_map/ppermute | solution.py:851
  55.7 13.5 %collective-permute-start.19 = (bf16[6,3,96,128]{3,2,1,0:T(8,128)(2,1)S(1)}, bf16[6,3,96,128]{3,2,1,0:T(8,128)(2,1)S(1)}, u32[]{:S(2)}, u32[]{:S(2)}) collective-permute-start(bf16[6,3,96,128]{3,2,1,0:T(8,128)(2,1)S(1)} %collective-permute-done.9.refs_9_), channel_id=1, source_target_pairs={{0,2},{1,3},{2,0},{3,1},{4,6},{5,7},{6,4},{7,5},{8,10},{9,11},{10,... | collective-permute-start | bytes 1327112 | tf_op jit(solution)/shard_map/ppermute | solution.py:846
  62.9 8.3 %collective-permute-start.18 = (bf16[6,3,96,128]{3,2,1,0:T(8,128)(2,1)S(1)}, bf16[6,3,96,128]{3,2,1,0:T(8,128)(2,1)S(1)}, u32[]{:S(2)}, u32[]{:S(2)}) collective-permute-start(bf16[6,3,96,128]{3,2,1,0:T(8,128)(2,1)S(1)} %collective-permute-done.13.refs_14_), channel_id=1, source_target_pairs={{0,4},{4,0},{8,12},{12,8},{16,20},{20,16},{24,28},{28,24},{1,5},{5... | collective-permute-start | bytes 1327112 | tf_op jit(solution)/shard_map/ppermute | solution.py:846
  63.4 5.8 %collective-permute-start.15 = (bf16[133,768]{1,0:T(8,128)(2,1)S(1)}, bf16[133,768]{1,0:T(8,128)(2,1)S(1)}, u32[]{:S(2)}, u32[]{:S(2)}) collective-permute-start(bf16[133,768]{1,0:T(8,128)(2,1)S(1)} %bitcast.56), channel_id=1, source_target_pairs={{0,2},{1,3},{2,0},{3,1},{4,6},{5,7},{6,4},{7,5},{8,10},{9,11},{10,... | collective-permute-start | bytes 612872 | tf_op jit(solution)/shard_map/ppermute | solution.py:846
  64.1 18.8 %collective-permute-start.16 = (bf16[133,768]{1,0:T(8,128)(2,1)S(1)}, bf16[133,768]{1,0:T(8,128)(2,1)S(1)}, u32[]{:S(2)}, u32[]{:S(2)}) collective-permute-start(bf16[133,768]{1,0:T(8,128)(2,1)S(1)} %bitcast.47), channel_id=1, source_target_pairs={{0,1},{1,0},{2,3},{3,2},{4,5},{5,4},{6,7},{7,6},{8,9},{9,8},{10,11... | collective-permute-start | bytes 612872 | tf_op jit(solution)/shard_map/ppermute | solution.py:846
  69.2 13.7 %collective-permute-start.17 = (bf16[133,768]{1,0:T(8,128)(2,1)S(1)}, bf16[133,768]{1,0:T(8,128)(2,1)S(1)}, u32[]{:S(2)}, u32[]{:S(2)}) collective-permute-start(bf16[133,768]{1,0:T(8,128)(2,1)S(1)} %collective-permute-done.15.xb), channel_id=1, source_target_pairs={{0,1},{1,0},{2,3},{3,2},{4,5},{5,4},{6,7},{7,6},{8,9},{9,8},{10,11... | collective-permute-start | bytes 612872 | tf_op jit(solution)/shard_map/ppermute | solution.py:846
  72.0 10.9 %collective-permute-start.21 = (bf16[133,768]{1,0:T(8,128)(2,1)S(1)}, bf16[133,768]{1,0:T(8,128)(2,1)S(1)}, u32[]{:S(2)}, u32[]{:S(2)}) collective-permute-start(bf16[133,768]{1,0:T(8,128)(2,1)S(1)} %bitcast.55), channel_id=1, source_target_pairs={{0,2},{1,3},{2,0},{3,1},{4,6},{5,7},{6,4},{7,5},{8,10},{9,11},{10,... | collective-permute-start | bytes 612872 | tf_op jit(solution)/shard_map/ppermute | solution.py:846
  95.3 2.5 %collective-permute-start.22 = (bf16[576,768]{1,0:T(8,128)(2,1)S(1)}, bf16[576,768]{1,0:T(8,128)(2,1)S(1)}, u32[]{:S(2)}, u32[]{:S(2)}) collective-permute-start(bf16[576,768]{1,0:T(8,128)(2,1)S(1)} %get-tuple-element.145.mine_ref), channel_id=1, source_target_pairs={{0,1},{1,0},{2,3},{3,2},{4,5},{5,4},{6,7},{7,6},{8,9},{9,8},{10,11... | collective-permute-start | bytes 2654216 | tf_op jit(solution)/shard_map/ppermute | solution.py:846
  105.4 3.0 %collective-permute-start.23 = (bf16[576,768]{1,0:T(8,128)(2,1)S(1)}, bf16[576,768]{1,0:T(8,128)(2,1)S(1)}, u32[]{:S(2)}, u32[]{:S(2)}) collective-permute-start(bf16[576,768]{1,0:T(8,128)(2,1)S(1)} %get-tuple-element.149.mine_ref), channel_id=1, source_target_pairs={{0,1},{1,0},{2,3},{3,2},{4,5},{5,4},{6,7},{7,6},{8,9},{9,8},{10,11... | collective-permute-start | bytes 2654216 | tf_op jit(solution)/shard_map/ppermute | solution.py:846
  105.6 2.6 %collective-permute-start.24 = (bf16[133,768]{1,0:T(8,128)(2,1)S(1)}, bf16[133,768]{1,0:T(8,128)(2,1)S(1)}, u32[]{:S(2)}, u32[]{:S(2)}) collective-permute-start(bf16[133,768]{1,0:T(8,128)(2,1)S(1)} %bitcast.43), channel_id=1, source_target_pairs={{0,1},{1,0},{2,3},{3,2},{4,5},{5,4},{6,7},{7,6},{8,9},{9,8},{10,11... | collective-permute-start | bytes 612872 | tf_op jit(solution)/shard_map/ppermute | solution.py:846
  106.0 2.4 collective-permute-start.25
  115.8 5.1 %collective-permute-start.27 = (bf16[576,768]{1,0:T(8,128)(2,1)S(1)}, bf16[576,768]{1,0:T(8,128)(2,1)S(1)}, u32[]{:S(2)}, u32[]{:S(2)}) collective-permute-start(bf16[576,768]{1,0:T(8,128)(2,1)S(1)} %get-tuple-element.158.mine_ref), channel_id=1, source_target_pairs={{0,1},{1,0},{2,3},{3,2},{4,5},{5,4},{6,7},{7,6},{8,9},{9,8},{10,11... | collective-permute-start | bytes 2654216 | tf_op jit(solution)/shard_map/ppermute | solution.py:846
  116.0 22.5 %collective-permute-start.26 = (bf16[133,768]{1,0:T(8,128)(2,1)S(1)}, bf16[133,768]{1,0:T(8,128)(2,1)S(1)}, u32[]{:S(2)}, u32[]{:S(2)}) collective-permute-start(bf16[133,768]{1,0:T(8,128)(2,1)S(1)} %get-tuple-element.255), channel_id=1, source_target_pairs={{0,2},{1,3},{2,0},{3,1},{4,6},{5,7},{6,4},{7,5},{8,10},{9,11},{10,... | collective-permute-start | bytes 612872 | tf_op jit(solution)/shard_map/ppermute | solution.py:846
  138.5 7.3 %collective-permute-start.28 = (bf16[288,768]{1,0:T(8,128)(2,1)}, bf16[288,768]{1,0:T(8,128)(2,1)S(1)}, u32[]{:S(2)}, u32[]{:S(2)}) collective-permute-start(bf16[288,768]{1,0:T(8,128)(2,1)} %slice.36), channel_id=1, source_target_pairs={{0,1},{1,0},{2,3},{3,2},{4,5},{5,4},{6,7},{7,6},{8,9},{9,8},{10,11... | collective-permute-start | bytes 1327112 | tf_op jit(solution)/shard_map/ppermute | solution.py:846
  146.5 19.1 %collective-permute-start.33 = (f32[16,768]{1,0:T(8,128)S(1)}, f32[16,768]{1,0:T(8,128)S(1)}, u32[]{:S(2)}, u32[]{:S(2)}) collective-permute-start(f32[16,768]{1,0:T(8,128)S(1)} %pad_maximum_fusion.3), channel_id=1, source_target_pairs={{0,1},{1,0},{2,3},{3,2},{4,5},{5,4},{6,7},{7,6},{8,9},{9,8},{10,11... | collective-permute-start | bytes 147464 | tf_op jit(solution)/shard_map/ppermute | solution.py:846
  161.7 22.0 %copy-start.32 = (bf16[6,3,96,128]{3,2,1,0:T(8,128)(2,1)S(1)}, bf16[6,3,96,128]{3,2,1,0:T(8,128)(2,1)}, u32[]{:S(2)}) copy-start(bf16[6,3,96,128]{3,2,1,0:T(8,128)(2,1)} %get-tuple-element.181) | copy-start | bytes 1327108
  161.7 31.5 %copy-start.28 = (bf16[6,3,96,128]{3,2,1,0:T(8,128)(2,1)S(1)}, bf16[6,3,96,128]{3,2,1,0:T(8,128)(2,1)}, u32[]{:S(2)}) copy-start(bf16[6,3,96,128]{3,2,1,0:T(8,128)(2,1)} %get-tuple-element.184) | copy-start | bytes 1327108
  161.7 17.0 %collective-permute-start.30 = (bf16[6,3,96,128]{3,2,1,0:T(8,128)(2,1)}, bf16[6,3,96,128]{3,2,1,0:T(8,128)(2,1)}, u32[]{:S(2)}, u32[]{:S(2)}) collective-permute-start(bf16[6,3,96,128]{3,2,1,0:T(8,128)(2,1)} %get-tuple-element.172), channel_id=1, source_target_pairs={{0,4},{4,0},{8,12},{12,8},{16,20},{20,16},{24,28},{28,24},{1,5},{5... | collective-permute-start | bytes 1327112 | tf_op jit(solution)/shard_map/ppermute | solution.py:846
  162.3 16.4 %collective-permute-start.31 = (bf16[6,3,96,128]{3,2,1,0:T(8,128)(2,1)}, bf16[6,3,96,128]{3,2,1,0:T(8,128)(2,1)S(1)}, u32[]{:S(2)}, u32[]{:S(2)}) collective-permute-start(bf16[6,3,96,128]{3,2,1,0:T(8,128)(2,1)} %get-tuple-element.173), channel_id=1, source_target_pairs={{0,2},{1,3},{2,0},{3,1},{4,6},{5,7},{6,4},{7,5},{8,10},{9,11},{10,... | collective-permute-start | bytes 1327112 | tf_op jit(solution)/shard_map/ppermute | solution.py:846
  162.7 16.0 %collective-permute-start.32 = (bf16[6,3,96,128]{3,2,1,0:T(8,128)(2,1)}, bf16[6,3,96,128]{3,2,1,0:T(8,128)(2,1)S(1)}, u32[]{:S(2)}, u32[]{:S(2)}) collective-permute-start(bf16[6,3,96,128]{3,2,1,0:T(8,128)(2,1)} %get-tuple-element.174), channel_id=1, source_target_pairs={{0,8},{4,12},{8,0},{12,4},{16,24},{20,28},{24,16},{28,20},{1,9},{5... | collective-permute-start | bytes 1327112 | tf_op jit(solution)/shard_map/ppermute | solution.py:851
  165.5 15.4 %copy-start.56 = (bf16[6,3,96,128]{3,2,1,0:T(8,128)(2,1)S(1)}, bf16[6,3,96,128]{3,2,1,0:T(8,128)(2,1)}, u32[]{:S(2)}) copy-start(bf16[6,3,96,128]{3,2,1,0:T(8,128)(2,1)} %get-tuple-element.183) | copy-start | bytes 1327108
  166.4 9.9 %collective-permute-start.34 = (f32[19,768]{1,0:T(8,128)S(1)}, f32[19,768]{1,0:T(8,128)S(1)}, u32[]{:S(2)}, u32[]{:S(2)}) collective-permute-start(f32[19,768]{1,0:T(8,128)S(1)} %pad_maximum_fusion.2), channel_id=1, source_target_pairs={{0,2},{1,3},{2,0},{3,1},{4,6},{5,7},{6,4},{7,5},{8,10},{9,11},{10,... | collective-permute-start | bytes 175112 | tf_op jit(solution)/shard_map/ppermute | solution.py:846
  167.7 20.3 %collective-permute-start.38 = (bf16[6,3,96,128]{3,2,1,0:T(8,128)(2,1)}, bf16[6,3,96,128]{3,2,1,0:T(8,128)(2,1)S(1)}, u32[]{:S(2)}, u32[]{:S(2)}) collective-permute-start(bf16[6,3,96,128]{3,2,1,0:T(8,128)(2,1)} %get-tuple-element.185), channel_id=1, source_target_pairs={{0,4},{4,0},{8,12},{12,8},{16,20},{20,16},{24,28},{28,24},{1,5},{5... | collective-permute-start | bytes 1327112 | tf_op jit(solution)/shard_map/ppermute | solution.py:846
  176.3 12.3 %collective-permute-start.40 = (bf16[6,3,96,128]{3,2,1,0:T(8,128)(2,1)}, bf16[6,3,96,128]{3,2,1,0:T(8,128)(2,1)S(1)}, u32[]{:S(2)}, u32[]{:S(2)}) collective-permute-start(bf16[6,3,96,128]{3,2,1,0:T(8,128)(2,1)} %get-tuple-element.188), channel_id=1, source_target_pairs={{0,8},{4,12},{8,0},{12,4},{16,24},{20,28},{24,16},{28,20},{1,9},{5... | collective-permute-start | bytes 1327112 | tf_op jit(solution)/shard_map/ppermute | solution.py:851
  180.0 18.9 %copy-start.31 = (bf16[6,3,96,128]{3,2,1,0:T(8,128)(2,1)S(1)}, bf16[6,3,96,128]{3,2,1,0:T(8,128)(2,1)}, u32[]{:S(2)}) copy-start(bf16[6,3,96,128]{3,2,1,0:T(8,128)(2,1)} %get-tuple-element.171) | copy-start | bytes 1327108
  180.1 13.2 %collective-permute-start.39 = (bf16[6,3,96,128]{3,2,1,0:T(8,128)(2,1)S(1)}, bf16[6,3,96,128]{3,2,1,0:T(8,128)(2,1)S(1)}, u32[]{:S(2)}, u32[]{:S(2)}) collective-permute-start(bf16[6,3,96,128]{3,2,1,0:T(8,128)(2,1)S(1)} %add_convert_fusion.6), channel_id=1, source_target_pairs={{0,2},{1,3},{2,0},{3,1},{4,6},{5,7},{6,4},{7,5},{8,10},{9,11},{10,... | collective-permute-start | bytes 1327112 | tf_op jit(solution)/shard_map/ppermute | solution.py:846
  180.9 25.0 %collective-permute-start.37 = (bf16[6,3,96,128]{3,2,1,0:T(8,128)(2,1)S(1)}, bf16[6,3,96,128]{3,2,1,0:T(8,128)(2,1)S(1)}, u32[]{:S(2)}, u32[]{:S(2)}) collective-permute-start(bf16[6,3,96,128]{3,2,1,0:T(8,128)(2,1)S(1)} %copy-done.56), channel_id=1, source_target_pairs={{0,2},{1,3},{2,0},{3,1},{4,6},{5,7},{6,4},{7,5},{8,10},{9,11},{10,... | collective-permute-start | bytes 1327112 | tf_op jit(solution)/shard_map/ppermute | solution.py:846
  182.1 4.4 %collective-permute-start.41 = (f32[19,768]{1,0:T(8,128)S(1)}, f32[19,768]{1,0:T(8,128)S(1)}, u32[]{:S(2)}, u32[]{:S(2)}) collective-permute-start(f32[19,768]{1,0:T(8,128)S(1)} %add.134), channel_id=1, source_target_pairs={{0,4},{4,0},{8,12},{12,8},{16,20},{20,16},{24,28},{28,24},{1,5},{5... | collective-permute-start | bytes 175112 | tf_op jit(solution)/shard_map/ppermute | solution.py:846
  183.8 22.2 %copy-start.36 = (bf16[6,3,96,128]{3,2,1,0:T(8,128)(2,1)S(1)}, bf16[6,3,96,128]{3,2,1,0:T(8,128)(2,1)}, u32[]{:S(2)}) copy-start(bf16[6,3,96,128]{3,2,1,0:T(8,128)(2,1)} %get-tuple-element.180) | copy-start | bytes 1327108
  186.5 19.5 %collective-permute-start.36 = (bf16[6,3,96,128]{3,2,1,0:T(8,128)(2,1)S(1)}, bf16[6,3,96,128]{3,2,1,0:T(8,128)(2,1)S(1)}, u32[]{:S(2)}, u32[]{:S(2)}) collective-permute-start(bf16[6,3,96,128]{3,2,1,0:T(8,128)(2,1)S(1)} %add_convert_fusion.7), channel_id=1, source_target_pairs={{0,4},{4,0},{8,12},{12,8},{16,20},{20,16},{24,28},{28,24},{1,5},{5... | collective-permute-start | bytes 1327112 | tf_op jit(solution)/shard_map/ppermute | solution.py:846
  193.4 12.6 %collective-permute-start.42 = (bf16[6,3,96,128]{3,2,1,0:T(8,128)(2,1)S(1)}, bf16[6,3,96,128]{3,2,1,0:T(8,128)(2,1)S(1)}, u32[]{:S(2)}, u32[]{:S(2)}) collective-permute-start(bf16[6,3,96,128]{3,2,1,0:T(8,128)(2,1)S(1)} %add_convert_fusion.5), channel_id=1, source_target_pairs={{0,8},{4,12},{24,16},{28,20},{1,9},{5,13},{25,17},{29,21},{2,10},{... | collective-permute-start | bytes 1327112 | tf_op jit(solution)/shard_map/ppermute | solution.py:851
  194.7 25.3 %collective-permute-start.29 = (bf16[6,3,96,128]{3,2,1,0:T(8,128)(2,1)S(1)}, bf16[6,3,96,128]{3,2,1,0:T(8,128)(2,1)S(1)}, u32[]{:S(2)}, u32[]{:S(2)}) collective-permute-start(bf16[6,3,96,128]{3,2,1,0:T(8,128)(2,1)S(1)} %copy-done.55), channel_id=1, source_target_pairs={{0,4},{4,0},{8,12},{12,8},{16,20},{20,16},{24,28},{28,24},{1,5},{5... | collective-permute-start | bytes 1327112 | tf_op jit(solution)/shard_map/ppermute | solution.py:846
  196.3 8.9 %collective-permute-start.43 = (f32[19,768]{1,0:T(8,128)S(1)}, f32[19,768]{1,0:T(8,128)S(1)}, u32[]{:S(2)}, u32[]{:S(2)}) collective-permute-start(f32[19,768]{1,0:T(8,128)S(1)} %add.138), channel_id=1, source_target_pairs={{0,8},{4,12},{8,0},{12,4},{16,24},{20,28},{24,16},{28,20},{1,9},{5... | collective-permute-start | bytes 175112 | tf_op jit(solution)/shard_map/ppermute | solution.py:846
  205.1 14.9 %collective-permute-start.35 = (bf16[6,3,96,128]{3,2,1,0:T(8,128)(2,1)S(1)}, bf16[6,3,96,128]{3,2,1,0:T(8,128)(2,1)S(1)}, u32[]{:S(2)}, u32[]{:S(2)}) collective-permute-start(bf16[6,3,96,128]{3,2,1,0:T(8,128)(2,1)S(1)} %add_convert_fusion.8), channel_id=1, source_target_pairs={{0,2},{1,3},{2,0},{3,1},{4,6},{5,7},{6,4},{7,5},{8,10},{9,11},{10,... | collective-permute-start | bytes 1327112 | tf_op jit(solution)/shard_map/ppermute | solution.py:846
  206.2 14.8 %copy-start.27 = (bf16[6,3,96,128]{3,2,1,0:T(8,128)(2,1)S(1)}, bf16[6,3,96,128]{3,2,1,0:T(8,128)(2,1)}, u32[]{:S(2)}) copy-start(bf16[6,3,96,128]{3,2,1,0:T(8,128)(2,1)} %get-tuple-element.200) | copy-start | bytes 1327108
  206.3 13.8 %collective-permute-start.45 = (bf16[6,3,96,128]{3,2,1,0:T(8,128)(2,1)S(1)}, bf16[6,3,96,128]{3,2,1,0:T(8,128)(2,1)S(1)}, u32[]{:S(2)}, u32[]{:S(2)}) collective-permute-start(bf16[6,3,96,128]{3,2,1,0:T(8,128)(2,1)S(1)} %add_convert_fusion.4), channel_id=1, source_target_pairs={{0,8},{4,12},{24,16},{28,20},{1,9},{5,13},{25,17},{29,21},{2,10},{... | collective-permute-start | bytes 1327112 | tf_op jit(solution)/shard_map/ppermute | solution.py:851
  207.7 12.4 %collective-permute-start.44 = (bf16[6,3,96,128]{3,2,1,0:T(8,128)(2,1)S(1)}, bf16[6,3,96,128]{3,2,1,0:T(8,128)(2,1)S(1)}, u32[]{:S(2)}, u32[]{:S(2)}) collective-permute-start(bf16[6,3,96,128]{3,2,1,0:T(8,128)(2,1)S(1)} %add_convert_fusion.4), channel_id=1, source_target_pairs={{8,16},{12,20},{16,8},{20,12},{9,17},{13,21},{17,9},{21,13},{10,18... | collective-permute-start | bytes 1327112 | tf_op jit(solution)/shard_map/ppermute | solution.py:851
  212.2 6.6 %collective-permute-start.46 = (f32[19,768]{1,0:T(8,128)S(1)}, f32[19,768]{1,0:T(8,128)S(1)}, u32[]{:S(2)}, u32[]{:S(2)}) collective-permute-start(f32[19,768]{1,0:T(8,128)S(1)} %add.141), channel_id=1, source_target_pairs={{0,16},{4,20},{8,24},{12,28},{16,0},{20,4},{24,8},{28,12},{1,17},{... | collective-permute-start | bytes 175112 | tf_op jit(solution)/shard_map/ppermute | solution.py:846
  218.8 10.8 %collective-permute-start.48 = (bf16[6,3,96,128]{3,2,1,0:T(8,128)(2,1)}, bf16[6,3,96,128]{3,2,1,0:T(8,128)(2,1)}, u32[]{:S(2)}, u32[]{:S(2)}) collective-permute-start(bf16[6,3,96,128]{3,2,1,0:T(8,128)(2,1)} %add_convert_fusion.2), channel_id=1, source_target_pairs={{0,2},{1,3},{2,0},{3,1},{4,6},{5,7},{6,4},{7,5},{8,10},{9,11},{10,... | collective-permute-start | bytes 1327112 | tf_op jit(solution)/shard_map/ppermute | solution.py:846
  221.1 15.6 %copy-start.50 = (f32[16,768]{1,0:T(8,128)S(1)}, f32[16,768]{1,0:T(8,128)}, u32[]{:S(2)}) copy-start(f32[16,768]{1,0:T(8,128)} %param.34) | copy-start | bytes 147460
  221.1 15.6 %copy-start.51 = (f32[16,768]{1,0:T(8,128)S(1)}, f32[16,768]{1,0:T(8,128)}, u32[]{:S(2)}) copy-start(f32[16,768]{1,0:T(8,128)} %param.35) | copy-start | bytes 147460
  221.3 8.9 %collective-permute-start.49 = (bf16[6,3,96,128]{3,2,1,0:T(8,128)(2,1)S(1)}, bf16[6,3,96,128]{3,2,1,0:T(8,128)(2,1)S(1)}, u32[]{:S(2)}, u32[]{:S(2)}) collective-permute-start(bf16[6,3,96,128]{3,2,1,0:T(8,128)(2,1)S(1)} %add_convert_fusion.1), channel_id=1, source_target_pairs={{0,8},{4,12},{8,0},{12,4},{16,24},{20,28},{24,16},{28,20},{1,9},{5... | collective-permute-start | bytes 1327112 | tf_op jit(solution)/shard_map/ppermute | solution.py:851
  224.0 8.4 %collective-permute-start.47 = (bf16[6,3,96,128]{3,2,1,0:T(8,128)(2,1)S(1)}, bf16[6,3,96,128]{3,2,1,0:T(8,128)(2,1)S(1)}, u32[]{:S(2)}, u32[]{:S(2)}) collective-permute-start(bf16[6,3,96,128]{3,2,1,0:T(8,128)(2,1)S(1)} %add_convert_fusion.3), channel_id=1, source_target_pairs={{0,4},{4,0},{8,12},{12,8},{16,20},{20,16},{24,28},{28,24},{1,5},{5... | collective-permute-start | bytes 1327112 | tf_op jit(solution)/shard_map/ppermute | solution.py:846
  225.5 10.2 %collective-permute-start.50 = (bf16[6,3,96,128]{3,2,1,0:T(8,128)(2,1)S(1)}, bf16[6,3,96,128]{3,2,1,0:T(8,128)(2,1)S(1)}, u32[]{:S(2)}, u32[]{:S(2)}) collective-permute-start(bf16[6,3,96,128]{3,2,1,0:T(8,128)(2,1)S(1)} %copy-done.35), channel_id=1, source_target_pairs={{8,16},{12,20},{16,8},{20,12},{9,17},{13,21},{17,9},{21,13},{10,18... | collective-permute-start | bytes 1327112 | tf_op jit(solution)/shard_map/ppermute | solution.py:851
  235.7 11.3 %collective-permute-start.51 = (bf16[133,768]{1,0:T(8,128)(2,1)S(1)}, bf16[133,768]{1,0:T(8,128)(2,1)S(1)}, u32[]{:S(2)}, u32[]{:S(2)}) collective-permute-start(bf16[133,768]{1,0:T(8,128)(2,1)S(1)} %get-tuple-element.253), channel_id=1, source_target_pairs={{0,2},{1,3},{2,0},{3,1},{4,6},{5,7},{6,4},{7,5},{8,10},{9,11},{10,... | collective-permute-start | bytes 612872 | tf_op jit(solution)/shard_map/ppermute | solution.py:846
  (45 other events, 252.4 us)

commit v4 on v3

--- a/solution.py
+++ b/solution.py
@@ -137,9 +137,9 @@
         pltpu.make_async_copy(whole, whole, sems.at[s]).wait()
 
         def fix(g, carry, s=s):
-            al[s, g, 3, :, 0:96] = jnp.concatenate(
-                [al[s, g, k, :, 96:128] for k in range(TILES)], axis=-1
-            )
+            rolled = [pltpu.roll(al[s, g, k], 32 + 32 * k, 1) for k in range(TILES)]
+            lane = lax.broadcasted_iota(jnp.int32, rolled[0].shape, 1)
+            al[s, g, 3] = jnp.where(lane < 32, rolled[0], jnp.where(lane < 64, rolled[1], rolled[2]))
             return carry
 
         lax.fori_loop(0, groups, fix, 0, unroll=16)
@@ -226,7 +226,7 @@
         product(act_ref.at[s], d2_ref, out_ref.at[s])
 
 
-def up_grads_body(h_ref, dpre_ref, later_ref, out_ref):
+def up_grads_body(h_ref, dpre_ref, out_ref):
     for s in range(2):
         product(h_ref, dpre_ref.at[s], out_ref.at[s])
 
@@ -243,16 +243,22 @@
     )(act, d_two)
 
 
-def up_grads(h_in, d_pre, later):
+def up_grads(h_in, d_pre):
     return pl.pallas_call(
         up_grads_body,
         out_shape=sds((2, 768, 768), BF),
-        in_specs=[VMEM_SPEC] * 2 + [ANY_SPEC],
+        in_specs=[VMEM_SPEC] * 2,
         out_specs=VMEM_SPEC,
         compiler_params=params(),
         cost_estimate=cost(1.4, 8),
         name="up_grads",
-    )(h_in, d_pre, later)
+    )(h_in, d_pre)
+
+
+def tile_of(vals, j):
+    if j < 3:
+        return vals[:, 96 * j : 96 * j + 128]
+    return pltpu.roll(vals[:, 256:384], 96, 1)
 
 
 def pack_body(places, pos_ref, me_ref, *refs):
@@ -267,7 +273,7 @@
 
     def put(s, b, blk):
         p = pos_ref[b]
-        al[s, p // GROUP, p % GROUP, :, 0:96] = blk
+        al[s, p // GROUP, p % GROUP] = blk
 
     def strip(i, carry, ref, first):
         rows = pl.ds(pl.multiple_of(i * 96, 96), 96)
@@ -275,7 +281,7 @@
             for half in range(2):
                 vals = ref[s, rows, half * 384 : half * 384 + 384]
                 for j in range(4):
-                    put(s, first + i * 8 + half * 4 + j, vals[:, 96 * j : 96 * j + 96])
+                    put(s, first + i * 8 + half * 4 + j, tile_of(vals, j))
         return carry
 
     def strip_qkv(i, carry):
@@ -283,7 +289,7 @@
         for part in range(3):
             vals = gq[rows, part * 384 : part * 384 + 384]
             for j in range(4):
-                put(j // 2, i * 6 + part * 2 + j % 2, vals[:, 96 * j : 96 * j + 96])
+                put(j // 2, i * 6 + part * 2 + j % 2, tile_of(vals, j))
         return carry
 
     loads[0].wait()
@@ -295,7 +301,7 @@
         for half in range(2):
             vals = go[i * 96 : i * 96 + 96, half * 384 : half * 384 + 384]
             for j in range(4):
-                put(i // 2, 48 + (i % 2) * 8 + half * 4 + j, vals[:, 96 * j : 96 * j + 96])
+                put(i // 2, 48 + (i % 2) * 8 + half * 4 + j, tile_of(vals, j))
     loads[3].wait()
     lax.fori_loop(0, 8, strip_qkv, 0, unroll=UNROLL)
 
@@ -305,8 +311,9 @@
 
         def fix(g, carry, s=s):
             last = al[s, g, 3]
+            low = lax.broadcasted_iota(jnp.int32, last.shape, 1) < 96
             for k in range(TILES):
-                al[s, g, k, :, 96:128] = last[:, 32 * k : 32 * k + 32]
+                al[s, g, k] = jnp.where(low, al[s, g, k], pltpu.roll(last, 96 - 32 * k, 1))
             return carry
 
         lax.fori_loop(0, groups, fix, 0, unroll=16)
@@ -589,7 +596,7 @@
     )(mine, other, normed, slope, *cots, shared, w1, w2)
 
 
-def attend_back_body(mine_ref, other_ref, d2_ref, n_ref, r_ref, sh_ref, wo_ref, wqkv_ref, x_ref, ctx_ref, later_ref, p_ref, q_ref, k_ref, v_ref, d1_ref, gq_ref, go_ref, part_ref, sums_ref, bsum_ref, d1b_ref, dproj_ref, dctx):
+def attend_back_body(mine_ref, other_ref, d2_ref, n_ref, r_ref, sh_ref, wo_ref, wqkv_ref, x_ref, ctx_ref, later_ref, p_ref, q_ref, k_ref, v_ref, d1_ref, gq_ref, go_ref, part_ref, send_ref, sums_ref, bsum_ref, d1b_ref, dproj_ref, dctx):
     h = pl.program_id(0)
     pairs = pl.num_programs(0)
     own = d1_ref.shape[0]
@@ -629,7 +636,9 @@
 
     @pl.when(h == pairs - 1)
     def _():
-        part_ref[...] = dot_back(dproj_ref[...], wqkv_ref[...]).astype(BF)
+        share = dot_back(dproj_ref[...], wqkv_ref[...]).astype(BF)
+        part_ref[...] = share[:own]
+        send_ref[...] = share[own:]
         product(ctx_ref, d1b_ref, go_ref, 128)
         product(x_ref, dproj_ref, gq_ref)
 
@@ -644,7 +653,8 @@
             sds((rows // 2, 768), F32),
             sds((768, 1152), BF),
             sds((384, 768), BF),
-            sds((rows, 768), BF),
+            sds((rows // 2, 768), BF),
+            sds((rows // 2, 768), BF),
             sds((8, 768), F32),
             sds((8, 384), F32),
         ),
@@ -669,7 +679,8 @@
             all_steps((rows // 2, 768)),
             all_steps((768, 1152)),
             all_steps((384, 768)),
-            all_steps((rows, 768)),
+            all_steps((rows // 2, 768)),
+            all_steps((rows // 2, 768)),
             all_steps((8, 768)),
             pl.BlockSpec((8, 128), lambda h: (0, h)),
         ),
@@ -687,8 +698,7 @@
 
 
 def finish_body(flags_ref, part_ref, other_ref, d1_ref, gin_ref, mem_ref):
-    own = d1_ref.shape[0]
-    d_zero = part_ref[:own, :].astype(F32) + other_ref[...].astype(F32) + d1_ref[...]
+    d_zero = part_ref[...].astype(F32) + other_ref[...].astype(F32) + d1_ref[...]
     gin_ref[...] = d_zero.astype(BF)
     mem_ref[...] = jnp.zeros_like(mem_ref)
     for k in range(2):
@@ -721,9 +731,11 @@
     if n_terms == 1:
         grads = [terms[0][b] for b in range(blocks)]
     else:
-        tiles = [sum(ref[0, k].astype(F32) for ref in terms) for k in range(TILES)]
-        grads = [tile[:, :96] for tile in tiles]
-        grads.append(jnp.concatenate([tile[:, 96:] for tile in tiles], axis=-1))
+        grads = []
+        for g in range(blocks // GROUP):
+            tiles = [sum(ref[g, k].astype(F32) for ref in terms) for k in range(TILES)]
+            grads += [tile[:, :96] for tile in tiles]
+            grads.append(jnp.concatenate([tile[:, 96:] for tile in tiles], axis=-1))
     every = range(blocks)
     gb = [g.astype(BF) for g in grads]
     lb, rb = [l_ref[b].astype(BF) for b in every], [r_ref[b].astype(BF) for b in every]
@@ -754,9 +766,10 @@
 
 def soap(terms, master, first, second, left, right, left_rot, right_rot):
     count = master.shape[0]
-    step = GROUP if len(terms) > 1 else 1
+    many = next(n for n in (3, 2, 1) if terms[0].shape[0] % n == 0)
+    step = many * GROUP if len(terms) > 1 else 1
     spec = pl.BlockSpec((step, 96, 96), lambda i: (i, 0, 0))
-    packed = pl.BlockSpec((1, TILES, 96, 128), lambda i: (i, 0, 0, 0))
+    packed = pl.BlockSpec((many, TILES, 96, 128), lambda i: (i, 0, 0, 0))
     full = sds(master.shape, F32)
     return pl.pallas_call(
         functools.partial(soap_body, len(terms)),
@@ -923,12 +936,10 @@
         ffn, core(ffn), normed, slope, cots, shared, w_up, w_down
     )
     d_hidden_other = core(d_hidden)
-    g_down = down_grads(act, d_two_b)
-    d_one, g_qkv, g_out, d_in, sums_one, head_sums = attend_back(
+    g_down, g_up = down_grads(act, d_two_b), up_grads(h_in, d_pre)
+    d_one, g_qkv, g_out, d_in, d_in_send, sums_one, head_sums = attend_back(
         d_hidden, d_hidden_other, d_two, normed, inverse, shared, w_out, w_qkv, x_in, context, g_down, probs, proj
     )
-    d_in_send = d_in[2 * RP :]
-
     def to_owner(arr):
         mine, other = arr[:quarter], yswap(arr[RP : RP + quarter])
         both = jnp.stack([mine, other])
@@ -937,7 +948,6 @@
     layer_out = to_owner(rows_out)
     me = after(me, layer_out)
     d_in_other = core(d_in_send)
-    g_up = up_grads(h_in, d_pre, d_in)
     grad_rows, memory_grad = finish(flags, d_in, d_in_other, d_one)
     grads = (g_down, g_up, g_out, g_qkv, memory_grad)
     vec = jnp.concatenate([sums_one[:3], sums_two[:3], memory_grad[:MEM]], axis=0)

time: 253 us -> 245 us (0.968)
  Pallas kernels: 79.8 us -> 75.3 us
  local copies, waits for them, and re-layouts: 19.2 us -> 16.4 us
    pallas_call x1, Pallas kernels: 9.67 us -> 6.88 us  [soap(): pl.pallas_call(functools.partial(soap_body, len(terms)), grid=(count // s...]
    unnamed x120 -> x106, local copies, waits for them, and re-layouts: 14.9 us -> 12.9 us
  transfers between devices with their start and end apart: 52 -> 52, of which waited for: 25 -> 24; matrix products, arithmetic and copies ran while one was open for 5% -> 6% of each run, Pallas kernels for 22% -> 21%
where the time goes in v4:
time: 245 us; the launch traced here: 241 us
  Pallas kernels  75.3 us (31%)
  waiting for transfers between devices  72.7 us (30%)
  starting transfers between devices  65.1 us (27%)
  local copies, waits for them, and re-layouts  16.4 us (7%)
  other arithmetic  8.47 us (3%)
  between operations  2.69 us (1%)
    ppermute x38, waiting for transfers between devices, swap(): return lambda v: lax.ppermute(v, axis, xor_pairs(size, step))  52.8 us
    ppermute x38, starting transfers between devices, swap(): return lambda v: lax.ppermute(v, axis, xor_pairs(size, step))  33.6 us
    ppermute x14, starting transfers between devices, along_z(): return lambda v: lax.ppermute(v, 'dp', z_pairs(pairs))  31.5 us
    ppermute x14, waiting for transfers between devices, along_z(): return lambda v: lax.ppermute(v, 'dp', z_pairs(pairs))  19.8 us
    pallas_call x1, Pallas kernels, attend_back(): pl.pallas_call(attend_back_body, grid=(pairs,), out_shape=(sds((rows // 2...  14.2 us
    unnamed x106, local copies, waits for them, and re-layouts  12.9 us
    pallas_call x1, Pallas kernels, pack_grads(): pl.pallas_call(functools.partial(pack_body, places), out_shape=(sds((8, 1...  12.2 us
    pallas_call x1, Pallas kernels, build_weights(): pl.pallas_call(functools.partial(weights_body, len(pieces), places), out_...  10 us
  transfers between devices with their start and end apart: 52, of which 24 were waited for; matrix products, arithmetic and copies ran while one was open for 6% of the time, Pallas kernels for 21%

profile of v4, /device:TPU:8, one launch (start us, length us, event | category | flops | bytes accessed | tf_op | source)
XLA Modules:
  0.0 240.6 jit_solution(18153837773707507000)
XLA Ops:
  0.7 1.3 copy-done.3
  2.1 1.6 collective-permute-start.3
  3.7 1.5 collective-permute-start.2
  5.2 3.5 %collective-permute-start.1 = (bf16[6,3,96,128]{3,2,1,0:T(8,128)(2,1)S(1)}, bf16[6,3,96,128]{3,2,1,0:T(8,128)(2,1)}, u32[]{:S(2)}, u32[]{:S(2)}) collective-permute-start(bf16[6,3,96,128]{3,2,1,0:T(8,128)(2,1)S(1)} %pack_owned.1.refs_0_), channel_id=1, source_target_pairs={{8,16},{12,20},{16,8},{20,12},{9,17},{13,21},{17,9},{21,13},{10,18... | collective-permute-start | bytes 1327112 | tf_op jit(solution)/shard_map/ppermute | solution.py:864
  9.4 1.2 dynamic_slice.43
  11.6 1.7 constant_dynamic-slice_fusion.1
  15.5 3.1 %collective-permute-done.1 = bf16[6,3,96,128]{3,2,1,0:T(8,128)(2,1)} collective-permute-done((bf16[6,3,96,128]{3,2,1,0:T(8,128)(2,1)S(1)}, bf16[6,3,96,128]{3,2,1,0:T(8,128)(2,1)}, u32[]{:S(2)}, u32[]{:S(2)}) %collective-permute-start.1) | collective-permute-done | bytes 442400 | tf_op jit(solution)/shard_map/ppermute | solution.py:864
  18.6 1.4 collective-permute-done.refs_4_
  19.9 2.3 collective-permute-start.6
  23.4 1.3 collective-permute-start.7
  24.8 7.9 %collective-permute-done.5.refs_3_ = bf16[6,3,96,128]{3,2,1,0:T(8,128)(2,1)S(1)} collective-permute-done((bf16[6,3,96,128]{3,2,1,0:T(8,128)(2,1)}, bf16[6,3,96,128]{3,2,1,0:T(8,128)(2,1)S(1)}, u32[]{:S(2)}, u32[]{:S(2)}) %collective-permute-start.5) | collective-permute-done | bytes 442400 | tf_op jit(solution)/shard_map/ppermute | solution.py:859
  34.6 1.5 collective-permute-start.9
  36.1 4.3 %collective-permute-start.11 = (bf16[6,3,96,128]{3,2,1,0:T(8,128)(2,1)S(1)}, bf16[6,3,96,128]{3,2,1,0:T(8,128)(2,1)S(1)}, u32[]{:S(2)}, u32[]{:S(2)}) collective-permute-start(bf16[6,3,96,128]{3,2,1,0:T(8,128)(2,1)S(1)} %collective-permute-done.6), channel_id=1, source_target_pairs={{8,0},{12,4},{16,24},{20,28},{9,1},{13,5},{17,25},{21,29},{10,2},{... | collective-permute-start | bytes 1327112 | tf_op jit(solution)/shard_map/ppermute | solution.py:864
  40.5 2.0 collective-permute-done.10.refs_10_
  43.2 7.8 %collective-permute-done.11 = bf16[6,3,96,128]{3,2,1,0:T(8,128)(2,1)S(1)} collective-permute-done((bf16[6,3,96,128]{3,2,1,0:T(8,128)(2,1)S(1)}, bf16[6,3,96,128]{3,2,1,0:T(8,128)(2,1)S(1)}, u32[]{:S(2)}, u32[]{:S(2)}) %collective-permute-start.11) | collective-permute-done | bytes 442400 | tf_op jit(solution)/shard_map/ppermute | solution.py:864
  51.0 1.2 add.132.refs_12_
  53.3 2.5 %collective-permute-start.20 = (bf16[6,3,96,128]{3,2,1,0:T(8,128)(2,1)S(1)}, bf16[6,3,96,128]{3,2,1,0:T(8,128)(2,1)S(1)}, u32[]{:S(2)}, u32[]{:S(2)}) collective-permute-start(bf16[6,3,96,128]{3,2,1,0:T(8,128)(2,1)S(1)} %collective-permute-done.5.refs_3_), channel_id=1, source_target_pairs={{0,8},{4,12},{8,0},{12,4},{16,24},{20,28},{24,16},{28,20},{1,9},{5... | collective-permute-start | bytes 1327112 | tf_op jit(solution)/shard_map/ppermute | solution.py:864
  55.7 1.5 collective-permute-start.19
  57.3 3.0 %collective-permute-done.14.refs_6_ = bf16[6,3,96,128]{3,2,1,0:T(8,128)(2,1)S(1)} collective-permute-done((bf16[6,3,96,128]{3,2,1,0:T(8,128)(2,1)S(1)}, bf16[6,3,96,128]{3,2,1,0:T(8,128)(2,1)S(1)}, u32[]{:S(2)}, u32[]{:S(2)}) %collective-permute-start.14) | collective-permute-done | bytes 442400 | tf_op jit(solution)/shard_map/ppermute | solution.py:864
  60.2 1.5 collective-permute-done.13.refs_14_
  61.7 1.1 collective-permute-done.12.refs_13_
  64.2 4.9 %collective-permute-done.15.xb = bf16[133,768]{1,0:T(8,128)(2,1)S(1)} collective-permute-done((bf16[133,768]{1,0:T(8,128)(2,1)S(1)}, bf16[133,768]{1,0:T(8,128)(2,1)S(1)}, u32[]{:S(2)}, u32[]{:S(2)}) %collective-permute-start.15) | collective-permute-done | bytes 204320 | tf_op jit(solution)/shard_map/ppermute | solution.py:859
  69.1 1.9 collective-permute-done.18.refs_15_
  72.9 10.0 %build_weights.1 = (bf16[768,1152]{1,0:T(8,128)(2,1)}, bf16[384,768]{1,0:T(8,128)(2,1)}, bf16[2,768,768]{2,1,0:T(8,128)(2,1)}, bf16[2,768,768]{2,1,0:T(8,128)(2,1)}) custom-call(s32[192]{0:T(256)} %pos_ref.3, s32[2]{0:T(128)} %get-tuple-element.154.me_ref, bf16[6,3,96,128]{3,2,1,0:T(8,128)(2,1)} %copy-done.10, ...), custom_call_target="tpu_custom_call" | custom-call | flops 100000000 | bytes 30000000 | tf_op jit(solution)/shard_map/build_weights/pallas_call | solution.py:190
  83.0 1.5 copy-done.7
  84.5 2.9 %project.1 = (bf16[576,1152]{1,0:T(8,128)(2,1)S(1)}, f32[576,768]{1,0:T(8,128)S(1)}, bf16[576,768]{1,0:T(8,128)(2,1)S(1)}) custom-call(s32[2]{0:T(128)S(1)} %get-tuple-element.122.flags_ref, bf16[133,768]{1,0:T(8,128)(2,1)S(1)} %bitcast.48, bf16[133,768]{1,0:T(8,128)(2,1)S(1)} %collective-permute-done.15.xb, ...), custom_call_target="tpu_custom_call" | custom-call | flops 1000000000 | bytes 5000000 | tf_op jit(solution)/shard_map/project/pallas_call | solution.py:387
  87.4 7.9 %attend.1 = (bf16[576,384]{1,0:T(8,128)(2,1)S(1)}, bf16[6,576,576]{2,1,0:T(8,128)(2,1)S(1)}, bf16[576,768]{1,0:T(8,128)(2,1)S(1)}) custom-call(s32[576,1]{1,0:T(8,128)S(1)} %copy.38.cq_ref, s32[1,576]{1,0:T(1,128)S(1)} %broadcast_in_dim.25.ck_ref, bf16[576,1152]{1,0:T(8,128)(2,1)S(1)} %get-tuple-element.144.q_ref.k_ref.v_ref, ...), custom_call_target="tpu_custom_call" | custom-call | flops 2500000000 | bytes 8000000 | tf_op jit(solution)/shard_map/attend/pallas_call | solution.py:453
  95.4 2.4 %collective-permute-done.22.other_ref = bf16[576,768]{1,0:T(8,128)(2,1)S(1)} collective-permute-done((bf16[576,768]{1,0:T(8,128)(2,1)S(1)}, bf16[576,768]{1,0:T(8,128)(2,1)S(1)}, u32[]{:S(2)}, u32[]{:S(2)}) %collective-permute-start.22) | collective-permute-done | bytes 884768 | tf_op jit(solution)/shard_map/ppermute | solution.py:859
  97.8 6.7 %feed.1 = (bf16[576,768]{1,0:T(8,128)(2,1)S(1)}, f32[576,768]{1,0:T(8,128)S(1)}, f32[576,1]{1,0:T(8,128)S(1)}, bf16[2,576,768]{2,1,0:T(8,128)(2,1)S(1)}, bf16[2,...) custom-call(bf16[576,768]{1,0:T(8,128)(2,1)S(1)} %get-tuple-element.146.mine_ref, ...), custom_call_target="tpu_custom_call" | custom-call | flops 2800000000 | bytes 16000000 | tf_op jit(solution)/shard_map/feed/pallas_call | solution.py:514
  105.3 2.0 collective-permute-done.24.cc
  107.6 7.3 %feed_back.1 = (bf16[288,768]{1,0:T(8,128)(2,1)S(1)}, f32[576,768]{1,0:T(8,128)S(1)}, bf16[576,768]{1,0:T(8,128)(2,1)S(1)}, bf16[2,576,768]{2,1,0:T(8,128)(2,1)S...) custom-call(bf16[576,768]{1,0:T(8,128)(2,1)S(1)} %get-tuple-element.150.mine_ref, ...), custom_call_target="tpu_custom_call" | custom-call | flops 2800000000 | bytes 16000000 | tf_op jit(solution)/shard_map/feed_back/pallas_call | solution.py:573
  115.1 1.5 collective-permute-start.26
  116.7 3.1 %down_grads.1.later_ref.refs_0_ = bf16[2,768,768]{2,1,0:T(8,128)(2,1)S(1)} custom-call(bf16[2,576,768]{2,1,0:T(8,128)(2,1)S(1)} %get-tuple-element.155.act_ref, bf16[576,768]{1,0:T(8,128)(2,1)S(1)} %get-tuple-element.156.d2_ref), custom_call_target="tpu_custom_call" | custom-call | flops 1400000000 | bytes 8000000 | tf_op jit(solution)/shard_map/down_grads/pallas_call | solution.py:235
  119.9 14.2 %attend_back.1 = (f32[288,768]{1,0:T(8,128)S(1)}, bf16[768,1152]{1,0:T(8,128)(2,1)S(1)}, bf16[384,768]{1,0:T(8,128)(2,1)S(1)}, bf16[288,768]{1,0:T(8,128)(2,1)S(...) custom-call(bf16[576,768]{1,0:T(8,128)(2,1)S(1)} %get-tuple-element.159.mine_ref, ...), custom_call_target="tpu_custom_call" | custom-call | flops 2038431744 | bytes 10485760 | tf_op jit(solution)/shard_map/attend_back/pallas_call | solution.py:649
  134.1 1.2 copy-done.9
  137.2 3.1 %up_grads.1.refs_1_ = bf16[2,768,768]{2,1,0:T(8,128)(2,1)S(1)} custom-call(bf16[576,768]{1,0:T(8,128)(2,1)S(1)} %get-tuple-element.157.h_ref, bf16[2,576,768]{2,1,0:T(8,128)(2,1)S(1)} %get-tuple-element.158.dpre_ref), custom_call_target="tpu_custom_call" | custom-call | flops 1400000000 | bytes 8000000 | tf_op jit(solution)/shard_map/up_grads/pallas_call | solution.py:247
  140.3 1.4 copy-done.6
  144.2 12.2 %pack_grads.1 = (f32[8,128]{1,0:T(8,128)}, bf16[6,3,96,128]{3,2,1,0:T(8,128)(2,1)}, bf16[6,3,96,128]{3,2,1,0:T(8,128)(2,1)}, bf16[6,3,96,128]{3,2,1,0:T(8,128)(2...) custom-call(s32[192]{0:T(256)} %pos_ref.3, ...), custom_call_target="tpu_custom_call" | custom-call | flops 100000000 | bytes 30000000 | tf_op jit(solution)/shard_map/pack_grads/pallas_call | solution.py:340
  157.6 2.8 %collective-permute-start.32 = (bf16[6,3,96,128]{3,2,1,0:T(8,128)(2,1)}, bf16[6,3,96,128]{3,2,1,0:T(8,128)(2,1)S(1)}, u32[]{:S(2)}, u32[]{:S(2)}) collective-permute-start(bf16[6,3,96,128]{3,2,1,0:T(8,128)(2,1)} %get-tuple-element.176), channel_id=1, source_target_pairs={{0,8},{4,12},{8,0},{12,4},{16,24},{20,28},{24,16},{28,20},{1,9},{5... | collective-permute-start | bytes 1327112 | tf_op jit(solution)/shard_map/ppermute | solution.py:864
  161.3 1.2 collective-permute-start.34
  162.6 1.5 collective-permute-start.38
  164.0 7.1 %collective-permute-done.34 = f32[19,768]{1,0:T(8,128)S(1)} collective-permute-done((f32[19,768]{1,0:T(8,128)S(1)}, f32[19,768]{1,0:T(8,128)S(1)}, u32[]{:S(2)}, u32[]{:S(2)}) %collective-permute-start.34) | collective-permute-done | bytes 58400 | tf_op jit(solution)/shard_map/ppermute | solution.py:859
  171.1 2.5 %collective-permute-start.40 = (bf16[6,3,96,128]{3,2,1,0:T(8,128)(2,1)}, bf16[6,3,96,128]{3,2,1,0:T(8,128)(2,1)S(1)}, u32[]{:S(2)}, u32[]{:S(2)}) collective-permute-start(bf16[6,3,96,128]{3,2,1,0:T(8,128)(2,1)} %get-tuple-element.190), channel_id=1, source_target_pairs={{0,8},{4,12},{8,0},{12,4},{16,24},{20,28},{24,16},{28,20},{1,9},{5... | collective-permute-start | bytes 1327112 | tf_op jit(solution)/shard_map/ppermute | solution.py:864
  173.6 1.2 add_convert_fusion.6
  175.7 1.2 collective-permute-start.37
  176.9 1.5 collective-permute-start.41
  178.5 2.7 %collective-permute-done.41 = f32[19,768]{1,0:T(8,128)S(1)} collective-permute-done((f32[19,768]{1,0:T(8,128)S(1)}, f32[19,768]{1,0:T(8,128)S(1)}, u32[]{:S(2)}, u32[]{:S(2)}) %collective-permute-start.41) | collective-permute-done | bytes 58400 | tf_op jit(solution)/shard_map/ppermute | solution.py:859
  181.3 1.5 collective-permute-start.36
  183.4 4.5 %collective-permute-done.39 = bf16[6,3,96,128]{3,2,1,0:T(8,128)(2,1)S(1)} collective-permute-done((bf16[6,3,96,128]{3,2,1,0:T(8,128)(2,1)S(1)}, bf16[6,3,96,128]{3,2,1,0:T(8,128)(2,1)S(1)}, u32[]{:S(2)}, u32[]{:S(2)}) %collective-permute-start.39) | collective-permute-done | bytes 442400 | tf_op jit(solution)/shard_map/ppermute | solution.py:859
  188.2 1.3 collective-permute-start.42
  189.5 1.5 collective-permute-start.29
  191.0 2.7 %collective-permute-start.43 = (f32[19,768]{1,0:T(8,128)S(1)}, f32[19,768]{1,0:T(8,128)S(1)}, u32[]{:S(2)}, u32[]{:S(2)}) collective-permute-start(f32[19,768]{1,0:T(8,128)S(1)} %add.138), channel_id=1, source_target_pairs={{0,8},{4,12},{8,0},{12,4},{16,24},{20,28},{24,16},{28,20},{1,9},{5... | collective-permute-start | bytes 175112 | tf_op jit(solution)/shard_map/ppermute | solution.py:859
  193.8 6.1 %collective-permute-done.43 = f32[19,768]{1,0:T(8,128)S(1)} collective-permute-done((f32[19,768]{1,0:T(8,128)S(1)}, f32[19,768]{1,0:T(8,128)S(1)}, u32[]{:S(2)}, u32[]{:S(2)}) %collective-permute-start.43) | collective-permute-done | bytes 58400 | tf_op jit(solution)/shard_map/ppermute | solution.py:859
  201.0 1.4 collective-permute-start.45
  202.5 3.4 %collective-permute-start.44 = (bf16[6,3,96,128]{3,2,1,0:T(8,128)(2,1)S(1)}, bf16[6,3,96,128]{3,2,1,0:T(8,128)(2,1)S(1)}, u32[]{:S(2)}, u32[]{:S(2)}) collective-permute-start(bf16[6,3,96,128]{3,2,1,0:T(8,128)(2,1)S(1)} %add_convert_fusion.4), channel_id=1, source_target_pairs={{8,16},{12,20},{16,8},{20,12},{9,17},{13,21},{17,9},{21,13},{10,18... | collective-permute-start | bytes 1327112 | tf_op jit(solution)/shard_map/ppermute | solution.py:864
  205.9 1.1 copy.41
  208.8 4.8 %collective-permute-done.46 = f32[19,768]{1,0:T(8,128)S(1)} collective-permute-done((f32[19,768]{1,0:T(8,128)S(1)}, f32[19,768]{1,0:T(8,128)S(1)}, u32[]{:S(2)}, u32[]{:S(2)}) %collective-permute-start.46) | collective-permute-done | bytes 58400 | tf_op jit(solution)/shard_map/ppermute | solution.py:859
  213.6 1.2 collective-permute-start.48
  215.9 2.6 %collective-permute-start.49 = (bf16[6,3,96,128]{3,2,1,0:T(8,128)(2,1)S(1)}, bf16[6,3,96,128]{3,2,1,0:T(8,128)(2,1)S(1)}, u32[]{:S(2)}, u32[]{:S(2)}) collective-permute-start(bf16[6,3,96,128]{3,2,1,0:T(8,128)(2,1)S(1)} %add_convert_fusion.1), channel_id=1, source_target_pairs={{0,8},{4,12},{8,0},{12,4},{16,24},{20,28},{24,16},{28,20},{1,9},{5... | collective-permute-start | bytes 1327112 | tf_op jit(solution)/shard_map/ppermute | solution.py:864
  218.7 1.5 collective-permute-start.47
  220.2 3.4 %collective-permute-start.50 = (bf16[6,3,96,128]{3,2,1,0:T(8,128)(2,1)S(1)}, bf16[6,3,96,128]{3,2,1,0:T(8,128)(2,1)S(1)}, u32[]{:S(2)}, u32[]{:S(2)}) collective-permute-start(bf16[6,3,96,128]{3,2,1,0:T(8,128)(2,1)S(1)} %copy-done.27), channel_id=1, source_target_pairs={{8,16},{12,20},{16,8},{20,12},{9,17},{13,21},{17,9},{21,13},{10,18... | collective-permute-start | bytes 1327112 | tf_op jit(solution)/shard_map/ppermute | solution.py:864
  224.9 2.2 collective-permute-done.47.refs_1_
  227.1 3.4 %collective-permute-done.50.refs_4_ = bf16[6,3,96,128]{3,2,1,0:T(8,128)(2,1)S(1)} collective-permute-done((bf16[6,3,96,128]{3,2,1,0:T(8,128)(2,1)S(1)}, bf16[6,3,96,128]{3,2,1,0:T(8,128)(2,1)S(1)}, u32[]{:S(2)}, u32[]{:S(2)}) %collective-permute-start.50) | collective-permute-done | bytes 442400 | tf_op jit(solution)/shard_map/ppermute | solution.py:864
  232.0 6.9 %soap.1 = (f32[24,96,96]{2,1,0:T(8,128)}, bf16[24,96,96]{2,1,0:T(8,128)(2,1)}, f32[24,96,96]{2,1,0:T(8,128)}, f32[24,96,96]{2,1,0:T(8,128)}, f32[24,96,96]{2,1,0:T(8,128)}, /*index=5*/f32[24,96,96]{2,1,0:T(8,128)}) custom-call(bf16[6,3,96,128]{3,2,1,0:T(8,128)(2,1)} %get-tuple-element.208.refs_0_, bf16[6,3,96,128]{3,2,1,0:T(8,128)(2,1)} %copy-done.41, ...), custom_call_target="tpu_custom_call" | custom-call | flops 300000000 | bytes 24000000 | tf_op jit(solution)/shard_map/soap/pallas_call | solution.py:774
  (208 shorter events, 29.5 us)
Async XLA Ops:
  2.1 12.5 %collective-permute-start.3 = (bf16[6,3,96,128]{3,2,1,0:T(8,128)(2,1)S(1)}, bf16[6,3,96,128]{3,2,1,0:T(8,128)(2,1)S(1)}, u32[]{:S(2)}, u32[]{:S(2)}) collective-permute-start(bf16[6,3,96,128]{3,2,1,0:T(8,128)(2,1)S(1)} %pack_owned.1.refs_0_), channel_id=1, source_target_pairs={{0,2},{1,3},{2,0},{3,1},{4,6},{5,7},{6,4},{7,5},{8,10},{9,11},{10,... | collective-permute-start | bytes 1327112 | tf_op jit(solution)/shard_map/ppermute | solution.py:859
  3.7 11.7 %collective-permute-start.2 = (bf16[6,3,96,128]{3,2,1,0:T(8,128)(2,1)S(1)}, bf16[6,3,96,128]{3,2,1,0:T(8,128)(2,1)}, u32[]{:S(2)}, u32[]{:S(2)}) collective-permute-start(bf16[6,3,96,128]{3,2,1,0:T(8,128)(2,1)S(1)} %pack_owned.1.refs_0_), channel_id=1, source_target_pairs={{0,4},{4,0},{8,12},{12,8},{16,20},{20,16},{24,28},{28,24},{1,5},{5... | collective-permute-start | bytes 1327112 | tf_op jit(solution)/shard_map/ppermute | solution.py:859
  5.2 13.3 %collective-permute-start.1 = (bf16[6,3,96,128]{3,2,1,0:T(8,128)(2,1)S(1)}, bf16[6,3,96,128]{3,2,1,0:T(8,128)(2,1)}, u32[]{:S(2)}, u32[]{:S(2)}) collective-permute-start(bf16[6,3,96,128]{3,2,1,0:T(8,128)(2,1)S(1)} %pack_owned.1.refs_0_), channel_id=1, source_target_pairs={{8,16},{12,20},{16,8},{20,12},{9,17},{13,21},{17,9},{21,13},{10,18... | collective-permute-start | bytes 1327112 | tf_op jit(solution)/shard_map/ppermute | solution.py:864
  8.7 11.2 %collective-permute-start = (bf16[6,3,96,128]{3,2,1,0:T(8,128)(2,1)S(1)}, bf16[6,3,96,128]{3,2,1,0:T(8,128)(2,1)}, u32[]{:S(2)}, u32[]{:S(2)}) collective-permute-start(bf16[6,3,96,128]{3,2,1,0:T(8,128)(2,1)S(1)} %pack_owned.1.refs_0_), channel_id=1, source_target_pairs={{0,8},{4,12},{8,0},{12,4},{16,24},{20,28},{24,16},{28,20},{1,9},{5... | collective-permute-start | bytes 1327112 | tf_op jit(solution)/shard_map/ppermute | solution.py:864
  8.8 15.9 %collective-permute-start.8 = (f32[1,1152]{1,0:T(1,128)}, f32[1,1152]{1,0:T(1,128)S(1)}, u32[]{:S(2)}, u32[]{:S(2)}) collective-permute-start(f32[1,1152]{1,0:T(1,128)} %param.30), channel_id=1, source_target_pairs={{0,2},{1,3},{2,0},{3,1},{4,6},{5,7},{6,4},{7,5},{8,10},{9,11},{10,... | collective-permute-start | bytes 13832 | tf_op jit(solution)/shard_map/ppermute | solution.py:859
  14.6 49.5 %copy-start.28 = (bf16[6,3,96,128]{3,2,1,0:T(8,128)(2,1)}, bf16[6,3,96,128]{3,2,1,0:T(8,128)(2,1)S(1)}, u32[]{:S(2)}) copy-start(bf16[6,3,96,128]{3,2,1,0:T(8,128)(2,1)S(1)} %collective-permute-done.3.refs_2_) | copy-start | bytes 1327108
  19.9 12.8 %collective-permute-start.6 = (bf16[6,3,96,128]{3,2,1,0:T(8,128)(2,1)}, bf16[6,3,96,128]{3,2,1,0:T(8,128)(2,1)S(1)}, u32[]{:S(2)}, u32[]{:S(2)}) collective-permute-start(bf16[6,3,96,128]{3,2,1,0:T(8,128)(2,1)} %collective-permute-done.refs_4_), channel_id=1, source_target_pairs={{8,16},{12,20},{16,8},{20,12},{9,17},{13,21},{17,9},{21,13},{10,18... | collective-permute-start | bytes 1327112 | tf_op jit(solution)/shard_map/ppermute | solution.py:864
  22.3 10.4 %collective-permute-start.4 = (bf16[6,3,96,128]{3,2,1,0:T(8,128)(2,1)}, bf16[6,3,96,128]{3,2,1,0:T(8,128)(2,1)S(1)}, u32[]{:S(2)}, u32[]{:S(2)}) collective-permute-start(bf16[6,3,96,128]{3,2,1,0:T(8,128)(2,1)} %collective-permute-done.refs_4_), channel_id=1, source_target_pairs={{0,4},{4,0},{8,12},{12,8},{16,20},{20,16},{24,28},{28,24},{1,5},{5... | collective-permute-start | bytes 1327112 | tf_op jit(solution)/shard_map/ppermute | solution.py:859
  22.9 9.8 %collective-permute-start.5 = (bf16[6,3,96,128]{3,2,1,0:T(8,128)(2,1)}, bf16[6,3,96,128]{3,2,1,0:T(8,128)(2,1)S(1)}, u32[]{:S(2)}, u32[]{:S(2)}) collective-permute-start(bf16[6,3,96,128]{3,2,1,0:T(8,128)(2,1)} %collective-permute-done.2.refs_1_), channel_id=1, source_target_pairs={{0,2},{1,3},{2,0},{3,1},{4,6},{5,7},{6,4},{7,5},{8,10},{9,11},{10,... | collective-permute-start | bytes 1327112 | tf_op jit(solution)/shard_map/ppermute | solution.py:859
  23.4 9.3 %collective-permute-start.7 = (bf16[6,3,96,128]{3,2,1,0:T(8,128)(2,1)}, bf16[6,3,96,128]{3,2,1,0:T(8,128)(2,1)S(1)}, u32[]{:S(2)}, u32[]{:S(2)}) collective-permute-start(bf16[6,3,96,128]{3,2,1,0:T(8,128)(2,1)} %collective-permute-done.1), channel_id=1, source_target_pairs={{8,0},{12,4},{16,24},{20,28},{9,1},{13,5},{17,25},{21,29},{10,2},{... | collective-permute-start | bytes 1327112 | tf_op jit(solution)/shard_map/ppermute | solution.py:864
  32.7 38.4 %copy-start.31 = (bf16[6,3,96,128]{3,2,1,0:T(8,128)(2,1)}, bf16[6,3,96,128]{3,2,1,0:T(8,128)(2,1)S(1)}, u32[]{:S(2)}) copy-start(bf16[6,3,96,128]{3,2,1,0:T(8,128)(2,1)S(1)} %collective-permute-done.5.refs_3_) | copy-start | bytes 1327108
  33.7 39.2 %copy-start.17 = (bf16[6,3,96,128]{3,2,1,0:T(8,128)(2,1)}, bf16[6,3,96,128]{3,2,1,0:T(8,128)(2,1)S(1)}, u32[]{:S(2)}) copy-start(bf16[6,3,96,128]{3,2,1,0:T(8,128)(2,1)S(1)} %add.131.refs_8_) | copy-start | bytes 1327108
  33.7 8.8 %collective-permute-start.10 = (bf16[6,3,96,128]{3,2,1,0:T(8,128)(2,1)S(1)}, bf16[6,3,96,128]{3,2,1,0:T(8,128)(2,1)S(1)}, u32[]{:S(2)}, u32[]{:S(2)}) collective-permute-start(bf16[6,3,96,128]{3,2,1,0:T(8,128)(2,1)S(1)} %add.131.refs_8_), channel_id=1, source_target_pairs={{0,2},{1,3},{2,0},{3,1},{4,6},{5,7},{6,4},{7,5},{8,10},{9,11},{10,... | collective-permute-start | bytes 1327112 | tf_op jit(solution)/shard_map/ppermute | solution.py:859
  34.6 8.4 %collective-permute-start.9 = (bf16[6,3,96,128]{3,2,1,0:T(8,128)(2,1)S(1)}, bf16[6,3,96,128]{3,2,1,0:T(8,128)(2,1)S(1)}, u32[]{:S(2)}, u32[]{:S(2)}) collective-permute-start(bf16[6,3,96,128]{3,2,1,0:T(8,128)(2,1)S(1)} %add.131.refs_8_), channel_id=1, source_target_pairs={{0,4},{4,0},{8,12},{12,8},{16,20},{20,16},{24,28},{28,24},{1,5},{5... | collective-permute-start | bytes 1327112 | tf_op jit(solution)/shard_map/ppermute | solution.py:859
  36.1 14.9 %collective-permute-start.11 = (bf16[6,3,96,128]{3,2,1,0:T(8,128)(2,1)S(1)}, bf16[6,3,96,128]{3,2,1,0:T(8,128)(2,1)S(1)}, u32[]{:S(2)}, u32[]{:S(2)}) collective-permute-start(bf16[6,3,96,128]{3,2,1,0:T(8,128)(2,1)S(1)} %collective-permute-done.6), channel_id=1, source_target_pairs={{8,0},{12,4},{16,24},{20,28},{9,1},{13,5},{17,25},{21,29},{10,2},{... | collective-permute-start | bytes 1327112 | tf_op jit(solution)/shard_map/ppermute | solution.py:864
  40.4 19.8 %collective-permute-start.14 = (bf16[6,3,96,128]{3,2,1,0:T(8,128)(2,1)S(1)}, bf16[6,3,96,128]{3,2,1,0:T(8,128)(2,1)S(1)}, u32[]{:S(2)}, u32[]{:S(2)}) collective-permute-start(bf16[6,3,96,128]{3,2,1,0:T(8,128)(2,1)S(1)} %collective-permute-done.3.refs_2_), channel_id=1, source_target_pairs={{0,8},{4,12},{8,0},{12,4},{16,24},{20,28},{24,16},{28,20},{1,9},{5... | collective-permute-start | bytes 1327112 | tf_op jit(solution)/shard_map/ppermute | solution.py:864
  43.2 27.9 %copy-start.33 = (bf16[6,3,96,128]{3,2,1,0:T(8,128)(2,1)}, bf16[6,3,96,128]{3,2,1,0:T(8,128)(2,1)S(1)}, u32[]{:S(2)}) copy-start(bf16[6,3,96,128]{3,2,1,0:T(8,128)(2,1)S(1)} %collective-permute-done.9.refs_9_) | copy-start | bytes 1327108
  52.1 20.8 %copy-start.18 = (bf16[6,3,96,128]{3,2,1,0:T(8,128)(2,1)}, bf16[6,3,96,128]{3,2,1,0:T(8,128)(2,1)S(1)}, u32[]{:S(2)}) copy-start(bf16[6,3,96,128]{3,2,1,0:T(8,128)(2,1)S(1)} %add.132.refs_12_) | copy-start | bytes 1327108
  52.2 9.5 %collective-permute-start.13 = (bf16[6,3,96,128]{3,2,1,0:T(8,128)(2,1)S(1)}, bf16[6,3,96,128]{3,2,1,0:T(8,128)(2,1)S(1)}, u32[]{:S(2)}, u32[]{:S(2)}) collective-permute-start(bf16[6,3,96,128]{3,2,1,0:T(8,128)(2,1)S(1)} %add.132.refs_12_), channel_id=1, source_target_pairs={{0,2},{1,3},{2,0},{3,1},{4,6},{5,7},{6,4},{7,5},{8,10},{9,11},{10,... | collective-permute-start | bytes 1327112 | tf_op jit(solution)/shard_map/ppermute | solution.py:859
  52.7 10.0 %collective-permute-start.12 = (bf16[6,3,96,128]{3,2,1,0:T(8,128)(2,1)S(1)}, bf16[6,3,96,128]{3,2,1,0:T(8,128)(2,1)S(1)}, u32[]{:S(2)}, u32[]{:S(2)}) collective-permute-start(bf16[6,3,96,128]{3,2,1,0:T(8,128)(2,1)S(1)} %add.132.refs_12_), channel_id=1, source_target_pairs={{0,4},{4,0},{8,12},{12,8},{16,20},{20,16},{24,28},{28,24},{1,5},{5... | collective-permute-start | bytes 1327112 | tf_op jit(solution)/shard_map/ppermute | solution.py:859
  53.3 15.9 %collective-permute-start.20 = (bf16[6,3,96,128]{3,2,1,0:T(8,128)(2,1)S(1)}, bf16[6,3,96,128]{3,2,1,0:T(8,128)(2,1)S(1)}, u32[]{:S(2)}, u32[]{:S(2)}) collective-permute-start(bf16[6,3,96,128]{3,2,1,0:T(8,128)(2,1)S(1)} %collective-permute-done.5.refs_3_), channel_id=1, source_target_pairs={{0,8},{4,12},{8,0},{12,4},{16,24},{20,28},{24,16},{28,20},{1,9},{5... | collective-permute-start | bytes 1327112 | tf_op jit(solution)/shard_map/ppermute | solution.py:864
  55.7 13.4 %collective-permute-start.19 = (bf16[6,3,96,128]{3,2,1,0:T(8,128)(2,1)S(1)}, bf16[6,3,96,128]{3,2,1,0:T(8,128)(2,1)S(1)}, u32[]{:S(2)}, u32[]{:S(2)}) collective-permute-start(bf16[6,3,96,128]{3,2,1,0:T(8,128)(2,1)S(1)} %collective-permute-done.9.refs_9_), channel_id=1, source_target_pairs={{0,2},{1,3},{2,0},{3,1},{4,6},{5,7},{6,4},{7,5},{8,10},{9,11},{10,... | collective-permute-start | bytes 1327112 | tf_op jit(solution)/shard_map/ppermute | solution.py:859
  62.8 8.3 %collective-permute-start.18 = (bf16[6,3,96,128]{3,2,1,0:T(8,128)(2,1)S(1)}, bf16[6,3,96,128]{3,2,1,0:T(8,128)(2,1)S(1)}, u32[]{:S(2)}, u32[]{:S(2)}) collective-permute-start(bf16[6,3,96,128]{3,2,1,0:T(8,128)(2,1)S(1)} %collective-permute-done.13.refs_14_), channel_id=1, source_target_pairs={{0,4},{4,0},{8,12},{12,8},{16,20},{20,16},{24,28},{28,24},{1,5},{5... | collective-permute-start | bytes 1327112 | tf_op jit(solution)/shard_map/ppermute | solution.py:859
  63.3 5.8 %collective-permute-start.15 = (bf16[133,768]{1,0:T(8,128)(2,1)S(1)}, bf16[133,768]{1,0:T(8,128)(2,1)S(1)}, u32[]{:S(2)}, u32[]{:S(2)}) collective-permute-start(bf16[133,768]{1,0:T(8,128)(2,1)S(1)} %bitcast.55), channel_id=1, source_target_pairs={{0,2},{1,3},{2,0},{3,1},{4,6},{5,7},{6,4},{7,5},{8,10},{9,11},{10,... | collective-permute-start | bytes 612872 | tf_op jit(solution)/shard_map/ppermute | solution.py:859
  64.2 18.8 %collective-permute-start.16 = (bf16[133,768]{1,0:T(8,128)(2,1)S(1)}, bf16[133,768]{1,0:T(8,128)(2,1)S(1)}, u32[]{:S(2)}, u32[]{:S(2)}) collective-permute-start(bf16[133,768]{1,0:T(8,128)(2,1)S(1)} %bitcast.47), channel_id=1, source_target_pairs={{0,1},{1,0},{2,3},{3,2},{4,5},{5,4},{6,7},{7,6},{8,9},{9,8},{10,11... | collective-permute-start | bytes 612872 | tf_op jit(solution)/shard_map/ppermute | solution.py:859
  69.1 13.9 %collective-permute-start.17 = (bf16[133,768]{1,0:T(8,128)(2,1)S(1)}, bf16[133,768]{1,0:T(8,128)(2,1)S(1)}, u32[]{:S(2)}, u32[]{:S(2)}) collective-permute-start(bf16[133,768]{1,0:T(8,128)(2,1)S(1)} %collective-permute-done.15.xb), channel_id=1, source_target_pairs={{0,1},{1,0},{2,3},{3,2},{4,5},{5,4},{6,7},{7,6},{8,9},{9,8},{10,11... | collective-permute-start | bytes 612872 | tf_op jit(solution)/shard_map/ppermute | solution.py:859
  71.9 11.1 %collective-permute-start.21 = (bf16[133,768]{1,0:T(8,128)(2,1)}, bf16[133,768]{1,0:T(8,128)(2,1)S(1)}, u32[]{:S(2)}, u32[]{:S(2)}) collective-permute-start(bf16[133,768]{1,0:T(8,128)(2,1)} %bitcast.38), channel_id=1, source_target_pairs={{0,2},{1,3},{2,0},{3,1},{4,6},{5,7},{6,4},{7,5},{8,10},{9,11},{10,... | collective-permute-start | bytes 612872 | tf_op jit(solution)/shard_map/ppermute | solution.py:859
  95.3 2.5 %collective-permute-start.22 = (bf16[576,768]{1,0:T(8,128)(2,1)S(1)}, bf16[576,768]{1,0:T(8,128)(2,1)S(1)}, u32[]{:S(2)}, u32[]{:S(2)}) collective-permute-start(bf16[576,768]{1,0:T(8,128)(2,1)S(1)} %get-tuple-element.146.mine_ref), channel_id=1, source_target_pairs={{0,1},{1,0},{2,3},{3,2},{4,5},{5,4},{6,7},{7,6},{8,9},{9,8},{10,11... | collective-permute-start | bytes 2654216 | tf_op jit(solution)/shard_map/ppermute | solution.py:859
  104.5 3.1 %collective-permute-start.23 = (bf16[576,768]{1,0:T(8,128)(2,1)S(1)}, bf16[576,768]{1,0:T(8,128)(2,1)S(1)}, u32[]{:S(2)}, u32[]{:S(2)}) collective-permute-start(bf16[576,768]{1,0:T(8,128)(2,1)S(1)} %get-tuple-element.150.mine_ref), channel_id=1, source_target_pairs={{0,1},{1,0},{2,3},{3,2},{4,5},{5,4},{6,7},{7,6},{8,9},{9,8},{10,11... | collective-permute-start | bytes 2654216 | tf_op jit(solution)/shard_map/ppermute | solution.py:859
  104.7 2.6 %collective-permute-start.24 = (bf16[133,768]{1,0:T(8,128)(2,1)S(1)}, bf16[133,768]{1,0:T(8,128)(2,1)S(1)}, u32[]{:S(2)}, u32[]{:S(2)}) collective-permute-start(bf16[133,768]{1,0:T(8,128)(2,1)S(1)} %bitcast.43), channel_id=1, source_target_pairs={{0,1},{1,0},{2,3},{3,2},{4,5},{5,4},{6,7},{7,6},{8,9},{9,8},{10,11... | collective-permute-start | bytes 612872 | tf_op jit(solution)/shard_map/ppermute | solution.py:859
  105.2 2.4 %collective-permute-start.25 = (bf16[133,768]{1,0:T(8,128)(2,1)S(1)}, bf16[133,768]{1,0:T(8,128)(2,1)S(1)}, u32[]{:S(2)}, u32[]{:S(2)}) collective-permute-start(bf16[133,768]{1,0:T(8,128)(2,1)S(1)} %collective-permute-done.21.later_ref.cb), channel_id=1, source_target_pairs={{0,1},{1,0},{2,3},{3,2},{4,5},{5,4},{6,7},{7,6},{8,9},{9,8},{10,11... | collective-permute-start | bytes 612872 | tf_op jit(solution)/shard_map/ppermute | solution.py:859
  114.9 4.9 %collective-permute-start.27 = (bf16[576,768]{1,0:T(8,128)(2,1)S(1)}, bf16[576,768]{1,0:T(8,128)(2,1)S(1)}, u32[]{:S(2)}, u32[]{:S(2)}) collective-permute-start(bf16[576,768]{1,0:T(8,128)(2,1)S(1)} %get-tuple-element.159.mine_ref), channel_id=1, source_target_pairs={{0,1},{1,0},{2,3},{3,2},{4,5},{5,4},{6,7},{7,6},{8,9},{9,8},{10,11... | collective-permute-start | bytes 2654216 | tf_op jit(solution)/shard_map/ppermute | solution.py:859
  115.1 26.6 %collective-permute-start.26 = (bf16[133,768]{1,0:T(8,128)(2,1)S(1)}, bf16[133,768]{1,0:T(8,128)(2,1)S(1)}, u32[]{:S(2)}, u32[]{:S(2)}) collective-permute-start(bf16[133,768]{1,0:T(8,128)(2,1)S(1)} %get-tuple-element.257), channel_id=1, source_target_pairs={{0,2},{1,3},{2,0},{3,1},{4,6},{5,7},{6,4},{7,5},{8,10},{9,11},{10,... | collective-permute-start | bytes 612872 | tf_op jit(solution)/shard_map/ppermute | solution.py:859
  137.1 5.0 %collective-permute-start.28 = (bf16[288,768]{1,0:T(8,128)(2,1)}, bf16[288,768]{1,0:T(8,128)(2,1)S(1)}, u32[]{:S(2)}, u32[]{:S(2)}) collective-permute-start(bf16[288,768]{1,0:T(8,128)(2,1)} %get-tuple-element.168), channel_id=1, source_target_pairs={{0,1},{1,0},{2,3},{3,2},{4,5},{5,4},{6,7},{7,6},{8,9},{9,8},{10,11... | collective-permute-start | bytes 1327112 | tf_op jit(solution)/shard_map/ppermute | solution.py:859
  143.6 16.8 %collective-permute-start.33 = (f32[16,768]{1,0:T(8,128)S(1)}, f32[16,768]{1,0:T(8,128)S(1)}, u32[]{:S(2)}, u32[]{:S(2)}) collective-permute-start(f32[16,768]{1,0:T(8,128)S(1)} %pad_maximum_fusion.3), channel_id=1, source_target_pairs={{0,1},{1,0},{2,3},{3,2},{4,5},{5,4},{6,7},{7,6},{8,9},{9,8},{10,11... | collective-permute-start | bytes 147464 | tf_op jit(solution)/shard_map/ppermute | solution.py:859
  156.4 22.0 %copy-start.26 = (bf16[6,3,96,128]{3,2,1,0:T(8,128)(2,1)S(1)}, bf16[6,3,96,128]{3,2,1,0:T(8,128)(2,1)}, u32[]{:S(2)}) copy-start(bf16[6,3,96,128]{3,2,1,0:T(8,128)(2,1)} %get-tuple-element.183) | copy-start | bytes 1327108
  156.4 31.5 %copy-start.22 = (bf16[6,3,96,128]{3,2,1,0:T(8,128)(2,1)S(1)}, bf16[6,3,96,128]{3,2,1,0:T(8,128)(2,1)}, u32[]{:S(2)}) copy-start(bf16[6,3,96,128]{3,2,1,0:T(8,128)(2,1)} %get-tuple-element.186) | copy-start | bytes 1327108
  156.4 17.1 %collective-permute-start.30 = (bf16[6,3,96,128]{3,2,1,0:T(8,128)(2,1)}, bf16[6,3,96,128]{3,2,1,0:T(8,128)(2,1)S(1)}, u32[]{:S(2)}, u32[]{:S(2)}) collective-permute-start(bf16[6,3,96,128]{3,2,1,0:T(8,128)(2,1)} %get-tuple-element.174), channel_id=1, source_target_pairs={{0,4},{4,0},{8,12},{12,8},{16,20},{20,16},{24,28},{28,24},{1,5},{5... | collective-permute-start | bytes 1327112 | tf_op jit(solution)/shard_map/ppermute | solution.py:859
  157.1 16.5 %collective-permute-start.31 = (bf16[6,3,96,128]{3,2,1,0:T(8,128)(2,1)}, bf16[6,3,96,128]{3,2,1,0:T(8,128)(2,1)S(1)}, u32[]{:S(2)}, u32[]{:S(2)}) collective-permute-start(bf16[6,3,96,128]{3,2,1,0:T(8,128)(2,1)} %get-tuple-element.175), channel_id=1, source_target_pairs={{0,2},{1,3},{2,0},{3,1},{4,6},{5,7},{6,4},{7,5},{8,10},{9,11},{10,... | collective-permute-start | bytes 1327112 | tf_op jit(solution)/shard_map/ppermute | solution.py:859
  157.6 16.0 %collective-permute-start.32 = (bf16[6,3,96,128]{3,2,1,0:T(8,128)(2,1)}, bf16[6,3,96,128]{3,2,1,0:T(8,128)(2,1)S(1)}, u32[]{:S(2)}, u32[]{:S(2)}) collective-permute-start(bf16[6,3,96,128]{3,2,1,0:T(8,128)(2,1)} %get-tuple-element.176), channel_id=1, source_target_pairs={{0,8},{4,12},{8,0},{12,4},{16,24},{20,28},{24,16},{28,20},{1,9},{5... | collective-permute-start | bytes 1327112 | tf_op jit(solution)/shard_map/ppermute | solution.py:864
  160.4 15.3 %copy-start.49 = (bf16[6,3,96,128]{3,2,1,0:T(8,128)(2,1)S(1)}, bf16[6,3,96,128]{3,2,1,0:T(8,128)(2,1)}, u32[]{:S(2)}) copy-start(bf16[6,3,96,128]{3,2,1,0:T(8,128)(2,1)} %get-tuple-element.185) | copy-start | bytes 1327108
  161.3 9.8 %collective-permute-start.34 = (f32[19,768]{1,0:T(8,128)S(1)}, f32[19,768]{1,0:T(8,128)S(1)}, u32[]{:S(2)}, u32[]{:S(2)}) collective-permute-start(f32[19,768]{1,0:T(8,128)S(1)} %pad_maximum_fusion.2), channel_id=1, source_target_pairs={{0,2},{1,3},{2,0},{3,1},{4,6},{5,7},{6,4},{7,5},{8,10},{9,11},{10,... | collective-permute-start | bytes 175112 | tf_op jit(solution)/shard_map/ppermute | solution.py:859
  162.6 20.2 %collective-permute-start.38 = (bf16[6,3,96,128]{3,2,1,0:T(8,128)(2,1)}, bf16[6,3,96,128]{3,2,1,0:T(8,128)(2,1)S(1)}, u32[]{:S(2)}, u32[]{:S(2)}) collective-permute-start(bf16[6,3,96,128]{3,2,1,0:T(8,128)(2,1)} %get-tuple-element.187), channel_id=1, source_target_pairs={{0,4},{4,0},{8,12},{12,8},{16,20},{20,16},{24,28},{28,24},{1,5},{5... | collective-permute-start | bytes 1327112 | tf_op jit(solution)/shard_map/ppermute | solution.py:859
  171.1 12.4 %collective-permute-start.40 = (bf16[6,3,96,128]{3,2,1,0:T(8,128)(2,1)}, bf16[6,3,96,128]{3,2,1,0:T(8,128)(2,1)S(1)}, u32[]{:S(2)}, u32[]{:S(2)}) collective-permute-start(bf16[6,3,96,128]{3,2,1,0:T(8,128)(2,1)} %get-tuple-element.190), channel_id=1, source_target_pairs={{0,8},{4,12},{8,0},{12,4},{16,24},{20,28},{24,16},{28,20},{1,9},{5... | collective-permute-start | bytes 1327112 | tf_op jit(solution)/shard_map/ppermute | solution.py:864
  174.8 18.9 %copy-start.25 = (bf16[6,3,96,128]{3,2,1,0:T(8,128)(2,1)S(1)}, bf16[6,3,96,128]{3,2,1,0:T(8,128)(2,1)}, u32[]{:S(2)}) copy-start(bf16[6,3,96,128]{3,2,1,0:T(8,128)(2,1)} %get-tuple-element.173) | copy-start | bytes 1327108
  174.8 13.2 %collective-permute-start.39 = (bf16[6,3,96,128]{3,2,1,0:T(8,128)(2,1)S(1)}, bf16[6,3,96,128]{3,2,1,0:T(8,128)(2,1)S(1)}, u32[]{:S(2)}, u32[]{:S(2)}) collective-permute-start(bf16[6,3,96,128]{3,2,1,0:T(8,128)(2,1)S(1)} %add_convert_fusion.6), channel_id=1, source_target_pairs={{0,2},{1,3},{2,0},{3,1},{4,6},{5,7},{6,4},{7,5},{8,10},{9,11},{10,... | collective-permute-start | bytes 1327112 | tf_op jit(solution)/shard_map/ppermute | solution.py:859
  175.7 25.0 %collective-permute-start.37 = (bf16[6,3,96,128]{3,2,1,0:T(8,128)(2,1)S(1)}, bf16[6,3,96,128]{3,2,1,0:T(8,128)(2,1)S(1)}, u32[]{:S(2)}, u32[]{:S(2)}) collective-permute-start(bf16[6,3,96,128]{3,2,1,0:T(8,128)(2,1)S(1)} %copy-done.49), channel_id=1, source_target_pairs={{0,2},{1,3},{2,0},{3,1},{4,6},{5,7},{6,4},{7,5},{8,10},{9,11},{10,... | collective-permute-start | bytes 1327112 | tf_op jit(solution)/shard_map/ppermute | solution.py:859
  176.9 4.4 %collective-permute-start.41 = (f32[19,768]{1,0:T(8,128)S(1)}, f32[19,768]{1,0:T(8,128)S(1)}, u32[]{:S(2)}, u32[]{:S(2)}) collective-permute-start(f32[19,768]{1,0:T(8,128)S(1)} %add.134), channel_id=1, source_target_pairs={{0,4},{4,0},{8,12},{12,8},{16,20},{20,16},{24,28},{28,24},{1,5},{5... | collective-permute-start | bytes 175112 | tf_op jit(solution)/shard_map/ppermute | solution.py:859
  178.5 22.3 %copy-start.29 = (bf16[6,3,96,128]{3,2,1,0:T(8,128)(2,1)S(1)}, bf16[6,3,96,128]{3,2,1,0:T(8,128)(2,1)}, u32[]{:S(2)}) copy-start(bf16[6,3,96,128]{3,2,1,0:T(8,128)(2,1)} %get-tuple-element.182) | copy-start | bytes 1327108
  181.3 19.5 %collective-permute-start.36 = (bf16[6,3,96,128]{3,2,1,0:T(8,128)(2,1)S(1)}, bf16[6,3,96,128]{3,2,1,0:T(8,128)(2,1)S(1)}, u32[]{:S(2)}, u32[]{:S(2)}) collective-permute-start(bf16[6,3,96,128]{3,2,1,0:T(8,128)(2,1)S(1)} %add_convert_fusion.7), channel_id=1, source_target_pairs={{0,4},{4,0},{8,12},{12,8},{16,20},{20,16},{24,28},{28,24},{1,5},{5... | collective-permute-start | bytes 1327112 | tf_op jit(solution)/shard_map/ppermute | solution.py:859
  188.2 12.6 %collective-permute-start.42 = (bf16[6,3,96,128]{3,2,1,0:T(8,128)(2,1)S(1)}, bf16[6,3,96,128]{3,2,1,0:T(8,128)(2,1)S(1)}, u32[]{:S(2)}, u32[]{:S(2)}) collective-permute-start(bf16[6,3,96,128]{3,2,1,0:T(8,128)(2,1)S(1)} %add_convert_fusion.5), channel_id=1, source_target_pairs={{0,8},{4,12},{24,16},{28,20},{1,9},{5,13},{25,17},{29,21},{2,10},{... | collective-permute-start | bytes 1327112 | tf_op jit(solution)/shard_map/ppermute | solution.py:864
  189.5 25.3 %collective-permute-start.29 = (bf16[6,3,96,128]{3,2,1,0:T(8,128)(2,1)S(1)}, bf16[6,3,96,128]{3,2,1,0:T(8,128)(2,1)S(1)}, u32[]{:S(2)}, u32[]{:S(2)}) collective-permute-start(bf16[6,3,96,128]{3,2,1,0:T(8,128)(2,1)S(1)} %copy-done.48), channel_id=1, source_target_pairs={{0,4},{4,0},{8,12},{12,8},{16,20},{20,16},{24,28},{28,24},{1,5},{5... | collective-permute-start | bytes 1327112 | tf_op jit(solution)/shard_map/ppermute | solution.py:859
  191.0 8.9 %collective-permute-start.43 = (f32[19,768]{1,0:T(8,128)S(1)}, f32[19,768]{1,0:T(8,128)S(1)}, u32[]{:S(2)}, u32[]{:S(2)}) collective-permute-start(f32[19,768]{1,0:T(8,128)S(1)} %add.138), channel_id=1, source_target_pairs={{0,8},{4,12},{8,0},{12,4},{16,24},{20,28},{24,16},{28,20},{1,9},{5... | collective-permute-start | bytes 175112 | tf_op jit(solution)/shard_map/ppermute | solution.py:859
  199.9 14.9 %collective-permute-start.35 = (bf16[6,3,96,128]{3,2,1,0:T(8,128)(2,1)S(1)}, bf16[6,3,96,128]{3,2,1,0:T(8,128)(2,1)S(1)}, u32[]{:S(2)}, u32[]{:S(2)}) collective-permute-start(bf16[6,3,96,128]{3,2,1,0:T(8,128)(2,1)S(1)} %add_convert_fusion.8), channel_id=1, source_target_pairs={{0,2},{1,3},{2,0},{3,1},{4,6},{5,7},{6,4},{7,5},{8,10},{9,11},{10,... | collective-permute-start | bytes 1327112 | tf_op jit(solution)/shard_map/ppermute | solution.py:859
  201.0 13.8 %collective-permute-start.45 = (bf16[6,3,96,128]{3,2,1,0:T(8,128)(2,1)S(1)}, bf16[6,3,96,128]{3,2,1,0:T(8,128)(2,1)S(1)}, u32[]{:S(2)}, u32[]{:S(2)}) collective-permute-start(bf16[6,3,96,128]{3,2,1,0:T(8,128)(2,1)S(1)} %add_convert_fusion.4), channel_id=1, source_target_pairs={{0,8},{4,12},{24,16},{28,20},{1,9},{5,13},{25,17},{29,21},{2,10},{... | collective-permute-start | bytes 1327112 | tf_op jit(solution)/shard_map/ppermute | solution.py:864
  202.5 12.3 %collective-permute-start.44 = (bf16[6,3,96,128]{3,2,1,0:T(8,128)(2,1)S(1)}, bf16[6,3,96,128]{3,2,1,0:T(8,128)(2,1)S(1)}, u32[]{:S(2)}, u32[]{:S(2)}) collective-permute-start(bf16[6,3,96,128]{3,2,1,0:T(8,128)(2,1)S(1)} %add_convert_fusion.4), channel_id=1, source_target_pairs={{8,16},{12,20},{16,8},{20,12},{9,17},{13,21},{17,9},{21,13},{10,18... | collective-permute-start | bytes 1327112 | tf_op jit(solution)/shard_map/ppermute | solution.py:864
  207.0 6.6 %collective-permute-start.46 = (f32[19,768]{1,0:T(8,128)S(1)}, f32[19,768]{1,0:T(8,128)S(1)}, u32[]{:S(2)}, u32[]{:S(2)}) collective-permute-start(f32[19,768]{1,0:T(8,128)S(1)} %add.141), channel_id=1, source_target_pairs={{0,16},{4,20},{8,24},{12,28},{16,0},{20,4},{24,8},{28,12},{1,17},{... | collective-permute-start | bytes 175112 | tf_op jit(solution)/shard_map/ppermute | solution.py:859
  213.6 10.7 %collective-permute-start.48 = (bf16[6,3,96,128]{3,2,1,0:T(8,128)(2,1)}, bf16[6,3,96,128]{3,2,1,0:T(8,128)(2,1)}, u32[]{:S(2)}, u32[]{:S(2)}) collective-permute-start(bf16[6,3,96,128]{3,2,1,0:T(8,128)(2,1)} %add_convert_fusion.2), channel_id=1, source_target_pairs={{0,2},{1,3},{2,0},{3,1},{4,6},{5,7},{6,4},{7,5},{8,10},{9,11},{10,... | collective-permute-start | bytes 1327112 | tf_op jit(solution)/shard_map/ppermute | solution.py:859
  215.7 15.6 %copy-start.43 = (f32[16,768]{1,0:T(8,128)S(1)}, f32[16,768]{1,0:T(8,128)}, u32[]{:S(2)}) copy-start(f32[16,768]{1,0:T(8,128)} %param.34) | copy-start | bytes 147460
  215.8 15.6 %copy-start.44 = (f32[16,768]{1,0:T(8,128)S(1)}, f32[16,768]{1,0:T(8,128)}, u32[]{:S(2)}) copy-start(f32[16,768]{1,0:T(8,128)} %param.35) | copy-start | bytes 147460
  215.9 8.9 %collective-permute-start.49 = (bf16[6,3,96,128]{3,2,1,0:T(8,128)(2,1)S(1)}, bf16[6,3,96,128]{3,2,1,0:T(8,128)(2,1)S(1)}, u32[]{:S(2)}, u32[]{:S(2)}) collective-permute-start(bf16[6,3,96,128]{3,2,1,0:T(8,128)(2,1)S(1)} %add_convert_fusion.1), channel_id=1, source_target_pairs={{0,8},{4,12},{8,0},{12,4},{16,24},{20,28},{24,16},{28,20},{1,9},{5... | collective-permute-start | bytes 1327112 | tf_op jit(solution)/shard_map/ppermute | solution.py:864
  218.7 8.4 %collective-permute-start.47 = (bf16[6,3,96,128]{3,2,1,0:T(8,128)(2,1)S(1)}, bf16[6,3,96,128]{3,2,1,0:T(8,128)(2,1)S(1)}, u32[]{:S(2)}, u32[]{:S(2)}) collective-permute-start(bf16[6,3,96,128]{3,2,1,0:T(8,128)(2,1)S(1)} %add_convert_fusion.3), channel_id=1, source_target_pairs={{0,4},{4,0},{8,12},{12,8},{16,20},{20,16},{24,28},{28,24},{1,5},{5... | collective-permute-start | bytes 1327112 | tf_op jit(solution)/shard_map/ppermute | solution.py:859
  220.2 10.2 %collective-permute-start.50 = (bf16[6,3,96,128]{3,2,1,0:T(8,128)(2,1)S(1)}, bf16[6,3,96,128]{3,2,1,0:T(8,128)(2,1)S(1)}, u32[]{:S(2)}, u32[]{:S(2)}) collective-permute-start(bf16[6,3,96,128]{3,2,1,0:T(8,128)(2,1)S(1)} %copy-done.27), channel_id=1, source_target_pairs={{8,16},{12,20},{16,8},{20,12},{9,17},{13,21},{17,9},{21,13},{10,18... | collective-permute-start | bytes 1327112 | tf_op jit(solution)/shard_map/ppermute | solution.py:864
  230.5 8.5 %collective-permute-start.51 = (bf16[133,768]{1,0:T(8,128)(2,1)S(1)}, bf16[133,768]{1,0:T(8,128)(2,1)S(1)}, u32[]{:S(2)}, u32[]{:S(2)}) collective-permute-start(bf16[133,768]{1,0:T(8,128)(2,1)S(1)} %get-tuple-element.255), channel_id=1, source_target_pairs={{0,2},{1,3},{2,0},{3,1},{4,6},{5,7},{6,4},{7,5},{8,10},{9,11},{10,... | collective-permute-start | bytes 612872 | tf_op jit(solution)/shard_map/ppermute | solution.py:859
  (38 other events, 246.1 us)

commit v5 on v4

--- a/solution.py
+++ b/solution.py
@@ -424,10 +424,10 @@
 
     q, k, v = q_ref[...], k_ref[...], v_ref[...]
     masks = head_masks(q.shape)
+    raws = [dot_back(jnp.where(masks[n], q, jnp.zeros_like(q)), k) for n in range(2)]
     outs = []
     for n in range(2):
-        qh = jnp.where(masks[n], q, jnp.zeros_like(q))
-        scores = jnp.where(vis[...] > 0.5, dot_back(qh, k) * HEAD_DIM ** (-0.5), -1000000000.0)
+        scores = jnp.where(vis[...] > 0.5, raws[n] * HEAD_DIM ** (-0.5), -1000000000.0)
         e = jnp.exp(scores - jnp.max(scores, axis=-1, keepdims=True))
         p = (e * (1.0 / jnp.sum(e, axis=-1, keepdims=True))).astype(BF)
         p_ref[n] = p
@@ -619,14 +619,12 @@
     q, k, v, dc = q_ref[...], k_ref[...], v_ref[...], dctx[h]
     masks = head_masks(q.shape)
     dqs, dks, dvs = [], [], []
+    dps = [dot_back(jnp.where(masks[m], dc, jnp.zeros_like(dc)), v) for m in range(2)]
     for m in range(2):
-        dch = jnp.where(masks[m], dc, jnp.zeros_like(dc))
-        p = p_ref[m]
-        dvs.append(inner_rows(p, dc))
-        dp = dot_back(dch, v)
-        pf = p.astype(F32)
-        row = jnp.sum(dp * pf, axis=-1, keepdims=True)
-        ds = (pf * (dp - row) * HEAD_DIM ** (-0.5)).astype(BF)
+        dvs.append(inner_rows(p_ref[m], dc))
+        pf = p_ref[m].astype(F32)
+        row = jnp.sum(dps[m] * pf, axis=-1, keepdims=True)
+        ds = (pf * (dps[m] - row) * HEAD_DIM ** (-0.5)).astype(BF)
         dqs.append(dot(ds, k))
         dks.append(inner_rows(ds, q))
     dq, dk, dv = (jnp.where(masks[0], d[0], d[1]) for d in (dqs, dks, dvs))

time: 245 us -> 242 us (0.988)
  transfers between devices with their start and end apart: 52 -> 52, of which waited for: 24 -> 24; matrix products, arithmetic and copies ran while one was open for 6% -> 6% of each run, Pallas kernels for 21% -> 20%
where the time goes in v5:
time: 242 us; the launch traced here: 239 us
  Pallas kernels  73.5 us (30%)
  waiting for transfers between devices  72.4 us (30%)
  starting transfers between devices  65.3 us (27%)
  local copies, waits for them, and re-layouts  16.4 us (7%)
  other arithmetic  8.47 us (4%)
  between operations  2.69 us (1%)
    ppermute x38, waiting for transfers between devices, swap(): return lambda v: lax.ppermute(v, axis, xor_pairs(size, step))  52.6 us
    ppermute x38, starting transfers between devices, swap(): return lambda v: lax.ppermute(v, axis, xor_pairs(size, step))  33.7 us
    ppermute x14, starting transfers between devices, along_z(): return lambda v: lax.ppermute(v, 'dp', z_pairs(pairs))  31.6 us
    ppermute x14, waiting for transfers between devices, along_z(): return lambda v: lax.ppermute(v, 'dp', z_pairs(pairs))  19.8 us
    pallas_call x1, Pallas kernels, attend_back(): pl.pallas_call(attend_back_body, grid=(pairs,), out_shape=(sds((rows // 2...  13.7 us
    unnamed x106, local copies, waits for them, and re-layouts  12.9 us
    pallas_call x1, Pallas kernels, pack_grads(): pl.pallas_call(functools.partial(pack_body, places), out_shape=(sds((8, 1...  12.2 us
    pallas_call x1, Pallas kernels, build_weights(): pl.pallas_call(functools.partial(weights_body, len(pieces), places), out_...  9.86 us
  transfers between devices with their start and end apart: 52, of which 24 were waited for; matrix products, arithmetic and copies ran while one was open for 6% of the time, Pallas kernels for 20%

profile of v5, /device:TPU:8, one launch (start us, length us, event | category | flops | bytes accessed | tf_op | source)
XLA Modules:
  0.0 238.8 jit_solution(9063203629992839957)
XLA Ops:
  0.7 1.3 copy-done.3
  2.1 1.6 collective-permute-start.3
  3.7 1.5 collective-permute-start.2
  5.2 3.5 %collective-permute-start.1 = (bf16[6,3,96,128]{3,2,1,0:T(8,128)(2,1)S(1)}, bf16[6,3,96,128]{3,2,1,0:T(8,128)(2,1)}, u32[]{:S(2)}, u32[]{:S(2)}) collective-permute-start(bf16[6,3,96,128]{3,2,1,0:T(8,128)(2,1)S(1)} %pack_owned.1.refs_0_), channel_id=1, source_target_pairs={{8,16},{12,20},{16,8},{20,12},{9,17},{13,21},{17,9},{21,13},{10,18... | collective-permute-start | bytes 1327112 | tf_op jit(solution)/shard_map/ppermute | solution.py:862
  9.4 1.2 dynamic_slice.43
  11.6 1.7 constant_dynamic-slice_fusion.1
  15.5 3.1 %collective-permute-done.1 = bf16[6,3,96,128]{3,2,1,0:T(8,128)(2,1)} collective-permute-done((bf16[6,3,96,128]{3,2,1,0:T(8,128)(2,1)S(1)}, bf16[6,3,96,128]{3,2,1,0:T(8,128)(2,1)}, u32[]{:S(2)}, u32[]{:S(2)}) %collective-permute-start.1) | collective-permute-done | bytes 442400 | tf_op jit(solution)/shard_map/ppermute | solution.py:862
  18.6 1.4 collective-permute-done.refs_4_
  19.9 2.3 collective-permute-start.6
  23.4 1.3 collective-permute-start.7
  24.8 7.9 %collective-permute-done.5.refs_3_ = bf16[6,3,96,128]{3,2,1,0:T(8,128)(2,1)S(1)} collective-permute-done((bf16[6,3,96,128]{3,2,1,0:T(8,128)(2,1)}, bf16[6,3,96,128]{3,2,1,0:T(8,128)(2,1)S(1)}, u32[]{:S(2)}, u32[]{:S(2)}) %collective-permute-start.5) | collective-permute-done | bytes 442400 | tf_op jit(solution)/shard_map/ppermute | solution.py:857
  34.6 1.5 collective-permute-start.9
  36.1 4.5 %collective-permute-start.11 = (bf16[6,3,96,128]{3,2,1,0:T(8,128)(2,1)S(1)}, bf16[6,3,96,128]{3,2,1,0:T(8,128)(2,1)S(1)}, u32[]{:S(2)}, u32[]{:S(2)}) collective-permute-start(bf16[6,3,96,128]{3,2,1,0:T(8,128)(2,1)S(1)} %collective-permute-done.6), channel_id=1, source_target_pairs={{8,0},{12,4},{16,24},{20,28},{9,1},{13,5},{17,25},{21,29},{10,2},{... | collective-permute-start | bytes 1327112 | tf_op jit(solution)/shard_map/ppermute | solution.py:862
  40.6 1.8 collective-permute-done.10.refs_10_
  43.2 7.8 %collective-permute-done.11 = bf16[6,3,96,128]{3,2,1,0:T(8,128)(2,1)S(1)} collective-permute-done((bf16[6,3,96,128]{3,2,1,0:T(8,128)(2,1)S(1)}, bf16[6,3,96,128]{3,2,1,0:T(8,128)(2,1)S(1)}, u32[]{:S(2)}, u32[]{:S(2)}) %collective-permute-start.11) | collective-permute-done | bytes 442400 | tf_op jit(solution)/shard_map/ppermute | solution.py:862
  51.0 1.2 add.132.refs_12_
  53.3 2.5 %collective-permute-start.20 = (bf16[6,3,96,128]{3,2,1,0:T(8,128)(2,1)S(1)}, bf16[6,3,96,128]{3,2,1,0:T(8,128)(2,1)S(1)}, u32[]{:S(2)}, u32[]{:S(2)}) collective-permute-start(bf16[6,3,96,128]{3,2,1,0:T(8,128)(2,1)S(1)} %collective-permute-done.5.refs_3_), channel_id=1, source_target_pairs={{0,8},{4,12},{8,0},{12,4},{16,24},{20,28},{24,16},{28,20},{1,9},{5... | collective-permute-start | bytes 1327112 | tf_op jit(solution)/shard_map/ppermute | solution.py:862
  55.7 1.5 collective-permute-start.19
  57.3 3.0 %collective-permute-done.14.refs_6_ = bf16[6,3,96,128]{3,2,1,0:T(8,128)(2,1)S(1)} collective-permute-done((bf16[6,3,96,128]{3,2,1,0:T(8,128)(2,1)S(1)}, bf16[6,3,96,128]{3,2,1,0:T(8,128)(2,1)S(1)}, u32[]{:S(2)}, u32[]{:S(2)}) %collective-permute-start.14) | collective-permute-done | bytes 442400 | tf_op jit(solution)/shard_map/ppermute | solution.py:862
  60.2 1.5 collective-permute-done.13.refs_14_
  61.7 1.1 collective-permute-done.12.refs_13_
  64.2 4.9 %collective-permute-done.15.xb = bf16[133,768]{1,0:T(8,128)(2,1)S(1)} collective-permute-done((bf16[133,768]{1,0:T(8,128)(2,1)S(1)}, bf16[133,768]{1,0:T(8,128)(2,1)S(1)}, u32[]{:S(2)}, u32[]{:S(2)}) %collective-permute-start.15) | collective-permute-done | bytes 204320 | tf_op jit(solution)/shard_map/ppermute | solution.py:857
  69.1 1.9 collective-permute-done.18.refs_15_
  72.9 9.9 %build_weights.1 = (bf16[768,1152]{1,0:T(8,128)(2,1)}, bf16[384,768]{1,0:T(8,128)(2,1)}, bf16[2,768,768]{2,1,0:T(8,128)(2,1)}, bf16[2,768,768]{2,1,0:T(8,128)(2,1)}) custom-call(s32[192]{0:T(256)} %pos_ref.3, s32[2]{0:T(128)} %get-tuple-element.154.me_ref, bf16[6,3,96,128]{3,2,1,0:T(8,128)(2,1)} %copy-done.10, ...), custom_call_target="tpu_custom_call" | custom-call | flops 100000000 | bytes 30000000 | tf_op jit(solution)/shard_map/build_weights/pallas_call | solution.py:190
  82.9 1.5 copy-done.7
  84.3 2.9 %project.1 = (bf16[576,1152]{1,0:T(8,128)(2,1)S(1)}, f32[576,768]{1,0:T(8,128)S(1)}, bf16[576,768]{1,0:T(8,128)(2,1)S(1)}) custom-call(s32[2]{0:T(128)S(1)} %get-tuple-element.122.flags_ref, bf16[133,768]{1,0:T(8,128)(2,1)S(1)} %bitcast.48, bf16[133,768]{1,0:T(8,128)(2,1)S(1)} %collective-permute-done.15.xb, ...), custom_call_target="tpu_custom_call" | custom-call | flops 1000000000 | bytes 5000000 | tf_op jit(solution)/shard_map/project/pallas_call | solution.py:387
  87.3 6.8 %attend.1 = (bf16[576,384]{1,0:T(8,128)(2,1)S(1)}, bf16[6,576,576]{2,1,0:T(8,128)(2,1)S(1)}, bf16[576,768]{1,0:T(8,128)(2,1)S(1)}) custom-call(s32[576,1]{1,0:T(8,128)S(1)} %copy.38.cq_ref, s32[1,576]{1,0:T(1,128)S(1)} %broadcast_in_dim.25.ck_ref, bf16[576,1152]{1,0:T(8,128)(2,1)S(1)} %get-tuple-element.144.q_ref.k_ref.v_ref, ...), custom_call_target="tpu_custom_call" | custom-call | flops 2500000000 | bytes 8000000 | tf_op jit(solution)/shard_map/attend/pallas_call | solution.py:453
  94.2 2.4 %collective-permute-done.22.other_ref = bf16[576,768]{1,0:T(8,128)(2,1)S(1)} collective-permute-done((bf16[576,768]{1,0:T(8,128)(2,1)S(1)}, bf16[576,768]{1,0:T(8,128)(2,1)S(1)}, u32[]{:S(2)}, u32[]{:S(2)}) %collective-permute-start.22) | collective-permute-done | bytes 884768 | tf_op jit(solution)/shard_map/ppermute | solution.py:857
  96.6 6.7 %feed.1 = (bf16[576,768]{1,0:T(8,128)(2,1)S(1)}, f32[576,768]{1,0:T(8,128)S(1)}, f32[576,1]{1,0:T(8,128)S(1)}, bf16[2,576,768]{2,1,0:T(8,128)(2,1)S(1)}, bf16[2,...) custom-call(bf16[576,768]{1,0:T(8,128)(2,1)S(1)} %get-tuple-element.146.mine_ref, ...), custom_call_target="tpu_custom_call" | custom-call | flops 2800000000 | bytes 16000000 | tf_op jit(solution)/shard_map/feed/pallas_call | solution.py:514
  104.1 2.0 collective-permute-done.24.cc
  106.4 7.3 %feed_back.1 = (bf16[288,768]{1,0:T(8,128)(2,1)S(1)}, f32[576,768]{1,0:T(8,128)S(1)}, bf16[576,768]{1,0:T(8,128)(2,1)S(1)}, bf16[2,576,768]{2,1,0:T(8,128)(2,1)S...) custom-call(bf16[576,768]{1,0:T(8,128)(2,1)S(1)} %get-tuple-element.150.mine_ref, ...), custom_call_target="tpu_custom_call" | custom-call | flops 2800000000 | bytes 16000000 | tf_op jit(solution)/shard_map/feed_back/pallas_call | solution.py:573
  113.9 1.5 collective-permute-start.26
  115.5 3.1 %down_grads.1.later_ref.refs_0_ = bf16[2,768,768]{2,1,0:T(8,128)(2,1)S(1)} custom-call(bf16[2,576,768]{2,1,0:T(8,128)(2,1)S(1)} %get-tuple-element.155.act_ref, bf16[576,768]{1,0:T(8,128)(2,1)S(1)} %get-tuple-element.156.d2_ref), custom_call_target="tpu_custom_call" | custom-call | flops 1400000000 | bytes 8000000 | tf_op jit(solution)/shard_map/down_grads/pallas_call | solution.py:235
  118.7 13.7 %attend_back.1 = (f32[288,768]{1,0:T(8,128)S(1)}, bf16[768,1152]{1,0:T(8,128)(2,1)S(1)}, bf16[384,768]{1,0:T(8,128)(2,1)S(1)}, bf16[288,768]{1,0:T(8,128)(2,1)S(...) custom-call(bf16[576,768]{1,0:T(8,128)(2,1)S(1)} %get-tuple-element.159.mine_ref, ...), custom_call_target="tpu_custom_call" | custom-call | flops 2038431744 | bytes 10485760 | tf_op jit(solution)/shard_map/attend_back/pallas_call | solution.py:647
  132.4 1.2 copy-done.9
  135.4 3.1 %up_grads.1.refs_1_ = bf16[2,768,768]{2,1,0:T(8,128)(2,1)S(1)} custom-call(bf16[576,768]{1,0:T(8,128)(2,1)S(1)} %get-tuple-element.157.h_ref, bf16[2,576,768]{2,1,0:T(8,128)(2,1)S(1)} %get-tuple-element.158.dpre_ref), custom_call_target="tpu_custom_call" | custom-call | flops 1400000000 | bytes 8000000 | tf_op jit(solution)/shard_map/up_grads/pallas_call | solution.py:247
  138.6 1.4 copy-done.6
  142.5 12.2 %pack_grads.1 = (f32[8,128]{1,0:T(8,128)}, bf16[6,3,96,128]{3,2,1,0:T(8,128)(2,1)}, bf16[6,3,96,128]{3,2,1,0:T(8,128)(2,1)}, bf16[6,3,96,128]{3,2,1,0:T(8,128)(2...) custom-call(s32[192]{0:T(256)} %pos_ref.3, ...), custom_call_target="tpu_custom_call" | custom-call | flops 100000000 | bytes 30000000 | tf_op jit(solution)/shard_map/pack_grads/pallas_call | solution.py:340
  155.9 2.8 %collective-permute-start.32 = (bf16[6,3,96,128]{3,2,1,0:T(8,128)(2,1)}, bf16[6,3,96,128]{3,2,1,0:T(8,128)(2,1)S(1)}, u32[]{:S(2)}, u32[]{:S(2)}) collective-permute-start(bf16[6,3,96,128]{3,2,1,0:T(8,128)(2,1)} %get-tuple-element.176), channel_id=1, source_target_pairs={{0,8},{4,12},{8,0},{12,4},{16,24},{20,28},{24,16},{28,20},{1,9},{5... | collective-permute-start | bytes 1327112 | tf_op jit(solution)/shard_map/ppermute | solution.py:862
  159.6 1.2 collective-permute-start.34
  160.8 1.5 collective-permute-start.38
  162.3 7.0 %collective-permute-done.34 = f32[19,768]{1,0:T(8,128)S(1)} collective-permute-done((f32[19,768]{1,0:T(8,128)S(1)}, f32[19,768]{1,0:T(8,128)S(1)}, u32[]{:S(2)}, u32[]{:S(2)}) %collective-permute-start.34) | collective-permute-done | bytes 58400 | tf_op jit(solution)/shard_map/ppermute | solution.py:857
  169.3 2.5 %collective-permute-start.40 = (bf16[6,3,96,128]{3,2,1,0:T(8,128)(2,1)}, bf16[6,3,96,128]{3,2,1,0:T(8,128)(2,1)S(1)}, u32[]{:S(2)}, u32[]{:S(2)}) collective-permute-start(bf16[6,3,96,128]{3,2,1,0:T(8,128)(2,1)} %get-tuple-element.190), channel_id=1, source_target_pairs={{0,8},{4,12},{8,0},{12,4},{16,24},{20,28},{24,16},{28,20},{1,9},{5... | collective-permute-start | bytes 1327112 | tf_op jit(solution)/shard_map/ppermute | solution.py:862
  171.9 1.2 add_convert_fusion.6
  174.0 1.2 collective-permute-start.37
  175.1 1.5 collective-permute-start.41
  176.8 2.7 %collective-permute-done.41 = f32[19,768]{1,0:T(8,128)S(1)} collective-permute-done((f32[19,768]{1,0:T(8,128)S(1)}, f32[19,768]{1,0:T(8,128)S(1)}, u32[]{:S(2)}, u32[]{:S(2)}) %collective-permute-start.41) | collective-permute-done | bytes 58400 | tf_op jit(solution)/shard_map/ppermute | solution.py:857
  179.5 1.5 collective-permute-start.36
  181.7 4.5 %collective-permute-done.39 = bf16[6,3,96,128]{3,2,1,0:T(8,128)(2,1)S(1)} collective-permute-done((bf16[6,3,96,128]{3,2,1,0:T(8,128)(2,1)S(1)}, bf16[6,3,96,128]{3,2,1,0:T(8,128)(2,1)S(1)}, u32[]{:S(2)}, u32[]{:S(2)}) %collective-permute-start.39) | collective-permute-done | bytes 442400 | tf_op jit(solution)/shard_map/ppermute | solution.py:857
  186.4 1.3 collective-permute-start.42
  187.7 1.5 collective-permute-start.29
  189.3 2.7 %collective-permute-start.43 = (f32[19,768]{1,0:T(8,128)S(1)}, f32[19,768]{1,0:T(8,128)S(1)}, u32[]{:S(2)}, u32[]{:S(2)}) collective-permute-start(f32[19,768]{1,0:T(8,128)S(1)} %add.138), channel_id=1, source_target_pairs={{0,8},{4,12},{8,0},{12,4},{16,24},{20,28},{24,16},{28,20},{1,9},{5... | collective-permute-start | bytes 175112 | tf_op jit(solution)/shard_map/ppermute | solution.py:857
  192.1 6.1 %collective-permute-done.43 = f32[19,768]{1,0:T(8,128)S(1)} collective-permute-done((f32[19,768]{1,0:T(8,128)S(1)}, f32[19,768]{1,0:T(8,128)S(1)}, u32[]{:S(2)}, u32[]{:S(2)}) %collective-permute-start.43) | collective-permute-done | bytes 58400 | tf_op jit(solution)/shard_map/ppermute | solution.py:857
  199.3 1.4 collective-permute-start.45
  200.7 3.4 %collective-permute-start.44 = (bf16[6,3,96,128]{3,2,1,0:T(8,128)(2,1)S(1)}, bf16[6,3,96,128]{3,2,1,0:T(8,128)(2,1)S(1)}, u32[]{:S(2)}, u32[]{:S(2)}) collective-permute-start(bf16[6,3,96,128]{3,2,1,0:T(8,128)(2,1)S(1)} %add_convert_fusion.4), channel_id=1, source_target_pairs={{8,16},{12,20},{16,8},{20,12},{9,17},{13,21},{17,9},{21,13},{10,18... | collective-permute-start | bytes 1327112 | tf_op jit(solution)/shard_map/ppermute | solution.py:862
  204.1 1.1 copy.41
  207.0 4.8 %collective-permute-done.46 = f32[19,768]{1,0:T(8,128)S(1)} collective-permute-done((f32[19,768]{1,0:T(8,128)S(1)}, f32[19,768]{1,0:T(8,128)S(1)}, u32[]{:S(2)}, u32[]{:S(2)}) %collective-permute-start.46) | collective-permute-done | bytes 58400 | tf_op jit(solution)/shard_map/ppermute | solution.py:857
  211.8 1.2 collective-permute-start.48
  214.2 2.6 %collective-permute-start.49 = (bf16[6,3,96,128]{3,2,1,0:T(8,128)(2,1)S(1)}, bf16[6,3,96,128]{3,2,1,0:T(8,128)(2,1)S(1)}, u32[]{:S(2)}, u32[]{:S(2)}) collective-permute-start(bf16[6,3,96,128]{3,2,1,0:T(8,128)(2,1)S(1)} %add_convert_fusion.1), channel_id=1, source_target_pairs={{0,8},{4,12},{8,0},{12,4},{16,24},{20,28},{24,16},{28,20},{1,9},{5... | collective-permute-start | bytes 1327112 | tf_op jit(solution)/shard_map/ppermute | solution.py:862
  216.9 1.5 collective-permute-start.47
  218.5 3.4 %collective-permute-start.50 = (bf16[6,3,96,128]{3,2,1,0:T(8,128)(2,1)S(1)}, bf16[6,3,96,128]{3,2,1,0:T(8,128)(2,1)S(1)}, u32[]{:S(2)}, u32[]{:S(2)}) collective-permute-start(bf16[6,3,96,128]{3,2,1,0:T(8,128)(2,1)S(1)} %copy-done.27), channel_id=1, source_target_pairs={{8,16},{12,20},{16,8},{20,12},{9,17},{13,21},{17,9},{21,13},{10,18... | collective-permute-start | bytes 1327112 | tf_op jit(solution)/shard_map/ppermute | solution.py:862
  223.1 2.2 collective-permute-done.47.refs_1_
  225.3 3.4 %collective-permute-done.50.refs_4_ = bf16[6,3,96,128]{3,2,1,0:T(8,128)(2,1)S(1)} collective-permute-done((bf16[6,3,96,128]{3,2,1,0:T(8,128)(2,1)S(1)}, bf16[6,3,96,128]{3,2,1,0:T(8,128)(2,1)S(1)}, u32[]{:S(2)}, u32[]{:S(2)}) %collective-permute-start.50) | collective-permute-done | bytes 442400 | tf_op jit(solution)/shard_map/ppermute | solution.py:862
  230.3 6.9 %soap.1 = (f32[24,96,96]{2,1,0:T(8,128)}, bf16[24,96,96]{2,1,0:T(8,128)(2,1)}, f32[24,96,96]{2,1,0:T(8,128)}, f32[24,96,96]{2,1,0:T(8,128)}, f32[24,96,96]{2,1,0:T(8,128)}, /*index=5*/f32[24,96,96]{2,1,0:T(8,128)}) custom-call(bf16[6,3,96,128]{3,2,1,0:T(8,128)(2,1)} %get-tuple-element.208.refs_0_, bf16[6,3,96,128]{3,2,1,0:T(8,128)(2,1)} %copy-done.41, ...), custom_call_target="tpu_custom_call" | custom-call | flops 300000000 | bytes 24000000 | tf_op jit(solution)/shard_map/soap/pallas_call | solution.py:772
  (208 shorter events, 29.4 us)
Async XLA Ops:
  2.1 12.5 %collective-permute-start.3 = (bf16[6,3,96,128]{3,2,1,0:T(8,128)(2,1)S(1)}, bf16[6,3,96,128]{3,2,1,0:T(8,128)(2,1)S(1)}, u32[]{:S(2)}, u32[]{:S(2)}) collective-permute-start(bf16[6,3,96,128]{3,2,1,0:T(8,128)(2,1)S(1)} %pack_owned.1.refs_0_), channel_id=1, source_target_pairs={{0,2},{1,3},{2,0},{3,1},{4,6},{5,7},{6,4},{7,5},{8,10},{9,11},{10,... | collective-permute-start | bytes 1327112 | tf_op jit(solution)/shard_map/ppermute | solution.py:857
  3.7 11.7 %collective-permute-start.2 = (bf16[6,3,96,128]{3,2,1,0:T(8,128)(2,1)S(1)}, bf16[6,3,96,128]{3,2,1,0:T(8,128)(2,1)}, u32[]{:S(2)}, u32[]{:S(2)}) collective-permute-start(bf16[6,3,96,128]{3,2,1,0:T(8,128)(2,1)S(1)} %pack_owned.1.refs_0_), channel_id=1, source_target_pairs={{0,4},{4,0},{8,12},{12,8},{16,20},{20,16},{24,28},{28,24},{1,5},{5... | collective-permute-start | bytes 1327112 | tf_op jit(solution)/shard_map/ppermute | solution.py:857
  5.2 13.3 %collective-permute-start.1 = (bf16[6,3,96,128]{3,2,1,0:T(8,128)(2,1)S(1)}, bf16[6,3,96,128]{3,2,1,0:T(8,128)(2,1)}, u32[]{:S(2)}, u32[]{:S(2)}) collective-permute-start(bf16[6,3,96,128]{3,2,1,0:T(8,128)(2,1)S(1)} %pack_owned.1.refs_0_), channel_id=1, source_target_pairs={{8,16},{12,20},{16,8},{20,12},{9,17},{13,21},{17,9},{21,13},{10,18... | collective-permute-start | bytes 1327112 | tf_op jit(solution)/shard_map/ppermute | solution.py:862
  8.7 11.2 %collective-permute-start = (bf16[6,3,96,128]{3,2,1,0:T(8,128)(2,1)S(1)}, bf16[6,3,96,128]{3,2,1,0:T(8,128)(2,1)}, u32[]{:S(2)}, u32[]{:S(2)}) collective-permute-start(bf16[6,3,96,128]{3,2,1,0:T(8,128)(2,1)S(1)} %pack_owned.1.refs_0_), channel_id=1, source_target_pairs={{0,8},{4,12},{8,0},{12,4},{16,24},{20,28},{24,16},{28,20},{1,9},{5... | collective-permute-start | bytes 1327112 | tf_op jit(solution)/shard_map/ppermute | solution.py:862
  8.8 15.9 %collective-permute-start.8 = (f32[1,1152]{1,0:T(1,128)}, f32[1,1152]{1,0:T(1,128)S(1)}, u32[]{:S(2)}, u32[]{:S(2)}) collective-permute-start(f32[1,1152]{1,0:T(1,128)} %param.30), channel_id=1, source_target_pairs={{0,2},{1,3},{2,0},{3,1},{4,6},{5,7},{6,4},{7,5},{8,10},{9,11},{10,... | collective-permute-start | bytes 13832 | tf_op jit(solution)/shard_map/ppermute | solution.py:857
  14.6 49.5 %copy-start.28 = (bf16[6,3,96,128]{3,2,1,0:T(8,128)(2,1)}, bf16[6,3,96,128]{3,2,1,0:T(8,128)(2,1)S(1)}, u32[]{:S(2)}) copy-start(bf16[6,3,96,128]{3,2,1,0:T(8,128)(2,1)S(1)} %collective-permute-done.3.refs_2_) | copy-start | bytes 1327108
  19.9 12.8 %collective-permute-start.6 = (bf16[6,3,96,128]{3,2,1,0:T(8,128)(2,1)}, bf16[6,3,96,128]{3,2,1,0:T(8,128)(2,1)S(1)}, u32[]{:S(2)}, u32[]{:S(2)}) collective-permute-start(bf16[6,3,96,128]{3,2,1,0:T(8,128)(2,1)} %collective-permute-done.refs_4_), channel_id=1, source_target_pairs={{8,16},{12,20},{16,8},{20,12},{9,17},{13,21},{17,9},{21,13},{10,18... | collective-permute-start | bytes 1327112 | tf_op jit(solution)/shard_map/ppermute | solution.py:862
  22.3 10.4 %collective-permute-start.4 = (bf16[6,3,96,128]{3,2,1,0:T(8,128)(2,1)}, bf16[6,3,96,128]{3,2,1,0:T(8,128)(2,1)S(1)}, u32[]{:S(2)}, u32[]{:S(2)}) collective-permute-start(bf16[6,3,96,128]{3,2,1,0:T(8,128)(2,1)} %collective-permute-done.refs_4_), channel_id=1, source_target_pairs={{0,4},{4,0},{8,12},{12,8},{16,20},{20,16},{24,28},{28,24},{1,5},{5... | collective-permute-start | bytes 1327112 | tf_op jit(solution)/shard_map/ppermute | solution.py:857
  22.9 9.8 %collective-permute-start.5 = (bf16[6,3,96,128]{3,2,1,0:T(8,128)(2,1)}, bf16[6,3,96,128]{3,2,1,0:T(8,128)(2,1)S(1)}, u32[]{:S(2)}, u32[]{:S(2)}) collective-permute-start(bf16[6,3,96,128]{3,2,1,0:T(8,128)(2,1)} %collective-permute-done.2.refs_1_), channel_id=1, source_target_pairs={{0,2},{1,3},{2,0},{3,1},{4,6},{5,7},{6,4},{7,5},{8,10},{9,11},{10,... | collective-permute-start | bytes 1327112 | tf_op jit(solution)/shard_map/ppermute | solution.py:857
  23.4 9.3 %collective-permute-start.7 = (bf16[6,3,96,128]{3,2,1,0:T(8,128)(2,1)}, bf16[6,3,96,128]{3,2,1,0:T(8,128)(2,1)S(1)}, u32[]{:S(2)}, u32[]{:S(2)}) collective-permute-start(bf16[6,3,96,128]{3,2,1,0:T(8,128)(2,1)} %collective-permute-done.1), channel_id=1, source_target_pairs={{8,0},{12,4},{16,24},{20,28},{9,1},{13,5},{17,25},{21,29},{10,2},{... | collective-permute-start | bytes 1327112 | tf_op jit(solution)/shard_map/ppermute | solution.py:862
  32.7 38.4 %copy-start.31 = (bf16[6,3,96,128]{3,2,1,0:T(8,128)(2,1)}, bf16[6,3,96,128]{3,2,1,0:T(8,128)(2,1)S(1)}, u32[]{:S(2)}) copy-start(bf16[6,3,96,128]{3,2,1,0:T(8,128)(2,1)S(1)} %collective-permute-done.5.refs_3_) | copy-start | bytes 1327108
  33.7 39.2 %copy-start.17 = (bf16[6,3,96,128]{3,2,1,0:T(8,128)(2,1)}, bf16[6,3,96,128]{3,2,1,0:T(8,128)(2,1)S(1)}, u32[]{:S(2)}) copy-start(bf16[6,3,96,128]{3,2,1,0:T(8,128)(2,1)S(1)} %add.131.refs_8_) | copy-start | bytes 1327108
  33.7 8.8 %collective-permute-start.10 = (bf16[6,3,96,128]{3,2,1,0:T(8,128)(2,1)S(1)}, bf16[6,3,96,128]{3,2,1,0:T(8,128)(2,1)S(1)}, u32[]{:S(2)}, u32[]{:S(2)}) collective-permute-start(bf16[6,3,96,128]{3,2,1,0:T(8,128)(2,1)S(1)} %add.131.refs_8_), channel_id=1, source_target_pairs={{0,2},{1,3},{2,0},{3,1},{4,6},{5,7},{6,4},{7,5},{8,10},{9,11},{10,... | collective-permute-start | bytes 1327112 | tf_op jit(solution)/shard_map/ppermute | solution.py:857
  34.6 8.4 %collective-permute-start.9 = (bf16[6,3,96,128]{3,2,1,0:T(8,128)(2,1)S(1)}, bf16[6,3,96,128]{3,2,1,0:T(8,128)(2,1)S(1)}, u32[]{:S(2)}, u32[]{:S(2)}) collective-permute-start(bf16[6,3,96,128]{3,2,1,0:T(8,128)(2,1)S(1)} %add.131.refs_8_), channel_id=1, source_target_pairs={{0,4},{4,0},{8,12},{12,8},{16,20},{20,16},{24,28},{28,24},{1,5},{5... | collective-permute-start | bytes 1327112 | tf_op jit(solution)/shard_map/ppermute | solution.py:857
  36.1 14.9 %collective-permute-start.11 = (bf16[6,3,96,128]{3,2,1,0:T(8,128)(2,1)S(1)}, bf16[6,3,96,128]{3,2,1,0:T(8,128)(2,1)S(1)}, u32[]{:S(2)}, u32[]{:S(2)}) collective-permute-start(bf16[6,3,96,128]{3,2,1,0:T(8,128)(2,1)S(1)} %collective-permute-done.6), channel_id=1, source_target_pairs={{8,0},{12,4},{16,24},{20,28},{9,1},{13,5},{17,25},{21,29},{10,2},{... | collective-permute-start | bytes 1327112 | tf_op jit(solution)/shard_map/ppermute | solution.py:862
  40.6 19.6 %collective-permute-start.14 = (bf16[6,3,96,128]{3,2,1,0:T(8,128)(2,1)S(1)}, bf16[6,3,96,128]{3,2,1,0:T(8,128)(2,1)S(1)}, u32[]{:S(2)}, u32[]{:S(2)}) collective-permute-start(bf16[6,3,96,128]{3,2,1,0:T(8,128)(2,1)S(1)} %collective-permute-done.3.refs_2_), channel_id=1, source_target_pairs={{0,8},{4,12},{8,0},{12,4},{16,24},{20,28},{24,16},{28,20},{1,9},{5... | collective-permute-start | bytes 1327112 | tf_op jit(solution)/shard_map/ppermute | solution.py:862
  43.2 27.9 %copy-start.33 = (bf16[6,3,96,128]{3,2,1,0:T(8,128)(2,1)}, bf16[6,3,96,128]{3,2,1,0:T(8,128)(2,1)S(1)}, u32[]{:S(2)}) copy-start(bf16[6,3,96,128]{3,2,1,0:T(8,128)(2,1)S(1)} %collective-permute-done.9.refs_9_) | copy-start | bytes 1327108
  52.1 20.8 %copy-start.18 = (bf16[6,3,96,128]{3,2,1,0:T(8,128)(2,1)}, bf16[6,3,96,128]{3,2,1,0:T(8,128)(2,1)S(1)}, u32[]{:S(2)}) copy-start(bf16[6,3,96,128]{3,2,1,0:T(8,128)(2,1)S(1)} %add.132.refs_12_) | copy-start | bytes 1327108
  52.2 9.5 %collective-permute-start.13 = (bf16[6,3,96,128]{3,2,1,0:T(8,128)(2,1)S(1)}, bf16[6,3,96,128]{3,2,1,0:T(8,128)(2,1)S(1)}, u32[]{:S(2)}, u32[]{:S(2)}) collective-permute-start(bf16[6,3,96,128]{3,2,1,0:T(8,128)(2,1)S(1)} %add.132.refs_12_), channel_id=1, source_target_pairs={{0,2},{1,3},{2,0},{3,1},{4,6},{5,7},{6,4},{7,5},{8,10},{9,11},{10,... | collective-permute-start | bytes 1327112 | tf_op jit(solution)/shard_map/ppermute | solution.py:857
  52.7 10.0 %collective-permute-start.12 = (bf16[6,3,96,128]{3,2,1,0:T(8,128)(2,1)S(1)}, bf16[6,3,96,128]{3,2,1,0:T(8,128)(2,1)S(1)}, u32[]{:S(2)}, u32[]{:S(2)}) collective-permute-start(bf16[6,3,96,128]{3,2,1,0:T(8,128)(2,1)S(1)} %add.132.refs_12_), channel_id=1, source_target_pairs={{0,4},{4,0},{8,12},{12,8},{16,20},{20,16},{24,28},{28,24},{1,5},{5... | collective-permute-start | bytes 1327112 | tf_op jit(solution)/shard_map/ppermute | solution.py:857
  53.3 15.9 %collective-permute-start.20 = (bf16[6,3,96,128]{3,2,1,0:T(8,128)(2,1)S(1)}, bf16[6,3,96,128]{3,2,1,0:T(8,128)(2,1)S(1)}, u32[]{:S(2)}, u32[]{:S(2)}) collective-permute-start(bf16[6,3,96,128]{3,2,1,0:T(8,128)(2,1)S(1)} %collective-permute-done.5.refs_3_), channel_id=1, source_target_pairs={{0,8},{4,12},{8,0},{12,4},{16,24},{20,28},{24,16},{28,20},{1,9},{5... | collective-permute-start | bytes 1327112 | tf_op jit(solution)/shard_map/ppermute | solution.py:862
  55.7 13.4 %collective-permute-start.19 = (bf16[6,3,96,128]{3,2,1,0:T(8,128)(2,1)S(1)}, bf16[6,3,96,128]{3,2,1,0:T(8,128)(2,1)S(1)}, u32[]{:S(2)}, u32[]{:S(2)}) collective-permute-start(bf16[6,3,96,128]{3,2,1,0:T(8,128)(2,1)S(1)} %collective-permute-done.9.refs_9_), channel_id=1, source_target_pairs={{0,2},{1,3},{2,0},{3,1},{4,6},{5,7},{6,4},{7,5},{8,10},{9,11},{10,... | collective-permute-start | bytes 1327112 | tf_op jit(solution)/shard_map/ppermute | solution.py:857
  62.8 8.3 %collective-permute-start.18 = (bf16[6,3,96,128]{3,2,1,0:T(8,128)(2,1)S(1)}, bf16[6,3,96,128]{3,2,1,0:T(8,128)(2,1)S(1)}, u32[]{:S(2)}, u32[]{:S(2)}) collective-permute-start(bf16[6,3,96,128]{3,2,1,0:T(8,128)(2,1)S(1)} %collective-permute-done.13.refs_14_), channel_id=1, source_target_pairs={{0,4},{4,0},{8,12},{12,8},{16,20},{20,16},{24,28},{28,24},{1,5},{5... | collective-permute-start | bytes 1327112 | tf_op jit(solution)/shard_map/ppermute | solution.py:857
  63.3 5.8 %collective-permute-start.15 = (bf16[133,768]{1,0:T(8,128)(2,1)S(1)}, bf16[133,768]{1,0:T(8,128)(2,1)S(1)}, u32[]{:S(2)}, u32[]{:S(2)}) collective-permute-start(bf16[133,768]{1,0:T(8,128)(2,1)S(1)} %bitcast.55), channel_id=1, source_target_pairs={{0,2},{1,3},{2,0},{3,1},{4,6},{5,7},{6,4},{7,5},{8,10},{9,11},{10,... | collective-permute-start | bytes 612872 | tf_op jit(solution)/shard_map/ppermute | solution.py:857
  64.2 18.6 %collective-permute-start.16 = (bf16[133,768]{1,0:T(8,128)(2,1)S(1)}, bf16[133,768]{1,0:T(8,128)(2,1)S(1)}, u32[]{:S(2)}, u32[]{:S(2)}) collective-permute-start(bf16[133,768]{1,0:T(8,128)(2,1)S(1)} %bitcast.47), channel_id=1, source_target_pairs={{0,1},{1,0},{2,3},{3,2},{4,5},{5,4},{6,7},{7,6},{8,9},{9,8},{10,11... | collective-permute-start | bytes 612872 | tf_op jit(solution)/shard_map/ppermute | solution.py:857
  69.1 13.7 %collective-permute-start.17 = (bf16[133,768]{1,0:T(8,128)(2,1)S(1)}, bf16[133,768]{1,0:T(8,128)(2,1)S(1)}, u32[]{:S(2)}, u32[]{:S(2)}) collective-permute-start(bf16[133,768]{1,0:T(8,128)(2,1)S(1)} %collective-permute-done.15.xb), channel_id=1, source_target_pairs={{0,1},{1,0},{2,3},{3,2},{4,5},{5,4},{6,7},{7,6},{8,9},{9,8},{10,11... | collective-permute-start | bytes 612872 | tf_op jit(solution)/shard_map/ppermute | solution.py:857
  71.9 10.9 %collective-permute-start.21 = (bf16[133,768]{1,0:T(8,128)(2,1)}, bf16[133,768]{1,0:T(8,128)(2,1)S(1)}, u32[]{:S(2)}, u32[]{:S(2)}) collective-permute-start(bf16[133,768]{1,0:T(8,128)(2,1)} %bitcast.38), channel_id=1, source_target_pairs={{0,2},{1,3},{2,0},{3,1},{4,6},{5,7},{6,4},{7,5},{8,10},{9,11},{10,... | collective-permute-start | bytes 612872 | tf_op jit(solution)/shard_map/ppermute | solution.py:857
  94.1 2.5 %collective-permute-start.22 = (bf16[576,768]{1,0:T(8,128)(2,1)S(1)}, bf16[576,768]{1,0:T(8,128)(2,1)S(1)}, u32[]{:S(2)}, u32[]{:S(2)}) collective-permute-start(bf16[576,768]{1,0:T(8,128)(2,1)S(1)} %get-tuple-element.146.mine_ref), channel_id=1, source_target_pairs={{0,1},{1,0},{2,3},{3,2},{4,5},{5,4},{6,7},{7,6},{8,9},{9,8},{10,11... | collective-permute-start | bytes 2654216 | tf_op jit(solution)/shard_map/ppermute | solution.py:857
  103.3 3.1 %collective-permute-start.23 = (bf16[576,768]{1,0:T(8,128)(2,1)S(1)}, bf16[576,768]{1,0:T(8,128)(2,1)S(1)}, u32[]{:S(2)}, u32[]{:S(2)}) collective-permute-start(bf16[576,768]{1,0:T(8,128)(2,1)S(1)} %get-tuple-element.150.mine_ref), channel_id=1, source_target_pairs={{0,1},{1,0},{2,3},{3,2},{4,5},{5,4},{6,7},{7,6},{8,9},{9,8},{10,11... | collective-permute-start | bytes 2654216 | tf_op jit(solution)/shard_map/ppermute | solution.py:857
  103.5 2.6 %collective-permute-start.24 = (bf16[133,768]{1,0:T(8,128)(2,1)S(1)}, bf16[133,768]{1,0:T(8,128)(2,1)S(1)}, u32[]{:S(2)}, u32[]{:S(2)}) collective-permute-start(bf16[133,768]{1,0:T(8,128)(2,1)S(1)} %bitcast.43), channel_id=1, source_target_pairs={{0,1},{1,0},{2,3},{3,2},{4,5},{5,4},{6,7},{7,6},{8,9},{9,8},{10,11... | collective-permute-start | bytes 612872 | tf_op jit(solution)/shard_map/ppermute | solution.py:857
  104.0 2.4 %collective-permute-start.25 = (bf16[133,768]{1,0:T(8,128)(2,1)S(1)}, bf16[133,768]{1,0:T(8,128)(2,1)S(1)}, u32[]{:S(2)}, u32[]{:S(2)}) collective-permute-start(bf16[133,768]{1,0:T(8,128)(2,1)S(1)} %collective-permute-done.21.later_ref.cb), channel_id=1, source_target_pairs={{0,1},{1,0},{2,3},{3,2},{4,5},{5,4},{6,7},{7,6},{8,9},{9,8},{10,11... | collective-permute-start | bytes 612872 | tf_op jit(solution)/shard_map/ppermute | solution.py:857
  113.7 5.0 %collective-permute-start.27 = (bf16[576,768]{1,0:T(8,128)(2,1)S(1)}, bf16[576,768]{1,0:T(8,128)(2,1)S(1)}, u32[]{:S(2)}, u32[]{:S(2)}) collective-permute-start(bf16[576,768]{1,0:T(8,128)(2,1)S(1)} %get-tuple-element.159.mine_ref), channel_id=1, source_target_pairs={{0,1},{1,0},{2,3},{3,2},{4,5},{5,4},{6,7},{7,6},{8,9},{9,8},{10,11... | collective-permute-start | bytes 2654216 | tf_op jit(solution)/shard_map/ppermute | solution.py:857
  113.9 26.1 %collective-permute-start.26 = (bf16[133,768]{1,0:T(8,128)(2,1)S(1)}, bf16[133,768]{1,0:T(8,128)(2,1)S(1)}, u32[]{:S(2)}, u32[]{:S(2)}) collective-permute-start(bf16[133,768]{1,0:T(8,128)(2,1)S(1)} %get-tuple-element.257), channel_id=1, source_target_pairs={{0,2},{1,3},{2,0},{3,1},{4,6},{5,7},{6,4},{7,5},{8,10},{9,11},{10,... | collective-permute-start | bytes 612872 | tf_op jit(solution)/shard_map/ppermute | solution.py:857
  135.3 5.0 %collective-permute-start.28 = (bf16[288,768]{1,0:T(8,128)(2,1)}, bf16[288,768]{1,0:T(8,128)(2,1)S(1)}, u32[]{:S(2)}, u32[]{:S(2)}) collective-permute-start(bf16[288,768]{1,0:T(8,128)(2,1)} %get-tuple-element.168), channel_id=1, source_target_pairs={{0,1},{1,0},{2,3},{3,2},{4,5},{5,4},{6,7},{7,6},{8,9},{9,8},{10,11... | collective-permute-start | bytes 1327112 | tf_op jit(solution)/shard_map/ppermute | solution.py:857
  141.9 16.8 %collective-permute-start.33 = (f32[16,768]{1,0:T(8,128)S(1)}, f32[16,768]{1,0:T(8,128)S(1)}, u32[]{:S(2)}, u32[]{:S(2)}) collective-permute-start(f32[16,768]{1,0:T(8,128)S(1)} %pad_maximum_fusion.3), channel_id=1, source_target_pairs={{0,1},{1,0},{2,3},{3,2},{4,5},{5,4},{6,7},{7,6},{8,9},{9,8},{10,11... | collective-permute-start | bytes 147464 | tf_op jit(solution)/shard_map/ppermute | solution.py:857
  154.7 22.0 %copy-start.26 = (bf16[6,3,96,128]{3,2,1,0:T(8,128)(2,1)S(1)}, bf16[6,3,96,128]{3,2,1,0:T(8,128)(2,1)}, u32[]{:S(2)}) copy-start(bf16[6,3,96,128]{3,2,1,0:T(8,128)(2,1)} %get-tuple-element.183) | copy-start | bytes 1327108
  154.7 31.6 %copy-start.22 = (bf16[6,3,96,128]{3,2,1,0:T(8,128)(2,1)S(1)}, bf16[6,3,96,128]{3,2,1,0:T(8,128)(2,1)}, u32[]{:S(2)}) copy-start(bf16[6,3,96,128]{3,2,1,0:T(8,128)(2,1)} %get-tuple-element.186) | copy-start | bytes 1327108
  154.7 17.1 %collective-permute-start.30 = (bf16[6,3,96,128]{3,2,1,0:T(8,128)(2,1)}, bf16[6,3,96,128]{3,2,1,0:T(8,128)(2,1)S(1)}, u32[]{:S(2)}, u32[]{:S(2)}) collective-permute-start(bf16[6,3,96,128]{3,2,1,0:T(8,128)(2,1)} %get-tuple-element.174), channel_id=1, source_target_pairs={{0,4},{4,0},{8,12},{12,8},{16,20},{20,16},{24,28},{28,24},{1,5},{5... | collective-permute-start | bytes 1327112 | tf_op jit(solution)/shard_map/ppermute | solution.py:857
  155.3 16.5 %collective-permute-start.31 = (bf16[6,3,96,128]{3,2,1,0:T(8,128)(2,1)}, bf16[6,3,96,128]{3,2,1,0:T(8,128)(2,1)S(1)}, u32[]{:S(2)}, u32[]{:S(2)}) collective-permute-start(bf16[6,3,96,128]{3,2,1,0:T(8,128)(2,1)} %get-tuple-element.175), channel_id=1, source_target_pairs={{0,2},{1,3},{2,0},{3,1},{4,6},{5,7},{6,4},{7,5},{8,10},{9,11},{10,... | collective-permute-start | bytes 1327112 | tf_op jit(solution)/shard_map/ppermute | solution.py:857
  155.9 16.0 %collective-permute-start.32 = (bf16[6,3,96,128]{3,2,1,0:T(8,128)(2,1)}, bf16[6,3,96,128]{3,2,1,0:T(8,128)(2,1)S(1)}, u32[]{:S(2)}, u32[]{:S(2)}) collective-permute-start(bf16[6,3,96,128]{3,2,1,0:T(8,128)(2,1)} %get-tuple-element.176), channel_id=1, source_target_pairs={{0,8},{4,12},{8,0},{12,4},{16,24},{20,28},{24,16},{28,20},{1,9},{5... | collective-permute-start | bytes 1327112 | tf_op jit(solution)/shard_map/ppermute | solution.py:862
  158.7 15.3 %copy-start.49 = (bf16[6,3,96,128]{3,2,1,0:T(8,128)(2,1)S(1)}, bf16[6,3,96,128]{3,2,1,0:T(8,128)(2,1)}, u32[]{:S(2)}) copy-start(bf16[6,3,96,128]{3,2,1,0:T(8,128)(2,1)} %get-tuple-element.185) | copy-start | bytes 1327108
  159.6 9.8 %collective-permute-start.34 = (f32[19,768]{1,0:T(8,128)S(1)}, f32[19,768]{1,0:T(8,128)S(1)}, u32[]{:S(2)}, u32[]{:S(2)}) collective-permute-start(f32[19,768]{1,0:T(8,128)S(1)} %pad_maximum_fusion.2), channel_id=1, source_target_pairs={{0,2},{1,3},{2,0},{3,1},{4,6},{5,7},{6,4},{7,5},{8,10},{9,11},{10,... | collective-permute-start | bytes 175112 | tf_op jit(solution)/shard_map/ppermute | solution.py:857
  160.8 20.2 %collective-permute-start.38 = (bf16[6,3,96,128]{3,2,1,0:T(8,128)(2,1)}, bf16[6,3,96,128]{3,2,1,0:T(8,128)(2,1)S(1)}, u32[]{:S(2)}, u32[]{:S(2)}) collective-permute-start(bf16[6,3,96,128]{3,2,1,0:T(8,128)(2,1)} %get-tuple-element.187), channel_id=1, source_target_pairs={{0,4},{4,0},{8,12},{12,8},{16,20},{20,16},{24,28},{28,24},{1,5},{5... | collective-permute-start | bytes 1327112 | tf_op jit(solution)/shard_map/ppermute | solution.py:857
  169.3 12.4 %collective-permute-start.40 = (bf16[6,3,96,128]{3,2,1,0:T(8,128)(2,1)}, bf16[6,3,96,128]{3,2,1,0:T(8,128)(2,1)S(1)}, u32[]{:S(2)}, u32[]{:S(2)}) collective-permute-start(bf16[6,3,96,128]{3,2,1,0:T(8,128)(2,1)} %get-tuple-element.190), channel_id=1, source_target_pairs={{0,8},{4,12},{8,0},{12,4},{16,24},{20,28},{24,16},{28,20},{1,9},{5... | collective-permute-start | bytes 1327112 | tf_op jit(solution)/shard_map/ppermute | solution.py:862
  173.0 18.9 %copy-start.25 = (bf16[6,3,96,128]{3,2,1,0:T(8,128)(2,1)S(1)}, bf16[6,3,96,128]{3,2,1,0:T(8,128)(2,1)}, u32[]{:S(2)}) copy-start(bf16[6,3,96,128]{3,2,1,0:T(8,128)(2,1)} %get-tuple-element.173) | copy-start | bytes 1327108
  173.1 13.2 %collective-permute-start.39 = (bf16[6,3,96,128]{3,2,1,0:T(8,128)(2,1)S(1)}, bf16[6,3,96,128]{3,2,1,0:T(8,128)(2,1)S(1)}, u32[]{:S(2)}, u32[]{:S(2)}) collective-permute-start(bf16[6,3,96,128]{3,2,1,0:T(8,128)(2,1)S(1)} %add_convert_fusion.6), channel_id=1, source_target_pairs={{0,2},{1,3},{2,0},{3,1},{4,6},{5,7},{6,4},{7,5},{8,10},{9,11},{10,... | collective-permute-start | bytes 1327112 | tf_op jit(solution)/shard_map/ppermute | solution.py:857
  174.0 25.0 %collective-permute-start.37 = (bf16[6,3,96,128]{3,2,1,0:T(8,128)(2,1)S(1)}, bf16[6,3,96,128]{3,2,1,0:T(8,128)(2,1)S(1)}, u32[]{:S(2)}, u32[]{:S(2)}) collective-permute-start(bf16[6,3,96,128]{3,2,1,0:T(8,128)(2,1)S(1)} %copy-done.49), channel_id=1, source_target_pairs={{0,2},{1,3},{2,0},{3,1},{4,6},{5,7},{6,4},{7,5},{8,10},{9,11},{10,... | collective-permute-start | bytes 1327112 | tf_op jit(solution)/shard_map/ppermute | solution.py:857
  175.1 4.4 %collective-permute-start.41 = (f32[19,768]{1,0:T(8,128)S(1)}, f32[19,768]{1,0:T(8,128)S(1)}, u32[]{:S(2)}, u32[]{:S(2)}) collective-permute-start(f32[19,768]{1,0:T(8,128)S(1)} %add.134), channel_id=1, source_target_pairs={{0,4},{4,0},{8,12},{12,8},{16,20},{20,16},{24,28},{28,24},{1,5},{5... | collective-permute-start | bytes 175112 | tf_op jit(solution)/shard_map/ppermute | solution.py:857
  176.8 22.2 %copy-start.29 = (bf16[6,3,96,128]{3,2,1,0:T(8,128)(2,1)S(1)}, bf16[6,3,96,128]{3,2,1,0:T(8,128)(2,1)}, u32[]{:S(2)}) copy-start(bf16[6,3,96,128]{3,2,1,0:T(8,128)(2,1)} %get-tuple-element.182) | copy-start | bytes 1327108
  179.5 19.5 %collective-permute-start.36 = (bf16[6,3,96,128]{3,2,1,0:T(8,128)(2,1)S(1)}, bf16[6,3,96,128]{3,2,1,0:T(8,128)(2,1)S(1)}, u32[]{:S(2)}, u32[]{:S(2)}) collective-permute-start(bf16[6,3,96,128]{3,2,1,0:T(8,128)(2,1)S(1)} %add_convert_fusion.7), channel_id=1, source_target_pairs={{0,4},{4,0},{8,12},{12,8},{16,20},{20,16},{24,28},{28,24},{1,5},{5... | collective-permute-start | bytes 1327112 | tf_op jit(solution)/shard_map/ppermute | solution.py:857
  186.4 12.6 %collective-permute-start.42 = (bf16[6,3,96,128]{3,2,1,0:T(8,128)(2,1)S(1)}, bf16[6,3,96,128]{3,2,1,0:T(8,128)(2,1)S(1)}, u32[]{:S(2)}, u32[]{:S(2)}) collective-permute-start(bf16[6,3,96,128]{3,2,1,0:T(8,128)(2,1)S(1)} %add_convert_fusion.5), channel_id=1, source_target_pairs={{0,8},{4,12},{24,16},{28,20},{1,9},{5,13},{25,17},{29,21},{2,10},{... | collective-permute-start | bytes 1327112 | tf_op jit(solution)/shard_map/ppermute | solution.py:862
  187.7 25.3 %collective-permute-start.29 = (bf16[6,3,96,128]{3,2,1,0:T(8,128)(2,1)S(1)}, bf16[6,3,96,128]{3,2,1,0:T(8,128)(2,1)S(1)}, u32[]{:S(2)}, u32[]{:S(2)}) collective-permute-start(bf16[6,3,96,128]{3,2,1,0:T(8,128)(2,1)S(1)} %copy-done.48), channel_id=1, source_target_pairs={{0,4},{4,0},{8,12},{12,8},{16,20},{20,16},{24,28},{28,24},{1,5},{5... | collective-permute-start | bytes 1327112 | tf_op jit(solution)/shard_map/ppermute | solution.py:857
  189.3 8.9 %collective-permute-start.43 = (f32[19,768]{1,0:T(8,128)S(1)}, f32[19,768]{1,0:T(8,128)S(1)}, u32[]{:S(2)}, u32[]{:S(2)}) collective-permute-start(f32[19,768]{1,0:T(8,128)S(1)} %add.138), channel_id=1, source_target_pairs={{0,8},{4,12},{8,0},{12,4},{16,24},{20,28},{24,16},{28,20},{1,9},{5... | collective-permute-start | bytes 175112 | tf_op jit(solution)/shard_map/ppermute | solution.py:857
  198.1 14.9 %collective-permute-start.35 = (bf16[6,3,96,128]{3,2,1,0:T(8,128)(2,1)S(1)}, bf16[6,3,96,128]{3,2,1,0:T(8,128)(2,1)S(1)}, u32[]{:S(2)}, u32[]{:S(2)}) collective-permute-start(bf16[6,3,96,128]{3,2,1,0:T(8,128)(2,1)S(1)} %add_convert_fusion.8), channel_id=1, source_target_pairs={{0,2},{1,3},{2,0},{3,1},{4,6},{5,7},{6,4},{7,5},{8,10},{9,11},{10,... | collective-permute-start | bytes 1327112 | tf_op jit(solution)/shard_map/ppermute | solution.py:857
  199.3 13.8 %collective-permute-start.45 = (bf16[6,3,96,128]{3,2,1,0:T(8,128)(2,1)S(1)}, bf16[6,3,96,128]{3,2,1,0:T(8,128)(2,1)S(1)}, u32[]{:S(2)}, u32[]{:S(2)}) collective-permute-start(bf16[6,3,96,128]{3,2,1,0:T(8,128)(2,1)S(1)} %add_convert_fusion.4), channel_id=1, source_target_pairs={{0,8},{4,12},{24,16},{28,20},{1,9},{5,13},{25,17},{29,21},{2,10},{... | collective-permute-start | bytes 1327112 | tf_op jit(solution)/shard_map/ppermute | solution.py:862
  200.7 12.3 %collective-permute-start.44 = (bf16[6,3,96,128]{3,2,1,0:T(8,128)(2,1)S(1)}, bf16[6,3,96,128]{3,2,1,0:T(8,128)(2,1)S(1)}, u32[]{:S(2)}, u32[]{:S(2)}) collective-permute-start(bf16[6,3,96,128]{3,2,1,0:T(8,128)(2,1)S(1)} %add_convert_fusion.4), channel_id=1, source_target_pairs={{8,16},{12,20},{16,8},{20,12},{9,17},{13,21},{17,9},{21,13},{10,18... | collective-permute-start | bytes 1327112 | tf_op jit(solution)/shard_map/ppermute | solution.py:862
  205.2 6.6 %collective-permute-start.46 = (f32[19,768]{1,0:T(8,128)S(1)}, f32[19,768]{1,0:T(8,128)S(1)}, u32[]{:S(2)}, u32[]{:S(2)}) collective-permute-start(f32[19,768]{1,0:T(8,128)S(1)} %add.141), channel_id=1, source_target_pairs={{0,16},{4,20},{8,24},{12,28},{16,0},{20,4},{24,8},{28,12},{1,17},{... | collective-permute-start | bytes 175112 | tf_op jit(solution)/shard_map/ppermute | solution.py:857
  211.8 10.7 %collective-permute-start.48 = (bf16[6,3,96,128]{3,2,1,0:T(8,128)(2,1)}, bf16[6,3,96,128]{3,2,1,0:T(8,128)(2,1)}, u32[]{:S(2)}, u32[]{:S(2)}) collective-permute-start(bf16[6,3,96,128]{3,2,1,0:T(8,128)(2,1)} %add_convert_fusion.2), channel_id=1, source_target_pairs={{0,2},{1,3},{2,0},{3,1},{4,6},{5,7},{6,4},{7,5},{8,10},{9,11},{10,... | collective-permute-start | bytes 1327112 | tf_op jit(solution)/shard_map/ppermute | solution.py:857
  214.0 15.6 %copy-start.43 = (f32[16,768]{1,0:T(8,128)S(1)}, f32[16,768]{1,0:T(8,128)}, u32[]{:S(2)}) copy-start(f32[16,768]{1,0:T(8,128)} %param.34) | copy-start | bytes 147460
  214.0 15.6 %copy-start.44 = (f32[16,768]{1,0:T(8,128)S(1)}, f32[16,768]{1,0:T(8,128)}, u32[]{:S(2)}) copy-start(f32[16,768]{1,0:T(8,128)} %param.35) | copy-start | bytes 147460
  214.2 8.9 %collective-permute-start.49 = (bf16[6,3,96,128]{3,2,1,0:T(8,128)(2,1)S(1)}, bf16[6,3,96,128]{3,2,1,0:T(8,128)(2,1)S(1)}, u32[]{:S(2)}, u32[]{:S(2)}) collective-permute-start(bf16[6,3,96,128]{3,2,1,0:T(8,128)(2,1)S(1)} %add_convert_fusion.1), channel_id=1, source_target_pairs={{0,8},{4,12},{8,0},{12,4},{16,24},{20,28},{24,16},{28,20},{1,9},{5... | collective-permute-start | bytes 1327112 | tf_op jit(solution)/shard_map/ppermute | solution.py:862
  216.9 8.4 %collective-permute-start.47 = (bf16[6,3,96,128]{3,2,1,0:T(8,128)(2,1)S(1)}, bf16[6,3,96,128]{3,2,1,0:T(8,128)(2,1)S(1)}, u32[]{:S(2)}, u32[]{:S(2)}) collective-permute-start(bf16[6,3,96,128]{3,2,1,0:T(8,128)(2,1)S(1)} %add_convert_fusion.3), channel_id=1, source_target_pairs={{0,4},{4,0},{8,12},{12,8},{16,20},{20,16},{24,28},{28,24},{1,5},{5... | collective-permute-start | bytes 1327112 | tf_op jit(solution)/shard_map/ppermute | solution.py:857
  218.5 10.2 %collective-permute-start.50 = (bf16[6,3,96,128]{3,2,1,0:T(8,128)(2,1)S(1)}, bf16[6,3,96,128]{3,2,1,0:T(8,128)(2,1)S(1)}, u32[]{:S(2)}, u32[]{:S(2)}) collective-permute-start(bf16[6,3,96,128]{3,2,1,0:T(8,128)(2,1)S(1)} %copy-done.27), channel_id=1, source_target_pairs={{8,16},{12,20},{16,8},{20,12},{9,17},{13,21},{17,9},{21,13},{10,18... | collective-permute-start | bytes 1327112 | tf_op jit(solution)/shard_map/ppermute | solution.py:862
  228.7 8.4 %collective-permute-start.51 = (bf16[133,768]{1,0:T(8,128)(2,1)S(1)}, bf16[133,768]{1,0:T(8,128)(2,1)S(1)}, u32[]{:S(2)}, u32[]{:S(2)}) collective-permute-start(bf16[133,768]{1,0:T(8,128)(2,1)S(1)} %get-tuple-element.255), channel_id=1, source_target_pairs={{0,2},{1,3},{2,0},{3,1},{4,6},{5,7},{6,4},{7,5},{8,10},{9,11},{10,... | collective-permute-start | bytes 612872 | tf_op jit(solution)/shard_map/ppermute | solution.py:857
  (38 other events, 243.2 us)

commit v6 on v5

--- a/solution.py
+++ b/solution.py
@@ -212,7 +212,7 @@
     )(pos, me, *pieces)
 
 
-def product(left, right, out, width=256):
+def product(left, right, out, width=384):
     def step(i, carry):
         col = pl.multiple_of(i * width, width)
         out[pl.ds(col, width), :] = inner_rows(left[:, pl.ds(col, width)], right[...]).astype(BF)
@@ -637,7 +637,7 @@
         share = dot_back(dproj_ref[...], wqkv_ref[...]).astype(BF)
         part_ref[...] = share[:own]
         send_ref[...] = share[own:]
-        product(ctx_ref, d1b_ref, go_ref, 128)
+        product(ctx_ref, d1b_ref, go_ref)
         product(x_ref, dproj_ref, gq_ref)
 
 

time: 242 us -> 241 us (level)
  no operation moved by 1% of the time
where the time goes in v6:
time: 241 us; the launch traced here: 237 us
  waiting for transfers between devices  72.4 us (30%)
  Pallas kernels  71.9 us (30%)
  starting transfers between devices  65.3 us (27%)
  local copies, waits for them, and re-layouts  16.4 us (7%)
  other arithmetic  8.47 us (4%)
  between operations  2.69 us (1%)
    ppermute x38, waiting for transfers between devices, swap(): return lambda v: lax.ppermute(v, axis, xor_pairs(size, step))  52.6 us
    ppermute x38, starting transfers between devices, swap(): return lambda v: lax.ppermute(v, axis, xor_pairs(size, step))  33.7 us
    ppermute x14, starting transfers between devices, along_z(): return lambda v: lax.ppermute(v, 'dp', z_pairs(pairs))  31.6 us
    ppermute x14, waiting for transfers between devices, along_z(): return lambda v: lax.ppermute(v, 'dp', z_pairs(pairs))  19.8 us
    unnamed x106, local copies, waits for them, and re-layouts  12.9 us
    pallas_call x1, Pallas kernels, attend_back(): pl.pallas_call(attend_back_body, grid=(pairs,), out_shape=(sds((rows // 2...  12.9 us
    pallas_call x1, Pallas kernels, pack_grads(): pl.pallas_call(functools.partial(pack_body, places), out_shape=(sds((8, 1...  12 us
    pallas_call x1, Pallas kernels, build_weights(): pl.pallas_call(functools.partial(weights_body, len(pieces), places), out_...  9.86 us
  transfers between devices with their start and end apart: 52, of which 24 were waited for; matrix products, arithmetic and copies ran while one was open for 6% of the time, Pallas kernels for 20%

profile of v6, /device:TPU:8, one launch (start us, length us, event | category | flops | bytes accessed | tf_op | source)
XLA Modules:
  0.0 237.2 jit_solution(6042073484601333774)
XLA Ops:
  0.7 1.3 copy-done.3
  2.1 1.6 collective-permute-start.3
  3.7 1.5 collective-permute-start.2
  5.2 3.5 %collective-permute-start.1 = (bf16[6,3,96,128]{3,2,1,0:T(8,128)(2,1)S(1)}, bf16[6,3,96,128]{3,2,1,0:T(8,128)(2,1)}, u32[]{:S(2)}, u32[]{:S(2)}) collective-permute-start(bf16[6,3,96,128]{3,2,1,0:T(8,128)(2,1)S(1)} %pack_owned.1.refs_0_), channel_id=1, source_target_pairs={{8,16},{12,20},{16,8},{20,12},{9,17},{13,21},{17,9},{21,13},{10,18... | collective-permute-start | bytes 1327112 | tf_op jit(solution)/shard_map/ppermute | solution.py:862
  9.4 1.2 dynamic_slice.43
  11.6 1.7 constant_dynamic-slice_fusion.1
  15.5 3.1 %collective-permute-done.1 = bf16[6,3,96,128]{3,2,1,0:T(8,128)(2,1)} collective-permute-done((bf16[6,3,96,128]{3,2,1,0:T(8,128)(2,1)S(1)}, bf16[6,3,96,128]{3,2,1,0:T(8,128)(2,1)}, u32[]{:S(2)}, u32[]{:S(2)}) %collective-permute-start.1) | collective-permute-done | bytes 442400 | tf_op jit(solution)/shard_map/ppermute | solution.py:862
  18.6 1.4 collective-permute-done.refs_4_
  19.9 2.3 collective-permute-start.6
  23.4 1.3 collective-permute-start.7
  24.8 7.9 %collective-permute-done.5.refs_3_ = bf16[6,3,96,128]{3,2,1,0:T(8,128)(2,1)S(1)} collective-permute-done((bf16[6,3,96,128]{3,2,1,0:T(8,128)(2,1)}, bf16[6,3,96,128]{3,2,1,0:T(8,128)(2,1)S(1)}, u32[]{:S(2)}, u32[]{:S(2)}) %collective-permute-start.5) | collective-permute-done | bytes 442400 | tf_op jit(solution)/shard_map/ppermute | solution.py:857
  34.6 1.5 collective-permute-start.9
  36.1 4.5 %collective-permute-start.11 = (bf16[6,3,96,128]{3,2,1,0:T(8,128)(2,1)S(1)}, bf16[6,3,96,128]{3,2,1,0:T(8,128)(2,1)S(1)}, u32[]{:S(2)}, u32[]{:S(2)}) collective-permute-start(bf16[6,3,96,128]{3,2,1,0:T(8,128)(2,1)S(1)} %collective-permute-done.6), channel_id=1, source_target_pairs={{8,0},{12,4},{16,24},{20,28},{9,1},{13,5},{17,25},{21,29},{10,2},{... | collective-permute-start | bytes 1327112 | tf_op jit(solution)/shard_map/ppermute | solution.py:862
  40.6 1.8 collective-permute-done.10.refs_10_
  43.2 7.8 %collective-permute-done.11 = bf16[6,3,96,128]{3,2,1,0:T(8,128)(2,1)S(1)} collective-permute-done((bf16[6,3,96,128]{3,2,1,0:T(8,128)(2,1)S(1)}, bf16[6,3,96,128]{3,2,1,0:T(8,128)(2,1)S(1)}, u32[]{:S(2)}, u32[]{:S(2)}) %collective-permute-start.11) | collective-permute-done | bytes 442400 | tf_op jit(solution)/shard_map/ppermute | solution.py:862
  51.0 1.2 add.132.refs_12_
  53.3 2.5 %collective-permute-start.20 = (bf16[6,3,96,128]{3,2,1,0:T(8,128)(2,1)S(1)}, bf16[6,3,96,128]{3,2,1,0:T(8,128)(2,1)S(1)}, u32[]{:S(2)}, u32[]{:S(2)}) collective-permute-start(bf16[6,3,96,128]{3,2,1,0:T(8,128)(2,1)S(1)} %collective-permute-done.5.refs_3_), channel_id=1, source_target_pairs={{0,8},{4,12},{8,0},{12,4},{16,24},{20,28},{24,16},{28,20},{1,9},{5... | collective-permute-start | bytes 1327112 | tf_op jit(solution)/shard_map/ppermute | solution.py:862
  55.7 1.5 collective-permute-start.19
  57.3 3.0 %collective-permute-done.14.refs_6_ = bf16[6,3,96,128]{3,2,1,0:T(8,128)(2,1)S(1)} collective-permute-done((bf16[6,3,96,128]{3,2,1,0:T(8,128)(2,1)S(1)}, bf16[6,3,96,128]{3,2,1,0:T(8,128)(2,1)S(1)}, u32[]{:S(2)}, u32[]{:S(2)}) %collective-permute-start.14) | collective-permute-done | bytes 442400 | tf_op jit(solution)/shard_map/ppermute | solution.py:862
  60.2 1.5 collective-permute-done.13.refs_14_
  61.7 1.1 collective-permute-done.12.refs_13_
  64.2 4.9 %collective-permute-done.15.xb = bf16[133,768]{1,0:T(8,128)(2,1)S(1)} collective-permute-done((bf16[133,768]{1,0:T(8,128)(2,1)S(1)}, bf16[133,768]{1,0:T(8,128)(2,1)S(1)}, u32[]{:S(2)}, u32[]{:S(2)}) %collective-permute-start.15) | collective-permute-done | bytes 204320 | tf_op jit(solution)/shard_map/ppermute | solution.py:857
  69.1 1.9 collective-permute-done.18.refs_15_
  72.9 9.9 %build_weights.1 = (bf16[768,1152]{1,0:T(8,128)(2,1)}, bf16[384,768]{1,0:T(8,128)(2,1)}, bf16[2,768,768]{2,1,0:T(8,128)(2,1)}, bf16[2,768,768]{2,1,0:T(8,128)(2,1)}) custom-call(s32[192]{0:T(256)} %pos_ref.3, s32[2]{0:T(128)} %get-tuple-element.154.me_ref, bf16[6,3,96,128]{3,2,1,0:T(8,128)(2,1)} %copy-done.10, ...), custom_call_target="tpu_custom_call" | custom-call | flops 100000000 | bytes 30000000 | tf_op jit(solution)/shard_map/build_weights/pallas_call | solution.py:190
  82.9 1.5 copy-done.7
  84.3 2.9 %project.1 = (bf16[576,1152]{1,0:T(8,128)(2,1)S(1)}, f32[576,768]{1,0:T(8,128)S(1)}, bf16[576,768]{1,0:T(8,128)(2,1)S(1)}) custom-call(s32[2]{0:T(128)S(1)} %get-tuple-element.122.flags_ref, bf16[133,768]{1,0:T(8,128)(2,1)S(1)} %bitcast.48, bf16[133,768]{1,0:T(8,128)(2,1)S(1)} %collective-permute-done.15.xb, ...), custom_call_target="tpu_custom_call" | custom-call | flops 1000000000 | bytes 5000000 | tf_op jit(solution)/shard_map/project/pallas_call | solution.py:387
  87.3 6.8 %attend.1 = (bf16[576,384]{1,0:T(8,128)(2,1)S(1)}, bf16[6,576,576]{2,1,0:T(8,128)(2,1)S(1)}, bf16[576,768]{1,0:T(8,128)(2,1)S(1)}) custom-call(s32[576,1]{1,0:T(8,128)S(1)} %copy.38.cq_ref, s32[1,576]{1,0:T(1,128)S(1)} %broadcast_in_dim.25.ck_ref, bf16[576,1152]{1,0:T(8,128)(2,1)S(1)} %get-tuple-element.144.q_ref.k_ref.v_ref, ...), custom_call_target="tpu_custom_call" | custom-call | flops 2500000000 | bytes 8000000 | tf_op jit(solution)/shard_map/attend/pallas_call | solution.py:453
  94.2 2.4 %collective-permute-done.22.other_ref = bf16[576,768]{1,0:T(8,128)(2,1)S(1)} collective-permute-done((bf16[576,768]{1,0:T(8,128)(2,1)S(1)}, bf16[576,768]{1,0:T(8,128)(2,1)S(1)}, u32[]{:S(2)}, u32[]{:S(2)}) %collective-permute-start.22) | collective-permute-done | bytes 884768 | tf_op jit(solution)/shard_map/ppermute | solution.py:857
  96.6 6.7 %feed.1 = (bf16[576,768]{1,0:T(8,128)(2,1)S(1)}, f32[576,768]{1,0:T(8,128)S(1)}, f32[576,1]{1,0:T(8,128)S(1)}, bf16[2,576,768]{2,1,0:T(8,128)(2,1)S(1)}, bf16[2,...) custom-call(bf16[576,768]{1,0:T(8,128)(2,1)S(1)} %get-tuple-element.146.mine_ref, ...), custom_call_target="tpu_custom_call" | custom-call | flops 2800000000 | bytes 16000000 | tf_op jit(solution)/shard_map/feed/pallas_call | solution.py:514
  104.1 2.0 collective-permute-done.24.cc
  106.4 7.3 %feed_back.1 = (bf16[288,768]{1,0:T(8,128)(2,1)S(1)}, f32[576,768]{1,0:T(8,128)S(1)}, bf16[576,768]{1,0:T(8,128)(2,1)S(1)}, bf16[2,576,768]{2,1,0:T(8,128)(2,1)S...) custom-call(bf16[576,768]{1,0:T(8,128)(2,1)S(1)} %get-tuple-element.150.mine_ref, ...), custom_call_target="tpu_custom_call" | custom-call | flops 2800000000 | bytes 16000000 | tf_op jit(solution)/shard_map/feed_back/pallas_call | solution.py:573
  113.9 1.5 collective-permute-start.26
  115.5 2.7 %down_grads.1.later_ref.refs_0_ = bf16[2,768,768]{2,1,0:T(8,128)(2,1)S(1)} custom-call(bf16[2,576,768]{2,1,0:T(8,128)(2,1)S(1)} %get-tuple-element.155.act_ref, bf16[576,768]{1,0:T(8,128)(2,1)S(1)} %get-tuple-element.156.d2_ref), custom_call_target="tpu_custom_call" | custom-call | flops 1400000000 | bytes 8000000 | tf_op jit(solution)/shard_map/down_grads/pallas_call | solution.py:235
  118.2 12.9 %attend_back.1 = (f32[288,768]{1,0:T(8,128)S(1)}, bf16[768,1152]{1,0:T(8,128)(2,1)S(1)}, bf16[384,768]{1,0:T(8,128)(2,1)S(1)}, bf16[288,768]{1,0:T(8,128)(2,1)S(...) custom-call(bf16[576,768]{1,0:T(8,128)(2,1)S(1)} %get-tuple-element.159.mine_ref, ...), custom_call_target="tpu_custom_call" | custom-call | flops 2038431744 | bytes 10485760 | tf_op jit(solution)/shard_map/attend_back/pallas_call | solution.py:647
  131.1 1.2 copy-done.9
  134.2 3.0 %up_grads.1.refs_1_ = bf16[2,768,768]{2,1,0:T(8,128)(2,1)S(1)} custom-call(bf16[576,768]{1,0:T(8,128)(2,1)S(1)} %get-tuple-element.157.h_ref, bf16[2,576,768]{2,1,0:T(8,128)(2,1)S(1)} %get-tuple-element.158.dpre_ref), custom_call_target="tpu_custom_call" | custom-call | flops 1400000000 | bytes 8000000 | tf_op jit(solution)/shard_map/up_grads/pallas_call | solution.py:247
  137.2 1.4 copy-done.6
  141.1 12.0 %pack_grads.1 = (f32[8,128]{1,0:T(8,128)}, bf16[6,3,96,128]{3,2,1,0:T(8,128)(2,1)}, bf16[6,3,96,128]{3,2,1,0:T(8,128)(2,1)}, bf16[6,3,96,128]{3,2,1,0:T(8,128)(2...) custom-call(s32[192]{0:T(256)} %pos_ref.3, ...), custom_call_target="tpu_custom_call" | custom-call | flops 100000000 | bytes 30000000 | tf_op jit(solution)/shard_map/pack_grads/pallas_call | solution.py:340
  154.2 2.8 %collective-permute-start.32 = (bf16[6,3,96,128]{3,2,1,0:T(8,128)(2,1)}, bf16[6,3,96,128]{3,2,1,0:T(8,128)(2,1)S(1)}, u32[]{:S(2)}, u32[]{:S(2)}) collective-permute-start(bf16[6,3,96,128]{3,2,1,0:T(8,128)(2,1)} %get-tuple-element.176), channel_id=1, source_target_pairs={{0,8},{4,12},{8,0},{12,4},{16,24},{20,28},{24,16},{28,20},{1,9},{5... | collective-permute-start | bytes 1327112 | tf_op jit(solution)/shard_map/ppermute | solution.py:862
  158.0 1.2 collective-permute-start.34
  159.2 1.5 collective-permute-start.38
  160.7 7.0 %collective-permute-done.34 = f32[19,768]{1,0:T(8,128)S(1)} collective-permute-done((f32[19,768]{1,0:T(8,128)S(1)}, f32[19,768]{1,0:T(8,128)S(1)}, u32[]{:S(2)}, u32[]{:S(2)}) %collective-permute-start.34) | collective-permute-done | bytes 58400 | tf_op jit(solution)/shard_map/ppermute | solution.py:857
  167.7 2.5 %collective-permute-start.40 = (bf16[6,3,96,128]{3,2,1,0:T(8,128)(2,1)}, bf16[6,3,96,128]{3,2,1,0:T(8,128)(2,1)S(1)}, u32[]{:S(2)}, u32[]{:S(2)}) collective-permute-start(bf16[6,3,96,128]{3,2,1,0:T(8,128)(2,1)} %get-tuple-element.190), channel_id=1, source_target_pairs={{0,8},{4,12},{8,0},{12,4},{16,24},{20,28},{24,16},{28,20},{1,9},{5... | collective-permute-start | bytes 1327112 | tf_op jit(solution)/shard_map/ppermute | solution.py:862
  170.2 1.2 add_convert_fusion.6
  172.4 1.2 collective-permute-start.37
  173.5 1.5 collective-permute-start.41
  175.1 2.7 %collective-permute-done.41 = f32[19,768]{1,0:T(8,128)S(1)} collective-permute-done((f32[19,768]{1,0:T(8,128)S(1)}, f32[19,768]{1,0:T(8,128)S(1)}, u32[]{:S(2)}, u32[]{:S(2)}) %collective-permute-start.41) | collective-permute-done | bytes 58400 | tf_op jit(solution)/shard_map/ppermute | solution.py:857
  177.9 1.5 collective-permute-start.36
  180.1 4.5 %collective-permute-done.39 = bf16[6,3,96,128]{3,2,1,0:T(8,128)(2,1)S(1)} collective-permute-done((bf16[6,3,96,128]{3,2,1,0:T(8,128)(2,1)S(1)}, bf16[6,3,96,128]{3,2,1,0:T(8,128)(2,1)S(1)}, u32[]{:S(2)}, u32[]{:S(2)}) %collective-permute-start.39) | collective-permute-done | bytes 442400 | tf_op jit(solution)/shard_map/ppermute | solution.py:857
  184.8 1.3 collective-permute-start.42
  186.1 1.5 collective-permute-start.29
  187.6 2.7 %collective-permute-start.43 = (f32[19,768]{1,0:T(8,128)S(1)}, f32[19,768]{1,0:T(8,128)S(1)}, u32[]{:S(2)}, u32[]{:S(2)}) collective-permute-start(f32[19,768]{1,0:T(8,128)S(1)} %add.138), channel_id=1, source_target_pairs={{0,8},{4,12},{8,0},{12,4},{16,24},{20,28},{24,16},{28,20},{1,9},{5... | collective-permute-start | bytes 175112 | tf_op jit(solution)/shard_map/ppermute | solution.py:857
  190.4 6.0 %collective-permute-done.43 = f32[19,768]{1,0:T(8,128)S(1)} collective-permute-done((f32[19,768]{1,0:T(8,128)S(1)}, f32[19,768]{1,0:T(8,128)S(1)}, u32[]{:S(2)}, u32[]{:S(2)}) %collective-permute-start.43) | collective-permute-done | bytes 58400 | tf_op jit(solution)/shard_map/ppermute | solution.py:857
  197.7 1.4 collective-permute-start.45
  199.1 3.4 %collective-permute-start.44 = (bf16[6,3,96,128]{3,2,1,0:T(8,128)(2,1)S(1)}, bf16[6,3,96,128]{3,2,1,0:T(8,128)(2,1)S(1)}, u32[]{:S(2)}, u32[]{:S(2)}) collective-permute-start(bf16[6,3,96,128]{3,2,1,0:T(8,128)(2,1)S(1)} %add_convert_fusion.4), channel_id=1, source_target_pairs={{8,16},{12,20},{16,8},{20,12},{9,17},{13,21},{17,9},{21,13},{10,18... | collective-permute-start | bytes 1327112 | tf_op jit(solution)/shard_map/ppermute | solution.py:862
  202.5 1.1 copy.41
  205.4 4.8 %collective-permute-done.46 = f32[19,768]{1,0:T(8,128)S(1)} collective-permute-done((f32[19,768]{1,0:T(8,128)S(1)}, f32[19,768]{1,0:T(8,128)S(1)}, u32[]{:S(2)}, u32[]{:S(2)}) %collective-permute-start.46) | collective-permute-done | bytes 58400 | tf_op jit(solution)/shard_map/ppermute | solution.py:857
  210.2 1.1 collective-permute-start.48
  212.5 2.6 %collective-permute-start.49 = (bf16[6,3,96,128]{3,2,1,0:T(8,128)(2,1)S(1)}, bf16[6,3,96,128]{3,2,1,0:T(8,128)(2,1)S(1)}, u32[]{:S(2)}, u32[]{:S(2)}) collective-permute-start(bf16[6,3,96,128]{3,2,1,0:T(8,128)(2,1)S(1)} %add_convert_fusion.1), channel_id=1, source_target_pairs={{0,8},{4,12},{8,0},{12,4},{16,24},{20,28},{24,16},{28,20},{1,9},{5... | collective-permute-start | bytes 1327112 | tf_op jit(solution)/shard_map/ppermute | solution.py:862
  215.3 1.6 collective-permute-start.47
  216.8 3.4 %collective-permute-start.50 = (bf16[6,3,96,128]{3,2,1,0:T(8,128)(2,1)S(1)}, bf16[6,3,96,128]{3,2,1,0:T(8,128)(2,1)S(1)}, u32[]{:S(2)}, u32[]{:S(2)}) collective-permute-start(bf16[6,3,96,128]{3,2,1,0:T(8,128)(2,1)S(1)} %copy-done.27), channel_id=1, source_target_pairs={{8,16},{12,20},{16,8},{20,12},{9,17},{13,21},{17,9},{21,13},{10,18... | collective-permute-start | bytes 1327112 | tf_op jit(solution)/shard_map/ppermute | solution.py:862
  221.4 2.2 collective-permute-done.47.refs_1_
  223.6 3.4 %collective-permute-done.50.refs_4_ = bf16[6,3,96,128]{3,2,1,0:T(8,128)(2,1)S(1)} collective-permute-done((bf16[6,3,96,128]{3,2,1,0:T(8,128)(2,1)S(1)}, bf16[6,3,96,128]{3,2,1,0:T(8,128)(2,1)S(1)}, u32[]{:S(2)}, u32[]{:S(2)}) %collective-permute-start.50) | collective-permute-done | bytes 442400 | tf_op jit(solution)/shard_map/ppermute | solution.py:862
  228.7 6.9 %soap.1 = (f32[24,96,96]{2,1,0:T(8,128)}, bf16[24,96,96]{2,1,0:T(8,128)(2,1)}, f32[24,96,96]{2,1,0:T(8,128)}, f32[24,96,96]{2,1,0:T(8,128)}, f32[24,96,96]{2,1,0:T(8,128)}, /*index=5*/f32[24,96,96]{2,1,0:T(8,128)}) custom-call(bf16[6,3,96,128]{3,2,1,0:T(8,128)(2,1)} %get-tuple-element.208.refs_0_, bf16[6,3,96,128]{3,2,1,0:T(8,128)(2,1)} %copy-done.41, ...), custom_call_target="tpu_custom_call" | custom-call | flops 300000000 | bytes 24000000 | tf_op jit(solution)/shard_map/soap/pallas_call | solution.py:772
  (208 shorter events, 29.5 us)
Async XLA Ops:
  2.1 12.5 %collective-permute-start.3 = (bf16[6,3,96,128]{3,2,1,0:T(8,128)(2,1)S(1)}, bf16[6,3,96,128]{3,2,1,0:T(8,128)(2,1)S(1)}, u32[]{:S(2)}, u32[]{:S(2)}) collective-permute-start(bf16[6,3,96,128]{3,2,1,0:T(8,128)(2,1)S(1)} %pack_owned.1.refs_0_), channel_id=1, source_target_pairs={{0,2},{1,3},{2,0},{3,1},{4,6},{5,7},{6,4},{7,5},{8,10},{9,11},{10,... | collective-permute-start | bytes 1327112 | tf_op jit(solution)/shard_map/ppermute | solution.py:857
  3.7 11.7 %collective-permute-start.2 = (bf16[6,3,96,128]{3,2,1,0:T(8,128)(2,1)S(1)}, bf16[6,3,96,128]{3,2,1,0:T(8,128)(2,1)}, u32[]{:S(2)}, u32[]{:S(2)}) collective-permute-start(bf16[6,3,96,128]{3,2,1,0:T(8,128)(2,1)S(1)} %pack_owned.1.refs_0_), channel_id=1, source_target_pairs={{0,4},{4,0},{8,12},{12,8},{16,20},{20,16},{24,28},{28,24},{1,5},{5... | collective-permute-start | bytes 1327112 | tf_op jit(solution)/shard_map/ppermute | solution.py:857
  5.2 13.3 %collective-permute-start.1 = (bf16[6,3,96,128]{3,2,1,0:T(8,128)(2,1)S(1)}, bf16[6,3,96,128]{3,2,1,0:T(8,128)(2,1)}, u32[]{:S(2)}, u32[]{:S(2)}) collective-permute-start(bf16[6,3,96,128]{3,2,1,0:T(8,128)(2,1)S(1)} %pack_owned.1.refs_0_), channel_id=1, source_target_pairs={{8,16},{12,20},{16,8},{20,12},{9,17},{13,21},{17,9},{21,13},{10,18... | collective-permute-start | bytes 1327112 | tf_op jit(solution)/shard_map/ppermute | solution.py:862
  8.7 11.2 %collective-permute-start = (bf16[6,3,96,128]{3,2,1,0:T(8,128)(2,1)S(1)}, bf16[6,3,96,128]{3,2,1,0:T(8,128)(2,1)}, u32[]{:S(2)}, u32[]{:S(2)}) collective-permute-start(bf16[6,3,96,128]{3,2,1,0:T(8,128)(2,1)S(1)} %pack_owned.1.refs_0_), channel_id=1, source_target_pairs={{0,8},{4,12},{8,0},{12,4},{16,24},{20,28},{24,16},{28,20},{1,9},{5... | collective-permute-start | bytes 1327112 | tf_op jit(solution)/shard_map/ppermute | solution.py:862
  8.8 15.9 %collective-permute-start.8 = (f32[1,1152]{1,0:T(1,128)}, f32[1,1152]{1,0:T(1,128)S(1)}, u32[]{:S(2)}, u32[]{:S(2)}) collective-permute-start(f32[1,1152]{1,0:T(1,128)} %param.30), channel_id=1, source_target_pairs={{0,2},{1,3},{2,0},{3,1},{4,6},{5,7},{6,4},{7,5},{8,10},{9,11},{10,... | collective-permute-start | bytes 13832 | tf_op jit(solution)/shard_map/ppermute | solution.py:857
  14.6 49.5 %copy-start.28 = (bf16[6,3,96,128]{3,2,1,0:T(8,128)(2,1)}, bf16[6,3,96,128]{3,2,1,0:T(8,128)(2,1)S(1)}, u32[]{:S(2)}) copy-start(bf16[6,3,96,128]{3,2,1,0:T(8,128)(2,1)S(1)} %collective-permute-done.3.refs_2_) | copy-start | bytes 1327108
  19.9 12.8 %collective-permute-start.6 = (bf16[6,3,96,128]{3,2,1,0:T(8,128)(2,1)}, bf16[6,3,96,128]{3,2,1,0:T(8,128)(2,1)S(1)}, u32[]{:S(2)}, u32[]{:S(2)}) collective-permute-start(bf16[6,3,96,128]{3,2,1,0:T(8,128)(2,1)} %collective-permute-done.refs_4_), channel_id=1, source_target_pairs={{8,16},{12,20},{16,8},{20,12},{9,17},{13,21},{17,9},{21,13},{10,18... | collective-permute-start | bytes 1327112 | tf_op jit(solution)/shard_map/ppermute | solution.py:862
  22.3 10.4 %collective-permute-start.4 = (bf16[6,3,96,128]{3,2,1,0:T(8,128)(2,1)}, bf16[6,3,96,128]{3,2,1,0:T(8,128)(2,1)S(1)}, u32[]{:S(2)}, u32[]{:S(2)}) collective-permute-start(bf16[6,3,96,128]{3,2,1,0:T(8,128)(2,1)} %collective-permute-done.refs_4_), channel_id=1, source_target_pairs={{0,4},{4,0},{8,12},{12,8},{16,20},{20,16},{24,28},{28,24},{1,5},{5... | collective-permute-start | bytes 1327112 | tf_op jit(solution)/shard_map/ppermute | solution.py:857
  22.9 9.8 %collective-permute-start.5 = (bf16[6,3,96,128]{3,2,1,0:T(8,128)(2,1)}, bf16[6,3,96,128]{3,2,1,0:T(8,128)(2,1)S(1)}, u32[]{:S(2)}, u32[]{:S(2)}) collective-permute-start(bf16[6,3,96,128]{3,2,1,0:T(8,128)(2,1)} %collective-permute-done.2.refs_1_), channel_id=1, source_target_pairs={{0,2},{1,3},{2,0},{3,1},{4,6},{5,7},{6,4},{7,5},{8,10},{9,11},{10,... | collective-permute-start | bytes 1327112 | tf_op jit(solution)/shard_map/ppermute | solution.py:857
  23.4 9.3 %collective-permute-start.7 = (bf16[6,3,96,128]{3,2,1,0:T(8,128)(2,1)}, bf16[6,3,96,128]{3,2,1,0:T(8,128)(2,1)S(1)}, u32[]{:S(2)}, u32[]{:S(2)}) collective-permute-start(bf16[6,3,96,128]{3,2,1,0:T(8,128)(2,1)} %collective-permute-done.1), channel_id=1, source_target_pairs={{8,0},{12,4},{16,24},{20,28},{9,1},{13,5},{17,25},{21,29},{10,2},{... | collective-permute-start | bytes 1327112 | tf_op jit(solution)/shard_map/ppermute | solution.py:862
  32.7 38.4 %copy-start.31 = (bf16[6,3,96,128]{3,2,1,0:T(8,128)(2,1)}, bf16[6,3,96,128]{3,2,1,0:T(8,128)(2,1)S(1)}, u32[]{:S(2)}) copy-start(bf16[6,3,96,128]{3,2,1,0:T(8,128)(2,1)S(1)} %collective-permute-done.5.refs_3_) | copy-start | bytes 1327108
  33.7 39.2 %copy-start.17 = (bf16[6,3,96,128]{3,2,1,0:T(8,128)(2,1)}, bf16[6,3,96,128]{3,2,1,0:T(8,128)(2,1)S(1)}, u32[]{:S(2)}) copy-start(bf16[6,3,96,128]{3,2,1,0:T(8,128)(2,1)S(1)} %add.131.refs_8_) | copy-start | bytes 1327108
  33.7 8.8 %collective-permute-start.10 = (bf16[6,3,96,128]{3,2,1,0:T(8,128)(2,1)S(1)}, bf16[6,3,96,128]{3,2,1,0:T(8,128)(2,1)S(1)}, u32[]{:S(2)}, u32[]{:S(2)}) collective-permute-start(bf16[6,3,96,128]{3,2,1,0:T(8,128)(2,1)S(1)} %add.131.refs_8_), channel_id=1, source_target_pairs={{0,2},{1,3},{2,0},{3,1},{4,6},{5,7},{6,4},{7,5},{8,10},{9,11},{10,... | collective-permute-start | bytes 1327112 | tf_op jit(solution)/shard_map/ppermute | solution.py:857
  34.6 8.4 %collective-permute-start.9 = (bf16[6,3,96,128]{3,2,1,0:T(8,128)(2,1)S(1)}, bf16[6,3,96,128]{3,2,1,0:T(8,128)(2,1)S(1)}, u32[]{:S(2)}, u32[]{:S(2)}) collective-permute-start(bf16[6,3,96,128]{3,2,1,0:T(8,128)(2,1)S(1)} %add.131.refs_8_), channel_id=1, source_target_pairs={{0,4},{4,0},{8,12},{12,8},{16,20},{20,16},{24,28},{28,24},{1,5},{5... | collective-permute-start | bytes 1327112 | tf_op jit(solution)/shard_map/ppermute | solution.py:857
  36.1 14.9 %collective-permute-start.11 = (bf16[6,3,96,128]{3,2,1,0:T(8,128)(2,1)S(1)}, bf16[6,3,96,128]{3,2,1,0:T(8,128)(2,1)S(1)}, u32[]{:S(2)}, u32[]{:S(2)}) collective-permute-start(bf16[6,3,96,128]{3,2,1,0:T(8,128)(2,1)S(1)} %collective-permute-done.6), channel_id=1, source_target_pairs={{8,0},{12,4},{16,24},{20,28},{9,1},{13,5},{17,25},{21,29},{10,2},{... | collective-permute-start | bytes 1327112 | tf_op jit(solution)/shard_map/ppermute | solution.py:862
  40.6 19.6 %collective-permute-start.14 = (bf16[6,3,96,128]{3,2,1,0:T(8,128)(2,1)S(1)}, bf16[6,3,96,128]{3,2,1,0:T(8,128)(2,1)S(1)}, u32[]{:S(2)}, u32[]{:S(2)}) collective-permute-start(bf16[6,3,96,128]{3,2,1,0:T(8,128)(2,1)S(1)} %collective-permute-done.3.refs_2_), channel_id=1, source_target_pairs={{0,8},{4,12},{8,0},{12,4},{16,24},{20,28},{24,16},{28,20},{1,9},{5... | collective-permute-start | bytes 1327112 | tf_op jit(solution)/shard_map/ppermute | solution.py:862
  43.2 27.9 %copy-start.33 = (bf16[6,3,96,128]{3,2,1,0:T(8,128)(2,1)}, bf16[6,3,96,128]{3,2,1,0:T(8,128)(2,1)S(1)}, u32[]{:S(2)}) copy-start(bf16[6,3,96,128]{3,2,1,0:T(8,128)(2,1)S(1)} %collective-permute-done.9.refs_9_) | copy-start | bytes 1327108
  52.1 20.8 %copy-start.18 = (bf16[6,3,96,128]{3,2,1,0:T(8,128)(2,1)}, bf16[6,3,96,128]{3,2,1,0:T(8,128)(2,1)S(1)}, u32[]{:S(2)}) copy-start(bf16[6,3,96,128]{3,2,1,0:T(8,128)(2,1)S(1)} %add.132.refs_12_) | copy-start | bytes 1327108
  52.2 9.5 %collective-permute-start.13 = (bf16[6,3,96,128]{3,2,1,0:T(8,128)(2,1)S(1)}, bf16[6,3,96,128]{3,2,1,0:T(8,128)(2,1)S(1)}, u32[]{:S(2)}, u32[]{:S(2)}) collective-permute-start(bf16[6,3,96,128]{3,2,1,0:T(8,128)(2,1)S(1)} %add.132.refs_12_), channel_id=1, source_target_pairs={{0,2},{1,3},{2,0},{3,1},{4,6},{5,7},{6,4},{7,5},{8,10},{9,11},{10,... | collective-permute-start | bytes 1327112 | tf_op jit(solution)/shard_map/ppermute | solution.py:857
  52.7 10.0 %collective-permute-start.12 = (bf16[6,3,96,128]{3,2,1,0:T(8,128)(2,1)S(1)}, bf16[6,3,96,128]{3,2,1,0:T(8,128)(2,1)S(1)}, u32[]{:S(2)}, u32[]{:S(2)}) collective-permute-start(bf16[6,3,96,128]{3,2,1,0:T(8,128)(2,1)S(1)} %add.132.refs_12_), channel_id=1, source_target_pairs={{0,4},{4,0},{8,12},{12,8},{16,20},{20,16},{24,28},{28,24},{1,5},{5... | collective-permute-start | bytes 1327112 | tf_op jit(solution)/shard_map/ppermute | solution.py:857
  53.3 15.9 %collective-permute-start.20 = (bf16[6,3,96,128]{3,2,1,0:T(8,128)(2,1)S(1)}, bf16[6,3,96,128]{3,2,1,0:T(8,128)(2,1)S(1)}, u32[]{:S(2)}, u32[]{:S(2)}) collective-permute-start(bf16[6,3,96,128]{3,2,1,0:T(8,128)(2,1)S(1)} %collective-permute-done.5.refs_3_), channel_id=1, source_target_pairs={{0,8},{4,12},{8,0},{12,4},{16,24},{20,28},{24,16},{28,20},{1,9},{5... | collective-permute-start | bytes 1327112 | tf_op jit(solution)/shard_map/ppermute | solution.py:862
  55.7 13.4 %collective-permute-start.19 = (bf16[6,3,96,128]{3,2,1,0:T(8,128)(2,1)S(1)}, bf16[6,3,96,128]{3,2,1,0:T(8,128)(2,1)S(1)}, u32[]{:S(2)}, u32[]{:S(2)}) collective-permute-start(bf16[6,3,96,128]{3,2,1,0:T(8,128)(2,1)S(1)} %collective-permute-done.9.refs_9_), channel_id=1, source_target_pairs={{0,2},{1,3},{2,0},{3,1},{4,6},{5,7},{6,4},{7,5},{8,10},{9,11},{10,... | collective-permute-start | bytes 1327112 | tf_op jit(solution)/shard_map/ppermute | solution.py:857
  62.8 8.3 %collective-permute-start.18 = (bf16[6,3,96,128]{3,2,1,0:T(8,128)(2,1)S(1)}, bf16[6,3,96,128]{3,2,1,0:T(8,128)(2,1)S(1)}, u32[]{:S(2)}, u32[]{:S(2)}) collective-permute-start(bf16[6,3,96,128]{3,2,1,0:T(8,128)(2,1)S(1)} %collective-permute-done.13.refs_14_), channel_id=1, source_target_pairs={{0,4},{4,0},{8,12},{12,8},{16,20},{20,16},{24,28},{28,24},{1,5},{5... | collective-permute-start | bytes 1327112 | tf_op jit(solution)/shard_map/ppermute | solution.py:857
  63.3 5.8 %collective-permute-start.15 = (bf16[133,768]{1,0:T(8,128)(2,1)S(1)}, bf16[133,768]{1,0:T(8,128)(2,1)S(1)}, u32[]{:S(2)}, u32[]{:S(2)}) collective-permute-start(bf16[133,768]{1,0:T(8,128)(2,1)S(1)} %bitcast.55), channel_id=1, source_target_pairs={{0,2},{1,3},{2,0},{3,1},{4,6},{5,7},{6,4},{7,5},{8,10},{9,11},{10,... | collective-permute-start | bytes 612872 | tf_op jit(solution)/shard_map/ppermute | solution.py:857
  64.2 18.6 %collective-permute-start.16 = (bf16[133,768]{1,0:T(8,128)(2,1)S(1)}, bf16[133,768]{1,0:T(8,128)(2,1)S(1)}, u32[]{:S(2)}, u32[]{:S(2)}) collective-permute-start(bf16[133,768]{1,0:T(8,128)(2,1)S(1)} %bitcast.47), channel_id=1, source_target_pairs={{0,1},{1,0},{2,3},{3,2},{4,5},{5,4},{6,7},{7,6},{8,9},{9,8},{10,11... | collective-permute-start | bytes 612872 | tf_op jit(solution)/shard_map/ppermute | solution.py:857
  69.1 13.7 %collective-permute-start.17 = (bf16[133,768]{1,0:T(8,128)(2,1)S(1)}, bf16[133,768]{1,0:T(8,128)(2,1)S(1)}, u32[]{:S(2)}, u32[]{:S(2)}) collective-permute-start(bf16[133,768]{1,0:T(8,128)(2,1)S(1)} %collective-permute-done.15.xb), channel_id=1, source_target_pairs={{0,1},{1,0},{2,3},{3,2},{4,5},{5,4},{6,7},{7,6},{8,9},{9,8},{10,11... | collective-permute-start | bytes 612872 | tf_op jit(solution)/shard_map/ppermute | solution.py:857
  71.9 10.9 %collective-permute-start.21 = (bf16[133,768]{1,0:T(8,128)(2,1)}, bf16[133,768]{1,0:T(8,128)(2,1)S(1)}, u32[]{:S(2)}, u32[]{:S(2)}) collective-permute-start(bf16[133,768]{1,0:T(8,128)(2,1)} %bitcast.38), channel_id=1, source_target_pairs={{0,2},{1,3},{2,0},{3,1},{4,6},{5,7},{6,4},{7,5},{8,10},{9,11},{10,... | collective-permute-start | bytes 612872 | tf_op jit(solution)/shard_map/ppermute | solution.py:857
  94.1 2.5 %collective-permute-start.22 = (bf16[576,768]{1,0:T(8,128)(2,1)S(1)}, bf16[576,768]{1,0:T(8,128)(2,1)S(1)}, u32[]{:S(2)}, u32[]{:S(2)}) collective-permute-start(bf16[576,768]{1,0:T(8,128)(2,1)S(1)} %get-tuple-element.146.mine_ref), channel_id=1, source_target_pairs={{0,1},{1,0},{2,3},{3,2},{4,5},{5,4},{6,7},{7,6},{8,9},{9,8},{10,11... | collective-permute-start | bytes 2654216 | tf_op jit(solution)/shard_map/ppermute | solution.py:857
  103.3 3.1 %collective-permute-start.23 = (bf16[576,768]{1,0:T(8,128)(2,1)S(1)}, bf16[576,768]{1,0:T(8,128)(2,1)S(1)}, u32[]{:S(2)}, u32[]{:S(2)}) collective-permute-start(bf16[576,768]{1,0:T(8,128)(2,1)S(1)} %get-tuple-element.150.mine_ref), channel_id=1, source_target_pairs={{0,1},{1,0},{2,3},{3,2},{4,5},{5,4},{6,7},{7,6},{8,9},{9,8},{10,11... | collective-permute-start | bytes 2654216 | tf_op jit(solution)/shard_map/ppermute | solution.py:857
  103.5 2.6 %collective-permute-start.24 = (bf16[133,768]{1,0:T(8,128)(2,1)S(1)}, bf16[133,768]{1,0:T(8,128)(2,1)S(1)}, u32[]{:S(2)}, u32[]{:S(2)}) collective-permute-start(bf16[133,768]{1,0:T(8,128)(2,1)S(1)} %bitcast.43), channel_id=1, source_target_pairs={{0,1},{1,0},{2,3},{3,2},{4,5},{5,4},{6,7},{7,6},{8,9},{9,8},{10,11... | collective-permute-start | bytes 612872 | tf_op jit(solution)/shard_map/ppermute | solution.py:857
  104.0 2.4 %collective-permute-start.25 = (bf16[133,768]{1,0:T(8,128)(2,1)S(1)}, bf16[133,768]{1,0:T(8,128)(2,1)S(1)}, u32[]{:S(2)}, u32[]{:S(2)}) collective-permute-start(bf16[133,768]{1,0:T(8,128)(2,1)S(1)} %collective-permute-done.21.later_ref.cb), channel_id=1, source_target_pairs={{0,1},{1,0},{2,3},{3,2},{4,5},{5,4},{6,7},{7,6},{8,9},{9,8},{10,11... | collective-permute-start | bytes 612872 | tf_op jit(solution)/shard_map/ppermute | solution.py:857
  113.7 4.5 %collective-permute-start.27 = (bf16[576,768]{1,0:T(8,128)(2,1)S(1)}, bf16[576,768]{1,0:T(8,128)(2,1)S(1)}, u32[]{:S(2)}, u32[]{:S(2)}) collective-permute-start(bf16[576,768]{1,0:T(8,128)(2,1)S(1)} %get-tuple-element.159.mine_ref), channel_id=1, source_target_pairs={{0,1},{1,0},{2,3},{3,2},{4,5},{5,4},{6,7},{7,6},{8,9},{9,8},{10,11... | collective-permute-start | bytes 2654216 | tf_op jit(solution)/shard_map/ppermute | solution.py:857
  113.9 24.7 %collective-permute-start.26 = (bf16[133,768]{1,0:T(8,128)(2,1)S(1)}, bf16[133,768]{1,0:T(8,128)(2,1)S(1)}, u32[]{:S(2)}, u32[]{:S(2)}) collective-permute-start(bf16[133,768]{1,0:T(8,128)(2,1)S(1)} %get-tuple-element.257), channel_id=1, source_target_pairs={{0,2},{1,3},{2,0},{3,1},{4,6},{5,7},{6,4},{7,5},{8,10},{9,11},{10,... | collective-permute-start | bytes 612872 | tf_op jit(solution)/shard_map/ppermute | solution.py:857
  134.1 4.8 %collective-permute-start.28 = (bf16[288,768]{1,0:T(8,128)(2,1)}, bf16[288,768]{1,0:T(8,128)(2,1)S(1)}, u32[]{:S(2)}, u32[]{:S(2)}) collective-permute-start(bf16[288,768]{1,0:T(8,128)(2,1)} %get-tuple-element.168), channel_id=1, source_target_pairs={{0,1},{1,0},{2,3},{3,2},{4,5},{5,4},{6,7},{7,6},{8,9},{9,8},{10,11... | collective-permute-start | bytes 1327112 | tf_op jit(solution)/shard_map/ppermute | solution.py:857
  140.5 16.5 %collective-permute-start.33 = (f32[16,768]{1,0:T(8,128)S(1)}, f32[16,768]{1,0:T(8,128)S(1)}, u32[]{:S(2)}, u32[]{:S(2)}) collective-permute-start(f32[16,768]{1,0:T(8,128)S(1)} %pad_maximum_fusion.3), channel_id=1, source_target_pairs={{0,1},{1,0},{2,3},{3,2},{4,5},{5,4},{6,7},{7,6},{8,9},{9,8},{10,11... | collective-permute-start | bytes 147464 | tf_op jit(solution)/shard_map/ppermute | solution.py:857
  153.1 21.9 %copy-start.26 = (bf16[6,3,96,128]{3,2,1,0:T(8,128)(2,1)S(1)}, bf16[6,3,96,128]{3,2,1,0:T(8,128)(2,1)}, u32[]{:S(2)}) copy-start(bf16[6,3,96,128]{3,2,1,0:T(8,128)(2,1)} %get-tuple-element.183) | copy-start | bytes 1327108
  153.1 31.5 %copy-start.22 = (bf16[6,3,96,128]{3,2,1,0:T(8,128)(2,1)S(1)}, bf16[6,3,96,128]{3,2,1,0:T(8,128)(2,1)}, u32[]{:S(2)}) copy-start(bf16[6,3,96,128]{3,2,1,0:T(8,128)(2,1)} %get-tuple-element.186) | copy-start | bytes 1327108
  153.1 17.1 %collective-permute-start.30 = (bf16[6,3,96,128]{3,2,1,0:T(8,128)(2,1)}, bf16[6,3,96,128]{3,2,1,0:T(8,128)(2,1)S(1)}, u32[]{:S(2)}, u32[]{:S(2)}) collective-permute-start(bf16[6,3,96,128]{3,2,1,0:T(8,128)(2,1)} %get-tuple-element.174), channel_id=1, source_target_pairs={{0,4},{4,0},{8,12},{12,8},{16,20},{20,16},{24,28},{28,24},{1,5},{5... | collective-permute-start | bytes 1327112 | tf_op jit(solution)/shard_map/ppermute | solution.py:857
  153.7 16.5 %collective-permute-start.31 = (bf16[6,3,96,128]{3,2,1,0:T(8,128)(2,1)}, bf16[6,3,96,128]{3,2,1,0:T(8,128)(2,1)S(1)}, u32[]{:S(2)}, u32[]{:S(2)}) collective-permute-start(bf16[6,3,96,128]{3,2,1,0:T(8,128)(2,1)} %get-tuple-element.175), channel_id=1, source_target_pairs={{0,2},{1,3},{2,0},{3,1},{4,6},{5,7},{6,4},{7,5},{8,10},{9,11},{10,... | collective-permute-start | bytes 1327112 | tf_op jit(solution)/shard_map/ppermute | solution.py:857
  154.2 16.0 %collective-permute-start.32 = (bf16[6,3,96,128]{3,2,1,0:T(8,128)(2,1)}, bf16[6,3,96,128]{3,2,1,0:T(8,128)(2,1)S(1)}, u32[]{:S(2)}, u32[]{:S(2)}) collective-permute-start(bf16[6,3,96,128]{3,2,1,0:T(8,128)(2,1)} %get-tuple-element.176), channel_id=1, source_target_pairs={{0,8},{4,12},{8,0},{12,4},{16,24},{20,28},{24,16},{28,20},{1,9},{5... | collective-permute-start | bytes 1327112 | tf_op jit(solution)/shard_map/ppermute | solution.py:862
  157.1 15.3 %copy-start.49 = (bf16[6,3,96,128]{3,2,1,0:T(8,128)(2,1)S(1)}, bf16[6,3,96,128]{3,2,1,0:T(8,128)(2,1)}, u32[]{:S(2)}) copy-start(bf16[6,3,96,128]{3,2,1,0:T(8,128)(2,1)} %get-tuple-element.185) | copy-start | bytes 1327108
  158.0 9.8 %collective-permute-start.34 = (f32[19,768]{1,0:T(8,128)S(1)}, f32[19,768]{1,0:T(8,128)S(1)}, u32[]{:S(2)}, u32[]{:S(2)}) collective-permute-start(f32[19,768]{1,0:T(8,128)S(1)} %pad_maximum_fusion.2), channel_id=1, source_target_pairs={{0,2},{1,3},{2,0},{3,1},{4,6},{5,7},{6,4},{7,5},{8,10},{9,11},{10,... | collective-permute-start | bytes 175112 | tf_op jit(solution)/shard_map/ppermute | solution.py:857
  159.2 20.2 %collective-permute-start.38 = (bf16[6,3,96,128]{3,2,1,0:T(8,128)(2,1)}, bf16[6,3,96,128]{3,2,1,0:T(8,128)(2,1)S(1)}, u32[]{:S(2)}, u32[]{:S(2)}) collective-permute-start(bf16[6,3,96,128]{3,2,1,0:T(8,128)(2,1)} %get-tuple-element.187), channel_id=1, source_target_pairs={{0,4},{4,0},{8,12},{12,8},{16,20},{20,16},{24,28},{28,24},{1,5},{5... | collective-permute-start | bytes 1327112 | tf_op jit(solution)/shard_map/ppermute | solution.py:857
  167.7 12.3 %collective-permute-start.40 = (bf16[6,3,96,128]{3,2,1,0:T(8,128)(2,1)}, bf16[6,3,96,128]{3,2,1,0:T(8,128)(2,1)S(1)}, u32[]{:S(2)}, u32[]{:S(2)}) collective-permute-start(bf16[6,3,96,128]{3,2,1,0:T(8,128)(2,1)} %get-tuple-element.190), channel_id=1, source_target_pairs={{0,8},{4,12},{8,0},{12,4},{16,24},{20,28},{24,16},{28,20},{1,9},{5... | collective-permute-start | bytes 1327112 | tf_op jit(solution)/shard_map/ppermute | solution.py:862
  171.4 18.9 %copy-start.25 = (bf16[6,3,96,128]{3,2,1,0:T(8,128)(2,1)S(1)}, bf16[6,3,96,128]{3,2,1,0:T(8,128)(2,1)}, u32[]{:S(2)}) copy-start(bf16[6,3,96,128]{3,2,1,0:T(8,128)(2,1)} %get-tuple-element.173) | copy-start | bytes 1327108
  171.4 13.2 %collective-permute-start.39 = (bf16[6,3,96,128]{3,2,1,0:T(8,128)(2,1)S(1)}, bf16[6,3,96,128]{3,2,1,0:T(8,128)(2,1)S(1)}, u32[]{:S(2)}, u32[]{:S(2)}) collective-permute-start(bf16[6,3,96,128]{3,2,1,0:T(8,128)(2,1)S(1)} %add_convert_fusion.6), channel_id=1, source_target_pairs={{0,2},{1,3},{2,0},{3,1},{4,6},{5,7},{6,4},{7,5},{8,10},{9,11},{10,... | collective-permute-start | bytes 1327112 | tf_op jit(solution)/shard_map/ppermute | solution.py:857
  172.4 25.0 %collective-permute-start.37 = (bf16[6,3,96,128]{3,2,1,0:T(8,128)(2,1)S(1)}, bf16[6,3,96,128]{3,2,1,0:T(8,128)(2,1)S(1)}, u32[]{:S(2)}, u32[]{:S(2)}) collective-permute-start(bf16[6,3,96,128]{3,2,1,0:T(8,128)(2,1)S(1)} %copy-done.49), channel_id=1, source_target_pairs={{0,2},{1,3},{2,0},{3,1},{4,6},{5,7},{6,4},{7,5},{8,10},{9,11},{10,... | collective-permute-start | bytes 1327112 | tf_op jit(solution)/shard_map/ppermute | solution.py:857
  173.5 4.4 %collective-permute-start.41 = (f32[19,768]{1,0:T(8,128)S(1)}, f32[19,768]{1,0:T(8,128)S(1)}, u32[]{:S(2)}, u32[]{:S(2)}) collective-permute-start(f32[19,768]{1,0:T(8,128)S(1)} %add.134), channel_id=1, source_target_pairs={{0,4},{4,0},{8,12},{12,8},{16,20},{20,16},{24,28},{28,24},{1,5},{5... | collective-permute-start | bytes 175112 | tf_op jit(solution)/shard_map/ppermute | solution.py:857
  175.1 22.3 %copy-start.29 = (bf16[6,3,96,128]{3,2,1,0:T(8,128)(2,1)S(1)}, bf16[6,3,96,128]{3,2,1,0:T(8,128)(2,1)}, u32[]{:S(2)}) copy-start(bf16[6,3,96,128]{3,2,1,0:T(8,128)(2,1)} %get-tuple-element.182) | copy-start | bytes 1327108
  177.9 19.5 %collective-permute-start.36 = (bf16[6,3,96,128]{3,2,1,0:T(8,128)(2,1)S(1)}, bf16[6,3,96,128]{3,2,1,0:T(8,128)(2,1)S(1)}, u32[]{:S(2)}, u32[]{:S(2)}) collective-permute-start(bf16[6,3,96,128]{3,2,1,0:T(8,128)(2,1)S(1)} %add_convert_fusion.7), channel_id=1, source_target_pairs={{0,4},{4,0},{8,12},{12,8},{16,20},{20,16},{24,28},{28,24},{1,5},{5... | collective-permute-start | bytes 1327112 | tf_op jit(solution)/shard_map/ppermute | solution.py:857
  184.8 12.6 %collective-permute-start.42 = (bf16[6,3,96,128]{3,2,1,0:T(8,128)(2,1)S(1)}, bf16[6,3,96,128]{3,2,1,0:T(8,128)(2,1)S(1)}, u32[]{:S(2)}, u32[]{:S(2)}) collective-permute-start(bf16[6,3,96,128]{3,2,1,0:T(8,128)(2,1)S(1)} %add_convert_fusion.5), channel_id=1, source_target_pairs={{0,8},{4,12},{24,16},{28,20},{1,9},{5,13},{25,17},{29,21},{2,10},{... | collective-permute-start | bytes 1327112 | tf_op jit(solution)/shard_map/ppermute | solution.py:862
  186.1 25.3 %collective-permute-start.29 = (bf16[6,3,96,128]{3,2,1,0:T(8,128)(2,1)S(1)}, bf16[6,3,96,128]{3,2,1,0:T(8,128)(2,1)S(1)}, u32[]{:S(2)}, u32[]{:S(2)}) collective-permute-start(bf16[6,3,96,128]{3,2,1,0:T(8,128)(2,1)S(1)} %copy-done.48), channel_id=1, source_target_pairs={{0,4},{4,0},{8,12},{12,8},{16,20},{20,16},{24,28},{28,24},{1,5},{5... | collective-permute-start | bytes 1327112 | tf_op jit(solution)/shard_map/ppermute | solution.py:857
  187.6 8.8 %collective-permute-start.43 = (f32[19,768]{1,0:T(8,128)S(1)}, f32[19,768]{1,0:T(8,128)S(1)}, u32[]{:S(2)}, u32[]{:S(2)}) collective-permute-start(f32[19,768]{1,0:T(8,128)S(1)} %add.138), channel_id=1, source_target_pairs={{0,8},{4,12},{8,0},{12,4},{16,24},{20,28},{24,16},{28,20},{1,9},{5... | collective-permute-start | bytes 175112 | tf_op jit(solution)/shard_map/ppermute | solution.py:857
  196.5 14.9 %collective-permute-start.35 = (bf16[6,3,96,128]{3,2,1,0:T(8,128)(2,1)S(1)}, bf16[6,3,96,128]{3,2,1,0:T(8,128)(2,1)S(1)}, u32[]{:S(2)}, u32[]{:S(2)}) collective-permute-start(bf16[6,3,96,128]{3,2,1,0:T(8,128)(2,1)S(1)} %add_convert_fusion.8), channel_id=1, source_target_pairs={{0,2},{1,3},{2,0},{3,1},{4,6},{5,7},{6,4},{7,5},{8,10},{9,11},{10,... | collective-permute-start | bytes 1327112 | tf_op jit(solution)/shard_map/ppermute | solution.py:857
  197.7 13.7 %collective-permute-start.45 = (bf16[6,3,96,128]{3,2,1,0:T(8,128)(2,1)S(1)}, bf16[6,3,96,128]{3,2,1,0:T(8,128)(2,1)S(1)}, u32[]{:S(2)}, u32[]{:S(2)}) collective-permute-start(bf16[6,3,96,128]{3,2,1,0:T(8,128)(2,1)S(1)} %add_convert_fusion.4), channel_id=1, source_target_pairs={{0,8},{4,12},{24,16},{28,20},{1,9},{5,13},{25,17},{29,21},{2,10},{... | collective-permute-start | bytes 1327112 | tf_op jit(solution)/shard_map/ppermute | solution.py:862
  199.1 12.3 %collective-permute-start.44 = (bf16[6,3,96,128]{3,2,1,0:T(8,128)(2,1)S(1)}, bf16[6,3,96,128]{3,2,1,0:T(8,128)(2,1)S(1)}, u32[]{:S(2)}, u32[]{:S(2)}) collective-permute-start(bf16[6,3,96,128]{3,2,1,0:T(8,128)(2,1)S(1)} %add_convert_fusion.4), channel_id=1, source_target_pairs={{8,16},{12,20},{16,8},{20,12},{9,17},{13,21},{17,9},{21,13},{10,18... | collective-permute-start | bytes 1327112 | tf_op jit(solution)/shard_map/ppermute | solution.py:862
  203.6 6.6 %collective-permute-start.46 = (f32[19,768]{1,0:T(8,128)S(1)}, f32[19,768]{1,0:T(8,128)S(1)}, u32[]{:S(2)}, u32[]{:S(2)}) collective-permute-start(f32[19,768]{1,0:T(8,128)S(1)} %add.141), channel_id=1, source_target_pairs={{0,16},{4,20},{8,24},{12,28},{16,0},{20,4},{24,8},{28,12},{1,17},{... | collective-permute-start | bytes 175112 | tf_op jit(solution)/shard_map/ppermute | solution.py:857
  210.2 10.7 %collective-permute-start.48 = (bf16[6,3,96,128]{3,2,1,0:T(8,128)(2,1)}, bf16[6,3,96,128]{3,2,1,0:T(8,128)(2,1)}, u32[]{:S(2)}, u32[]{:S(2)}) collective-permute-start(bf16[6,3,96,128]{3,2,1,0:T(8,128)(2,1)} %add_convert_fusion.2), channel_id=1, source_target_pairs={{0,2},{1,3},{2,0},{3,1},{4,6},{5,7},{6,4},{7,5},{8,10},{9,11},{10,... | collective-permute-start | bytes 1327112 | tf_op jit(solution)/shard_map/ppermute | solution.py:857
  212.3 15.7 %copy-start.43 = (f32[16,768]{1,0:T(8,128)S(1)}, f32[16,768]{1,0:T(8,128)}, u32[]{:S(2)}) copy-start(f32[16,768]{1,0:T(8,128)} %param.34) | copy-start | bytes 147460
  212.3 15.6 %copy-start.44 = (f32[16,768]{1,0:T(8,128)S(1)}, f32[16,768]{1,0:T(8,128)}, u32[]{:S(2)}) copy-start(f32[16,768]{1,0:T(8,128)} %param.35) | copy-start | bytes 147460
  212.5 8.9 %collective-permute-start.49 = (bf16[6,3,96,128]{3,2,1,0:T(8,128)(2,1)S(1)}, bf16[6,3,96,128]{3,2,1,0:T(8,128)(2,1)S(1)}, u32[]{:S(2)}, u32[]{:S(2)}) collective-permute-start(bf16[6,3,96,128]{3,2,1,0:T(8,128)(2,1)S(1)} %add_convert_fusion.1), channel_id=1, source_target_pairs={{0,8},{4,12},{8,0},{12,4},{16,24},{20,28},{24,16},{28,20},{1,9},{5... | collective-permute-start | bytes 1327112 | tf_op jit(solution)/shard_map/ppermute | solution.py:862
  215.3 8.4 %collective-permute-start.47 = (bf16[6,3,96,128]{3,2,1,0:T(8,128)(2,1)S(1)}, bf16[6,3,96,128]{3,2,1,0:T(8,128)(2,1)S(1)}, u32[]{:S(2)}, u32[]{:S(2)}) collective-permute-start(bf16[6,3,96,128]{3,2,1,0:T(8,128)(2,1)S(1)} %add_convert_fusion.3), channel_id=1, source_target_pairs={{0,4},{4,0},{8,12},{12,8},{16,20},{20,16},{24,28},{28,24},{1,5},{5... | collective-permute-start | bytes 1327112 | tf_op jit(solution)/shard_map/ppermute | solution.py:857
  216.8 10.2 %collective-permute-start.50 = (bf16[6,3,96,128]{3,2,1,0:T(8,128)(2,1)S(1)}, bf16[6,3,96,128]{3,2,1,0:T(8,128)(2,1)S(1)}, u32[]{:S(2)}, u32[]{:S(2)}) collective-permute-start(bf16[6,3,96,128]{3,2,1,0:T(8,128)(2,1)S(1)} %copy-done.27), channel_id=1, source_target_pairs={{8,16},{12,20},{16,8},{20,12},{9,17},{13,21},{17,9},{21,13},{10,18... | collective-permute-start | bytes 1327112 | tf_op jit(solution)/shard_map/ppermute | solution.py:862
  227.0 8.5 %collective-permute-start.51 = (bf16[133,768]{1,0:T(8,128)(2,1)S(1)}, bf16[133,768]{1,0:T(8,128)(2,1)S(1)}, u32[]{:S(2)}, u32[]{:S(2)}) collective-permute-start(bf16[133,768]{1,0:T(8,128)(2,1)S(1)} %get-tuple-element.255), channel_id=1, source_target_pairs={{0,2},{1,3},{2,0},{3,1},{4,6},{5,7},{6,4},{7,5},{8,10},{9,11},{10,... | collective-permute-start | bytes 612872 | tf_op jit(solution)/shard_map/ppermute | solution.py:857
  (38 other events, 242.1 us)
